TPU v7x, 128 devices: a whole 4x4x4 slice. The times are simulated.
128 devices in a mesh: expert: 16 (over z, x), tensor: 8 (over y, core).
Axes of the slice: x: 4, y: 4, z: 4, core: 2. Of those that a mesh axis runs over, the one named last changes fastest.
Arguments:
- inputs: bfloat16 [4096, 2048], P(('expert', 'tensor')), may hold values from -6 to 6
- gain_attn: float32 [2048], P('expert'), may hold values from 0.5 to 1.5
- w_q: float32 [2048, 3072], P('expert', 'tensor'), may hold values from -0.125 to 0.125
- w_dkv: float32 [2048, 576], P('expert'), may hold values from -0.125 to 0.125
- gain_latent: float32 [512], P('expert'), may hold values from 0.5 to 1.5
- w_uk: float32 [512, 2048], P('expert', 'tensor'), may hold values from -0.25 to 0.25
- w_uv: float32 [512, 2048], P('expert', 'tensor'), may hold values from -0.25 to 0.25
- w_o: float32 [2048, 2048], P('tensor', 'expert'), may hold values from -1 to 1
- gain_ffn: float32 [2048], P('expert'), may hold values from 0.5 to 1.5
- w_router: float32 [2048, 64], P('expert'), may hold values from -0.0625 to 0.0625
- w_sg: float32 [2048, 2816], P('expert', 'tensor'), may hold values from -0.125 to 0.125
- w_su: float32 [2048, 2816], P('expert', 'tensor'), may hold values from -0.125 to 0.125
- w_sd: float32 [2816, 2048], P('tensor', 'expert'), may hold values from -0.109375 to 0.109375
- w_eg: float32 [64, 1408, 2048], P('expert', 'tensor'), may hold values from -0.125 to 0.125
- w_eu: float32 [64, 1408, 2048], P('expert', 'tensor'), may hold values from -0.125 to 0.125
- w_ed: float32 [64, 1408, 2048], P('expert', 'tensor'), may hold values from -4 to 4
- routes: int32 [4096, 6], P('expert'), may hold values from 0 to 63, all different within a row; in each aligned block of 256 rows (0 to 255, 256 to 511, ...) at most 36 rows name the same one
- seq_lengths: int32 [3], replicated, may hold values from 1 to 3968, 4096 in all
- piece_starts: int32 [8], replicated, may hold values from 0 to 3840, as said below
- out_grad: bfloat16 [4096, 2048], P(('expert', 'tensor')), may hold values from -6 to 6
Outputs:
- layer_out: bfloat16 [4096, 2048], P(('expert', 'tensor'))
- grad_inputs: bfloat16 [4096, 2048], P(('expert', 'tensor'))
- grad_gain_attn: float32 [2048], P('expert')
- grad_w_q: float32 [2048, 3072], P('expert', 'tensor')
- grad_w_dkv: float32 [2048, 576], P('expert')
- grad_gain_latent: float32 [512], P('expert')
- grad_w_uk: float32 [512, 2048], P('expert', 'tensor')
- grad_w_uv: float32 [512, 2048], P('expert', 'tensor')
- grad_w_o: float32 [2048, 2048], P('tensor', 'expert')
- grad_gain_ffn: float32 [2048], P('expert')
- grad_w_router: float32 [2048, 64], P('expert')
- grad_w_sg: float32 [2048, 2816], P('expert', 'tensor')
- grad_w_su: float32 [2048, 2816], P('expert', 'tensor')
- grad_w_sd: float32 [2816, 2048], P('tensor', 'expert')
- grad_w_eg: float32 [64, 1408, 2048], P('expert', 'tensor')
- grad_w_eu: float32 [64, 1408, 2048], P('expert', 'tensor')
- grad_w_ed: float32 [64, 1408, 2048], P('expert', 'tensor')
Inputs may be any that keep to these rules, and one draw needn't show every extreme that they name: `routes`: each row names 6 different experts; in the 256 rows of one index of the expert axis no expert is named more than 36 times, and in some such block one expert is named exactly 36 times. `seq_lengths`: the lengths sum to 4096; the longest is 3968. `piece_starts`: piece p starts within positions 2 * 256 * p to 2 * 256 * (p + 1) - 256, so pieces are disjoint and in order.
All inputs are finite; a program needn't handle non-finite values.
Results may differ from a plain program's by a relative error of at most 0.033.
Values may be sent and summed in bfloat16 or wider, within the bound.
No kernel may reach another device: no remote copies, remote signals or barrier semaphores. Data moves between devices by JAX's collectives and lax.ppermute only.
A program may use at most 320 MiB of HBM per device.

v0:
```python
import math

import jax
import jax.numpy as jnp
from jax import lax
from jax.sharding import PartitionSpec as P

DN = 128
DR = 64
TOP = 6
PIECE = 256


EPS = 1e-06
NEG = -1e30


def inv_rms(values):
    return lax.rsqrt(jnp.mean(values * values, axis=-1, keepdims=True) + EPS)


def norm_back(grad, normed, row_scale, gain):
    scaled = grad * gain
    inner_mean = jnp.mean(scaled * normed, axis=-1, keepdims=True)
    return (row_scale * (scaled - normed * inner_mean), jnp.sum(grad * normed, axis=0))


def rotate(values, cosine, sine):
    half_dim = values.shape[-1] // 2
    first_half = values[..., :half_dim]
    second = values[..., half_dim:]
    return jnp.concatenate(
        [first_half * cosine - second * sine, second * cosine + first_half * sine], axis=-1
    )


def unrotate(grad, cosine, sine):
    half_dim = grad.shape[-1] // 2
    first_half = grad[..., :half_dim]
    second = grad[..., half_dim:]
    return jnp.concatenate(
        [first_half * cosine + second * sine, second * cosine - first_half * sine], axis=-1
    )


def tables(position):
    inv_freq = 10000.0 ** (-(2.0 * jnp.arange(DR // 2, dtype=jnp.float32)) / DR)
    angles = position.astype(jnp.float32)[:, None] * inv_freq[None, :]
    return (jnp.cos(angles), jnp.sin(angles))


def locate(row_ids, seq_lengths, piece_starts):
    seq_ends = jnp.cumsum(seq_lengths)
    starts = seq_ends - seq_lengths
    member = (
        (row_ids[:, None] >= starts[None, :]) & (row_ids[:, None] < seq_ends[None, :])
    ).astype(jnp.int32)
    seq_id = jnp.sum(member * jnp.arange(seq_lengths.shape[0], dtype=jnp.int32)[None, :], axis=1)
    position = row_ids - jnp.sum(member * starts[None, :], axis=1)
    inside = (
        (row_ids[:, None] >= piece_starts[None, :])
        & (row_ids[:, None] < piece_starts[None, :] + PIECE)
    ).astype(jnp.int32)
    piece_id = (
        jnp.sum(inside * (jnp.arange(piece_starts.shape[0], dtype=jnp.int32) + 1)[None, :], axis=1)
        - 1
    )
    return (seq_id, position, piece_id)


def allowed(rows_q, seq_q, piece_q, rows_k, seq_k, piece_k):
    same_seq = seq_q[:, None] == seq_k[None, :]
    before = rows_k[None, :] <= rows_q[:, None]
    picture = (piece_q[:, None] == piece_k[None, :]) & (piece_q[:, None] >= 0)
    return same_seq & (before | picture)


def dot_nn(left, right):
    return jnp.dot(left, right, preferred_element_type=jnp.float32)


def dot_nt(left, right):
    return lax.dot_general(
        left, right, (((1,), (1,)), ((), ())), preferred_element_type=jnp.float32
    )


def dot_tn(left, right):
    return lax.dot_general(
        left, right, (((0,), (0,)), ((), ())), preferred_element_type=jnp.float32
    )


def silu_slope(values):
    sigmoid_v = jax.nn.sigmoid(values)
    return sigmoid_v * (1.0 + values * (1.0 - sigmoid_v))


def body(
    inputs,
    gain_attn,
    w_q,
    w_dkv,
    gain_latent,
    w_uk,
    w_uv,
    w_o,
    gain_ffn,
    w_router,
    w_sg,
    w_su,
    w_sd,
    w_eg,
    w_eu,
    w_ed,
    routes,
    seq_lengths,
    piece_starts,
    out_grad,
):
    half_type = jnp.bfloat16
    wide = jnp.float32
    tens_count = lax.axis_size("tensor")
    exp_count = lax.axis_size("expert")
    tens_index = lax.axis_index("tensor")
    exp_index = lax.axis_index("expert")
    own_rows = inputs.shape[0]
    group_rows = own_rows * tens_count
    head_count = w_q.shape[1] // (DN + DR)
    value_dim = w_o.shape[0] // head_count
    score_scale = (DN + DR) ** (-0.5)
    (
        wq_b,
        wuk_b,
        wuv_b,
        wo_b,
        wsg_b,
        wsu_b,
        wsd_b,
        wdkv_b,
        wrouter_b,
        gain_one_b,
        gain_two_b,
        gain_lat_b,
    ) = (
        lax.all_gather(w_q.astype(half_type), "expert", axis=0, tiled=True),
        lax.all_gather(w_uk.astype(half_type), "expert", axis=0, tiled=True),
        lax.all_gather(w_uv.astype(half_type), "expert", axis=0, tiled=True),
        lax.all_gather(w_o.astype(half_type), "expert", axis=1, tiled=True),
        lax.all_gather(w_sg.astype(half_type), "expert", axis=0, tiled=True),
        lax.all_gather(w_su.astype(half_type), "expert", axis=0, tiled=True),
        lax.all_gather(w_sd.astype(half_type), "expert", axis=1, tiled=True),
        lax.all_gather(w_dkv.astype(half_type), "expert", axis=0, tiled=True),
        lax.all_gather(w_router.astype(half_type), "expert", axis=0, tiled=True),
        lax.all_gather(gain_attn.astype(half_type), "expert", axis=0, tiled=True),
        lax.all_gather(gain_ffn.astype(half_type), "expert", axis=0, tiled=True),
        lax.all_gather(gain_latent.astype(half_type), "expert", axis=0, tiled=True),
    )
    gain_one = gain_one_b.astype(wide)
    gain_two = gain_two_b.astype(wide)
    gain_lat = gain_lat_b.astype(wide)
    weg_b = w_eg.astype(half_type)
    weu_b = w_eu.astype(half_type)
    wed_b = w_ed.astype(half_type)
    lat_dim = gain_lat.shape[0]
    in_rows, grad_rows_in = (
        lax.all_gather(inputs, "tensor", axis=0, tiled=True),
        lax.all_gather(out_grad, "tensor", axis=0, tiled=True),
    )
    in_wide = in_rows.astype(wide)
    out_wide = grad_rows_in.astype(wide)
    model_width = in_rows.shape[1]
    rows_q = exp_index * group_rows + jnp.arange(group_rows, dtype=jnp.int32)
    seq_q, pos_q, piece_q = locate(rows_q, seq_lengths, piece_starts)
    cos_q, sin_q = tables(pos_q)
    scale_one = inv_rms(in_wide)
    normed_one = in_wide * scale_one
    h_one = (normed_one * gain_one).astype(half_type)
    latent_all = dot_nn(h_one, wdkv_b)
    lat_part = latent_all[:, :lat_dim]
    scale_lat = inv_rms(lat_part)
    normed_lat = lat_part * scale_lat
    c_norm = (normed_lat * gain_lat).astype(half_type)
    k_rot = rotate(latent_all[:, lat_dim:], cos_q, sin_q).astype(half_type)
    q_raw = dot_nn(h_one, wq_b).reshape(group_rows, head_count, DN + DR)
    q_nope = q_raw[:, :, :DN].astype(half_type)
    q_pe = rotate(q_raw[:, :, DN:], cos_q[:, None, :], sin_q[:, None, :]).astype(half_type)
    key_local = dot_nn(c_norm, wuk_b).astype(half_type)
    val_local = dot_nn(c_norm, wuv_b).astype(half_type)
    key_all, val_all, rot_all = (
        lax.all_gather(key_local, "expert", axis=0, tiled=True),
        lax.all_gather(val_local, "expert", axis=0, tiled=True),
        lax.all_gather(k_rot, "expert", axis=0, tiled=True),
    )
    key_total = key_all.shape[0]
    key_block = math.gcd(key_total, 512)
    block_count = key_total // key_block
    rows_k = jnp.arange(key_total, dtype=jnp.int32)
    seq_k, pos_k, piece_k = locate(rows_k, seq_lengths, piece_starts)
    block_items = (
        key_all.reshape(block_count, key_block, head_count, DN),
        val_all.reshape(block_count, key_block, head_count, value_dim),
        rot_all.reshape(block_count, key_block, DR),
        rows_k.reshape(block_count, key_block),
        seq_k.reshape(block_count, key_block),
        piece_k.reshape(block_count, key_block),
    )

    def block_scores(block_item):
        key_blk, val_blk, rot_blk, rows_blk, seq_blk, piece_blk = block_item
        raw_scores = jnp.einsum("qhd,khd->hqk", q_nope, key_blk, preferred_element_type=wide)
        raw_scores = raw_scores + jnp.einsum(
            "qhd,kd->hqk", q_pe, rot_blk, preferred_element_type=wide
        )
        key_mask = allowed(rows_q, seq_q, piece_q, rows_blk, seq_blk, piece_blk)[None]
        return (raw_scores * score_scale, key_mask)

    def sweep_max(acc_state, block_item):
        row_top, row_sum = acc_state
        scores, key_mask = block_scores(block_item)
        new_top = jnp.maximum(row_top, jnp.max(jnp.where(key_mask, scores, NEG), axis=-1))
        row_sum = row_sum * jnp.exp(row_top - new_top) + jnp.sum(
            jnp.where(key_mask, jnp.exp(scores - new_top[..., None]), 0.0), axis=-1
        )
        return ((new_top, row_sum), None)

    (row_top, row_sum), unused_max = lax.scan(
        sweep_max,
        (jnp.full((head_count, group_rows), NEG, wide), jnp.zeros((head_count, group_rows), wide)),
        block_items,
    )
    log_total = row_top + jnp.log(row_sum)

    def sweep_out(acc_state, block_item):
        scores, key_mask = block_scores(block_item)
        weights = jnp.where(key_mask, jnp.exp(scores - log_total[..., None]), 0.0).astype(half_type)
        return (
            acc_state
            + jnp.einsum("hqk,khd->qhd", weights, block_item[1], preferred_element_type=wide),
            None,
        )

    attn_acc, unused_out = lax.scan(
        sweep_out, jnp.zeros((group_rows, head_count, value_dim), wide), block_items
    )
    attn_heads = attn_acc.astype(half_type).reshape(group_rows, head_count * value_dim)
    attn_out = lax.psum(dot_nn(attn_heads, wo_b).astype(jnp.bfloat16), "tensor").astype(jnp.float32)
    mid = in_wide + attn_out
    scale_two = inv_rms(mid)
    normed_two = mid * scale_two
    h_two = (normed_two * gain_two).astype(half_type)
    logits = dot_nn(h_two, wrouter_b)
    router_probs = jax.nn.softmax(logits, axis=-1)
    experts_all = logits.shape[1]
    choose = (routes[:, :, None] == jnp.arange(experts_all, dtype=jnp.int32)[None, None, :]).astype(
        wide
    )
    gate_values = jnp.sum(choose * router_probs[:, None, :], axis=-1).astype(half_type).astype(wide)
    shared_gate = dot_nn(h_two, wsg_b)
    shared_up = dot_nn(h_two, wsu_b)
    shared_hidden = (jax.nn.silu(shared_gate) * shared_up).astype(half_type)
    shared_out = dot_nn(shared_hidden, wsd_b)
    exp_local = w_eg.shape[0]
    slot_count = max(2, 3 * group_rows * TOP // (2 * experts_all))
    flat_routes = routes.reshape(-1)
    one_hot = (flat_routes[:, None] == jnp.arange(experts_all, dtype=jnp.int32)[None, :]).astype(
        jnp.int32
    )
    slot_rank = jnp.sum((jnp.cumsum(one_hot, axis=0) - 1) * one_hot, axis=1)
    pair_slot = flat_routes * slot_count + slot_rank
    pair_token = jnp.arange(group_rows * TOP, dtype=jnp.int32) // TOP
    slot_token = (
        jnp.full((experts_all * slot_count,), group_rows, jnp.int32).at[pair_slot].set(pair_token)
    )
    padded = jnp.concatenate([h_two, jnp.zeros((1, model_width), half_type)], axis=0)
    sending = padded[slot_token].reshape(exp_count, exp_local, slot_count, model_width)
    received = lax.all_to_all(sending, "expert", split_axis=0, concat_axis=0, tiled=True)
    expert_gate = jnp.einsum("sjcd,jfd->sjcf", received, weg_b, preferred_element_type=wide)
    expert_up = jnp.einsum("sjcd,jfd->sjcf", received, weu_b, preferred_element_type=wide)
    expert_hidden = (jax.nn.silu(expert_gate) * expert_up).astype(half_type)
    expert_out = jnp.einsum("sjcf,jfd->sjcd", expert_hidden, wed_b, preferred_element_type=wide)
    returned = lax.all_to_all(
        expert_out.astype(jnp.bfloat16), "expert", split_axis=0, concat_axis=0, tiled=True
    ).astype(expert_out.dtype)
    returned, kept_in, gate_pre, up_pre = (returned, received, expert_gate, expert_up)
    back_width = returned.shape[-1]
    slot_out = returned.reshape(experts_all * slot_count, back_width)
    pair_out = slot_out[pair_slot].reshape(group_rows, TOP, back_width)
    routed_out = jnp.sum(gate_values[:, :, None] * pair_out, axis=1)
    ffn_part = shared_out + routed_out
    ffn_own = lax.psum_scatter(
        ffn_part.astype(jnp.bfloat16), "tensor", scatter_dimension=0, tiled=True
    ).astype(jnp.float32)
    mid_own = lax.dynamic_slice_in_dim(mid, tens_index * own_rows, own_rows, 0)
    layer_out = (mid_own + ffn_own).astype(half_type)
    d_shared_hidden = dot_nt(grad_rows_in, wsd_b)
    grad_sd = dot_tn(shared_hidden, grad_rows_in)
    d_shared_gate = (d_shared_hidden * shared_up * silu_slope(shared_gate)).astype(half_type)
    d_shared_up = (d_shared_hidden * jax.nn.silu(shared_gate)).astype(half_type)
    grad_sg = dot_tn(h_two, d_shared_gate)
    grad_su = dot_tn(h_two, d_shared_up)
    d_h_part = dot_nt(d_shared_gate, wsg_b) + dot_nt(d_shared_up, wsu_b)
    d_gate_part = jnp.sum(pair_out * out_wide[:, None, :], axis=-1)
    slot_gate = (
        jnp.zeros((experts_all * slot_count,), wide).at[pair_slot].set(gate_values.reshape(-1))
    )
    grad_padded = jnp.concatenate([grad_rows_in, jnp.zeros((1, model_width), half_type)], axis=0)
    d_slots = (slot_gate[:, None] * grad_padded[slot_token].astype(wide)).astype(half_type)
    d_slots = d_slots.reshape(exp_count, exp_local, slot_count, model_width)
    d_received = lax.all_to_all(d_slots, "expert", split_axis=0, concat_axis=0, tiled=True)
    hidden_again = (jax.nn.silu(gate_pre) * up_pre).astype(half_type)
    d_expert_hidden = jnp.einsum("sjcd,jfd->sjcf", d_received, wed_b, preferred_element_type=wide)
    grad_ed = jnp.einsum("sjcf,sjcd->jfd", hidden_again, d_received, preferred_element_type=wide)
    d_expert_gate = (d_expert_hidden * up_pre * silu_slope(gate_pre)).astype(half_type)
    d_expert_up = (d_expert_hidden * jax.nn.silu(gate_pre)).astype(half_type)
    grad_eg = jnp.einsum("sjcf,sjcd->jfd", d_expert_gate, kept_in, preferred_element_type=wide)
    grad_eu = jnp.einsum("sjcf,sjcd->jfd", d_expert_up, kept_in, preferred_element_type=wide)
    d_expert_in = jnp.einsum("sjcf,jfd->sjcd", d_expert_gate, weg_b, preferred_element_type=wide)
    d_expert_in = d_expert_in + jnp.einsum(
        "sjcf,jfd->sjcd", d_expert_up, weu_b, preferred_element_type=wide
    )
    d_back = lax.all_to_all(
        d_expert_in.astype(jnp.bfloat16), "expert", split_axis=0, concat_axis=0, tiled=True
    ).astype(d_expert_in.dtype)
    d_pair = d_back.reshape(experts_all * slot_count, model_width)[pair_slot].reshape(
        group_rows, TOP, model_width
    )
    d_h_part = d_h_part + jnp.sum(d_pair, axis=1)
    d_h_sum, d_gate = (
        lax.psum(d_h_part.astype(jnp.bfloat16), "tensor").astype(jnp.float32),
        lax.psum(d_gate_part.astype(jnp.bfloat16), "tensor").astype(jnp.float32),
    )
    d_router = jnp.sum(d_gate[:, :, None] * choose, axis=1)
    d_logits = (
        router_probs * (d_router - jnp.sum(router_probs * d_router, axis=-1, keepdims=True))
    ).astype(half_type)
    grad_router = dot_tn(h_two, d_logits)
    d_h_two = d_h_sum + dot_nt(d_logits, wrouter_b)
    d_mid_norm, grad_gain_two = norm_back(d_h_two, normed_two, scale_two, gain_two)
    d_mid = d_mid_norm + out_wide
    d_attn_b = d_mid.astype(half_type)
    grad_o = dot_tn(attn_heads, d_attn_b)
    d_heads = dot_nt(d_attn_b, wo_b).astype(half_type).reshape(group_rows, head_count, value_dim)

    def sweep_delta(acc_state, block_item):
        scores, key_mask = block_scores(block_item)
        weights = jnp.where(key_mask, jnp.exp(scores - log_total[..., None]), 0.0)
        d_probs = jnp.einsum("qhd,khd->hqk", d_heads, block_item[1], preferred_element_type=wide)
        return (acc_state + jnp.sum(weights * d_probs, axis=-1), None)

    row_delta, unused_delta = lax.scan(
        sweep_delta, jnp.zeros((head_count, group_rows), wide), block_items
    )

    def sweep_grad(acc_state, block_item):
        dq_nope, dq_pe = acc_state
        scores, key_mask = block_scores(block_item)
        weights = jnp.where(key_mask, jnp.exp(scores - log_total[..., None]), 0.0)
        d_probs = jnp.einsum("qhd,khd->hqk", d_heads, block_item[1], preferred_element_type=wide)
        d_scores = (weights * (d_probs - row_delta[..., None])).astype(half_type)
        dq_nope = dq_nope + jnp.einsum(
            "hqk,khd->qhd", d_scores, block_item[0], preferred_element_type=wide
        )
        dq_pe = dq_pe + jnp.einsum(
            "hqk,kd->qhd", d_scores, block_item[2], preferred_element_type=wide
        )
        d_keys = (
            jnp.einsum("hqk,qhd->khd", d_scores, q_nope, preferred_element_type=wide) * score_scale
        )
        d_rot = jnp.einsum("hqk,qhd->kd", d_scores, q_pe, preferred_element_type=wide) * score_scale
        d_vals = jnp.einsum(
            "hqk,qhd->khd", weights.astype(half_type), d_heads, preferred_element_type=wide
        )
        return ((dq_nope, dq_pe), (d_keys, d_vals, d_rot))

    (dq_nope, dq_pe), (dk_blocks, dv_blocks, dr_blocks) = lax.scan(
        sweep_grad,
        (
            jnp.zeros((group_rows, head_count, DN), wide),
            jnp.zeros((group_rows, head_count, DR), wide),
        ),
        block_items,
    )
    dq_pe_raw = unrotate(dq_pe * score_scale, cos_q[:, None, :], sin_q[:, None, :])
    d_queries = (
        jnp.concatenate([dq_nope * score_scale, dq_pe_raw], axis=-1)
        .astype(half_type)
        .reshape(group_rows, -1)
    )
    grad_q = dot_tn(h_one, d_queries)
    d_one_part = dot_nt(d_queries, wq_b)
    d_key_rows, d_val_rows, d_rot_rows = (
        lax.psum_scatter(
            dk_blocks.reshape(key_total, -1).astype(jnp.bfloat16),
            "expert",
            scatter_dimension=0,
            tiled=True,
        ).astype(jnp.float32),
        lax.psum_scatter(
            dv_blocks.reshape(key_total, -1).astype(jnp.bfloat16),
            "expert",
            scatter_dimension=0,
            tiled=True,
        ).astype(jnp.float32),
        lax.psum_scatter(
            dr_blocks.reshape(key_total, DR).astype(jnp.bfloat16),
            "expert",
            scatter_dimension=0,
            tiled=True,
        ).astype(jnp.float32),
    )
    d_key_b = d_key_rows.astype(half_type)
    d_val_b = d_val_rows.astype(half_type)
    grad_uk = dot_tn(c_norm, d_key_b)
    grad_uv = dot_tn(c_norm, d_val_b)
    d_cnorm_part = dot_nt(d_key_b, wuk_b) + dot_nt(d_val_b, wuv_b)
    d_one_sum, d_cnorm, d_rot_sum = (
        lax.psum(d_one_part.astype(jnp.bfloat16), "tensor").astype(jnp.float32),
        lax.psum(d_cnorm_part.astype(jnp.bfloat16), "tensor").astype(jnp.float32),
        lax.psum(d_rot_rows.astype(jnp.bfloat16), "tensor").astype(jnp.float32),
    )
    d_kpe = unrotate(d_rot_sum, cos_q, sin_q)
    d_lat, grad_gain_lat = norm_back(d_cnorm, normed_lat, scale_lat, gain_lat)
    d_latent_all = jnp.concatenate([d_lat, d_kpe], axis=-1).astype(half_type)
    grad_dkv = dot_tn(h_one, d_latent_all)
    d_h_one = d_one_sum + dot_nt(d_latent_all, wdkv_b)
    d_in_norm, grad_gain_one = norm_back(d_h_one, normed_one, scale_one, gain_one)
    d_inputs = d_in_norm + d_mid
    grad_inputs = lax.dynamic_slice_in_dim(d_inputs, tens_index * own_rows, own_rows, 0).astype(
        half_type
    )
    (
        sum_q,
        sum_uk,
        sum_uv,
        sum_o,
        sum_sg,
        sum_su,
        sum_sd,
        sum_dkv,
        sum_router,
        sum_gain_one,
        sum_gain_two,
        sum_gain_lat,
    ) = (
        lax.psum_scatter(
            grad_q.astype(jnp.bfloat16), "expert", scatter_dimension=0, tiled=True
        ).astype(jnp.float32),
        lax.psum_scatter(
            grad_uk.astype(jnp.bfloat16), "expert", scatter_dimension=0, tiled=True
        ).astype(jnp.float32),
        lax.psum_scatter(
            grad_uv.astype(jnp.bfloat16), "expert", scatter_dimension=0, tiled=True
        ).astype(jnp.float32),
        lax.psum_scatter(
            grad_o.astype(jnp.bfloat16), "expert", scatter_dimension=1, tiled=True
        ).astype(jnp.float32),
        lax.psum_scatter(
            grad_sg.astype(jnp.bfloat16), "expert", scatter_dimension=0, tiled=True
        ).astype(jnp.float32),
        lax.psum_scatter(
            grad_su.astype(jnp.bfloat16), "expert", scatter_dimension=0, tiled=True
        ).astype(jnp.float32),
        lax.psum_scatter(
            grad_sd.astype(jnp.bfloat16), "expert", scatter_dimension=1, tiled=True
        ).astype(jnp.float32),
        lax.psum_scatter(
            grad_dkv.astype(jnp.bfloat16), "expert", scatter_dimension=0, tiled=True
        ).astype(jnp.float32),
        lax.psum_scatter(
            grad_router.astype(jnp.bfloat16), "expert", scatter_dimension=0, tiled=True
        ).astype(jnp.float32),
        lax.psum_scatter(
            grad_gain_one.astype(jnp.bfloat16), "expert", scatter_dimension=0, tiled=True
        ).astype(jnp.float32),
        lax.psum_scatter(
            grad_gain_two.astype(jnp.bfloat16), "expert", scatter_dimension=0, tiled=True
        ).astype(jnp.float32),
        lax.psum_scatter(
            grad_gain_lat.astype(jnp.bfloat16), "expert", scatter_dimension=0, tiled=True
        ).astype(jnp.float32),
    )
    return (
        layer_out,
        grad_inputs,
        sum_gain_one,
        sum_q,
        sum_dkv,
        sum_gain_lat,
        sum_uk,
        sum_uv,
        sum_o,
        sum_gain_two,
        sum_router,
        sum_sg,
        sum_su,
        sum_sd,
        grad_eg,
        grad_eu,
        grad_ed,
    )


def solution(mesh):
    placed = (
        P(("expert", "tensor"), None),
        P("expert"),
        P("expert", "tensor"),
        P("expert", None),
        P("expert"),
        P("expert", "tensor"),
        P("expert", "tensor"),
        P("tensor", "expert"),
        P("expert"),
        P("expert", None),
        P("expert", "tensor"),
        P("expert", "tensor"),
        P("tensor", "expert"),
        P("expert", "tensor", None),
        P("expert", "tensor", None),
        P("expert", "tensor", None),
        P("expert", None),
        P(),
        P(),
        P(("expert", "tensor"), None),
    )
    return jax.shard_map(
        body,
        mesh=mesh,
        in_specs=placed,
        out_specs=(
            P(("expert", "tensor"), None),
            P(("expert", "tensor"), None),
            P("expert"),
            P("expert", "tensor"),
            P("expert", None),
            P("expert"),
            P("expert", "tensor"),
            P("expert", "tensor"),
            P("tensor", "expert"),
            P("expert"),
            P("expert", None),
            P("expert", "tensor"),
            P("expert", "tensor"),
            P("tensor", "expert"),
            P("expert", "tensor", None),
            P("expert", "tensor", None),
            P("expert", "tensor", None),
        ),
        check_vma=False,
    )
```

profile of v0, /device:TPU:1, one launch (start us, length us, event | category | flops | bytes accessed | tf_op | source)
XLA Modules:
  0.0 2521.3 jit_solution(12175521363459221731)
XLA Ops:
  12.0 18.9 all-gather
  33.9 30.1 %all-reduce.2 = bf16[512]{0:T(512)(128)(2,1)S(1)} all-reduce(bf16[512]{0:T(512)(128)(2,1)S(1)} %dynamic-update-slice), channel_id=1, replica_groups=mesh['expert'=16,'tensor'=8] {'expert'}, use_global_device_ids=true, to_apply=%add.2 | all-reduce | flops 512 | bytes 2048
  64.7 17.1 all_gather.57
  91.9 18.4 all_gather.55
  115.1 15.6 all-gather.1
  131.4 18.1 reduce-window.19
  154.6 19.7 all_gather.60
  187.3 28.6 %while.54 = (s32[]{:T(128)}, f32[2,256]{1,0:T(2,128)S(1)}, f32[2,256]{1,0:T(2,128)S(1)}, s32[256]{0:T(256)S(1)}, s32[8,512]{1,0:T(8,128)}, /*index=5*/s32[8,512]...) while((s32[]{:T(128)}, f32[2,256]{1,0:T(2,128)S(1)}, ...), condition=%wide.region_11.12_spmd.clone, body=%wide.region_8.11_spmd.clone.sunk | while | flops 103287808 | bytes 5163176 | solution.py:227
  216.5 12.1 all-gather.17.cloned.1.call-done
  232.5 57.9 %while.55 = (s32[]{:T(128)}, f32[256,2,128]{0,2,1:T(8,128)}, bf16[8,512,2,128]{3,2,1,0:T(2,128)(2,1)}, s32[256]{0:T(256)S(1)}, s32[8,512]{1,0:T(8,128)}, /*index...) while((s32[]{:T(128)}, f32[256,2,128]{0,2,1:T(8,128)}, ...), condition=%wide.region_13.14_spmd.clone, body=%wide.region_12.13_spmd.clone.sunk | while | flops 170000896 | bytes 5269739 | solution.py:243
  301.7 56.7 %all-reduce.12.cloned.1.call-done = bf16[256,2048]{1,0:T(8,128)(2,1)} async-done(((bf16[256,2048]{1,0:T(8,128)(2,1)}), bf16[256,2048]{1,0:T(8,128)(2,1)}) %all-reduce.12.cloned.1.call-update) | async-done | bytes 1048592 | tf_op jit(solution)/shard_map/psum | solution.py:247
  361.0 10.0 gather_fusion
  371.0 13.1 reshape.755
  384.0 12.3 copy.263
  403.9 145.6 %all_gather.66 = bf16[2048,64]{0,1:T(8,128)(2,1)S(1)} all-gather(bf16[128,64]{0,1:T(8,128)(2,1)S(1)} %convert_element_type.354), channel_id=1, replica_groups=mesh['expert'=16,'tensor'=8] {'expert'}, dimensions={0}, use_global_device_ids=true | all-gather | bytes 278528 | tf_op jit(solution)/shard_map/all_gather | solution.py:154
  551.0 9.8 gather_fusion.2
  560.8 14.5 reshape.766
  591.1 19.4 copy.270
  615.9 13.1 fusion.100
  629.0 13.2 fusion.102
  642.2 95.4 %all-to-all-done.2 = bf16[16,4,36,2048]{3,1,2,0:T(4,128)(2,1)} async-done(((bf16[16,4,36,2048]{3,1,2,0:T(4,128)(2,1)}), bf16[16,4,36,2048]{3,1,2,0:T(4,128)(2,1)}, u32[]{:S(2)}, u32[]{:S(2)}) %all-to-all-start.2) | async-done | bytes 9437216 | tf_op jit(solution)/shard_map/all_to_all | solution.py:310
  737.7 15.6 fusion.123
  753.3 13.6 fusion.115
  766.8 13.6 fusion.91
  780.4 12.7 copy.272
  808.2 19.4 copy.266
  827.6 107.5 %all-to-all-done.3 = bf16[16,4,36,2048]{3,1,2,0:T(4,128)(2,1)} async-done(((bf16[16,4,36,2048]{3,1,2,0:T(4,128)(2,1)}), bf16[16,4,36,2048]{3,1,2,0:T(4,128)(2,1)}, u32[]{:S(2)}, u32[]{:S(2)}) %all-to-all-start.3) | async-done | bytes 9437216 | tf_op jit(solution)/shard_map/all_to_all | solution.py:322
  935.1 9.2 all-to-all-start.1
  952.6 135.8 %all-gather.27.cloned.1.call-done = bf16[2048,352]{0,1:T(8,128)(2,1)} async-done(((bf16[128,352]{0,1:T(8,128)(2,1)}), bf16[2048,352]{0,1:T(8,128)(2,1)}) %all-gather.27.cloned.1.call-update) | async-done | bytes 1441808 | tf_op jit(solution)/shard_map/all_gather | solution.py:151
  1091.0 45.3 %all-gather.29.cloned.1.call-done = bf16[352,2048]{1,0:T(8,128)(2,1)} async-done(((bf16[352,128]{1,0:T(8,128)(2,1)}), bf16[352,2048]{1,0:T(8,128)(2,1)}) %all-gather.29.cloned.1.call-update) | async-done | bytes 1441808 | tf_op jit(solution)/shard_map/all_gather | solution.py:152
  1140.6 15.5 copy_convert_fusion
  1156.1 21.3 copy.274
  1177.4 19.3 reshape.768
  1196.7 18.9 gather_fusion.3
  1215.6 15.0 reshape.761
  1230.6 9.9 reduce_sum.231
  1244.0 15.5 copy_convert_fusion.1
  1259.5 21.5 copy.268
  1281.1 19.4 reshape.764
  1300.5 18.9 gather_fusion.1
  1319.4 15.0 reshape.758
  1334.5 12.3 multiply_reduce_fusion
  1346.8 13.7 psum.44
  1367.0 45.5 %while.56 = (s32[]{:T(128)}, f32[2,256]{1,0:T(2,128)S(1)}, s32[256]{0:T(256)S(1)}, s32[8,512]{1,0:T(8,128)}, s32[8,512]{1,0:T(8,128)}, /*index=5*/s32[256]{0:T(2...) while((s32[]{:T(128)}, f32[2,256]{1,0:T(2,128)S(1)}, ...), condition=%wide.region_35.36_spmd.clone, body=%wide.region_33.35_spmd.clone.sunk | while | flops 170132480 | bytes 5409971 | solution.py:351
  1412.5 86.7 %while.57 = (s32[]{:T(128)}, f32[256,2,128]{0,2,1:T(8,128)S(1)}, f32[256,2,64]{0,2,1:T(8,128)S(1)}, bf16[8,512,2,128]{3,1,2,0:T(8,128)(2,1)}, bf16[8,512,2,128]{...) while((s32[]{:T(128)}, f32[256,2,128]{0,2,1:T(8,128)S(1)}, ...), condition=%wide.region_37.38_spmd.clone, body=%wide.region_36.37_spmd.clone.sunk | while | flops 439452160 | bytes 11697884 | solution.py:376
  1538.8 39.8 %reduce-scatter.28.cloned.1.call-done = bf16[256,256]{0,1:T(8,128)(2,1)} async-done(((bf16[4096,256]{0,1:T(8,128)(2,1)}), bf16[256,256]{0,1:T(8,128)(2,1)}) %reduce-scatter.28.cloned.1.call-update) | async-done | bytes 131088 | tf_op jit(solution)/shard_map/reduce_scatter | solution.py:393
  1579.7 75.9 %reduce-scatter.30.cloned.1.call-done = bf16[256,256]{0,1:T(8,128)(2,1)} async-done(((bf16[4096,256]{0,1:T(8,128)(2,1)}), bf16[256,256]{0,1:T(8,128)(2,1)}) %reduce-scatter.30.cloned.1.call-update) | async-done | bytes 131088 | tf_op jit(solution)/shard_map/reduce_scatter | solution.py:399
  1673.1 59.1 %reduce-scatter.46.cloned.1.call-done = bf16[128,352]{1,0:T(8,128)(2,1)} async-done(((bf16[2048,352]{1,0:T(8,128)(2,1)}), bf16[128,352]{1,0:T(8,128)(2,1)}) %reduce-scatter.46.cloned.1.call-update) | async-done | bytes 90128
  1733.9 74.3 %reduce-scatter.48.cloned.1.call-done = bf16[128,352]{1,0:T(8,128)(2,1)} async-done(((bf16[2048,352]{1,0:T(8,128)(2,1)}), bf16[128,352]{1,0:T(8,128)(2,1)}) %reduce-scatter.48.cloned.1.call-update) | async-done | bytes 90128
  1809.9 74.3 %reduce-scatter.50.cloned.1.call-done = bf16[128,352]{1,0:T(8,128)(2,1)} async-done(((bf16[2048,352]{1,0:T(8,128)(2,1)}), bf16[128,352]{1,0:T(8,128)(2,1)}) %reduce-scatter.50.cloned.1.call-update) | async-done | bytes 90128
  1885.9 73.0 %reduce-scatter.32.cloned.1.call-done = bf16[256,64]{0,1:T(8,128)(2,1)} async-done(((bf16[4096,64]{0,1:T(8,128)(2,1)}), bf16[256,64]{0,1:T(8,128)(2,1)}) %reduce-scatter.32.cloned.1.call-update) | async-done | bytes 32784 | tf_op jit(solution)/shard_map/reduce_scatter | solution.py:405
  1958.9 23.4 psum.47
  1983.6 40.8 %all-reduce.16.cloned.1.call-done = (bf16[256,2048]{1,0:T(8,128)(2,1)}, bf16[256,512]{0,1:T(8,128)(2,1)}) async-done(((bf16[256,2048]{1,0:T(8,128)(2,1)}, bf16[256,512]{0,1:T(8,128)(2,1)}), (bf16[256,2048]{1,0:T(8,128)(2,1)}, bf16[256,512]{0,1:T(8,128)(2,1)})) %all-reduce.16.cloned.1.call-update) | async-done | bytes 1310736 | tf_op jit(solution)/shard_map/psum | solution.py:418
  2035.1 17.5 fusion.110
  2052.6 17.7 fusion.104
  2070.3 17.7 fusion.107
  2088.1 12.0 reduce-scatter.44.cloned.1.call-done
  2101.5 30.9 %reduce-scatter.26.cloned.1.call-done = bf16[32,2048]{1,0:T(8,128)(2,1)} async-done(((bf16[256,2048]{1,0:T(8,128)(2,1)}), bf16[32,2048]{1,0:T(8,128)(2,1)}) %reduce-scatter.26.cloned.1.call-update) | async-done | bytes 131088 | tf_op jit(solution)/shard_map/reduce_scatter | solution.py:291
  2134.1 74.6 %reduce-scatter.42.cloned.1.call-done = bf16[128,256]{1,0:T(8,128)(2,1)} async-done(((bf16[2048,256]{1,0:T(8,128)(2,1)}), bf16[128,256]{1,0:T(8,128)(2,1)}) %reduce-scatter.42.cloned.1.call-update) | async-done | bytes 65552
  2210.4 74.9 %reduce-scatter.34.cloned.1.call-done = bf16[128,384]{1,0:T(8,128)(2,1)} async-done(((bf16[2048,384]{1,0:T(8,128)(2,1)}), bf16[128,384]{1,0:T(8,128)(2,1)}) %reduce-scatter.34.cloned.1.call-update) | async-done | bytes 98320 | tf_op jit(solution)/shard_map/reduce_scatter | solution.py:446
  2286.8 73.0 %reduce-scatter.36.cloned.1.call-done = bf16[32,256]{1,0:T(8,128)(2,1)} async-done(((bf16[512,256]{1,0:T(8,128)(2,1)}), bf16[32,256]{1,0:T(8,128)(2,1)}) %reduce-scatter.36.cloned.1.call-update) | async-done | bytes 16400 | tf_op jit(solution)/shard_map/reduce_scatter | solution.py:449
  2361.2 73.2 %reduce-scatter.38.cloned.1.call-done = bf16[32,256]{1,0:T(8,128)(2,1)} async-done(((bf16[512,256]{1,0:T(8,128)(2,1)}), bf16[32,256]{1,0:T(8,128)(2,1)}) %reduce-scatter.38.cloned.1.call-update) | async-done | bytes 16400 | tf_op jit(solution)/shard_map/reduce_scatter | solution.py:452
  2440.8 32.8 %all-reduce.6 = (bf16[2048]{0:T(1024)(128)(2,1)S(1)}, bf16[512]{0:T(512)(128)(2,1)S(1)}, bf16[2048]{0:T(1024)(128)(2,1)S(1)}) all-reduce(bf16[2048]{0:T(1024)(128)(2,1)S(1)} %get-tuple-element.935, bf16[512]{0:T(512)(128)(2,1)S(1)} %get-tuple-element.937, ...), channel_id=6, replica_groups=mesh['expert'=16,'tensor'=8] {'expert'}, use_global_device_ids=true, to_apply=%region_47.48.clone | all-reduce | flops 4608 | bytes 18432
  2477.2 35.5 %reduce-scatter.40.cloned.1.call-done = bf16[128,576]{1,0:T(8,128)(2,1)} async-done(((bf16[2048,576]{1,0:T(8,128)(2,1)}), bf16[128,576]{1,0:T(8,128)(2,1)}) %reduce-scatter.40.cloned.1.call-update) | async-done | bytes 147472
  (795 shorter events, 438.9 us)
Async XLA Ops:
  7.2 74.7 %all-gather.13.cloned.1.call-start = ((), (), s32[]{:S(2)}) async-start(), calls=%async_computation.17 | async-start | bytes 1179648 | tf_op jit(solution)/shard_map/all_gather | solution.py:167
  7.9 79.7 %all-gather.15.cloned.1.call-start = ((), (), s32[]{:S(2)}) async-start(), calls=%async_computation.18 | async-start | bytes 2506752 | tf_op jit(solution)/shard_map/all_gather | solution.py:153
  9.6 142.3 %all-gather.21.cloned.1.call-start = ((), (), s32[]{:S(2)}) async-start(), calls=%async_computation.21 | async-start | bytes 1671168 | tf_op jit(solution)/shard_map/all_gather | solution.py:146
  11.3 170.1 %all-gather.19.cloned.1.call-start = ((), (), s32[]{:S(2)}) async-start(), calls=%async_computation.20 | async-start | bytes 2228224 | tf_op jit(solution)/shard_map/all_gather | solution.py:191
  31.0 121.0 %copy-start.67 = (f32[16,1,128]{2,1,0:T(1,128)}, f32[16,1,128]{2,1,0:T(1,128)S(1)}, u32[]{:S(2)}) copy-start(f32[16,1,128]{2,1,0:T(1,128)S(1)} %convert_element_type.425) | copy-start | bytes 24580
  63.9 26.8 %copy-start.72 = (f32[512]{0:T(512)}, f32[512]{0:T(512)S(1)}, u32[]{:S(2)}) copy-start(f32[512]{0:T(512)S(1)} %convert_element_type.335) | copy-start | bytes 6148
  83.5 68.5 %copy-start.81 = (f32[256]{0:T(256)}, f32[256]{0:T(256)S(1)}, u32[]{:S(2)}) copy-start(f32[256]{0:T(256)S(1)} %add_rsqrt_fusion.2) | copy-start | bytes 3076
  90.5 63.8 %copy-start.20 = (f32[256,576]{0,1:T(8,128)}, f32[256,576]{0,1:T(8,128)S(1)}, u32[]{:S(2)}) copy-start(f32[256,576]{0,1:T(8,128)S(1)} %fusion.185) | copy-start | bytes 1769476
  90.9 40.5 %copy-start.22 = (bf16[256,512]{0,1:T(8,128)(2,1)}, bf16[256,512]{0,1:T(8,128)(2,1)S(1)}, u32[]{:S(2)}) copy-start(bf16[256,512]{0,1:T(8,128)(2,1)S(1)} %multiply_convert_fusion.3) | copy-start | bytes 786436
  91.8 136.7 %all-gather.17.cloned.1.call-start = ((), (), s32[]{:S(2)}) async-start(), calls=%async_computation.19 | async-start | bytes 2228224 | tf_op jit(solution)/shard_map/all_gather | solution.py:192
  111.3 180.5 %all-gather.23.cloned.1.call-start = ((), (), s32[]{:S(2)}) async-start(), calls=%async_computation.22 | async-start | bytes 1114112 | tf_op jit(solution)/shard_map/all_gather | solution.py:149
  112.1 246.4 %all-reduce.12.cloned.1.call-start = ((), (), s32[]{:S(2)}) async-start(), calls=%async_computation.23 | async-start | bytes 2097152 | tf_op jit(solution)/shard_map/psum | solution.py:247
  112.1 42.3 %copy-start.92 = (f32[32]{0:T(128)}, f32[32]{0:T(128)S(1)}, u32[]{:S(2)}) copy-start(f32[32]{0:T(128)S(1)} %multiply_power_fusion) | copy-start | bytes 388
  113.8 40.6 %copy-start.88 = (f32[256]{0:T(256)}, f32[256]{0:T(256)S(1)}, u32[]{:S(2)}) copy-start(f32[256]{0:T(256)S(1)} %subtract_convert_fusion.2) | copy-start | bytes 3076
  154.6 30.7 %copy-start.55 = (f32[256,32]{0,1:T(8,128)}, f32[256,32]{0,1:T(8,128)S(1)}, u32[]{:S(2)}) copy-start(f32[256,32]{0,1:T(8,128)S(1)} %get-tuple-element.1098) | copy-start | bytes 98308
  154.6 30.7 %copy-start.57 = (f32[256,32]{0,1:T(8,128)}, f32[256,32]{0,1:T(8,128)S(1)}, u32[]{:S(2)}) copy-start(f32[256,32]{0,1:T(8,128)S(1)} %get-tuple-element.1099) | copy-start | bytes 98308
  290.5 69.8 %copy-start = (bf16[256,2,128]{2,0,1:T(8,128)(2,1)}, bf16[256,2,128]{2,0,1:T(8,128)(2,1)S(1)}, u32[]{:S(2)}) copy-start(bf16[256,2,128]{2,0,1:T(8,128)(2,1)S(1)} %get-tuple-element.1745) | copy-start | bytes 393220
  290.5 69.8 %copy-start.4 = (bf16[8,512,2,128]{3,1,2,0:T(8,128)(2,1)}, bf16[8,512,2,128]{3,1,2,0:T(8,128)(2,1)S(1)}, u32[]{:S(2)}) copy-start(bf16[8,512,2,128]{3,1,2,0:T(8,128)(2,1)S(1)} %get-tuple-element.1756) | copy-start | bytes 6291460
  290.5 69.8 %copy-start.12 = (bf16[256,2,64]{0,2,1:T(8,128)(2,1)}, bf16[256,2,64]{0,2,1:T(8,128)(2,1)S(1)}, u32[]{:S(2)}) copy-start(bf16[256,2,64]{0,2,1:T(8,128)(2,1)S(1)} %get-tuple-element.1761) | copy-start | bytes 196612
  290.5 69.8 %copy-start.51 = (s32[256]{0:T(256)}, s32[256]{0:T(256)S(1)}, u32[]{:S(2)}) copy-start(s32[256]{0:T(256)S(1)} %get-tuple-element.1820) | copy-start | bytes 3076
  290.5 69.8 %copy-start.53 = (s32[256]{0:T(256)}, s32[256]{0:T(256)S(1)}, u32[]{:S(2)}) copy-start(s32[256]{0:T(256)S(1)} %get-tuple-element.1823) | copy-start | bytes 3076
  290.5 67.9 %copy-start.6 = (bf16[256,2048]{1,0:T(8,128)(2,1)S(1)}, bf16[256,2048]{1,0:T(8,128)(2,1)}, u32[]{:S(2)}) copy-start(bf16[256,2048]{1,0:T(8,128)(2,1)} %all-gather.13.cloned.1.call-done) | copy-start | bytes 3145732
  291.8 68.4 %copy-start.42 = (bf16[256,2,128]{0,2,1:T(8,128)(2,1)}, bf16[256,2,128]{0,2,1:T(8,128)(2,1)S(1)}, u32[]{:S(2)}) copy-start(bf16[256,2,128]{0,2,1:T(8,128)(2,1)S(1)} %convert_element_type.343) | copy-start | bytes 393220
  294.6 65.7 %copy-start.69 = (f32[16,1,128]{2,1,0:T(1,128)S(1)}, f32[16,1,128]{2,1,0:T(1,128)}, u32[]{:S(2)}) copy-start(f32[16,1,128]{2,1,0:T(1,128)} %convert_element_type.426) | copy-start | bytes 24580
  360.9 727.5 %copy-start.2 = (bf16[256,2048]{1,0:T(8,128)(2,1)}, bf16[256,2048]{1,0:T(8,128)(2,1)S(1)}, u32[]{:S(2)}) copy-start(bf16[256,2048]{1,0:T(8,128)(2,1)S(1)} %multiply_convert_fusion.1) | copy-start | bytes 3145732
  396.3 214.2 %all-to-all-start = ((bf16[16,4,36,2048]{3,1,2,0:T(4,128)(2,1)}), bf16[16,4,36,2048]{3,1,2,0:T(4,128)(2,1)}, u32[]{:S(2)}, u32[]{:S(2)}) async-start(bf16[16,4,36,2048]{3,1,2,0:T(4,128)(2,1)} %copy.263), calls=%async_computation | async-start | bytes 18874368 | tf_op jit(solution)/shard_map/all_to_all | solution.py:277
  403.2 146.4 %all-gather.31.cloned.1.call-start = ((), (), s32[]{:S(2)}) async-start(), calls=%async_computation.28 | async-start | bytes 1179648 | tf_op jit(solution)/shard_map/all_gather | solution.py:168
  610.5 127.2 %all-to-all-start.2 = ((bf16[16,4,36,2048]{3,1,2,0:T(4,128)(2,1)}), bf16[16,4,36,2048]{3,1,2,0:T(4,128)(2,1)}, u32[]{:S(2)}, u32[]{:S(2)}) async-start(bf16[16,4,36,2048]{3,1,2,0:T(4,128)(2,1)} %copy.270), calls=%async_computation.3 | async-start | bytes 18874368 | tf_op jit(solution)/shard_map/all_to_all | solution.py:310
  793.1 141.9 %all-to-all-start.3 = ((bf16[16,4,36,2048]{3,1,2,0:T(4,128)(2,1)}), bf16[16,4,36,2048]{3,1,2,0:T(4,128)(2,1)}, u32[]{:S(2)}, u32[]{:S(2)}) async-start(bf16[16,4,36,2048]{3,1,2,0:T(4,128)(2,1)} %copy.272), calls=%async_computation.4 | async-start | bytes 18874368 | tf_op jit(solution)/shard_map/all_to_all | solution.py:322
  801.7 148.2 %all-gather.25.cloned.1.call-start = ((), (), s32[]{:S(2)}) async-start(), calls=%async_computation.24 | async-start | bytes 1531904 | tf_op jit(solution)/shard_map/all_gather | solution.py:150
  827.6 116.7 %copy-start.61 = (f32[128,352]{0,1:T(8,128)S(1)}, f32[128,352]{0,1:T(8,128)}, u32[]{:S(2)}) copy-start(f32[128,352]{0,1:T(8,128)} %param.39) | copy-start | bytes 540676
  827.6 117.4 %copy-start.62 = (f32[352,128]{1,0:T(8,128)S(1)}, f32[352,128]{1,0:T(8,128)}, u32[]{:S(2)}) copy-start(f32[352,128]{1,0:T(8,128)} %param.40) | copy-start | bytes 540676
  827.6 118.2 %copy-start.14 = (bf16[256,2048]{1,0:T(8,128)(2,1)S(1)}, bf16[256,2048]{1,0:T(8,128)(2,1)}, u32[]{:S(2)}) copy-start(bf16[256,2048]{1,0:T(8,128)(2,1)} %all-gather.31.cloned.1.call-done) | copy-start | bytes 3145732
  935.1 309.0 %all-to-all-start.1 = ((bf16[16,4,36,2048]{3,1,2,0:T(4,128)(2,1)}), bf16[16,4,36,2048]{3,1,2,0:T(4,128)(2,1)}, u32[]{:S(2)}, u32[]{:S(2)}) async-start(bf16[16,4,36,2048]{3,1,2,0:T(4,128)(2,1)} %copy.266), calls=%async_computation.1 | async-start | bytes 18874368 | tf_op jit(solution)/shard_map/all_to_all | solution.py:282
  944.2 144.1 %all-gather.27.cloned.1.call-start = ((), (), s32[]{:S(2)}) async-start(), calls=%async_computation.25 | async-start | bytes 1531904 | tf_op jit(solution)/shard_map/all_gather | solution.py:151
  945.0 191.4 %all-gather.29.cloned.1.call-start = ((), (), s32[]{:S(2)}) async-start(), calls=%async_computation.26 | async-start | bytes 1531904 | tf_op jit(solution)/shard_map/all_gather | solution.py:152
  945.7 415.0 %all-reduce.14.cloned.1.call-start = ((), (), s32[]{:S(2)}) async-start(), calls=%async_computation.29 | async-start | bytes 2097152 | tf_op jit(solution)/shard_map/psum | solution.py:330
  1091.0 48.9 %copy-start.24 = (bf16[2048,352]{0,1:T(8,128)(2,1)S(1)}, bf16[2048,352]{0,1:T(8,128)(2,1)}, u32[]{:S(2)}) copy-start(bf16[2048,352]{0,1:T(8,128)(2,1)} %all-gather.25.cloned.1.call-done) | copy-start | bytes 4325380
  1244.0 334.6 %reduce-scatter.28.cloned.1.call-start = ((), (), s32[]{:S(2)}) async-start(), calls=%async_computation.30 | async-start | bytes 2228224 | tf_op jit(solution)/shard_map/reduce_scatter | solution.py:393
  1334.4 26.3 %copy-start.8 = (bf16[256,2048]{1,0:T(8,128)(2,1)S(1)}, bf16[256,2048]{1,0:T(8,128)(2,1)}, u32[]{:S(2)}) copy-start(bf16[256,2048]{1,0:T(8,128)(2,1)} %all-gather.13.cloned.1.call-done) | copy-start | bytes 3145732
  1367.0 45.5 %copy-start.19 = (f32[256,2,128]{0,2,1:T(8,128)S(1)}, f32[256,2,128]{0,2,1:T(8,128)}, u32[]{:S(2)}) copy-start(f32[256,2,128]{0,2,1:T(8,128)} %custom-call.4) | copy-start | bytes 786436
  1367.0 45.5 %copy-start.26 = (f32[256,2,64]{0,2,1:T(8,128)S(1)}, f32[256,2,64]{0,2,1:T(8,128)}, u32[]{:S(2)}) copy-start(f32[256,2,64]{0,2,1:T(8,128)} %custom-call.5) | copy-start | bytes 393220
  1507.6 148.1 %reduce-scatter.30.cloned.1.call-start = ((), (), s32[]{:S(2)}) async-start(), calls=%async_computation.31 | async-start | bytes 2228224 | tf_op jit(solution)/shard_map/reduce_scatter | solution.py:399
  1515.9 216.3 %reduce-scatter.46.cloned.1.call-start = ((), (), s32[]{:S(2)}) async-start(), calls=%async_computation.39 | async-start | bytes 1671168
  1522.3 285.9 %reduce-scatter.48.cloned.1.call-start = ((), (), s32[]{:S(2)}) async-start(), calls=%async_computation.40 | async-start | bytes 1671168
  1527.6 356.6 %reduce-scatter.50.cloned.1.call-start = ((), (), s32[]{:S(2)}) async-start(), calls=%async_computation.41 | async-start | bytes 1671168
  1532.8 426.1 %reduce-scatter.32.cloned.1.call-start = ((), (), s32[]{:S(2)}) async-start(), calls=%async_computation.32 | async-start | bytes 557056 | tf_op jit(solution)/shard_map/reduce_scatter | solution.py:405
  1534.8 43.7 %copy-start.29 = (bf16[512,256]{1,0:T(8,128)(2,1)S(1)}, bf16[512,256]{1,0:T(8,128)(2,1)}, u32[]{:S(2)}) copy-start(bf16[512,256]{1,0:T(8,128)(2,1)} %copy-done.28) | copy-start | bytes 786436
  1534.9 489.5 %all-reduce.16.cloned.1.call-start = ((), (), s32[]{:S(2)}) async-start(), calls=%async_computation.42 | async-start | bytes 2621440 | tf_op jit(solution)/shard_map/psum | solution.py:418
  1535.0 120.7 %copy-start.31 = (bf16[512,256]{1,0:T(8,128)(2,1)S(1)}, bf16[512,256]{1,0:T(8,128)(2,1)}, u32[]{:S(2)}) copy-start(bf16[512,256]{1,0:T(8,128)(2,1)} %copy-done.30) | copy-start | bytes 786436
  1657.5 442.6 %reduce-scatter.44.cloned.1.call-start = ((), (), s32[]{:S(2)}) async-start(), calls=%async_computation.38 | async-start | bytes 557056
  1661.4 471.0 %reduce-scatter.26.cloned.1.call-start = ((), (), s32[]{:S(2)}) async-start(), calls=%async_computation.27 | async-start | bytes 1179648 | tf_op jit(solution)/shard_map/reduce_scatter | solution.py:291
  1664.9 543.8 %reduce-scatter.42.cloned.1.call-start = ((), (), s32[]{:S(2)}) async-start(), calls=%async_computation.37 | async-start | bytes 1114112
  1668.5 616.8 %reduce-scatter.34.cloned.1.call-start = ((), (), s32[]{:S(2)}) async-start(), calls=%async_computation.33 | async-start | bytes 1671168 | tf_op jit(solution)/shard_map/reduce_scatter | solution.py:446
  1670.5 311.8 %copy-start.89 = (f32[256]{0:T(256)S(1)}, f32[256]{0:T(256)}, u32[]{:S(2)}) copy-start(f32[256]{0:T(256)} %copy-done.88) | copy-start | bytes 3076
  1670.5 311.8 %copy-start.93 = (f32[32]{0:T(128)S(1)}, f32[32]{0:T(128)}, u32[]{:S(2)}) copy-start(f32[32]{0:T(128)} %copy-done.92) | copy-start | bytes 388
  1670.5 312.0 %copy-start.49 = (bf16[256,256]{0,1:T(8,128)(2,1)S(1)}, bf16[256,256]{0,1:T(8,128)(2,1)}, u32[]{:S(2)}) copy-start(bf16[256,256]{0,1:T(8,128)(2,1)} %reduce-scatter.30.cloned.1.call-done) | copy-start | bytes 393220
  1670.6 353.8 %copy-start.21 = (f32[256,576]{0,1:T(8,128)S(1)}, f32[256,576]{0,1:T(8,128)}, u32[]{:S(2)}) copy-start(f32[256,576]{0,1:T(8,128)} %copy-done.20) | copy-start | bytes 1769476
  1670.6 353.8 %copy-start.73 = (f32[512]{0:T(512)S(1)}, f32[512]{0:T(512)}, u32[]{:S(2)}) copy-start(f32[512]{0:T(512)} %copy-done.72) | copy-start | bytes 6148
  1670.6 353.8 %copy-start.87 = (f32[256]{0:T(256)S(1)}, f32[256]{0:T(256)}, u32[]{:S(2)}) copy-start(f32[256]{0:T(256)} %copy-done.86) | copy-start | bytes 3076
  1670.6 689.3 %reduce-scatter.36.cloned.1.call-start = ((), (), s32[]{:S(2)}) async-start(), calls=%async_computation.34 | async-start | bytes 278528 | tf_op jit(solution)/shard_map/reduce_scatter | solution.py:449
  1671.7 762.7 %reduce-scatter.38.cloned.1.call-start = ((), (), s32[]{:S(2)}) async-start(), calls=%async_computation.35 | async-start | bytes 278528 | tf_op jit(solution)/shard_map/reduce_scatter | solution.py:452
  1983.6 529.2 %reduce-scatter.40.cloned.1.call-start = ((), (), s32[]{:S(2)}) async-start(), calls=%async_computation.36 | async-start | bytes 2785280
  2070.3 365.4 %copy-start.45 = (bf16[256,2048]{1,0:T(8,128)(2,1)S(1)}, bf16[256,2048]{1,0:T(8,128)(2,1)}, u32[]{:S(2)}) copy-start(bf16[256,2048]{1,0:T(8,128)(2,1)} %get-tuple-element.1068) | copy-start | bytes 3145732
  (77 other events, 656.4 us)
Sparse Core Ops, SparseCore 0:
  9.7 26.9 all-gather.12
  39.5 48.1 all-gather.14
  90.3 43.0 all-gather.20
  136.0 45.2 all-gather.18
  183.9 44.6 all-gather.16
  231.1 42.4 all-gather.22
  294.7 63.6 all-reduce.11
  405.7 25.1 all-gather.30
  805.2 141.2 all-gather.24
  949.1 139.2 all-gather.26
  1091.1 45.2 all-gather.28
  1244.1 60.9 all-reduce.13
  1507.7 70.8 reduce-scatter.27
  1582.0 73.5 reduce-scatter.29
  1659.3 72.8 reduce-scatter.45
  1735.3 72.8 reduce-scatter.47
  1811.3 72.8 reduce-scatter.49
  1887.2 71.6 reduce-scatter.31
  1962.1 62.2 all-reduce.15
  2027.8 72.2 reduce-scatter.43
  2102.5 29.8 reduce-scatter.25
  2135.6 73.1 reduce-scatter.41
  2212.3 72.9 reduce-scatter.33
  2288.6 71.2 reduce-scatter.35
  2363.0 71.2 reduce-scatter.37
  2437.9 74.8 reduce-scatter.39
where the time goes:
time: 2540 us; the launch traced here: 2520 us
  waiting for transfers between devices  1280 us (50%)
  local copies, waits for them, and re-layouts  403 us (16%)
  blocking collectives  335 us (13%)
  matrix products  323 us (13%)
  other arithmetic  133 us (5%)
  starting transfers between devices  31 us (1%)
    unnamed x32, waiting for transfers between devices  332 us
    all_gather x1, blocking collectives, body(): lax.all_gather(w_router.astype(half_type), 'expert', axis=0, tiled=True)  146 us
    all_gather x1, waiting for transfers between devices, body(): lax.all_gather(w_su.astype(half_type), 'expert', axis=0, tiled=True)  136 us
    all_to_all x1, waiting for transfers between devices, body(): lax.all_to_all(d_expert_in.astype(jnp.bfloat16), 'expert', split_axis=0,...  107 us
    all_to_all x1, waiting for transfers between devices, body(): lax.all_to_all(d_slots, 'expert', split_axis=0, concat_axis=0, tiled=True)  95.4 us
    reduce_scatter x1, waiting for transfers between devices, body(): lax.psum_scatter(dv_blocks.reshape(key_total, -1).astype(jnp.bfloat16), '...  75.9 us
    reduce_scatter x1, waiting for transfers between devices, body(): lax.psum_scatter(grad_q.astype(jnp.bfloat16), 'expert', scatter_dimension...  74.9 us
    reduce_scatter x1, waiting for transfers between devices, body(): lax.psum_scatter(grad_uv.astype(jnp.bfloat16), 'expert', scatter_dimensio...  73.2 us
  transfers between devices with their start and end apart: 30, of which 22 were waited for; matrix products, arithmetic and copies ran while one was open for 24% of the time, Pallas kernels for 0%

commit v1 on v0

v1 whole, which is shorter than its diff:
```python
import jax
import jax.numpy as jnp
from jax import lax
from jax.experimental import pallas as pl
from jax.experimental.pallas import tpu as pltpu
from jax.sharding import Mesh, PartitionSpec as P

D = 2048
H_DEV = 2
DN = 128
DR = 64
KVL = 512
PIECE = 256
EXPERTS = 64
ROWS = 256
OWN = 32
SLOTS = 40
FFH = 704
SHP = 384
KEYS = 4096
CHUNK = 512
EPS = 1e-06
NEG = -1e30
SCALE = (DN + DR) ** (-0.5)
EX = ("z", "x")
HALF = jnp.bfloat16
WIDE = jnp.float32


def dot_nn(left, right):
    return jnp.dot(left, right, preferred_element_type=WIDE)


def dot_nt(left, right):
    return lax.dot_general(left, right, (((1,), (1,)), ((), ())), preferred_element_type=WIDE)


def dot_tn(left, right):
    return lax.dot_general(left, right, (((0,), (0,)), ((), ())), preferred_element_type=WIDE)


def inv_rms(values):
    return lax.rsqrt(jnp.mean(values * values, axis=-1, keepdims=True) + EPS)


def norm_back(grad, normed, row_scale, gain):
    scaled = grad * gain
    inner_mean = jnp.mean(scaled * normed, axis=-1, keepdims=True)
    return (row_scale * (scaled - normed * inner_mean), jnp.sum(grad * normed, axis=0))


def swap_core(value):
    return lax.ppermute(value, "c", [(0, 1), (1, 0)])


def shift_y(value, by):
    return lax.ppermute(value, "y", [(i, (i + by) % 4) for i in range(4)])


def spread(value, axes):
    return lax.all_to_all(value, axes, split_axis=0, concat_axis=0, tiled=True)


def gather_rows(value, yi, ci):
    n = value.shape[1]
    block = jnp.zeros((4, OWN, n), value.dtype)
    block = lax.dynamic_update_slice(block, value[None], (yi, 0, 0))
    for by in (1, 2, 3):
        block = lax.dynamic_update_slice(block, shift_y(value, by)[None], ((yi - by) % 4, 0, 0))
    other = swap_core(block)
    first = jnp.where(ci == 0, block, other)
    second = jnp.where(ci == 0, other, block)
    return jnp.stack([first, second], axis=1).reshape(ROWS, n)


def sum_rows(value, ci):
    n = value.shape[1]
    parts = value.reshape(4, 2, OWN, n)
    mine = lax.dynamic_index_in_dim(parts, ci, 1, keepdims=False)
    theirs = lax.dynamic_index_in_dim(parts, 1 - ci, 1, keepdims=False)
    pair = (mine.astype(WIDE) + swap_core(theirs).astype(WIDE)).astype(HALF)
    return jnp.sum(spread(pair, "y").astype(WIDE), axis=0)


def sum_experts(value):
    rows, width = value.shape
    parts = spread(value.reshape(16, rows // 16, width), EX)
    return jnp.sum(parts.astype(WIDE), axis=0)


def spans(row_ids, seq_lengths, piece_starts):
    ends = jnp.cumsum(seq_lengths)
    starts = ends - seq_lengths
    member = (row_ids[:, None] >= starts[None, :]) & (row_ids[:, None] < ends[None, :])
    member = member.astype(jnp.int32)
    low = jnp.sum(member * starts[None, :], axis=1)
    end = jnp.sum(member * ends[None, :], axis=1)
    inside = (row_ids[:, None] >= piece_starts[None, :]) & (
        row_ids[:, None] < piece_starts[None, :] + PIECE
    )
    piece_last = jnp.max(jnp.where(inside, piece_starts[None, :] + (PIECE - 1), -1), axis=1)
    high = jnp.where(piece_last >= 0, jnp.minimum(piece_last, end - 1), row_ids)
    return row_ids - low, low, high


def head_query(q_ref, head):
    lane = lax.broadcasted_iota(jnp.int32, (ROWS, 128), 1)
    rot = q_ref[:, 256:384]
    rot = jnp.where((lane // 32) % 2 == head, rot, jnp.zeros_like(rot))
    return jnp.concatenate([q_ref[:, 128 * head : 128 * head + 128], rot], axis=1)


def attend_kernel(q_ref, kv_ref, low_ref, high_ref, p_ref, o_ref, s_ref):
    low = low_ref[...]
    high = high_ref[...]
    for head in range(H_DEV):
        query = head_query(q_ref, head)

        def scores_step(i, top):
            at = pl.multiple_of(i * CHUNK, CHUNK)
            key = jnp.concatenate(
                [
                    kv_ref[pl.ds(at, CHUNK), 128 * head : 128 * head + 128],
                    kv_ref[pl.ds(at, CHUNK), 512:640],
                ],
                axis=1,
            )
            scores = dot_nt(key, query) * SCALE
            col = lax.broadcasted_iota(jnp.int32, (CHUNK, ROWS), 0) + at
            scores = jnp.where((col >= low) & (col <= high), scores, NEG)
            s_ref[pl.ds(at, CHUNK), :] = scores
            return jnp.maximum(top, jnp.max(scores.reshape(CHUNK // 8, 8, ROWS), axis=0))

        top = lax.fori_loop(
            0, KEYS // CHUNK, scores_step, jnp.full((8, ROWS), NEG, WIDE)
        )
        top = jnp.max(top, axis=0, keepdims=True)

        def exp_step(i, total):
            at = pl.multiple_of(i * CHUNK, CHUNK)
            weights = jnp.exp(s_ref[pl.ds(at, CHUNK), :] - top)
            s_ref[pl.ds(at, CHUNK), :] = weights
            return total + jnp.sum(weights.reshape(CHUNK // 8, 8, ROWS), axis=0)

        total = lax.fori_loop(0, KEYS // CHUNK, exp_step, jnp.zeros((8, ROWS), WIDE))
        inverse = 1.0 / jnp.sum(total, axis=0, keepdims=True)

        def value_step(i, acc):
            at = pl.multiple_of(i * CHUNK, CHUNK)
            probs = (s_ref[pl.ds(at, CHUNK), :] * inverse).astype(HALF)
            p_ref[head, pl.ds(at, CHUNK), :] = probs
            value = kv_ref[pl.ds(at, CHUNK), 256 + 128 * head : 384 + 128 * head]
            return acc + dot_tn(value, probs)

        out = lax.fori_loop(0, KEYS // CHUNK, value_step, jnp.zeros((DN, ROWS), WIDE))
        o_ref[:, 128 * head : 128 * head + 128] = out.T


def attend(queries, kv_all, low, high):
    vmem = pl.BlockSpec(memory_space=pltpu.VMEM)
    return pl.pallas_call(
        attend_kernel,
        out_shape=(
            jax.ShapeDtypeStruct((H_DEV, KEYS, ROWS), HALF),
            jax.ShapeDtypeStruct((ROWS, H_DEV * DN), WIDE),
        ),
        in_specs=[vmem] * 4,
        out_specs=(vmem, vmem),
        scratch_shapes=[pltpu.VMEM((KEYS, ROWS), WIDE)],
        compiler_params=pltpu.CompilerParams(vmem_limit_bytes=40 * 1024 * 1024),
        cost_estimate=pl.CostEstimate(
            flops=2 * H_DEV * ROWS * KEYS * 384, bytes_accessed=12 << 20, transcendentals=2 << 20
        ),
    )(queries, kv_all, low, high)


def attend_back_kernel(q_ref, kv_ref, p_ref, do_ref, delta_ref, dkv_ref, dq_ref, acc_ref):
    acc_ref[...] = jnp.zeros_like(acc_ref)
    query = [head_query(q_ref, head) for head in range(H_DEV)]

    def step(i, carry):
        at = pl.multiple_of(i * CHUNK, CHUNK)
        rot = kv_ref[pl.ds(at, CHUNK), 512:640]
        d_rot = jnp.zeros((CHUNK, 128), WIDE)
        for head in range(H_DEV):
            d_out = do_ref[:, 128 * head : 128 * head + 128]
            value = kv_ref[pl.ds(at, CHUNK), 256 + 128 * head : 384 + 128 * head]
            probs = p_ref[head, pl.ds(at, CHUNK), :]
            d_probs = dot_nt(value, d_out)
            d_scores = (
                probs.astype(WIDE) * (d_probs - delta_ref[head : head + 1, :])
            ).astype(HALF)
            d_key = dot_nn(d_scores, query[head]) * SCALE
            dkv_ref[pl.ds(at, CHUNK), 128 * head : 128 * head + 128] = d_key[:, :128].astype(HALF)
            d_rot = d_rot + d_key[:, 128:]
            dkv_ref[pl.ds(at, CHUNK), 256 + 128 * head : 384 + 128 * head] = dot_nn(
                probs, d_out
            ).astype(HALF)
            key = jnp.concatenate(
                [kv_ref[pl.ds(at, CHUNK), 128 * head : 128 * head + 128], rot], axis=1
            )
            acc_ref[head] += dot_tn(key, d_scores)
        dkv_ref[pl.ds(at, CHUNK), 512:640] = d_rot.astype(HALF)
        return carry

    lax.fori_loop(0, KEYS // CHUNK, step, 0)
    lane = lax.broadcasted_iota(jnp.int32, (ROWS, 128), 1)
    d_rot = jnp.zeros((ROWS, 128), WIDE)
    for head in range(H_DEV):
        d_query = acc_ref[head].T * SCALE
        dq_ref[:, 128 * head : 128 * head + 128] = d_query[:, :128]
        d_rot = jnp.where((lane // 32) % 2 == head, d_query[:, 128:], d_rot)
    dq_ref[:, 256:384] = d_rot


def attend_back(queries, kv_all, probs, d_heads, delta):
    vmem = pl.BlockSpec(memory_space=pltpu.VMEM)
    return pl.pallas_call(
        attend_back_kernel,
        out_shape=(
            jax.ShapeDtypeStruct((KEYS, 640), HALF),
            jax.ShapeDtypeStruct((ROWS, 384), WIDE),
        ),
        in_specs=[vmem] * 5,
        out_specs=(vmem, vmem),
        scratch_shapes=[pltpu.VMEM((H_DEV, 256, ROWS), WIDE)],
        compiler_params=pltpu.CompilerParams(vmem_limit_bytes=40 * 1024 * 1024),
        cost_estimate=pl.CostEstimate(
            flops=2 * H_DEV * ROWS * KEYS * 768, bytes_accessed=16 << 20, transcendentals=0
        ),
    )(queries, kv_all, probs, d_heads, delta)


def pack_query_columns(w):
    return jnp.concatenate(
        [w[:, 0:128], w[:, 192:320], w[:, 128:160], w[:, 320:352], w[:, 160:192], w[:, 352:384]],
        axis=1,
    )


def unpack_query_columns(w):
    return jnp.concatenate(
        [w[:, 0:128], w[:, 256:288], w[:, 320:352], w[:, 128:256], w[:, 288:320], w[:, 352:384]],
        axis=1,
    )


def pad_cols(w, width):
    return jnp.pad(w, ((0, 0), (0, width - w.shape[1])))


def silu_parts(gate):
    sig = jax.nn.sigmoid(gate)
    return gate * sig, sig * (1.0 + gate * (1.0 - sig))


def body(
    inputs,
    gain_attn,
    w_q,
    w_dkv,
    gain_latent,
    w_uk,
    w_uv,
    w_o,
    gain_ffn,
    w_router,
    w_sg,
    w_su,
    w_sd,
    w_eg,
    w_eu,
    w_ed,
    routes,
    seq_lengths,
    piece_starts,
    out_grad,
):
    zi, xi, yi, ci = (lax.axis_index(name) for name in ("z", "x", "y", "c"))
    ei = zi * 4 + xi
    ti = yi * 2 + ci

    gain_cols = jnp.stack([gain_attn, gain_ffn, jnp.pad(gain_latent, (0, 96))], axis=1)
    w_router_perm = w_router.reshape(128, 16, 4).transpose(0, 2, 1).reshape(128, EXPERTS)
    first_pack = jnp.concatenate(
        [
            pack_query_columns(w_q),
            w_dkv,
            w_router_perm,
            jnp.concatenate([w_uk, w_uv], axis=1).reshape(128, 128),
            w_o.T,
            pad_cols(gain_cols, 128),
        ],
        axis=1,
    ).astype(HALF)
    first_all = lax.all_gather(first_pack, EX, axis=0, tiled=True)
    second_pack = jnp.concatenate(
        [pad_cols(w_sg, SHP), pad_cols(w_su, SHP), pad_cols(w_sd.T, SHP)], axis=1
    ).astype(HALF)

    in_rows = gather_rows(inputs, yi, ci)
    g_rows = gather_rows(out_grad, yi, ci)

    weg_b = spread(w_eg.astype(HALF), "y").reshape(FFH, D)
    weu_b = spread(w_eu.astype(HALF), "y").reshape(FFH, D)
    wed_b = spread(w_ed.astype(HALF), "y").reshape(FFH, D)

    wq_b = first_all[:, 0:384]
    blk_b = first_all[:, 384:1024]
    wkv_b = first_all[:, 1024:1152].reshape(KVL, 512)
    wot_b = first_all[:, 1152:1408]
    pick = jnp.eye(8, 128, dtype=HALF)
    gains = dot_nt(pick, first_all[:, 1408:1536])
    gain_one = gains[0]
    gain_two = gains[1]
    gain_lat = gains[2].reshape(16, 128)[:, :32].reshape(KVL)

    routes_t = routes.T
    expert_ids = 4 * lax.broadcasted_iota(jnp.int32, (16, 1, ROWS), 0) + yi
    named = jnp.max((routes_t[None] == expert_ids).astype(WIDE), axis=1)
    earlier = (
        lax.broadcasted_iota(jnp.int32, (ROWS, ROWS), 0)
        < lax.broadcasted_iota(jnp.int32, (ROWS, ROWS), 1)
    ).astype(HALF)
    rank = dot_nn(named.astype(HALF), earlier)
    slot_ids = lax.broadcasted_iota(jnp.int32, (16, SLOTS, ROWS), 1).astype(WIDE)
    picked = (named[:, None, :] > 0.5) & (rank[:, None, :] == slot_ids)
    select = picked.astype(HALF).reshape(16 * SLOTS, ROWS)

    def half_cols(value):
        return lax.dynamic_slice_in_dim(value, ci * (D // 2), D // 2, value.ndim - 1)

    def join_halves(mine):
        other = swap_core(mine)
        return jnp.concatenate(
            [jnp.where(ci == 0, mine, other), jnp.where(ci == 0, other, mine)], axis=1
        )

    g_half = half_cols(g_rows)
    g_sent = dot_nn(select, g_half).astype(HALF).reshape(16, SLOTS, D // 2)
    g_slots = join_halves(spread(g_sent, EX).reshape(16 * SLOTS, D // 2))

    row_ids = ei * ROWS + jnp.arange(ROWS, dtype=jnp.int32)
    position, low, high = spans(row_ids, seq_lengths, piece_starts)
    inv_freq = 10000.0 ** (-(2.0 * jnp.arange(DR // 2, dtype=WIDE)) / DR)
    angles = position.astype(WIDE)[:, None] * inv_freq[None, :]
    cosine, sine = jnp.cos(angles), jnp.sin(angles)
    cos4 = jnp.concatenate([cosine] * 4, axis=1)
    sin4 = jnp.concatenate([-sine, -sine, sine, sine], axis=1)

    def swap_halves(v):
        return jnp.concatenate([v[:, 64:], v[:, :64]], axis=1)

    in_wide = in_rows.astype(WIDE)
    h_one = (in_wide * inv_rms(in_wide) * gain_one).astype(HALF)
    latent_all = dot_nn(h_one, blk_b)
    lat_part = latent_all[:, :KVL]
    scale_lat = inv_rms(lat_part)
    normed_lat = lat_part * scale_lat
    c_norm = (normed_lat * gain_lat).astype(HALF)
    rope_a, rope_b = latent_all[:, 512:544], latent_all[:, 544:576]
    rope = jnp.concatenate([rope_a, rope_a, rope_b, rope_b], axis=1)
    k_rot = rope * cos4 + swap_halves(rope) * sin4
    kv_local = jnp.concatenate([dot_nn(c_norm, wkv_b), k_rot], axis=1).astype(HALF)
    kv_all = lax.all_gather(kv_local, EX, axis=0, tiled=True)
    q_raw = dot_nn(h_one, wq_b)
    q_rot = q_raw[:, 256:]
    q_rot = q_rot * cos4 + swap_halves(q_rot) * sin4
    queries = jnp.concatenate([q_raw[:, :256], q_rot], axis=1).astype(HALF)
    second_all = lax.all_gather(second_pack, EX, axis=0, tiled=True)
    probs, heads_wide = attend(queries, kv_all, low[None, :], high[None, :])
    attn_heads = heads_wide.astype(HALF)
    attn_own = sum_rows(dot_nt(attn_heads, wot_b).astype(HALF), ci)

    in_own = inputs.astype(WIDE)
    g_own = out_grad.astype(WIDE)
    mid_own = in_own + attn_own
    scale_two = inv_rms(mid_own)
    normed_two = mid_own * scale_two
    h_two_own = (normed_two * gain_two).astype(HALF)
    h_two = gather_rows(h_two_own, yi, ci)

    rope_router_b = blk_b[:, 512:640]
    logits_t = lax.dot_general(
        rope_router_b, h_two, (((0,), (1,)), ((), ())), preferred_element_type=WIDE
    )[64:]
    probs_t = jax.nn.softmax(logits_t, axis=0)
    gate_t = lax.dynamic_slice_in_dim(probs_t, yi * 16, 16, 0).astype(HALF).astype(WIDE)
    gated = jnp.where(picked, gate_t[:, None, :], 0.0)
    slot_gate = jnp.sum(gated, axis=2)
    gated = gated.astype(HALF).reshape(16 * SLOTS, ROWS)

    x_sent = dot_nn(select, half_cols(h_two)).astype(HALF).reshape(16, SLOTS, D // 2)
    x_sent = jnp.concatenate(
        [x_sent, jnp.broadcast_to(slot_gate[:, :, None], (16, SLOTS, 128)).astype(HALF)], axis=2
    )
    x_recv = spread(x_sent, EX).reshape(16 * SLOTS, D // 2 + 128)
    x_slots = join_halves(x_recv[:, : D // 2])
    gate_slots = x_recv[:, D // 2 : D // 2 + 1].astype(WIDE)

    wgu_b = second_all[:, : 2 * SHP]
    wsdt_b = second_all[:, 2 * SHP :]
    shared_pre = dot_nn(h_two, wgu_b)
    shared_gate, shared_up = shared_pre[:, :SHP], shared_pre[:, SHP:]
    shared_silu, shared_slope = silu_parts(shared_gate)
    shared_hidden = (shared_silu * shared_up).astype(HALF)
    shared_out = dot_nt(shared_hidden, wsdt_b)
    d_shared_hidden = dot_nn(g_rows, wsdt_b)
    d_shared_pre = jnp.concatenate(
        [d_shared_hidden * shared_up * shared_slope, d_shared_hidden * shared_silu], axis=1
    ).astype(HALF)
    d_shared_in = dot_nt(d_shared_pre, wgu_b)
    shared_grads = jnp.concatenate(
        [
            dot_tn(h_two, d_shared_pre).astype(HALF),
            dot_tn(g_rows, shared_hidden).astype(HALF),
        ],
        axis=1,
    )

    expert_gate = dot_nt(x_slots, weg_b)
    expert_up = dot_nt(x_slots, weu_b)
    expert_silu, expert_slope = silu_parts(expert_gate)
    expert_hidden = (expert_silu * expert_up).astype(HALF)
    expert_out = dot_nn(expert_hidden, wed_b).astype(HALF)

    def pair_sum(value):
        mine = half_cols(value)
        theirs = lax.dynamic_slice_in_dim(value, (1 - ci) * (D // 2), D // 2, 1)
        total = mine.astype(WIDE) + swap_core(theirs).astype(WIDE)
        return total.astype(HALF).reshape(16, SLOTS, D // 2)

    out_back = spread(pair_sum(expert_out), EX).reshape(16 * SLOTS, D // 2)
    d_slot_out = (g_slots.astype(WIDE) * gate_slots).astype(HALF)
    d_expert_hidden = dot_nt(d_slot_out, wed_b)
    d_expert_gate = (d_expert_hidden * expert_up * expert_slope).astype(HALF)
    d_expert_up = (d_expert_hidden * expert_silu).astype(HALF)
    d_expert_in = (dot_nn(d_expert_gate, weg_b) + dot_nn(d_expert_up, weu_b)).astype(HALF)
    in_back = spread(pair_sum(d_expert_in), EX).reshape(16 * SLOTS, D // 2)

    def expert_grad(left, right):
        grad = dot_tn(left, right).astype(HALF).reshape(4, FFH // 4, D)
        return spread(grad, "y").astype(WIDE)

    grad_ed = expert_grad(expert_hidden, d_slot_out)
    grad_eg = expert_grad(d_expert_gate, x_slots)
    grad_eu = expert_grad(d_expert_up, x_slots)

    def place_half(value):
        zero = jnp.zeros_like(value)
        return jnp.concatenate(
            [jnp.where(ci == 0, value, zero), jnp.where(ci == 0, zero, value)], axis=1
        )

    routed_out = dot_tn(gated, out_back)
    ffn_part = (shared_out + place_half(routed_out)).astype(HALF)
    slot_dots = dot_nt(out_back, g_half).reshape(16, SLOTS, ROWS)
    d_route_t = jnp.sum(jnp.where(picked, slot_dots, 0.0), axis=1).astype(HALF)
    lane_at = (
        lax.broadcasted_iota(jnp.int32, (16, 128), 0) + yi * 16
        == lax.broadcasted_iota(jnp.int32, (16, 128), 1)
    ).astype(HALF)
    d_route_part = dot_tn(d_route_t, lane_at)
    d_h_part = d_shared_in + place_half(dot_tn(select, in_back))
    back_own = sum_rows(jnp.concatenate([d_h_part, d_route_part], axis=1).astype(HALF), ci)
    layer_out = (mid_own + sum_rows(ffn_part, ci)).astype(HALF)

    logits_own = dot_nn(h_two_own, rope_router_b)[:, 64:]
    probs_own = jax.nn.softmax(logits_own, axis=-1)
    d_route = back_own[:, D : D + EXPERTS]
    d_logits = (
        probs_own * (d_route - jnp.sum(probs_own * d_route, axis=-1, keepdims=True))
    ).astype(HALF)
    d_logits_pad = jnp.pad(d_logits, ((0, 0), (64, 0)))
    d_h_two = back_own[:, :D] + dot_nt(d_logits_pad, rope_router_b)
    d_mid_norm, gain_two_part = norm_back(d_h_two, normed_two, scale_two, gain_two)
    d_mid_own = d_mid_norm + g_own
    mid_all = gather_rows(
        jnp.concatenate([d_mid_own.astype(HALF), d_logits_pad], axis=1), yi, ci
    )
    d_attn_b = mid_all[:, :D]
    d_logits_all = mid_all[:, D + 64 :]

    grad_ot = dot_tn(d_attn_b, attn_heads).astype(HALF)
    d_heads = dot_nn(d_attn_b, wot_b).astype(HALF)
    delta = jnp.sum(
        (d_heads.astype(WIDE) * heads_wide).reshape(ROWS, H_DEV, DN), axis=2
    ).T
    shared_sum = lax.psum_scatter(
        jnp.concatenate([shared_grads, grad_ot], axis=1), EX, scatter_dimension=0, tiled=True
    ).astype(WIDE)
    d_kv, d_q = attend_back(queries, kv_all, probs, d_heads, delta)
    d_kv_rows = sum_experts(d_kv)
    d_q_rot = d_q[:, 256:]
    d_q_rot = d_q_rot * cos4 - swap_halves(d_q_rot) * sin4
    d_queries = jnp.concatenate([d_q[:, :256], d_q_rot], axis=1).astype(HALF)
    grad_q = sum_experts(dot_tn(h_one, d_queries).astype(HALF))
    d_one_own = sum_rows(dot_nt(d_queries, wq_b).astype(HALF), ci)
    d_kv_b = d_kv_rows[:, :512].astype(HALF)
    grad_kv = sum_experts(dot_tn(c_norm, d_kv_b).astype(HALF))
    d_lat_part = jnp.concatenate([dot_nt(d_kv_b, wkv_b), d_kv_rows[:, 512:]], axis=1)
    d_lat_own = sum_rows(d_lat_part.astype(HALF), ci)

    def own_rows(value):
        return lax.dynamic_slice_in_dim(value, ti * OWN, OWN, 0)

    cos_own, sin_own = own_rows(cos4), own_rows(sin4)
    d_rope = d_lat_own[:, 512:]
    d_rope = d_rope * cos_own - swap_halves(d_rope) * sin_own
    d_rope = jnp.concatenate(
        [d_rope[:, 0:32] + d_rope[:, 32:64], d_rope[:, 64:96] + d_rope[:, 96:128]], axis=1
    )
    d_lat, gain_lat_part = norm_back(
        d_lat_own[:, :512], own_rows(normed_lat), own_rows(scale_lat), gain_lat
    )
    d_latent = jnp.concatenate([d_lat, d_rope], axis=1).astype(HALF)
    d_latent_pad = jnp.pad(d_latent, ((0, 0), (0, 64)))
    d_h_one = d_one_own + dot_nt(d_latent_pad, blk_b)
    scale_one = inv_rms(in_own)
    normed_one = in_own * scale_one
    d_in_norm, gain_one_part = norm_back(d_h_one, normed_one, scale_one, gain_one)
    grad_inputs = (d_mid_own + d_in_norm).astype(HALF)

    d_latent_all = gather_rows(d_latent_pad, yi, ci)
    grad_dkv = dot_tn(h_one, lax.dynamic_slice_in_dim(d_latent_all, ti * 72, 72, 1))
    grad_router = dot_tn(h_two, lax.dynamic_slice_in_dim(d_logits_all, ti * 8, 8, 1))
    gain_lat_wide = jnp.pad(gain_lat_part.reshape(16, 32), ((0, 0), (0, 96))).reshape(D)
    gain_rows = jnp.stack([gain_one_part, gain_two_part, gain_lat_wide], axis=0).astype(HALF)
    gain_at = (
        lax.broadcasted_iota(jnp.int32, (3, 48), 0) == lax.broadcasted_iota(jnp.int32, (3, 48), 1)
    ).astype(HALF)
    last_part = jnp.concatenate([grad_dkv, grad_router, dot_tn(gain_rows, gain_at)], axis=1)
    last_sum = sum_experts(last_part.astype(HALF))
    last_all = spread(
        jnp.broadcast_to(last_sum.astype(HALF)[None], (8, 128, 128)), ("y", "c")
    )
    sum_dkv = last_all[:, :, :72].transpose(1, 0, 2).reshape(128, 576).astype(WIDE)
    sum_router = last_all[:, :, 72:80].transpose(1, 0, 2).reshape(128, 4, 16)
    sum_router = sum_router.transpose(0, 2, 1).reshape(128, EXPERTS).astype(WIDE)
    gain_sums = jnp.sum(last_all[:, :, 80:83].astype(WIDE), axis=0)

    return (
        layer_out,
        grad_inputs,
        gain_sums[:, 0],
        unpack_query_columns(grad_q),
        sum_dkv,
        gain_sums[:32, 2],
        grad_kv[:, :256],
        grad_kv[:, 256:],
        shared_sum[:, 3 * SHP :].T,
        gain_sums[:, 1],
        sum_router,
        shared_sum[:, :352],
        shared_sum[:, SHP : SHP + 352],
        shared_sum[:, 2 * SHP : 2 * SHP + 352].T,
        grad_eg,
        grad_eu,
        grad_ed,
    )


def solution(mesh):
    grid = Mesh(mesh.devices.reshape(4, 4, 4, 2), ("z", "x", "y", "c"))
    ten = ("y", "c")
    rows = P(("z", "x", "y", "c"), None)
    wide = P(EX, ten)
    tall = P(ten, EX)
    expert = P(EX, ten, None)
    return jax.shard_map(
        body,
        mesh=grid,
        in_specs=(
            rows,
            P(EX),
            wide,
            P(EX, None),
            P(EX),
            wide,
            wide,
            tall,
            P(EX),
            P(EX, None),
            wide,
            wide,
            tall,
            expert,
            expert,
            expert,
            P(EX, None),
            P(),
            P(),
            rows,
        ),
        out_specs=(
            rows,
            rows,
            P(EX),
            wide,
            P(EX, None),
            P(EX),
            wide,
            wide,
            tall,
            P(EX),
            P(EX, None),
            wide,
            wide,
            tall,
            expert,
            expert,
            expert,
        ),
        check_vma=False,
    )
```

time: 2540 us -> 808 us (0.32)
  waiting for transfers between devices: 1280 us -> 349 us
  local copies, waits for them, and re-layouts: 403 us -> 56.3 us
  blocking collectives: 335 us -> 0 us
  matrix products: 323 us -> 97.6 us
  starting transfers between devices: 31 us -> 155 us
  other arithmetic: 133 us -> 102 us
    reduce_scatter x7 -> x0, waiting for transfers between devices: 441 us -> none  [the longest x1 75.9 us: body(): lax.psum_scatter(dv_blocks.reshape(key_total, -1).astype(jnp.bfloat16), '...]
    unnamed x32 -> x5, waiting for transfers between devices: 332 us -> 0.07 us
    dot_general x138 -> x14, matrix products: 284 us -> 31.1 us  [the longest x13 29.7 us: dot_nn(): return jnp.dot(left, right, preferred_element_type=WIDE)]
    all_gather x6 -> x0, blocking collectives: 236 us -> none  [the longest x1 146 us: body(): lax.all_gather(w_router.astype(half_type), 'expert', axis=0, tiled=True)]
    reshape x12 -> x6, local copies, waits for them, and re-layouts: 146 us -> 3.81 us  [the longest x2 2.5 us: body(): wkv_b = first_all[:, 1024:1152].reshape(KVL, 512)]
    all_gather x10 -> x3, waiting for transfers between devices: 203 us -> 99.9 us  [the longest x1 54.5 us: body(): first_all = lax.all_gather(first_pack, EX, axis=0, tiled=True)]
    psum x3 -> x0, waiting for transfers between devices: 97.5 us -> none  [the longest x1 56.7 us: body(): lax.psum(dot_nn(attn_heads, wo_b).astype(jnp.bfloat16), 'tensor')]
    convert_element_type x9 -> x1, local copies, waits for them, and re-layouts: 77.2 us -> 0.63 us  [body(): sum_router.transpose(0, 2, 1).reshape(128, EXPERTS).astype(WIDE)]
  transfers between devices with their start and end apart: 30 -> 53, of which waited for: 22 -> 29; matrix products, arithmetic and copies ran while one was open for 24% -> 27% of each run, Pallas kernels for 0% -> 2%
where the time goes in v1:
time: 808 us; the launch traced here: 796 us
  waiting for transfers between devices  349 us (43%)
  starting transfers between devices  155 us (19%)
  other arithmetic  102 us (13%)
  matrix products  97.6 us (12%)
  local copies, waits for them, and re-layouts  56.3 us (7%)
  Pallas kernels  19.4 us (2%)
  between operations  15.9 us (2%)
    all_to_all x20, waiting for transfers between devices, spread(): return lax.all_to_all(value, axes, split_axis=0, concat_axis=0, tiled=True)  209 us
    all_to_all x20, starting transfers between devices, spread(): return lax.all_to_all(value, axes, split_axis=0, concat_axis=0, tiled=True)  105 us
    all_gather x1, waiting for transfers between devices, body(): first_all = lax.all_gather(first_pack, EX, axis=0, tiled=True)  54.5 us
    all_gather x1, waiting for transfers between devices, body(): kv_all = lax.all_gather(kv_local, EX, axis=0, tiled=True)  45.3 us
    ppermute x15, waiting for transfers between devices, shift_y(): return lax.ppermute(value, 'y', [(i, (i + by) % 4) for i in range(4)])  39.7 us
    dot_general x12, matrix products, dot_nt(): lax.dot_general(left, right, (((1,), (1,)), ((), ())), preferred_element_...  36.6 us
    dot_general x14, matrix products, dot_tn(): lax.dot_general(left, right, (((0,), (0,)), ((), ())), preferred_element_...  29.9 us
    dot_general x13, matrix products, dot_nn(): return jnp.dot(left, right, preferred_element_type=WIDE)  29.7 us
  transfers between devices with their start and end apart: 53, of which 29 were waited for; matrix products, arithmetic and copies ran while one was open for 27% of the time, Pallas kernels for 2%

profile of v1, /device:TPU:1, one launch (start us, length us, event | category | flops | bytes accessed | tf_op | source)
XLA Modules:
  0.0 796.0 jit_solution(17562765464957249413)
XLA Ops:
  30.9 54.5 %all-gather.4.cloned.1.call-done = bf16[2048,1536]{0,1:T(8,128)(2,1)} async-done(((bf16[128,1536]{0,1:T(8,128)(2,1)}), bf16[2048,1536]{0,1:T(8,128)(2,1)}) %all-gather.4.cloned.1.call-update) | async-done | bytes 6291472 | tf_op jit(solution)/shard_map/all_gather | solution.py:296
  109.3 45.3 %all-gather.6.cloned.1.call-done.kv_ref = bf16[4096,640]{1,0:T(8,128)(2,1)} async-done(((bf16[256,640]{1,0:T(8,128)(2,1)}), bf16[4096,640]{1,0:T(8,128)(2,1)}) %all-gather.6.cloned.1.call-update) | async-done | bytes 5242896 | tf_op jit(solution)/shard_map/all_gather | solution.py:365
  157.1 10.0 %shard_map.323 = (bf16[2,4096,256]{2,1,0:T(8,128)(2,1)S(1)}, f32[256,256]{1,0:T(8,128)S(1)}) custom-call(bf16[256,384]{1,0:T(8,128)(2,1)S(1)} %pad_maximum_fusion.12.q_ref, bf16[4096,640]{1,0:T(8,128)(2,1)S(1)} %copy-done.1, s32[1,256]{1,0:T(1,128)S(1)} %bitcast.245, s32[1,256]{1,0:T(1,128)S(1)} %reshape_select_fusion.high_ref), custom_call_target="tpu_custom_call" | custom-call | flops 1610612736 | bytes 12582912 | tf_op jit(solution)/shard_map/pallas_call | solution.py:161
  174.1 4.0 all-to-all-start
  179.5 7.6 all-to-all-done
  189.9 5.0 all-to-all-start.7
  206.0 4.7 convert_element_type.355
  213.6 4.6 all-to-all-start.2
  223.9 25.4 %all-to-all-done.2 = bf16[4,176,2048]{2,1,0:T(8,128)(2,1)} async-done(((bf16[4,176,2048]{2,1,0:T(8,128)(2,1)}), bf16[4,176,2048]{2,1,0:T(8,128)(2,1)}, u32[]{:S(2)}, u32[]{:S(2)}) %all-to-all-start.2) | async-done | bytes 2883616 | tf_op jit(solution)/shard_map/all_to_all | solution.py:61
  249.3 8.1 %all-to-all-start.1 = ((bf16[16,40,1152]{2,1,0:T(8,128)(2,1)}), bf16[16,40,1152]{2,1,0:T(8,128)(2,1)S(1)}, u32[]{:S(2)}, u32[]{:S(2)}) async-start(bf16[16,40,1152]{2,1,0:T(8,128)(2,1)} %pad_maximum_fusion.2), calls=%async_computation.1 | async-start | bytes 2949120 | tf_op jit(solution)/shard_map/all_to_all | solution.py:61
  259.4 4.7 convert_element_type.356
  264.7 12.3 %all-to-all-done.1 = bf16[16,40,1152]{2,1,0:T(8,128)(2,1)S(1)} async-done(((bf16[16,40,1152]{2,1,0:T(8,128)(2,1)}), bf16[16,40,1152]{2,1,0:T(8,128)(2,1)S(1)}, u32[]{:S(2)}, u32[]{:S(2)}) %all-to-all-start.1) | async-done | bytes 1474592 | tf_op jit(solution)/shard_map/all_to_all | solution.py:61
  277.0 4.6 all-to-all-start.3
  283.3 3.9 collective-permute-start.16
  288.5 4.7 convert_element_type.358
  293.2 19.4 %all-to-all-done.3 = bf16[4,176,2048]{2,1,0:T(8,128)(2,1)} async-done(((bf16[4,176,2048]{2,1,0:T(8,128)(2,1)}), bf16[4,176,2048]{2,1,0:T(8,128)(2,1)}, u32[]{:S(2)}, u32[]{:S(2)}) %all-to-all-start.3) | async-done | bytes 2883616 | tf_op jit(solution)/shard_map/all_to_all | solution.py:61
  312.6 4.6 all-to-all-start.4
  317.2 3.5 broadcast_select_fusion.1
  322.3 6.4 fusion.144
  328.8 5.7 fusion.143
  334.5 12.8 %all-to-all-done.4 = bf16[4,176,2048]{2,1,0:T(8,128)(2,1)} async-done(((bf16[4,176,2048]{2,1,0:T(8,128)(2,1)}), bf16[4,176,2048]{2,1,0:T(8,128)(2,1)}, u32[]{:S(2)}, u32[]{:S(2)}) %all-to-all-start.4) | async-done | bytes 2883616 | tf_op jit(solution)/shard_map/all_to_all | solution.py:61
  347.2 6.3 multiply_convert_fusion.1
  353.5 5.0 convolution_convert_fusion.4
  358.7 6.0 collective-permute-start.10
  364.7 4.1 fusion.159
  368.8 4.1 add_convert_fusion
  375.8 8.3 %all-to-all-start.5 = ((bf16[16,40,1024]{2,1,0:T(8,128)(2,1)}), bf16[16,40,1024]{2,1,0:T(8,128)(2,1)S(1)}, u32[]{:S(2)}, u32[]{:S(2)}) async-start(bf16[16,40,1024]{2,1,0:T(8,128)(2,1)} %bitcast.41), calls=%async_computation.5 | async-start | bytes 2621440 | tf_op jit(solution)/shard_map/all_to_all | solution.py:61
  387.5 16.3 %all-to-all-done.5 = bf16[16,40,1024]{2,1,0:T(8,128)(2,1)S(1)} async-done(((bf16[16,40,1024]{2,1,0:T(8,128)(2,1)}), bf16[16,40,1024]{2,1,0:T(8,128)(2,1)S(1)}, u32[]{:S(2)}, u32[]{:S(2)}) %all-to-all-start.5) | async-done | bytes 1310752 | tf_op jit(solution)/shard_map/all_to_all | solution.py:61
  403.8 4.8 all-to-all-start.8
  415.6 10.8 %all-to-all-done.8 = bf16[16,40,1024]{2,1,0:T(8,128)(2,1)} async-done(((bf16[16,40,1024]{2,1,0:T(8,128)(2,1)}), bf16[16,40,1024]{2,1,0:T(8,128)(2,1)}, u32[]{:S(2)}, u32[]{:S(2)}) %all-to-all-start.8) | async-done | bytes 1310752 | tf_op jit(solution)/shard_map/all_to_all | solution.py:61
  431.9 3.7 collective-permute-start.18
  436.1 4.1 convolution_convert_fusion.1
  441.1 4.4 all-to-all-start.9
  445.5 6.1 convolution_convert_fusion.3
  451.7 4.0 convolution_convert_fusion.2
  455.7 4.7 all-to-all-start.17
  470.5 26.7 %collective-permute-done.19 = bf16[32,2176]{1,0:T(8,128)(2,1)S(1)} collective-permute-done((bf16[32,2176]{1,0:T(8,128)(2,1)S(1)}, bf16[32,2176]{1,0:T(8,128)(2,1)S(1)}, u32[]{:S(2)}, u32[]{:S(2)}) %collective-permute-start.19) | collective-permute-done | bytes 139296 | tf_op jit(solution)/shard_map/ppermute | solution.py:57
  501.2 4.7 all-to-all-start.18
  517.3 21.9 %all-to-all-done.18 = bf16[4,176,2048]{2,1,0:T(8,128)(2,1)} async-done(((bf16[4,176,2048]{2,1,0:T(8,128)(2,1)}), bf16[4,176,2048]{2,1,0:T(8,128)(2,1)}, u32[]{:S(2)}, u32[]{:S(2)}) %all-to-all-start.18) | async-done | bytes 2883616 | tf_op jit(solution)/shard_map/all_to_all | solution.py:61
  539.3 4.6 all-to-all-start.19
  554.0 9.3 %shard_map.324 = (bf16[4096,640]{1,0:T(8,128)(2,1)S(1)}, f32[256,384]{1,0:T(8,128)S(1)}) custom-call(bf16[256,384]{1,0:T(8,128)(2,1)S(1)} %pad_maximum_fusion.12.q_ref, bf16[4096,640]{1,0:T(8,128)(2,1)} %all-gather.6.cloned.1.call-done.kv_ref, bf16[2,4096,256]{2,1,0:T(8,128)(2,1)S(1)} %copy-done.3, bf16[256,256]{1,0:T(8,128)(2,1)S(1)} %get-tuple-element.108.do_ref, ...), custom_call_target="tpu_custom_call" | custom-call | flops 3221225472 | bytes 16777216 | tf_op jit(solution)/shard_map/pallas_call | solution.py:218
  563.7 4.0 convolution_convert_fusion.7
  576.3 4.1 all-to-all-start.6
  582.6 4.9 all-to-all-done.6
  587.4 4.1 all-to-all-start.10
  591.6 3.6 convolution_convert_fusion
  595.2 3.3 all-to-all-done.10
  598.5 5.1 all-to-all-start.11
  607.2 9.0 %pad_maximum_fusion = bf16[2048,1408]{0,1:T(8,128)(2,1)} fusion(bf16[2048,256]{0,1:T(8,128)(2,1)S(1)} %convolution_convert_fusion.8, bf16[2048,384]{0,1:T(8,128)(2,1)} %convolution_convert_fusion.5, bf16[2048,768]{0,1:T(8,128)(2,1)S(1)} %copy-done.4), kind=kLoop, calls=%fused_computation | loop fusion | flops 17301504 | bytes 11534336 | tf_op jit(solution)/shard_map/concatenate | solution.py:490
  616.2 8.3 %copy.132 = bf16[2048,1408]{1,0:T(8,128)(2,1)} copy(bf16[2048,1408]{0,1:T(8,128)(2,1)} %pad_maximum_fusion) | data formatting | bytes 11534336
  627.6 41.8 %all-to-all-done.11 = bf16[16,256,640]{2,1,0:T(8,128)(2,1)} async-done(((bf16[16,256,640]{2,1,0:T(8,128)(2,1)}), bf16[16,256,640]{2,1,0:T(8,128)(2,1)}, u32[]{:S(2)}, u32[]{:S(2)}) %all-to-all-start.11) | async-done | bytes 5242912 | tf_op jit(solution)/shard_map/all_to_all | solution.py:61
  669.5 9.2 %all-to-all-start.15 = ((bf16[16,128,384]{2,1,0:T(8,128)(2,1)}), bf16[16,128,384]{2,1,0:T(8,128)(2,1)}, u32[]{:S(2)}, u32[]{:S(2)}) async-start(bf16[16,128,384]{2,1,0:T(8,128)(2,1)} %bitcast.260), calls=%async_computation.15 | async-start | bytes 3145728 | tf_op jit(solution)/shard_map/all_to_all | solution.py:61
  683.8 5.1 convert_element_type.421
  688.9 5.1 convert_element_type.423
  694.0 5.2 convert_element_type.425
  702.6 3.4 reduce.2
  716.8 4.1 all-to-all-done.12
  731.8 3.7 fusion.74
  738.3 7.0 all-to-all-start.13
  747.5 8.8 %all-to-all-done.13 = bf16[16,128,128]{1,2,0:T(8,128)(2,1)S(1)} async-done(((bf16[16,128,128]{1,2,0:T(8,128)(2,1)}), bf16[16,128,128]{1,2,0:T(8,128)(2,1)S(1)}, u32[]{:S(2)}, u32[]{:S(2)}) %all-to-all-start.13) | async-done | bytes 524320 | tf_op jit(solution)/shard_map/all_to_all | solution.py:61
  756.2 3.6 all-to-all-start.16
  760.8 9.1 %all-to-all-done.16 = bf16[16,32,512]{2,1,0:T(8,128)(2,1)S(1)} async-done(((bf16[16,32,512]{2,1,0:T(8,128)(2,1)}), bf16[16,32,512]{2,1,0:T(8,128)(2,1)S(1)}, u32[]{:S(2)}, u32[]{:S(2)}) %all-to-all-start.16) | async-done | bytes 524320 | tf_op jit(solution)/shard_map/all_to_all | solution.py:61
  770.6 6.4 all-to-all-start.14
  777.7 5.8 all-to-all-done.14
  (470 shorter events, 203.7 us)
Async XLA Ops:
  7.2 78.2 %all-gather.4.cloned.1.call-start = ((), (), s32[]{:S(2)}) async-start(), calls=%async_computation.21 | async-start | bytes 6684672 | tf_op jit(solution)/shard_map/all_gather | solution.py:296
  14.9 139.7 %all-gather.6.cloned.1.call-start = ((), (), s32[]{:S(2)}) async-start(), calls=%async_computation.22 | async-start | bytes 5570560 | tf_op jit(solution)/shard_map/all_gather | solution.py:365
  15.0 8.4 %collective-permute-start = (bf16[32,2048]{1,0:T(8,128)(2,1)}, bf16[32,2048]{1,0:T(8,128)(2,1)S(1)}, u32[]{:S(2)}, u32[]{:S(2)}) collective-permute-start(bf16[32,2048]{1,0:T(8,128)(2,1)} %param.20), channel_id=1, source_target_pairs={{0,2},{2,4},{4,6},{6,0},{1,3},{3,5},{5,7},{7,1},{8,10},{10,12},{12... | collective-permute-start | bytes 393224 | tf_op jit(solution)/shard_map/ppermute | solution.py:57
  17.2 8.5 %collective-permute-start.1 = (bf16[32,2048]{1,0:T(8,128)(2,1)}, bf16[32,2048]{1,0:T(8,128)(2,1)S(1)}, u32[]{:S(2)}, u32[]{:S(2)}) collective-permute-start(bf16[32,2048]{1,0:T(8,128)(2,1)} %param.20), channel_id=1, source_target_pairs={{0,4},{2,6},{4,0},{6,2},{1,5},{3,7},{5,1},{7,3},{8,12},{10,14},{12... | collective-permute-start | bytes 393224 | tf_op jit(solution)/shard_map/ppermute | solution.py:57
  19.8 5.9 collective-permute-start.2
  25.8 3.2 collective-permute-start.3
  28.6 79.8 %copy-start.23 = (f32[256,32]{1,0:T(8,128)}, f32[256,32]{1,0:T(8,128)S(1)}, u32[]{:S(2)}) copy-start(f32[256,32]{1,0:T(8,128)S(1)} %get-tuple-element.99) | copy-start | bytes 98308
  86.6 101.2 %copy-start.50 = (f32[1,2048]{1,0:T(1,128)}, f32[1,2048]{1,0:T(1,128)S(1)}, u32[]{:S(2)}) copy-start(f32[1,2048]{1,0:T(1,128)S(1)} %get-tuple-element.90) | copy-start | bytes 24580
  97.9 5.3 collective-permute-start.12
  99.2 6.9 collective-permute-start.13
  101.6 70.1 %collective-permute-start.14 = (bf16[32,2048]{1,0:T(8,128)(2,1)S(1)}, bf16[32,2048]{1,0:T(8,128)(2,1)}, u32[]{:S(2)}, u32[]{:S(2)}) collective-permute-start(bf16[32,2048]{1,0:T(8,128)(2,1)S(1)} %copy-done.36), channel_id=1, source_target_pairs={{0,6},{2,0},{4,2},{6,4},{1,7},{3,1},{5,3},{7,5},{8,14},{10,8},{12,... | collective-permute-start | bytes 393224 | tf_op jit(solution)/shard_map/ppermute | solution.py:57
  102.9 118.2 %copy-start.66 = (pred[16,256]{1,0:T(8,128)(4,1)}, pred[16,256]{1,0:T(8,128)(4,1)S(1)}, u32[]{:S(2)}) copy-start(pred[16,256]{1,0:T(8,128)(4,1)S(1)} %broadcast_compare_fusion) | copy-start | bytes 12292
  103.1 69.8 %copy-start.58 = (f32[16,256]{1,0:T(8,128)}, f32[16,256]{1,0:T(8,128)S(1)}, u32[]{:S(2)}) copy-start(f32[16,256]{1,0:T(8,128)S(1)} %fusion.76) | copy-start | bytes 49156
  170.9 2.3 collective-permute-start.4
  172.6 5.5 collective-permute-start.15
  172.7 48.4 %copy-start.79 = (f32[40]{0:T(128)}, f32[40]{0:T(128)S(1)}, u32[]{:S(2)}) copy-start(f32[40]{0:T(128)S(1)} %iota_convert_fusion) | copy-start | bytes 484
  174.1 12.9 %all-to-all-start = ((bf16[4,32,2048]{2,1,0:T(8,128)(2,1)}), bf16[4,32,2048]{2,1,0:T(8,128)(2,1)S(1)}, u32[]{:S(2)}, u32[]{:S(2)}) async-start(bf16[4,32,2048]{2,1,0:T(8,128)(2,1)} %fusion.32), calls=%async_computation | async-start | bytes 1048576 | tf_op jit(solution)/shard_map/all_to_all | solution.py:61
  188.0 9.5 %collective-permute-start.5 = (bf16[32,2048]{1,0:T(8,128)(2,1)S(1)}, bf16[32,2048]{1,0:T(8,128)(2,1)S(1)}, u32[]{:S(2)}, u32[]{:S(2)}) collective-permute-start(bf16[32,2048]{1,0:T(8,128)(2,1)S(1)} %get-tuple-element.38), channel_id=1, source_target_pairs={{0,2},{2,4},{4,6},{6,0},{1,3},{3,5},{5,7},{7,1},{8,10},{10,12},{12... | collective-permute-start | bytes 393224 | tf_op jit(solution)/shard_map/ppermute | solution.py:57
  189.9 22.7 %all-to-all-start.7 = ((bf16[16,40,1024]{2,1,0:T(8,128)(2,1)}), bf16[16,40,1024]{2,1,0:T(8,128)(2,1)S(1)}, u32[]{:S(2)}, u32[]{:S(2)}) async-start(bf16[16,40,1024]{2,1,0:T(8,128)(2,1)} %bitcast.53), calls=%async_computation.7 | async-start | bytes 2621440 | tf_op jit(solution)/shard_map/all_to_all | solution.py:61
  194.9 5.4 collective-permute-start.6
  196.8 5.5 collective-permute-start.7
  203.0 15.3 %collective-permute-start.8 = (bf16[4,32,2048]{2,1,0:T(8,128)(2,1)}, bf16[4,32,2048]{2,1,0:T(8,128)(2,1)}, u32[]{:S(2)}, u32[]{:S(2)}) collective-permute-start(bf16[4,32,2048]{2,1,0:T(8,128)(2,1)} %bitcast_dynamic-update-slice_fusion.8), channel_id=1, source_target_pairs={{0,1},{1,0},{2,3},{3,2},{4,5},{5,4},{6,7},{7,6},{8,9},{9,8},{10,11... | collective-permute-start | bytes 1572872 | tf_op jit(solution)/shard_map/ppermute | solution.py:53
  213.6 35.7 %all-to-all-start.2 = ((bf16[4,176,2048]{2,1,0:T(8,128)(2,1)}), bf16[4,176,2048]{2,1,0:T(8,128)(2,1)}, u32[]{:S(2)}, u32[]{:S(2)}) async-start(bf16[4,176,2048]{2,1,0:T(8,128)(2,1)} %convert_element_type.355), calls=%async_computation.2 | async-start | bytes 5767168 | tf_op jit(solution)/shard_map/all_to_all | solution.py:61
  249.3 27.6 %all-to-all-start.1 = ((bf16[16,40,1152]{2,1,0:T(8,128)(2,1)}), bf16[16,40,1152]{2,1,0:T(8,128)(2,1)S(1)}, u32[]{:S(2)}, u32[]{:S(2)}) async-start(bf16[16,40,1152]{2,1,0:T(8,128)(2,1)} %pad_maximum_fusion.2), calls=%async_computation.1 | async-start | bytes 2949120 | tf_op jit(solution)/shard_map/all_to_all | solution.py:61
  277.0 35.6 %all-to-all-start.3 = ((bf16[4,176,2048]{2,1,0:T(8,128)(2,1)}), bf16[4,176,2048]{2,1,0:T(8,128)(2,1)}, u32[]{:S(2)}, u32[]{:S(2)}) async-start(bf16[4,176,2048]{2,1,0:T(8,128)(2,1)} %convert_element_type.356), calls=%async_computation.3 | async-start | bytes 5767168 | tf_op jit(solution)/shard_map/all_to_all | solution.py:61
  281.6 127.1 %all-gather.8.cloned.1.call-start = ((), (), s32[]{:S(2)}) async-start(), calls=%async_computation.23 | async-start | bytes 5013504 | tf_op jit(solution)/shard_map/all_gather | solution.py:370
  283.3 33.9 %collective-permute-start.16 = (bf16[640,1024]{1,0:T(8,128)(2,1)}, bf16[640,1024]{1,0:T(8,128)(2,1)}, u32[]{:S(2)}, u32[]{:S(2)}) collective-permute-start(bf16[640,1024]{1,0:T(8,128)(2,1)} %bitcast.264), channel_id=1, source_target_pairs={{0,1},{1,0},{2,3},{3,2},{4,5},{5,4},{6,7},{7,6},{8,9},{9,8},{10,11... | collective-permute-start | bytes 3932168 | tf_op jit(solution)/shard_map/ppermute | solution.py:53
  288.5 32.3 %collective-permute-start.9 = (bf16[640,1024]{1,0:T(8,128)(2,1)}, bf16[640,1024]{1,0:T(8,128)(2,1)}, u32[]{:S(2)}, u32[]{:S(2)}) collective-permute-start(bf16[640,1024]{1,0:T(8,128)(2,1)} %slice.330), channel_id=1, source_target_pairs={{0,1},{1,0},{2,3},{3,2},{4,5},{5,4},{6,7},{7,6},{8,9},{9,8},{10,11... | collective-permute-start | bytes 3932168 | tf_op jit(solution)/shard_map/ppermute | solution.py:53
  312.6 34.6 %all-to-all-start.4 = ((bf16[4,176,2048]{2,1,0:T(8,128)(2,1)}), bf16[4,176,2048]{2,1,0:T(8,128)(2,1)}, u32[]{:S(2)}, u32[]{:S(2)}) async-start(bf16[4,176,2048]{2,1,0:T(8,128)(2,1)} %convert_element_type.358), calls=%async_computation.4 | async-start | bytes 5767168 | tf_op jit(solution)/shard_map/all_to_all | solution.py:61
  358.7 15.5 %collective-permute-start.10 = (bf16[640,1024]{1,0:T(8,128)(2,1)S(1)}, bf16[640,1024]{1,0:T(8,128)(2,1)S(1)}, u32[]{:S(2)}, u32[]{:S(2)}) collective-permute-start(bf16[640,1024]{1,0:T(8,128)(2,1)S(1)} %constant_dynamic-slice_fusion.1), channel_id=1, source_target_pairs={{0,1},{1,0},{2,3},{3,2},{4,5},{5,4},{6,7},{7,6},{8,9},{9,8},{10,11... | collective-permute-start | bytes 3932168 | tf_op jit(solution)/shard_map/ppermute | solution.py:53
  374.2 10.0 %collective-permute-start.17 = (bf16[640,1024]{1,0:T(8,128)(2,1)}, bf16[640,1024]{1,0:T(8,128)(2,1)}, u32[]{:S(2)}, u32[]{:S(2)}) collective-permute-start(bf16[640,1024]{1,0:T(8,128)(2,1)} %constant_dynamic-slice_fusion), channel_id=1, source_target_pairs={{0,1},{1,0},{2,3},{3,2},{4,5},{5,4},{6,7},{7,6},{8,9},{9,8},{10,11... | collective-permute-start | bytes 3932168 | tf_op jit(solution)/shard_map/ppermute | solution.py:53
  375.8 28.0 %all-to-all-start.5 = ((bf16[16,40,1024]{2,1,0:T(8,128)(2,1)}), bf16[16,40,1024]{2,1,0:T(8,128)(2,1)S(1)}, u32[]{:S(2)}, u32[]{:S(2)}) async-start(bf16[16,40,1024]{2,1,0:T(8,128)(2,1)} %bitcast.41), calls=%async_computation.5 | async-start | bytes 2621440 | tf_op jit(solution)/shard_map/all_to_all | solution.py:61
  403.8 22.7 %all-to-all-start.8 = ((bf16[16,40,1024]{2,1,0:T(8,128)(2,1)}), bf16[16,40,1024]{2,1,0:T(8,128)(2,1)}, u32[]{:S(2)}, u32[]{:S(2)}) async-start(bf16[16,40,1024]{2,1,0:T(8,128)(2,1)} %bitcast.55), calls=%async_computation.8 | async-start | bytes 2621440 | tf_op jit(solution)/shard_map/all_to_all | solution.py:61
  431.9 8.3 %collective-permute-start.18 = (bf16[4,32,2176]{2,1,0:T(8,128)(2,1)S(1)}, bf16[4,32,2176]{2,1,0:T(8,128)(2,1)S(1)}, u32[]{:S(2)}, u32[]{:S(2)}) collective-permute-start(bf16[4,32,2176]{2,1,0:T(8,128)(2,1)S(1)} %fusion.43), channel_id=1, source_target_pairs={{0,1},{1,0},{2,3},{3,2},{4,5},{5,4},{6,7},{7,6},{8,9},{9,8},{10,11... | collective-permute-start | bytes 1671176 | tf_op jit(solution)/shard_map/ppermute | solution.py:53
  441.1 14.5 %all-to-all-start.9 = ((bf16[4,32,2176]{2,1,0:T(8,128)(2,1)}), bf16[4,32,2176]{2,1,0:T(8,128)(2,1)}, u32[]{:S(2)}, u32[]{:S(2)}) async-start(bf16[4,32,2176]{2,1,0:T(8,128)(2,1)} %fusion.29), calls=%async_computation.9 | async-start | bytes 1114112 | tf_op jit(solution)/shard_map/all_to_all | solution.py:61
  455.7 45.6 %all-to-all-start.17 = ((bf16[4,176,2048]{2,1,0:T(8,128)(2,1)}), bf16[4,176,2048]{2,1,0:T(8,128)(2,1)}, u32[]{:S(2)}, u32[]{:S(2)}) async-start(bf16[4,176,2048]{2,1,0:T(8,128)(2,1)} %bitcast.278), calls=%async_computation.17 | async-start | bytes 5767168 | tf_op jit(solution)/shard_map/all_to_all | solution.py:61
  463.9 33.3 %collective-permute-start.19 = (bf16[32,2176]{1,0:T(8,128)(2,1)S(1)}, bf16[32,2176]{1,0:T(8,128)(2,1)S(1)}, u32[]{:S(2)}, u32[]{:S(2)}) collective-permute-start(bf16[32,2176]{1,0:T(8,128)(2,1)S(1)} %pad_maximum_fusion.14), channel_id=1, source_target_pairs={{0,2},{2,4},{4,6},{6,0},{1,3},{3,5},{5,7},{7,1},{8,10},{10,12},{12... | collective-permute-start | bytes 417800 | tf_op jit(solution)/shard_map/ppermute | solution.py:57
  465.4 35.1 %collective-permute-start.20 = (bf16[32,2176]{1,0:T(8,128)(2,1)S(1)}, bf16[32,2176]{1,0:T(8,128)(2,1)S(1)}, u32[]{:S(2)}, u32[]{:S(2)}) collective-permute-start(bf16[32,2176]{1,0:T(8,128)(2,1)S(1)} %pad_maximum_fusion.14), channel_id=1, source_target_pairs={{0,4},{2,6},{4,0},{6,2},{1,5},{3,7},{5,1},{7,3},{8,12},{10,14},{12... | collective-permute-start | bytes 417800 | tf_op jit(solution)/shard_map/ppermute | solution.py:57
  467.8 38.1 %collective-permute-start.21 = (bf16[32,2176]{1,0:T(8,128)(2,1)S(1)}, bf16[32,2176]{1,0:T(8,128)(2,1)}, u32[]{:S(2)}, u32[]{:S(2)}) collective-permute-start(bf16[32,2176]{1,0:T(8,128)(2,1)S(1)} %pad_maximum_fusion.14), channel_id=1, source_target_pairs={{0,6},{2,0},{4,2},{6,4},{1,7},{3,1},{5,3},{7,5},{8,14},{10,8},{12,... | collective-permute-start | bytes 417800 | tf_op jit(solution)/shard_map/ppermute | solution.py:57
  501.2 38.0 %all-to-all-start.18 = ((bf16[4,176,2048]{2,1,0:T(8,128)(2,1)}), bf16[4,176,2048]{2,1,0:T(8,128)(2,1)}, u32[]{:S(2)}, u32[]{:S(2)}) async-start(bf16[4,176,2048]{2,1,0:T(8,128)(2,1)} %bitcast.277), calls=%async_computation.18 | async-start | bytes 5767168 | tf_op jit(solution)/shard_map/all_to_all | solution.py:61
  507.5 7.6 collective-permute-start.22
  515.1 56.1 %collective-permute-start.11 = (bf16[4,32,2048]{2,1,0:T(8,128)(2,1)}, bf16[4,32,2048]{2,1,0:T(8,128)(2,1)}, u32[]{:S(2)}, u32[]{:S(2)}) collective-permute-start(bf16[4,32,2048]{2,1,0:T(8,128)(2,1)} %dynamic-slice_bitcast_fusion.1), channel_id=1, source_target_pairs={{0,1},{1,0},{2,3},{3,2},{4,5},{5,4},{6,7},{7,6},{8,9},{9,8},{10,11... | collective-permute-start | bytes 1572872 | tf_op jit(solution)/shard_map/ppermute | solution.py:53
  539.3 37.0 %all-to-all-start.19 = ((bf16[4,176,2048]{2,1,0:T(8,128)(2,1)}), bf16[4,176,2048]{2,1,0:T(8,128)(2,1)}, u32[]{:S(2)}, u32[]{:S(2)}) async-start(bf16[4,176,2048]{2,1,0:T(8,128)(2,1)} %bitcast.276), calls=%async_computation.19 | async-start | bytes 5767168 | tf_op jit(solution)/shard_map/all_to_all | solution.py:61
  568.7 22.8 %copy-start.53 = (bf16[256,384]{1,0:T(8,128)(2,1)S(1)}, bf16[256,384]{1,0:T(8,128)(2,1)}, u32[]{:S(2)}) copy-start(bf16[256,384]{1,0:T(8,128)(2,1)} %copy-done.52) | copy-start | bytes 589828
  568.7 11.7 %collective-permute-start.23 = (bf16[4,32,2048]{2,1,0:T(8,128)(2,1)}, bf16[4,32,2048]{2,1,0:T(8,128)(2,1)}, u32[]{:S(2)}, u32[]{:S(2)}) collective-permute-start(bf16[4,32,2048]{2,1,0:T(8,128)(2,1)} %dynamic-slice_bitcast_fusion), channel_id=1, source_target_pairs={{0,1},{1,0},{2,3},{3,2},{4,5},{5,4},{6,7},{7,6},{8,9},{9,8},{10,11... | collective-permute-start | bytes 1572872 | tf_op jit(solution)/shard_map/ppermute | solution.py:53
  576.3 11.1 %all-to-all-start.6 = ((bf16[4,32,2048]{2,1,0:T(8,128)(2,1)}), bf16[4,32,2048]{2,1,0:T(8,128)(2,1)}, u32[]{:S(2)}, u32[]{:S(2)}) async-start(bf16[4,32,2048]{2,1,0:T(8,128)(2,1)} %fusion.31), calls=%async_computation.6 | async-start | bytes 1048576 | tf_op jit(solution)/shard_map/all_to_all | solution.py:61
  587.4 11.1 %all-to-all-start.10 = ((bf16[4,32,2048]{2,1,0:T(8,128)(2,1)}), bf16[4,32,2048]{2,1,0:T(8,128)(2,1)}, u32[]{:S(2)}, u32[]{:S(2)}) async-start(bf16[4,32,2048]{2,1,0:T(8,128)(2,1)} %fusion.30), calls=%async_computation.10 | async-start | bytes 1048576 | tf_op jit(solution)/shard_map/all_to_all | solution.py:61
  598.5 70.9 %all-to-all-start.11 = ((bf16[16,256,640]{2,1,0:T(8,128)(2,1)}), bf16[16,256,640]{2,1,0:T(8,128)(2,1)}, u32[]{:S(2)}, u32[]{:S(2)}) async-start(bf16[16,256,640]{2,1,0:T(8,128)(2,1)} %bitcast.244), calls=%async_computation.11 | async-start | bytes 10485760 | tf_op jit(solution)/shard_map/all_to_all | solution.py:61
  603.7 182.3 %reduce-scatter.4.cloned.1.call-start = ((), (), s32[]{:S(2)}) async-start(), calls=%async_computation.24 | async-start | bytes 6127616
  627.6 53.2 %copy-start.74 = (f32[256]{0:T(256)S(1)}, f32[256]{0:T(256)}, u32[]{:S(2)}) copy-start(f32[256]{0:T(256)} %copy-done.73) | copy-start | bytes 3076
  669.5 42.3 %all-to-all-start.15 = ((bf16[16,128,384]{2,1,0:T(8,128)(2,1)}), bf16[16,128,384]{2,1,0:T(8,128)(2,1)}, u32[]{:S(2)}, u32[]{:S(2)}) async-start(bf16[16,128,384]{2,1,0:T(8,128)(2,1)} %bitcast.260), calls=%async_computation.15 | async-start | bytes 3145728 | tf_op jit(solution)/shard_map/all_to_all | solution.py:61
  706.4 4.6 collective-permute-start.24
  709.8 22.0 %copy-start.19 = (bf16[32,2048]{1,0:T(8,128)(2,1)S(1)}, bf16[32,2048]{1,0:T(8,128)(2,1)}, u32[]{:S(2)}) copy-start(bf16[32,2048]{1,0:T(8,128)(2,1)} %param.20) | copy-start | bytes 393220
  709.8 22.0 %copy-start.57 = (f32[1,2048]{1,0:T(1,128)S(1)}, f32[1,2048]{1,0:T(1,128)}, u32[]{:S(2)}) copy-start(f32[1,2048]{1,0:T(1,128)} %copy-done.56) | copy-start | bytes 24580
  709.8 22.0 %copy-start.77 = (f32[32]{0:T(128)S(1)}, f32[32]{0:T(128)}, u32[]{:S(2)}) copy-start(f32[32]{0:T(128)} %add_rsqrt_fusion.2) | copy-start | bytes 388
  711.8 9.1 %all-to-all-start.12 = ((bf16[4,32,640]{2,1,0:T(8,128)(2,1)}), bf16[4,32,640]{2,1,0:T(8,128)(2,1)S(1)}, u32[]{:S(2)}, u32[]{:S(2)}) async-start(bf16[4,32,640]{2,1,0:T(8,128)(2,1)} %fusion.58), calls=%async_computation.12 | async-start | bytes 327680 | tf_op jit(solution)/shard_map/all_to_all | solution.py:61
  723.5 4.1 collective-permute-start.25
  723.8 4.7 collective-permute-start.26
  725.6 3.6 collective-permute-start.27
  729.8 6.0 collective-permute-start.28
  738.3 21.6 %copy-start.72 = (f32[32]{0:T(128)S(1)}, f32[32]{0:T(128)}, u32[]{:S(2)}) copy-start(f32[32]{0:T(128)} %copy-done.70) | copy-start | bytes 388
  738.3 17.9 %all-to-all-start.13 = ((bf16[16,128,128]{1,2,0:T(8,128)(2,1)}), bf16[16,128,128]{1,2,0:T(8,128)(2,1)S(1)}, u32[]{:S(2)}, u32[]{:S(2)}) async-start(bf16[16,128,128]{1,2,0:T(8,128)(2,1)} %pad_maximum_fusion.6), calls=%async_computation.13 | async-start | bytes 1048576 | tf_op jit(solution)/shard_map/all_to_all | solution.py:61
  756.2 13.7 %all-to-all-start.16 = ((bf16[16,32,512]{2,1,0:T(8,128)(2,1)}), bf16[16,32,512]{2,1,0:T(8,128)(2,1)S(1)}, u32[]{:S(2)}, u32[]{:S(2)}) async-start(bf16[16,32,512]{2,1,0:T(8,128)(2,1)} %bitcast.97), calls=%async_computation.16 | async-start | bytes 1048576 | tf_op jit(solution)/shard_map/all_to_all | solution.py:61
  770.6 12.9 %all-to-all-start.14 = ((bf16[8,128,128]{1,2,0:T(8,128)(2,1)}), bf16[8,128,128]{1,2,0:T(8,128)(2,1)S(1)}, u32[]{:S(2)}, u32[]{:S(2)}) async-start(bf16[8,128,128]{1,2,0:T(8,128)(2,1)} %broadcast_in_dim.165), calls=%async_computation.14 | async-start | bytes 524288 | tf_op jit(solution)/shard_map/all_to_all | solution.py:61
  (81 other events, 624.7 us)
Sparse Core Ops, SparseCore 0:
  15.1 70.2 all-gather.3
  98.0 56.6 all-gather.5
  285.1 60.1 all-gather.7
  624.6 119.8 reduce-scatter.3

commit v2 on v1

v2 whole, which is shorter than its diff:
```python
import jax
import jax.numpy as jnp
from jax import lax
from jax.experimental import pallas as pl
from jax.experimental.layout import Layout, with_layout_constraint
from jax.experimental.pallas import tpu as pltpu
from jax.sharding import Mesh, PartitionSpec as P

D = 2048
H_DEV = 2
DN = 128
DV = 128
DR = 64
KVL = 512
PIECE = 256
EXPERTS = 64
ROWS = 256
OWN = 32
SLOTS = 40
FFH = 704
FFS = 176
FFP = 768
SHP = 384
KEYS = 4096
CHUNK = 512
EPS = 1e-06
NEG = -1e30
SCALE = (DN + DR) ** (-0.5)
EX = ("z", "x")
HALF = jnp.bfloat16
WIDE = jnp.float32


def dot_nn(left, right):
    return jnp.dot(left, right, preferred_element_type=WIDE)


def dot_nt(left, right):
    return lax.dot_general(left, right, (((1,), (1,)), ((), ())), preferred_element_type=WIDE)


def dot_tn(left, right):
    return lax.dot_general(left, right, (((0,), (0,)), ((), ())), preferred_element_type=WIDE)


def inv_rms(values):
    return lax.rsqrt(jnp.mean(values * values, axis=-1, keepdims=True) + EPS)


def norm_back(grad, normed, row_scale, gain):
    scaled = grad * gain
    inner_mean = jnp.mean(scaled * normed, axis=-1, keepdims=True)
    return (row_scale * (scaled - normed * inner_mean), jnp.sum(grad * normed, axis=0))


def row_major(value):
    return with_layout_constraint(value, Layout(major_to_minor=(0, 1)))


def swap_core(value):
    return lax.ppermute(value, "c", [(0, 1), (1, 0)])


def shift_y(value, by):
    return lax.ppermute(value, "y", [(i, (i + by) % 4) for i in range(4)])


def spread(value, axes):
    return lax.all_to_all(value, axes, split_axis=0, concat_axis=0, tiled=True)


def gather_rows(value, yi, ci):
    n = value.shape[1]
    block = jnp.zeros((4, OWN, n), value.dtype)
    block = lax.dynamic_update_slice(block, value[None], (yi, 0, 0))
    for by in (1, 2, 3):
        block = lax.dynamic_update_slice(block, shift_y(value, by)[None], ((yi - by) % 4, 0, 0))
    other = swap_core(block)
    first = jnp.where(ci == 0, block, other)
    second = jnp.where(ci == 0, other, block)
    return jnp.stack([first, second], axis=1).reshape(ROWS, n)


def core_sum(value, ci):
    parts = value.reshape(4, 2, OWN, value.shape[1])
    mine = lax.dynamic_index_in_dim(parts, ci, 1, keepdims=False)
    theirs = lax.dynamic_index_in_dim(parts, 1 - ci, 1, keepdims=False)
    return (mine.astype(WIDE) + swap_core(theirs).astype(WIDE)).astype(HALF)


def row_sum(pair, yi):
    total = lax.dynamic_index_in_dim(pair, yi, 0, keepdims=False).astype(WIDE)
    for by in (1, 2, 3):
        piece = lax.dynamic_index_in_dim(pair, (yi + by) % 4, 0, keepdims=False)
        total = total + shift_y(piece, by).astype(WIDE)
    return total


def sum_rows(value, yi, ci):
    return row_sum(core_sum(value, ci), yi)


def sum_experts(value):
    rows, width = value.shape
    parts = spread(value.reshape(16, rows // 16, width), EX)
    return jnp.sum(parts.astype(WIDE), axis=0)


def spans(row_ids, seq_lengths, piece_starts):
    ends = jnp.cumsum(seq_lengths)
    starts = ends - seq_lengths
    member = (row_ids[:, None] >= starts[None, :]) & (row_ids[:, None] < ends[None, :])
    member = member.astype(jnp.int32)
    low = jnp.sum(member * starts[None, :], axis=1)
    end = jnp.sum(member * ends[None, :], axis=1)
    inside = (row_ids[:, None] >= piece_starts[None, :]) & (
        row_ids[:, None] < piece_starts[None, :] + PIECE
    )
    piece_last = jnp.max(jnp.where(inside, piece_starts[None, :] + (PIECE - 1), -1), axis=1)
    high = jnp.where(piece_last >= 0, jnp.minimum(piece_last, end - 1), row_ids)
    return row_ids - low, low, high


def head_query(q_ref, head):
    lane = lax.broadcasted_iota(jnp.int32, (ROWS, 128), 1)
    rot = q_ref[:, 256:384]
    rot = jnp.where((lane // 32) % 2 == head, rot, jnp.zeros_like(rot))
    return jnp.concatenate([q_ref[:, 128 * head : 128 * head + 128], rot], axis=1)


def attend_kernel(q_ref, kv_ref, rot_ref, low_ref, high_ref, p_ref, o_ref, s_ref):
    low = low_ref[...]
    high = high_ref[...]
    for head in range(H_DEV):
        query = head_query(q_ref, head)

        def scores_step(i, top):
            at = pl.multiple_of(i * CHUNK, CHUNK)
            key = jnp.concatenate(
                [
                    kv_ref[pl.ds(at, CHUNK), 128 * head : 128 * head + 128],
                    rot_ref[pl.ds(at, CHUNK), :],
                ],
                axis=1,
            )
            scores = dot_nt(key, query) * SCALE
            col = lax.broadcasted_iota(jnp.int32, (CHUNK, ROWS), 0) + at
            scores = jnp.where((col >= low) & (col <= high), scores, NEG)
            s_ref[pl.ds(at, CHUNK), :] = scores
            return jnp.maximum(top, jnp.max(scores.reshape(CHUNK // 8, 8, ROWS), axis=0))

        top = lax.fori_loop(
            0, KEYS // CHUNK, scores_step, jnp.full((8, ROWS), NEG, WIDE)
        )
        top = jnp.max(top, axis=0, keepdims=True)

        def exp_step(i, total):
            at = pl.multiple_of(i * CHUNK, CHUNK)
            weights = jnp.exp(s_ref[pl.ds(at, CHUNK), :] - top)
            s_ref[pl.ds(at, CHUNK), :] = weights
            return total + jnp.sum(weights.reshape(CHUNK // 8, 8, ROWS), axis=0)

        total = lax.fori_loop(0, KEYS // CHUNK, exp_step, jnp.zeros((8, ROWS), WIDE))
        inverse = 1.0 / jnp.sum(total, axis=0, keepdims=True)

        def value_step(i, acc):
            at = pl.multiple_of(i * CHUNK, CHUNK)
            probs = (s_ref[pl.ds(at, CHUNK), :] * inverse).astype(HALF)
            p_ref[head, pl.ds(at, CHUNK), :] = probs
            value = kv_ref[pl.ds(at, CHUNK), 256 + 128 * head : 384 + 128 * head]
            return acc + dot_tn(value, probs)

        out = lax.fori_loop(0, KEYS // CHUNK, value_step, jnp.zeros((DN, ROWS), WIDE))
        o_ref[:, 128 * head : 128 * head + 128] = out.T


def attend(queries, kv_all, rot_all, low, high):
    vmem = pl.BlockSpec(memory_space=pltpu.VMEM)
    return pl.pallas_call(
        attend_kernel,
        out_shape=(
            jax.ShapeDtypeStruct((H_DEV, KEYS, ROWS), HALF),
            jax.ShapeDtypeStruct((ROWS, H_DEV * DN), WIDE),
        ),
        in_specs=[vmem] * 5,
        out_specs=(vmem, vmem),
        scratch_shapes=[pltpu.VMEM((KEYS, ROWS), WIDE)],
        compiler_params=pltpu.CompilerParams(vmem_limit_bytes=40 * 1024 * 1024),
        cost_estimate=pl.CostEstimate(
            flops=2 * H_DEV * ROWS * KEYS * 384, bytes_accessed=12 << 20, transcendentals=2 << 20
        ),
    )(queries, kv_all, rot_all, low, high)


def attend_back_kernel(
    core_ref, q_ref, kv_ref, rot_ref, p_ref, dmid_ref, wot_ref, wkv_ref, o_ref,
    keep_ref, send_ref, dkv_ref, dq_ref, acc_ref, do_ref, delta_ref, qf_ref,
):
    step = pl.program_id(0)

    @pl.when(step == 0)
    def _():
        acc_ref[...] = jnp.zeros_like(acc_ref)
        d_heads = dot_nn(dmid_ref[...], wot_ref[...]).astype(HALF)
        do_ref[...] = d_heads
        product = d_heads.astype(WIDE) * o_ref[...]
        for head in range(H_DEV):
            delta_ref[8 * head : 8 * head + 8, :] = lax.dot_general(
                jnp.ones((8, 128), WIDE),
                product[:, 128 * head : 128 * head + 128],
                (((1,), (1,)), ((), ())),
                precision=lax.Precision.HIGHEST,
                preferred_element_type=WIDE,
            )
            qf_ref[head] = head_query(q_ref, head)

    rot = rot_ref[...]
    d_rot = jnp.zeros((CHUNK, 128), WIDE)
    for head in range(H_DEV):
        d_out = do_ref[:, 128 * head : 128 * head + 128]
        value = kv_ref[:, 256 + 128 * head : 384 + 128 * head]
        probs = p_ref[head]
        d_probs = dot_nt(value, d_out)
        d_scores = (
            probs.astype(WIDE) * (d_probs - delta_ref[8 * head : 8 * head + 1, :])
        ).astype(HALF)
        d_key = dot_nn(d_scores, qf_ref[head]) * SCALE
        dkv_ref[:, 128 * head : 128 * head + 128] = d_key[:, :128].astype(HALF)
        d_rot = d_rot + d_key[:, 128:]
        dkv_ref[:, 256 + 128 * head : 384 + 128 * head] = dot_nn(probs, d_out).astype(HALF)
        key = jnp.concatenate([kv_ref[:, 128 * head : 128 * head + 128], rot], axis=1)
        acc_ref[head] += dot_tn(key, d_scores)
    d_lat = dot_nt(dkv_ref[...], wkv_ref[...]).astype(HALF)
    d_rot = d_rot.astype(HALF)

    def write(target, core):
        for block in range(CHUNK // ROWS):
            for y in range(4):
                row = ROWS * block + OWN * (2 * y + core)
                target[y, block, :, :512] = d_lat[row : row + OWN]
                target[y, block, :, 512:] = d_rot[row : row + OWN]

    @pl.when(core_ref[0] == 0)
    def _():
        write(keep_ref, 0)
        write(send_ref, 1)

    @pl.when(core_ref[0] != 0)
    def _():
        write(keep_ref, 1)
        write(send_ref, 0)

    @pl.when(step == KEYS // CHUNK - 1)
    def _():
        lane = lax.broadcasted_iota(jnp.int32, (ROWS, 128), 1)
        d_q_rot = jnp.zeros((ROWS, 128), WIDE)
        for head in range(H_DEV):
            d_query = acc_ref[head].T * SCALE
            dq_ref[:, 128 * head : 128 * head + 128] = d_query[:, :128]
            d_q_rot = jnp.where((lane // 32) % 2 == head, d_query[:, 128:], d_q_rot)
        dq_ref[:, 256:384] = d_q_rot


def attend_back(ci, queries, kv_all, rot_all, probs, d_mid, wot, wkv, heads):
    def whole(*shape):
        return pl.BlockSpec(shape, lambda i, core: (0,) * len(shape))

    share = jax.ShapeDtypeStruct((4, 16, OWN, 640), HALF)
    share_spec = pl.BlockSpec((4, CHUNK // ROWS, OWN, 640), lambda i, core: (0, i, 0, 0))
    return pl.pallas_call(
        attend_back_kernel,
        out_shape=(
            share,
            share,
            jax.ShapeDtypeStruct((KEYS, 512), HALF),
            jax.ShapeDtypeStruct((ROWS, 384), WIDE),
        ),
        grid_spec=pltpu.PrefetchScalarGridSpec(
            num_scalar_prefetch=1,
            grid=(KEYS // CHUNK,),
            in_specs=[
                whole(ROWS, 384),
                pl.BlockSpec((CHUNK, 512), lambda i, core: (i, 0)),
                pl.BlockSpec((CHUNK, 128), lambda i, core: (i, 0)),
                pl.BlockSpec((H_DEV, CHUNK, ROWS), lambda i, core: (0, i, 0)),
                whole(ROWS, D),
                whole(D, 256),
                whole(KVL, 512),
                whole(ROWS, 256),
            ],
            out_specs=(
                share_spec,
                share_spec,
                pl.BlockSpec((CHUNK, 512), lambda i, core: (i, 0)),
                whole(ROWS, 384),
            ),
            scratch_shapes=[
                pltpu.VMEM((H_DEV, 256, ROWS), WIDE),
                pltpu.VMEM((ROWS, H_DEV * DV), HALF),
                pltpu.VMEM((8 * H_DEV, ROWS), WIDE),
                pltpu.VMEM((H_DEV, ROWS, 256), HALF),
            ],
        ),
        compiler_params=pltpu.CompilerParams(vmem_limit_bytes=32 * 1024 * 1024),
        cost_estimate=pl.CostEstimate(
            flops=2 * H_DEV * ROWS * KEYS * 768 + 2 * KEYS * 512 * 512,
            bytes_accessed=24 << 20,
            transcendentals=0,
        ),
    )(ci.reshape(1), queries, kv_all, rot_all, probs, d_mid, wot, wkv, heads)


def expert_kernel(at_ref, x_ref, xo_ref, g_ref, go_ref, *rest):
    pieces = rest[:12]
    keep_in, send_in, keep_out, send_out, x_out, dso_out, hid_out, dpre_out = rest[12:20]
    wg_ref, wu_ref, wd_ref, dots_ref, sems = rest[20:]
    copies = []
    for part, target in enumerate((wg_ref, wu_ref, wd_ref)):
        for k in range(4):
            copy = pltpu.make_async_copy(
                pieces[4 * part + k],
                target.at[pl.ds(FFS * k, FFS), :],
                sems.at[4 * part + k],
            )
            copy.start()
            copies.append(copy)
        target[FFH:, :] = jnp.zeros((FFP - FFH, D), HALF)
    first = at_ref[0] == 0
    half = D // 2
    own = x_ref[:, :half]
    other = xo_ref[:, :half]
    x_out[:, :half] = jnp.where(first, own, other)
    x_out[:, half:] = jnp.where(first, other, own)
    gate = x_ref[:, half : half + 1].astype(WIDE)
    own = (g_ref[...].astype(WIDE) * gate).astype(HALF)
    other = (go_ref[...].astype(WIDE) * gate).astype(HALF)
    dso_out[:, :half] = jnp.where(first, own, other)
    dso_out[:, half:] = jnp.where(first, other, own)
    for copy in copies:
        copy.wait()

    def hidden_step(i, carry):
        at = pl.multiple_of(i * 256, 256)
        x = x_out[...]
        pre_gate = dot_nt(x, wg_ref[pl.ds(at, 256), :])
        pre_up = dot_nt(x, wu_ref[pl.ds(at, 256), :])
        d_hidden = dot_nt(dso_out[...], wd_ref[pl.ds(at, 256), :])
        sig = 1.0 / (1.0 + jnp.exp(-pre_gate))
        act = pre_gate * sig
        hid_out[:, pl.ds(at, 256)] = (act * pre_up).astype(HALF)
        slope = sig * (1.0 + pre_gate * (1.0 - sig))
        dpre_out[:, pl.ds(at, 256)] = (d_hidden * pre_up * slope).astype(HALF)
        dpre_out[:, pl.ds(pl.multiple_of(at + FFP, 256), 256)] = (d_hidden * act).astype(HALF)
        return carry

    lax.fori_loop(0, FFP // 256, hidden_step, 0)

    dots_ref[...] = jnp.zeros_like(dots_ref)

    def output_step(i, carry):
        at = pl.multiple_of(i * 256, 256)
        to = pl.multiple_of((i % 4) * 256, 256)
        own_side = (i // 4) == at_ref[0]
        d_in = dot_nn(dpre_out[:, :FFP], wg_ref[:, pl.ds(at, 256)])
        d_in = d_in + dot_nn(dpre_out[:, FFP:], wu_ref[:, pl.ds(at, 256)])
        d_in = d_in.astype(HALF)
        out = dot_nn(hid_out[...], wd_ref[:, pl.ds(at, 256)])
        g = jnp.where(own_side, g_ref[:, pl.ds(to, 256)], go_ref[:, pl.ds(to, 256)])
        dots = out * g.astype(WIDE)
        dots_ref[...] += dots[:, :128] + dots[:, 128:]
        out = out.astype(HALF)

        @pl.when(own_side)
        def _():
            keep_in[:, pl.ds(to, 256)] = d_in
            keep_out[:, pl.ds(to, 256)] = out

        @pl.when(jnp.logical_not(own_side))
        def _():
            send_in[:, pl.ds(to, 256)] = d_in
            send_out[:, pl.ds(to, 256)] = out

        return carry

    lax.fori_loop(0, D // 256, output_step, 0)
    total = jnp.sum(dots_ref[...], axis=1, keepdims=True)
    keep_in[:, half:] = jnp.broadcast_to(total, (16 * SLOTS, 128)).astype(HALF)
    send_in[:, half:] = jnp.zeros((16 * SLOTS, 128), HALF)


def run_expert(ci, x_own, x_other, g_own, g_other, pieces):
    rows = 16 * SLOTS
    vmem = pl.BlockSpec(memory_space=pltpu.VMEM)
    return pl.pallas_call(
        expert_kernel,
        out_shape=(
            jax.ShapeDtypeStruct((rows, D // 2 + 128), HALF),
            jax.ShapeDtypeStruct((rows, D // 2 + 128), HALF),
            jax.ShapeDtypeStruct((rows, D // 2), HALF),
            jax.ShapeDtypeStruct((rows, D // 2), HALF),
            jax.ShapeDtypeStruct((rows, D), HALF),
            jax.ShapeDtypeStruct((rows, D), HALF),
            jax.ShapeDtypeStruct((rows, FFP), HALF),
            jax.ShapeDtypeStruct((rows, 2 * FFP), HALF),
        ),
        in_specs=[pl.BlockSpec(memory_space=pltpu.SMEM)]
        + [vmem] * 4
        + [pl.BlockSpec(memory_space=pl.ANY)] * 12,
        out_specs=(vmem,) * 8,
        scratch_shapes=[pltpu.VMEM((FFP, D), HALF)] * 3
        + [pltpu.VMEM((rows, 128), WIDE), pltpu.SemaphoreType.DMA((12,))],
        compiler_params=pltpu.CompilerParams(vmem_limit_bytes=52 * 1024 * 1024),
        cost_estimate=pl.CostEstimate(
            flops=12 * rows * D * FFP, bytes_accessed=28 << 20, transcendentals=rows * FFP
        ),
    )(ci.reshape(1), x_own, x_other, g_own, g_other, *pieces)


def place_kernel(at_ref, *refs):
    out_ref = refs[4]
    step = pl.program_id(0)
    for k in range(4):

        @pl.when(step == k)
        def _():
            out_ref[0] = refs[k][...].astype(WIDE)


def place_pieces(yi, pieces):
    return pl.pallas_call(
        place_kernel,
        out_shape=jax.ShapeDtypeStruct((4, FFS, D), WIDE),
        grid_spec=pltpu.PrefetchScalarGridSpec(
            num_scalar_prefetch=1,
            grid=(4,),
            in_specs=[pl.BlockSpec((FFS, D), lambda k, at: (0, 0))] * 4,
            out_specs=pl.BlockSpec((1, FFS, D), lambda k, at: ((at[0] + k) % 4, 0, 0)),
        ),
        compiler_params=pltpu.CompilerParams(vmem_limit_bytes=24 * 1024 * 1024),
        cost_estimate=pl.CostEstimate(flops=1, bytes_accessed=1, transcendentals=0),
    )(yi.reshape(1), *pieces)


def late_kernel(dq_ref, wq_ref, so_ref, gated_ref, out_ref, core_ref, late_ref):
    late_ref[:, :D] = dot_nt(dq_ref[...], wq_ref[...]).astype(HALF)
    routed = dot_tn(gated_ref[...], out_ref[...])
    half = D // 2
    first = (core_ref[0] == 0).astype(WIDE)
    late_ref[:, D : D + half] = (so_ref[:, :half] + routed * first).astype(HALF)
    late_ref[:, D + half :] = (so_ref[:, half:] + routed * (1.0 - first)).astype(HALF)


def late_products(ci, d_queries, wq, shared_out, gated, out_back):
    vmem = pl.BlockSpec(memory_space=pltpu.VMEM)
    return pl.pallas_call(
        late_kernel,
        out_shape=jax.ShapeDtypeStruct((ROWS, 2 * D), HALF),
        in_specs=[vmem] * 5 + [pl.BlockSpec(memory_space=pltpu.SMEM)],
        out_specs=vmem,
        compiler_params=pltpu.CompilerParams(vmem_limit_bytes=32 * 1024 * 1024),
        cost_estimate=pl.CostEstimate(flops=1, bytes_accessed=1, transcendentals=0),
    )(d_queries, wq, shared_out, gated, out_back, ci.reshape(1))


def rest_kernel(
    h_two_ref, dsp_ref, g_ref, sh_ref, h_one_ref, dq_ref, dmid_ref, heads_ref, c_ref, dkv_ref,
    out_ref, kv_ref,
):
    def step(i, carry):
        at = pl.multiple_of(i * 256, 256)
        rows = pl.ds(at, 256)
        out_ref[rows, 0:768] = dot_tn(h_two_ref[:, rows], dsp_ref[...]).astype(HALF)
        out_ref[rows, 768:1152] = dot_tn(g_ref[:, rows], sh_ref[...]).astype(HALF)
        out_ref[rows, 1152:1536] = dot_tn(h_one_ref[:, rows], dq_ref[...]).astype(HALF)
        out_ref[rows, 1536:1792] = dot_tn(dmid_ref[:, rows], heads_ref[...]).astype(HALF)
        return carry

    lax.fori_loop(0, D // 256, step, 0)
    kv_ref[...] = jnp.zeros_like(kv_ref)

    def kv_step(i, carry):
        rows = pl.ds(pl.multiple_of(i * CHUNK, CHUNK), CHUNK)
        kv_ref[...] += dot_tn(c_ref[rows, 0:KVL], dkv_ref[rows, :])
        return carry

    lax.fori_loop(0, KEYS // CHUNK, kv_step, 0)
    for e in range(16):
        for block in range(4):
            row = 128 * e + 32 * block
            out_ref[row : row + 32, 1792:1920] = kv_ref[
                32 * e : 32 * e + 32, 128 * block : 128 * block + 128
            ].astype(HALF)


def rest_products(*operands):
    vmem = pl.BlockSpec(memory_space=pltpu.VMEM)
    return pl.pallas_call(
        rest_kernel,
        out_shape=jax.ShapeDtypeStruct((D, 1920), HALF),
        in_specs=[vmem] * 10,
        out_specs=vmem,
        scratch_shapes=[pltpu.VMEM((KVL, 512), WIDE)],
        compiler_params=pltpu.CompilerParams(vmem_limit_bytes=48 * 1024 * 1024),
        cost_estimate=pl.CostEstimate(flops=1, bytes_accessed=1, transcendentals=0),
    )(*operands)


def pack_query_columns(w):
    return jnp.concatenate(
        [w[:, 0:128], w[:, 192:320], w[:, 128:160], w[:, 320:352], w[:, 160:192], w[:, 352:384]],
        axis=1,
    )


def unpack_query_columns(w):
    return jnp.concatenate(
        [w[:, 0:128], w[:, 256:288], w[:, 320:352], w[:, 128:256], w[:, 288:320], w[:, 352:384]],
        axis=1,
    )


def pad_cols(w, width):
    return jnp.pad(w, ((0, 0), (0, width - w.shape[1])))


def silu_parts(gate):
    sig = jax.nn.sigmoid(gate)
    return gate * sig, sig * (1.0 + gate * (1.0 - sig))


def body(
    inputs,
    gain_attn,
    w_q,
    w_dkv,
    gain_latent,
    w_uk,
    w_uv,
    w_o,
    gain_ffn,
    w_router,
    w_sg,
    w_su,
    w_sd,
    w_eg,
    w_eu,
    w_ed,
    routes,
    seq_lengths,
    piece_starts,
    out_grad,
):
    zi, xi, yi, ci = (lax.axis_index(name) for name in ("z", "x", "y", "c"))
    ei = zi * 4 + xi
    ti = yi * 2 + ci

    def half_cols(value):
        return lax.dynamic_slice_in_dim(value, ci * (D // 2), D // 2, value.ndim - 1)

    def place_half(value):
        zero = jnp.zeros_like(value)
        return jnp.concatenate(
            [jnp.where(ci == 0, value, zero), jnp.where(ci == 0, zero, value)], axis=1
        )

    def swap_halves(v):
        return jnp.concatenate([v[:, 64:], v[:, :64]], axis=1)

    def own_rows(value):
        return lax.dynamic_slice_in_dim(value, ti * OWN, OWN, 0)

    def sent_pieces(weight):
        return [
            lax.dynamic_index_in_dim(weight, (yi + by) % 4, 0, keepdims=False).astype(HALF)
            for by in range(4)
        ]

    def moved_pieces(sent):
        return [sent[0]] + [shift_y(sent[by], by) for by in (1, 2, 3)]

    def own_pieces(grad):
        return [grad[FFS * by : FFS * (by + 1)] for by in range(4)]

    gain_cols = jnp.stack([gain_attn, gain_ffn, jnp.pad(gain_latent, (0, 96))], axis=1)
    w_router_perm = w_router.reshape(128, 16, 4).transpose(0, 2, 1).reshape(128, EXPERTS)
    first_pack = jnp.concatenate(
        [
            w_dkv,
            w_router_perm,
            jnp.concatenate([w_uk, w_uv], axis=1).reshape(128, 128),
            pad_cols(gain_cols, 128),
            pack_query_columns(w_q),
            w_o.T,
        ],
        axis=1,
    ).astype(HALF)
    first_all = lax.all_gather(first_pack, EX, axis=0, tiled=True)
    gate_sent, up_sent, down_sent = sent_pieces(w_eg), sent_pieces(w_eu), sent_pieces(w_ed)
    gate_sent, up_sent, inputs_b, out_grad_b = lax.optimization_barrier(
        (gate_sent, up_sent, inputs, out_grad)
    )
    gate_pieces = moved_pieces(gate_sent)
    in_rows = gather_rows(inputs_b, yi, ci)
    g_rows = gather_rows(out_grad_b, yi, ci)
    second_pack = jnp.concatenate(
        [pad_cols(w_sg, SHP), pad_cols(w_su, SHP), pad_cols(w_sd.T, SHP)], axis=1
    ).astype(HALF)

    row_ids = ei * ROWS + jnp.arange(ROWS, dtype=jnp.int32)
    position, low, high = spans(row_ids, seq_lengths, piece_starts)
    inv_freq = 10000.0 ** (-(2.0 * jnp.arange(DR // 2, dtype=WIDE)) / DR)
    angles = position.astype(WIDE)[:, None] * inv_freq[None, :]
    cosine, sine = jnp.cos(angles), jnp.sin(angles)
    cos4 = jnp.concatenate([cosine] * 4, axis=1)
    sin4 = jnp.concatenate([-sine, -sine, sine, sine], axis=1)

    routes_t = routes.T
    expert_ids = 4 * lax.broadcasted_iota(jnp.int32, (16, 1, ROWS), 0) + yi
    named = jnp.max((routes_t[None] == expert_ids).astype(WIDE), axis=1)
    earlier = (
        lax.broadcasted_iota(jnp.int32, (ROWS, ROWS), 0)
        < lax.broadcasted_iota(jnp.int32, (ROWS, ROWS), 1)
    ).astype(HALF)
    rank = dot_nn(named.astype(HALF), earlier)
    slot_ids = lax.broadcasted_iota(jnp.int32, (16, SLOTS, ROWS), 1).astype(WIDE)
    picked = (named[:, None, :] > 0.5) & (rank[:, None, :] == slot_ids)
    select = picked.astype(HALF).reshape(16 * SLOTS, ROWS)

    in_wide = in_rows.astype(WIDE)
    normed_in = in_wide * inv_rms(in_wide)
    first_all, gate_pieces, up_sent, down_sent, second_pack = lax.optimization_barrier(
        (first_all, gate_pieces, up_sent, down_sent, second_pack)
    )
    normed_in, cos4, sin4, select = lax.optimization_barrier((normed_in, cos4, sin4, select))

    blk_b = first_all[:, 0:640]
    wkv_b = first_all[:, 640:768]
    pick = jnp.eye(8, 128, dtype=HALF)
    gains = dot_nt(pick, first_all[:, 768:896])
    wq_b = first_all[:, 896:1280]
    wot_b = first_all[:, 1280:1536]
    gain_one = gains[0]
    gain_two = gains[1]
    gain_lat = gains[2].reshape(16, 128)[:, :32].reshape(KVL)
    h_one = (normed_in * gain_one).astype(HALF)
    latent_all = dot_nn(h_one, blk_b)
    lat_part = latent_all[:, :KVL]
    scale_lat = inv_rms(lat_part)
    normed_lat = lat_part * scale_lat
    c_norm = (normed_lat * gain_lat).astype(HALF)
    rope_a, rope_b = latent_all[:, 512:544], latent_all[:, 544:576]
    rope = jnp.concatenate([rope_a, rope_a, rope_b, rope_b], axis=1)
    k_rot = rope * cos4 + swap_halves(rope) * sin4
    c_local = jnp.concatenate([c_norm, k_rot.astype(HALF)], axis=1)
    g_half = half_cols(g_rows)
    g_sent = dot_nn(select, g_half).astype(HALF).reshape(16, SLOTS, D // 2)
    c_local, up_sent, down_sent, g_sent, wq_b, wkv_b = lax.optimization_barrier(
        (c_local, up_sent, down_sent, g_sent, wq_b, wkv_b)
    )
    g_recv = spread(g_sent, EX).reshape(16 * SLOTS, D // 2)
    c_all = lax.all_gather(c_local, EX, axis=0, tiled=True)
    up_pieces = moved_pieces(up_sent)
    down_first = [down_sent[0], shift_y(down_sent[1], 1), None, shift_y(down_sent[3], 3)]
    wkv_b = wkv_b.reshape(KVL, 512)
    q_raw = dot_nn(h_one, wq_b)
    q_rot = q_raw[:, 256:]
    q_rot = q_rot * cos4 + swap_halves(q_rot) * sin4
    queries = jnp.concatenate([q_raw[:, :256], q_rot], axis=1).astype(HALF)
    c_all, queries, wot_b, wkv_b, up_pieces, down_first, g_recv, second_pack, down_sent = (
        lax.optimization_barrier(
            (c_all, queries, wot_b, wkv_b, up_pieces, down_first, g_recv, second_pack, down_sent)
        )
    )

    second_all = lax.all_gather(second_pack, EX, axis=0, tiled=True)
    kv_all = dot_nn(c_all[:, :KVL], wkv_b).astype(HALF)
    rot_all = c_all[:, KVL:]
    probs, heads_wide = attend(queries, kv_all, rot_all, low[None, :], high[None, :])
    attn_heads = heads_wide.astype(HALF)
    attn_own = sum_rows(dot_nt(attn_heads, wot_b).astype(HALF), yi, ci)

    in_own = inputs.astype(WIDE)
    mid_own = in_own + attn_own
    scale_two = inv_rms(mid_own)
    normed_two = mid_own * scale_two
    h_two_own = (normed_two * gain_two).astype(HALF)
    h_two = gather_rows(h_two_own, yi, ci)

    rope_router_b = blk_b[:, 512:640]
    logits_t = lax.dot_general(
        rope_router_b, h_two, (((0,), (1,)), ((), ())), preferred_element_type=WIDE
    )[64:]
    probs_t = jax.nn.softmax(logits_t, axis=0)
    gate_t = lax.dynamic_slice_in_dim(probs_t, yi * 16, 16, 0).astype(HALF).astype(WIDE)
    gated = jnp.where(picked, gate_t[:, None, :], 0.0)
    slot_gate = jnp.sum(gated, axis=2)
    gated = gated.astype(HALF).reshape(16 * SLOTS, ROWS)
    x_sent = dot_nn(select, half_cols(h_two)).astype(HALF).reshape(16, SLOTS, D // 2)
    slot_gate = jnp.broadcast_to(slot_gate[:, :, None], (16, SLOTS, 128)).astype(HALF)
    x_sent = jnp.concatenate([x_sent, slot_gate], axis=2)
    x_sent, g_own, down_sent, h_two = lax.optimization_barrier((x_sent, g_recv, down_sent, h_two))
    x_own = spread(x_sent, EX).reshape(16 * SLOTS, D // 2 + 128)
    g_other = swap_core(g_own)
    down_pieces = [down_first[0], down_first[1], shift_y(down_sent[2], 2), down_first[3]]

    wgu_b = second_all[:, : 2 * SHP]
    wsdt_b = second_all[:, 2 * SHP :]
    shared_pre = dot_nn(h_two, wgu_b)
    shared_gate, shared_up = shared_pre[:, :SHP], shared_pre[:, SHP:]
    shared_silu, shared_slope = silu_parts(shared_gate)
    shared_hidden = (shared_silu * shared_up).astype(HALF)
    shared_out = dot_nt(shared_hidden, wsdt_b)
    d_shared_hidden = dot_nn(g_rows, wsdt_b)
    d_shared_pre = jnp.concatenate(
        [d_shared_hidden * shared_up * shared_slope, d_shared_hidden * shared_silu], axis=1
    ).astype(HALF)
    d_shared_in = dot_nt(d_shared_pre, wgu_b)
    x_own, g_other, down_pieces, shared_out, d_shared_in, d_shared_pre, shared_hidden = (
        lax.optimization_barrier(
            (x_own, g_other, down_pieces, shared_out, d_shared_in, d_shared_pre, shared_hidden)
        )
    )

    x_other = swap_core(x_own)
    keep_in, send_in, keep_out, send_out, x_slots, d_slot_out, expert_hidden, d_expert_pre = (
        run_expert(
            ci, x_own, x_other, g_own, g_other, gate_pieces + up_pieces + down_pieces
        )
    )

    def pair(keep, send):
        return (keep.astype(WIDE) + swap_core(send).astype(WIDE)).astype(HALF)

    in_sent = pair(keep_in, send_in)
    gate_parts = own_pieces(dot_tn(d_expert_pre[:, :FFP], x_slots).astype(HALF))
    in_sent, gate_parts, keep_out, send_out, d_slot_out, expert_hidden, d_expert_pre = (
        lax.optimization_barrier(
            (in_sent, gate_parts, keep_out, send_out, d_slot_out, expert_hidden, d_expert_pre)
        )
    )
    in_recv = spread(in_sent.reshape(16, SLOTS, D // 2 + 128), EX)
    gate_back = [gate_parts[0], shift_y(gate_parts[1], -1), None, shift_y(gate_parts[3], -3)]
    out_sent = pair(keep_out, send_out)
    up_parts = own_pieces(dot_tn(d_expert_pre[:, FFP:], x_slots).astype(HALF))
    down_parts = own_pieces(dot_tn(expert_hidden, d_slot_out).astype(HALF))
    in_recv, out_sent, gate_parts, gate_back, up_parts, down_parts = lax.optimization_barrier(
        (in_recv, out_sent, gate_parts, gate_back, up_parts, down_parts)
    )

    in_back = in_recv[:, :, : D // 2].reshape(16 * SLOTS, D // 2)
    slot_dots = in_recv[:, :, D // 2 : D // 2 + 1].astype(WIDE)
    d_route_t = jnp.sum(jnp.where(picked, slot_dots, 0.0), axis=1).astype(HALF)
    lane_at = (
        lax.broadcasted_iota(jnp.int32, (16, 128), 0) + yi * 16
        == lax.broadcasted_iota(jnp.int32, (16, 128), 1)
    ).astype(HALF)
    d_route_part = dot_tn(d_route_t, lane_at)
    d_h_part = d_shared_in + place_half(dot_tn(select, in_back))
    back_part = jnp.concatenate([d_h_part, d_route_part], axis=1).astype(HALF)
    back_own = sum_rows(back_part, yi, ci)

    logits_own = dot_nn(h_two_own, rope_router_b)[:, 64:]
    probs_own = jax.nn.softmax(logits_own, axis=-1)
    d_route = back_own[:, D : D + EXPERTS]
    d_logits = (
        probs_own * (d_route - jnp.sum(probs_own * d_route, axis=-1, keepdims=True))
    ).astype(HALF)
    d_logits_pad = jnp.pad(d_logits, ((0, 0), (64, 0)))
    d_h_two = back_own[:, :D] + dot_nt(d_logits_pad, rope_router_b)
    d_mid_norm, gain_two_part = norm_back(d_h_two, normed_two, scale_two, gain_two)
    d_mid_own = d_mid_norm + out_grad.astype(WIDE)
    d_attn_b = gather_rows(d_mid_own.astype(HALF), yi, ci)
    d_attn_b, up_parts = lax.optimization_barrier((d_attn_b, up_parts))

    up_back = [up_parts[0], shift_y(up_parts[1], -1), None, shift_y(up_parts[3], -3)]
    lat_keep, lat_send, d_kv, d_q = attend_back(
        ci, queries, kv_all, rot_all, probs, d_attn_b, wot_b, wkv_b, heads_wide
    )
    lat_keep, lat_send, d_kv, d_q, up_parts, up_back = lax.optimization_barrier(
        (lat_keep, lat_send, d_kv, d_q, up_parts, up_back)
    )
    lat_pair = pair(lat_keep, lat_send)
    lat_pair, d_kv, d_q, d_attn_b, d_shared_pre, shared_hidden, out_sent = lax.optimization_barrier(
        (lat_pair, d_kv, d_q, d_attn_b, d_shared_pre, shared_hidden, out_sent)
    )
    out_back = spread(out_sent.reshape(16, SLOTS, D // 2), EX).reshape(16 * SLOTS, D // 2)
    lat_total = lax.dynamic_index_in_dim(lat_pair, yi, 0, keepdims=False).astype(WIDE)
    lat_pieces = [
        shift_y(lax.dynamic_index_in_dim(lat_pair, (yi + by) % 4, 0, keepdims=False), by)
        for by in (1, 2, 3)
    ]

    d_q_rot = d_q[:, 256:]
    d_q_rot = d_q_rot * cos4 - swap_halves(d_q_rot) * sin4
    d_queries = jnp.concatenate([d_q[:, :256], d_q_rot], axis=1).astype(HALF)
    rest_grads = rest_products(
        h_two, d_shared_pre, g_rows, shared_hidden, h_one, d_queries, d_attn_b, attn_heads, c_all, d_kv
    )
    for piece in lat_pieces:
        lat_total = lat_total + piece.astype(WIDE)
    lat_total, d_queries, out_back, down_parts, up_parts, rest_grads = lax.optimization_barrier(
        (lat_total.astype(HALF), d_queries, out_back, down_parts, up_parts, rest_grads)
    )
    rest_sum = lax.psum_scatter(rest_grads, EX, scatter_dimension=0, tiled=True)
    lat_parts = spread(lat_total, EX)
    down_back = [down_parts[0], shift_y(down_parts[1], -1), None, shift_y(down_parts[3], -3)]
    late_parts = late_products(ci, d_queries, wq_b, shared_out, gated, out_back)
    late_own = sum_rows(late_parts, yi, ci)
    lat_parts, down_parts, down_back, late_own = lax.optimization_barrier(
        (lat_parts, down_parts, down_back, late_own)
    )
    d_one_own = late_own[:, :D]
    layer_out = (mid_own + late_own[:, D:]).astype(HALF)
    d_lat_own = jnp.sum(lat_parts.astype(WIDE), axis=0)

    cos_own, sin_own = own_rows(cos4), own_rows(sin4)
    d_rope = d_lat_own[:, 512:]
    d_rope = d_rope * cos_own - swap_halves(d_rope) * sin_own
    d_rope = jnp.concatenate(
        [d_rope[:, 0:32] + d_rope[:, 32:64], d_rope[:, 64:96] + d_rope[:, 96:128]], axis=1
    )
    d_lat, grad_gain_lat = norm_back(
        d_lat_own[:, :512], own_rows(normed_lat), own_rows(scale_lat), gain_lat
    )
    d_latent_pad = jnp.pad(jnp.concatenate([d_lat, d_rope], axis=1).astype(HALF), ((0, 0), (0, 64)))
    d_both = jnp.concatenate([d_latent_pad, d_logits_pad], axis=1)
    d_both = spread(jnp.broadcast_to(d_both[None], (8, OWN, 768)), ("y", "c")).reshape(ROWS, 768)
    d_both, up_parts, down_parts, down_back, gate_parts = lax.optimization_barrier(
        (d_both, up_parts, down_parts, down_back, gate_parts)
    )
    d_latent = d_both[:, :576]
    d_logits_all = d_both[:, 704:768]
    down_back[2] = shift_y(down_parts[2], -2)
    gate_back[2] = shift_y(gate_parts[2], -2)
    up_back[2] = shift_y(up_parts[2], -2)
    d_h_one = d_one_own + dot_nt(d_latent_pad, blk_b)
    scale_one = inv_rms(in_own)
    normed_one = in_own * scale_one
    d_in_norm, gain_one_part = norm_back(d_h_one, normed_one, scale_one, gain_one)
    grad_inputs = (d_mid_own + d_in_norm).astype(HALF)

    grad_router = dot_tn(h_two, lax.dynamic_slice_in_dim(d_logits_all, ti * 8, 8, 1))
    grad_dkv = dot_tn(h_one, lax.dynamic_slice_in_dim(d_latent, ti * 72, 72, 1))
    gain_lat_wide = jnp.pad(grad_gain_lat.reshape(16, 32), ((0, 0), (0, 96))).reshape(D)
    gain_rows = jnp.stack([gain_one_part, gain_two_part, gain_lat_wide], axis=0).astype(HALF)
    gain_at = (
        lax.broadcasted_iota(jnp.int32, (3, 48), 0) == lax.broadcasted_iota(jnp.int32, (3, 48), 1)
    ).astype(HALF)
    last_part = jnp.concatenate([grad_dkv, grad_router, dot_tn(gain_rows, gain_at)], axis=1)
    last_parts = spread(last_part.astype(HALF).reshape(16, 128, 128), EX)
    last_parts, down_back = lax.optimization_barrier((last_parts, down_back))
    grad_ed = place_pieces(yi, down_back)
    last_sum = jnp.sum(last_parts.astype(WIDE), axis=0)
    last_all = spread(
        jnp.broadcast_to(last_sum.astype(HALF)[None], (8, 128, 128)), ("y", "c")
    )
    last_all, gate_back, up_back = lax.optimization_barrier((last_all, gate_back, up_back))
    grad_eg = place_pieces(yi, gate_back)
    grad_eu = place_pieces(yi, up_back)
    rest_sum = rest_sum.astype(WIDE)
    sum_kv = rest_sum[:, 1792:].reshape(4, 32, 128).transpose(1, 0, 2).reshape(32, 512)
    sum_dkv = last_all[:, :, :72].transpose(1, 0, 2).reshape(128, 576).astype(WIDE)
    sum_router = last_all[:, :, 72:80].transpose(1, 0, 2).reshape(128, 4, 16)
    sum_router = sum_router.transpose(0, 2, 1).reshape(128, EXPERTS).astype(WIDE)
    gain_sums = jnp.sum(last_all[:, :, 80:83].astype(WIDE), axis=0)

    return (
        layer_out,
        grad_inputs,
        gain_sums[:, 0],
        unpack_query_columns(rest_sum[:, 1152:1536]),
        sum_dkv,
        gain_sums[:32, 2],
        sum_kv[:, :256],
        sum_kv[:, 256:],
        rest_sum[:, 1536:1792].T,
        gain_sums[:, 1],
        sum_router,
        rest_sum[:, :352],
        rest_sum[:, SHP : SHP + 352],
        rest_sum[:, 2 * SHP : 2 * SHP + 352].T,
        grad_eg,
        grad_eu,
        grad_ed,
    )


def solution(mesh):
    grid = Mesh(mesh.devices.reshape(4, 4, 4, 2), ("z", "x", "y", "c"))
    ten = ("y", "c")
    rows = P(("z", "x", "y", "c"), None)
    wide = P(EX, ten)
    tall = P(ten, EX)
    expert = P(EX, ten, None)
    return jax.shard_map(
        body,
        mesh=grid,
        in_specs=(
            rows,
            P(EX),
            wide,
            P(EX, None),
            P(EX),
            wide,
            wide,
            tall,
            P(EX),
            P(EX, None),
            wide,
            wide,
            tall,
            expert,
            expert,
            expert,
            P(EX, None),
            P(),
            P(),
            rows,
        ),
        out_specs=(
            rows,
            rows,
            P(EX),
            wide,
            P(EX, None),
            P(EX),
            wide,
            wide,
            tall,
            P(EX),
            P(EX, None),
            wide,
            wide,
            tall,
            expert,
            expert,
            expert,
        ),
        check_vma=False,
    )
```

time: 808 us -> 576 us (0.71)
  waiting for transfers between devices: 349 us -> 193 us
  Pallas kernels: 19.4 us -> 76.2 us
  matrix products: 97.6 us -> 43.9 us
  other arithmetic: 102 us -> 49.1 us
  starting transfers between devices: 155 us -> 116 us
  local copies, waits for them, and re-layouts: 56.3 us -> 70.3 us
    all_to_all x20 -> x8, waiting for transfers between devices: 209 us -> 38.8 us  [spread(): return lax.all_to_all(value, axes, split_axis=0, concat_axis=0, tiled=True)]
    ppermute x15 -> x42, waiting for transfers between devices: 39.7 us -> 122 us  [shift_y(): return lax.ppermute(value, 'y', [(i, (i + by) % 4) for i in range(4)])]
    all_to_all x20 -> x8, starting transfers between devices: 105 us -> 45.6 us  [spread(): return lax.all_to_all(value, axes, split_axis=0, concat_axis=0, tiled=True)]
    pallas_call x1 -> x7, Pallas kernels: 9.33 us -> 66.2 us  [the longest x1 26.6 us: run_expert(): pl.pallas_call(expert_kernel, out_shape=(jax.ShapeDtypeStruct((rows, D //...]
    all_gather x1, waiting for transfers between devices: 54.5 us -> 3.16 us  [body(): first_all = lax.all_gather(first_pack, EX, axis=0, tiled=True)]
    all_gather x1, waiting for transfers between devices: 45.3 us -> 8.72 us  [body(): c_all = lax.all_gather(c_local, EX, axis=0, tiled=True)]
    ppermute x15 -> x42, starting transfers between devices: 21.4 us -> 54.7 us  [shift_y(): return lax.ppermute(value, 'y', [(i, (i + by) % 4) for i in range(4)])]
    convert_element_type x16 -> x14, other arithmetic: 43 us -> 16.6 us  [the longest x3 6.62 us: pair(): return (keep.astype(WIDE) + swap_core(send).astype(WIDE)).astype(HALF)]
  transfers between devices with their start and end apart: 53 -> 66, of which waited for: 29 -> 43; matrix products, arithmetic and copies ran while one was open for 27% -> 19% of each run, Pallas kernels for 2% -> 9%
where the time goes in v2:
time: 576 us; the launch traced here: 565 us
  waiting for transfers between devices  193 us (34%)
  starting transfers between devices  116 us (20%)
  Pallas kernels  76.2 us (13%)
  local copies, waits for them, and re-layouts  70.3 us (12%)
  other arithmetic  49.1 us (9%)
  matrix products  43.9 us (8%)
  between operations  16.1 us (3%)
    ppermute x42, waiting for transfers between devices, shift_y(): return lax.ppermute(value, 'y', [(i, (i + by) % 4) for i in range(4)])  122 us
    ppermute x42, starting transfers between devices, shift_y(): return lax.ppermute(value, 'y', [(i, (i + by) % 4) for i in range(4)])  54.7 us
    all_to_all x8, starting transfers between devices, spread(): return lax.all_to_all(value, axes, split_axis=0, concat_axis=0, tiled=True)  45.6 us
    all_to_all x8, waiting for transfers between devices, spread(): return lax.all_to_all(value, axes, split_axis=0, concat_axis=0, tiled=True)  38.8 us
    pallas_call x1, Pallas kernels, run_expert(): pl.pallas_call(expert_kernel, out_shape=(jax.ShapeDtypeStruct((rows, D //...  26.6 us
    unnamed x193, local copies, waits for them, and re-layouts  22.9 us
    ppermute x12, waiting for transfers between devices, swap_core(): return lax.ppermute(value, 'c', [(0, 1), (1, 0)])  18.4 us
    dot_general x9, matrix products, dot_nn(): return jnp.dot(left, right, preferred_element_type=WIDE)  16.5 us
  transfers between devices with their start and end apart: 66, of which 43 were waited for; matrix products, arithmetic and copies ran while one was open for 19% of the time, Pallas kernels for 9%

profile of v2, /device:TPU:1, one launch (start us, length us, event | category | flops | bytes accessed | tf_op | source)
XLA Modules:
  0.0 565.0 jit_solution(14018687578929318482)
XLA Ops:
  15.7 7.1 %fusion.28 = (bf16[176,2048]{1,0:T(8,128)(2,1)}, bf16[176,2048]{1,0:T(8,128)(2,1)}, bf16[176,2048]{1,0:T(8,128)(2,1)}, bf16[176,2048]{1,0:T(8,128)(2,1)}, bf16[1...) fusion(f32[4,176,2048]{2,1,0:T(8,128)} %param.33, ...), kind=kLoop, calls=%fused_computation.75 | loop fusion | bytes 11534352 | tf_op jit(solution)/shard_map/convert_element_type | solution.py:574
  22.8 2.1 collective-permute-start.7
  24.9 2.6 collective-permute-start.8
  32.6 4.5 fusion.36
  47.0 3.3 collective-permute-start.10
  59.6 13.4 %collective-permute-done.5.rest_2_ = bf16[176,2048]{1,0:T(8,128)(2,1)} collective-permute-done((bf16[176,2048]{1,0:T(8,128)(2,1)}, bf16[176,2048]{1,0:T(8,128)(2,1)}, u32[]{:S(2)}, u32[]{:S(2)}) %collective-permute-start.5) | collective-permute-done | bytes 720928 | tf_op jit(solution)/shard_map/ppermute | solution.py:65
  73.0 4.0 collective-permute-done.6.rest_3_
  77.1 3.2 all-gather.4.cloned.1.call-done
  83.3 2.9 fusion.7
  91.6 5.0 all-to-all-start
  96.7 2.2 collective-permute-start.11
  106.6 2.3 slice.308.wot_ref
  110.3 4.9 collective-permute-done.11.rest_5_
  115.2 17.0 %collective-permute-done.12.rest_6_ = bf16[176,2048]{1,0:T(8,128)(2,1)} collective-permute-done((bf16[176,2048]{1,0:T(8,128)(2,1)}, bf16[176,2048]{1,0:T(8,128)(2,1)}, u32[]{:S(2)}, u32[]{:S(2)}) %collective-permute-start.12) | collective-permute-done | bytes 720928 | tf_op jit(solution)/shard_map/ppermute | solution.py:65
  132.2 13.9 %collective-permute-done.14.rest_9_ = bf16[176,2048]{1,0:T(8,128)(2,1)} collective-permute-done((bf16[176,2048]{1,0:T(8,128)(2,1)}, bf16[176,2048]{1,0:T(8,128)(2,1)}, u32[]{:S(2)}, u32[]{:S(2)}) %collective-permute-start.14) | collective-permute-done | bytes 720928 | tf_op jit(solution)/shard_map/ppermute | solution.py:65
  147.2 8.7 %all-gather.6.cloned.1.call-done.c_ref = bf16[4096,640]{1,0:T(8,128)(2,1)} async-done(((bf16[256,640]{1,0:T(8,128)(2,1)}), bf16[4096,640]{1,0:T(8,128)(2,1)}) %all-gather.6.cloned.1.call-update) | async-done | bytes 5242896 | tf_op jit(solution)/shard_map/all_gather | solution.py:661
  157.3 5.0 convolution_convert_fusion.kv_ref
  162.4 10.0 %shard_map.323 = (bf16[2,4096,256]{2,1,0:T(8,128)(2,1)S(1)}, f32[256,256]{1,0:T(8,128)S(1)}) custom-call(bf16[256,384]{1,0:T(8,128)(2,1)S(1)} %pad_maximum_fusion.7.q_ref, bf16[4096,512]{1,0:T(8,128)(2,1)S(1)} %convolution_convert_fusion.kv_ref, bf16[4096,128]{1,0:T(8,128)(2,1)S(1)} %slice.310.rot_ref, s32[1,256]{1,0:T(1,128)S(1)} %bitcast.276, ...), custom_call_target="tpu_custom_call" | custom-call | flops 1610612736 | bytes 12582912 | tf_op jit(solution)/shard_map/pallas_call | solution.py:179
  181.0 2.4 collective-permute-start.18
  185.7 3.8 collective-permute-done.18
  191.5 2.2 collective-permute-start.21
  195.9 2.7 collective-permute-done.21
  198.9 2.2 collective-permute-start.23
  210.5 5.4 all-to-all-start.1
  217.6 3.1 fusion.3
  224.6 2.4 fusion.1
  227.8 10.5 %all-to-all-done.1 = bf16[16,40,1152]{2,1,0:T(8,128)(2,1)} async-done(((bf16[16,40,1152]{2,1,0:T(8,128)(2,1)}), bf16[16,40,1152]{2,1,0:T(8,128)(2,1)}, u32[]{:S(2)}, u32[]{:S(2)}) %all-to-all-start.1) | async-done | bytes 1474592 | tf_op jit(solution)/shard_map/all_to_all | solution.py:69
  240.4 3.1 collective-permute-done.26.xo_ref
  246.8 26.6 %shard_map.324 = (bf16[640,1152]{1,0:T(8,128)(2,1)}, bf16[640,1152]{1,0:T(8,128)(2,1)}, bf16[640,1024]{1,0:T(8,128)(2,1)}, bf16[640,1024]{1,0:T(8,128)(2,1)}, bf...) custom-call(s32[1]{0:T(128)} %bitcast.52.at_ref.core_ref, ...), custom_call_target="tpu_custom_call" | custom-call | flops 12079595520 | bytes 29360128 | tf_op jit(solution)/shard_map/pallas_call | solution.py:394
  273.9 4.7 convolution_convert_fusion.3
  282.5 4.6 all-to-all-start.2
  287.1 4.8 convolution_convert_fusion.1
  295.3 2.9 convolution_convert_fusion.2
  300.3 2.9 add_convert_fusion.2
  303.2 7.9 %collective-permute-done.29.refs_1_ = bf16[176,2048]{1,0:T(8,128)(2,1)S(1)} collective-permute-done((bf16[176,2048]{1,0:T(8,128)(2,1)S(1)}, bf16[176,2048]{1,0:T(8,128)(2,1)S(1)}, u32[]{:S(2)}, u32[]{:S(2)}) %collective-permute-start.29) | collective-permute-done | bytes 720928 | tf_op jit(solution)/shard_map/ppermute | solution.py:65
  325.4 3.4 collective-permute-done.32
  333.3 3.2 collective-permute-start.36
  337.8 4.4 collective-permute-done.36
  348.1 11.5 %shard_map.325 = (bf16[4,16,32,640]{3,2,1,0:T(8,128)(2,1)S(1)}, bf16[4,16,32,640]{3,2,1,0:T(8,128)(2,1)S(1)}, bf16[4096,512]{1,0:T(8,128)(2,1)S(1)}, f32[256,384]{1,0:T(8,128)S(1)}) custom-call(s32[1]{0:T(128)} %bitcast.52.at_ref.core_ref, bf16[256,384]{1,0:T(8,128)(2,1)S(1)} %copy-done.34, bf16[4096,512]{1,0:T(8,128)(2,1)S(1)} %copy-done.38, ...), custom_call_target="tpu_custom_call" | custom-call | flops 5368709120 | bytes 25165824 | tf_op jit(solution)/shard_map/pallas_call | solution.py:270
  359.6 3.7 collective-permute-done.39.refs_1_
  363.3 2.9 collective-permute-done.40.refs_3_
  367.8 4.5 collective-permute-done.41
  372.3 2.2 add_convert_fusion
  374.5 6.7 %all-to-all-start.3 = ((bf16[16,40,1024]{2,1,0:T(8,128)(2,1)}), bf16[16,40,1024]{2,1,0:T(8,128)(2,1)}, u32[]{:S(2)}, u32[]{:S(2)}) async-start(bf16[16,40,1024]{2,1,0:T(8,128)(2,1)} %bitcast.283), calls=%async_computation.3 | async-start | bytes 2621440 | tf_op jit(solution)/shard_map/all_to_all | solution.py:69
  381.4 3.0 dynamic-slice_bitcast_fusion.3
  387.3 14.7 %shard_map.326 = bf16[2048,1920]{1,0:T(8,128)(2,1)} custom-call(bf16[256,2048]{1,0:T(8,128)(2,1)S(1)} %bitcast.267, bf16[256,768]{1,0:T(8,128)(2,1)S(1)} %copy-done.10, bf16[256,2048]{1,0:T(8,128)(2,1)S(1)} %bitcast.273, bf16[256,384]{1,0:T(8,128)(2,1)S(1)} %copy-done.14, bf16[256,2048]{1,0:T(8,128)(2,1)S(1)} %multiply_convert_fusion.h_one_ref, ...), custom_call_target="tpu_custom_call" | custom-call | flops 1 | bytes 1 | tf_op jit(solution)/shard_map/pallas_call | solution.py:497
  402.1 13.5 %collective-permute-done.42 = bf16[16,32,640]{2,1,0:T(8,128)(2,1)} collective-permute-done((bf16[16,32,640]{2,1,0:T(8,128)(2,1)}, bf16[16,32,640]{2,1,0:T(8,128)(2,1)}, u32[]{:S(2)}, u32[]{:S(2)}) %collective-permute-start.42) | collective-permute-done | bytes 655392 | tf_op jit(solution)/shard_map/ppermute | solution.py:65
  415.9 2.8 fusion.17
  422.0 2.5 shard_map.327
  426.5 2.3 collective-permute-done.47
  430.9 3.2 collective-permute-start.49
  438.0 6.7 %all-to-all-start.4 = ((bf16[16,32,640]{2,1,0:T(8,128)(2,1)}), bf16[16,32,640]{2,1,0:T(8,128)(2,1)}, u32[]{:S(2)}, u32[]{:S(2)}) async-start(bf16[16,32,640]{2,1,0:T(8,128)(2,1)} %fusion.17), calls=%async_computation.4 | async-start | bytes 1310720 | tf_op jit(solution)/shard_map/all_to_all | solution.py:69
  448.3 11.9 %all-to-all-done.4 = bf16[16,32,640]{2,1,0:T(8,128)(2,1)} async-done(((bf16[16,32,640]{2,1,0:T(8,128)(2,1)}), bf16[16,32,640]{2,1,0:T(8,128)(2,1)}, u32[]{:S(2)}, u32[]{:S(2)}) %all-to-all-start.4) | async-done | bytes 655392 | tf_op jit(solution)/shard_map/all_to_all | solution.py:69
  468.3 6.0 %all-to-all-start.5 = ((bf16[8,32,768]{2,1,0:T(8,128)(2,1)}), bf16[8,32,768]{2,1,0:T(8,128)(2,1)}, u32[]{:S(2)}, u32[]{:S(2)}) async-start(bf16[8,32,768]{2,1,0:T(8,128)(2,1)} %broadcast_in_dim.173), calls=%async_computation.5 | async-start | bytes 786432 | tf_op jit(solution)/shard_map/all_to_all | solution.py:69
  474.3 4.1 fusion.73
  487.8 6.0 %all-to-all-start.6 = ((bf16[16,128,128]{1,2,0:T(8,128)(2,1)}), bf16[16,128,128]{1,2,0:T(8,128)(2,1)S(1)}, u32[]{:S(2)}, u32[]{:S(2)}) async-start(bf16[16,128,128]{1,2,0:T(8,128)(2,1)} %pad_maximum_fusion.4), calls=%async_computation.6 | async-start | bytes 1048576 | tf_op jit(solution)/shard_map/all_to_all | solution.py:69
  497.5 11.2 %all-to-all-done.6 = bf16[16,128,128]{1,2,0:T(8,128)(2,1)S(1)} async-done(((bf16[16,128,128]{1,2,0:T(8,128)(2,1)}), bf16[16,128,128]{1,2,0:T(8,128)(2,1)S(1)}, u32[]{:S(2)}, u32[]{:S(2)}) %all-to-all-start.6) | async-done | bytes 524320 | tf_op jit(solution)/shard_map/all_to_all | solution.py:69
  509.7 5.2 all-to-all-start.7
  514.9 2.3 fusion.72
  518.3 2.9 shard_map.330
  521.2 13.6 %collective-permute-done.53.refs_2_ = bf16[176,2048]{1,0:T(8,128)(2,1)} collective-permute-done((bf16[176,2048]{1,0:T(8,128)(2,1)}, bf16[176,2048]{1,0:T(8,128)(2,1)}, u32[]{:S(2)}, u32[]{:S(2)}) %collective-permute-start.53) | collective-permute-done | bytes 720928 | tf_op jit(solution)/shard_map/ppermute | solution.py:65
  534.8 3.4 all-to-all-done.7
  540.5 4.0 shard_map.329
  545.6 4.0 shard_map.328
  (482 shorter events, 178.6 us)
Async XLA Ops:
  7.2 73.0 %all-gather.4.cloned.1.call-start = ((), (), s32[]{:S(2)}) async-start(), calls=%async_computation.9 | async-start | bytes 6684672 | tf_op jit(solution)/shard_map/all_gather | solution.py:597
  15.5 140.5 %all-gather.6.cloned.1.call-start = ((), (), s32[]{:S(2)}) async-start(), calls=%async_computation.10 | async-start | bytes 5570560 | tf_op jit(solution)/shard_map/all_gather | solution.py:661
  22.8 16.4 %collective-permute-start.7 = (bf16[32,2048]{1,0:T(8,128)(2,1)S(1)}, bf16[32,2048]{1,0:T(8,128)(2,1)S(1)}, u32[]{:S(2)}, u32[]{:S(2)}) collective-permute-start(bf16[32,2048]{1,0:T(8,128)(2,1)S(1)} %copy-done.59), channel_id=1, source_target_pairs={{0,2},{2,4},{4,6},{6,0},{1,3},{3,5},{5,7},{7,1},{8,10},{10,12},{12... | collective-permute-start | bytes 393224 | tf_op jit(solution)/shard_map/ppermute | solution.py:65
  24.9 18.1 %collective-permute-start.8 = (bf16[32,2048]{1,0:T(8,128)(2,1)S(1)}, bf16[32,2048]{1,0:T(8,128)(2,1)S(1)}, u32[]{:S(2)}, u32[]{:S(2)}) collective-permute-start(bf16[32,2048]{1,0:T(8,128)(2,1)S(1)} %copy-done.59), channel_id=1, source_target_pairs={{0,4},{2,6},{4,0},{6,2},{1,5},{3,7},{5,1},{7,3},{8,12},{10,14},{12... | collective-permute-start | bytes 393224 | tf_op jit(solution)/shard_map/ppermute | solution.py:65
  27.6 17.3 %collective-permute-start.9 = (bf16[32,2048]{1,0:T(8,128)(2,1)S(1)}, bf16[32,2048]{1,0:T(8,128)(2,1)S(1)}, u32[]{:S(2)}, u32[]{:S(2)}) collective-permute-start(bf16[32,2048]{1,0:T(8,128)(2,1)S(1)} %copy-done.59), channel_id=1, source_target_pairs={{0,6},{2,0},{4,2},{6,4},{1,7},{3,1},{5,3},{7,5},{8,14},{10,8},{12,... | collective-permute-start | bytes 393224 | tf_op jit(solution)/shard_map/ppermute | solution.py:65
  28.6 12.2 %collective-permute-start = (bf16[32,2048]{1,0:T(8,128)(2,1)S(1)}, bf16[32,2048]{1,0:T(8,128)(2,1)}, u32[]{:S(2)}, u32[]{:S(2)}) collective-permute-start(bf16[32,2048]{1,0:T(8,128)(2,1)S(1)} %copy-done.57), channel_id=1, source_target_pairs={{0,2},{2,4},{4,6},{6,0},{1,3},{3,5},{5,7},{7,1},{8,10},{10,12},{12... | collective-permute-start | bytes 393224 | tf_op jit(solution)/shard_map/ppermute | solution.py:65
  29.0 17.9 %collective-permute-start.1 = (bf16[32,2048]{1,0:T(8,128)(2,1)S(1)}, bf16[32,2048]{1,0:T(8,128)(2,1)S(1)}, u32[]{:S(2)}, u32[]{:S(2)}) collective-permute-start(bf16[32,2048]{1,0:T(8,128)(2,1)S(1)} %copy-done.57), channel_id=1, source_target_pairs={{0,4},{2,6},{4,0},{6,2},{1,5},{3,7},{5,1},{7,3},{8,12},{10,14},{12... | collective-permute-start | bytes 393224 | tf_op jit(solution)/shard_map/ppermute | solution.py:65
  39.2 11.7 %collective-permute-start.2 = (bf16[32,2048]{1,0:T(8,128)(2,1)S(1)}, bf16[32,2048]{1,0:T(8,128)(2,1)S(1)}, u32[]{:S(2)}, u32[]{:S(2)}) collective-permute-start(bf16[32,2048]{1,0:T(8,128)(2,1)S(1)} %copy-done.57), channel_id=1, source_target_pairs={{0,6},{2,0},{4,2},{6,4},{1,7},{3,1},{5,3},{7,5},{8,14},{10,8},{12,... | collective-permute-start | bytes 393224 | tf_op jit(solution)/shard_map/ppermute | solution.py:65
  40.8 17.8 %collective-permute-start.4 = (bf16[176,2048]{1,0:T(8,128)(2,1)}, bf16[176,2048]{1,0:T(8,128)(2,1)S(1)}, u32[]{:S(2)}, u32[]{:S(2)}) collective-permute-start(bf16[176,2048]{1,0:T(8,128)(2,1)} %get-tuple-element.182), channel_id=1, source_target_pairs={{0,2},{2,4},{4,6},{6,0},{1,3},{3,5},{5,7},{7,1},{8,10},{10,12},{12... | collective-permute-start | bytes 2162696 | tf_op jit(solution)/shard_map/ppermute | solution.py:65
  43.0 30.0 %collective-permute-start.5 = (bf16[176,2048]{1,0:T(8,128)(2,1)}, bf16[176,2048]{1,0:T(8,128)(2,1)}, u32[]{:S(2)}, u32[]{:S(2)}) collective-permute-start(bf16[176,2048]{1,0:T(8,128)(2,1)} %get-tuple-element.183), channel_id=1, source_target_pairs={{0,4},{2,6},{4,0},{6,2},{1,5},{3,7},{5,1},{7,3},{8,12},{10,14},{12... | collective-permute-start | bytes 2162696 | tf_op jit(solution)/shard_map/ppermute | solution.py:65
  44.8 32.2 %collective-permute-start.6 = (bf16[176,2048]{1,0:T(8,128)(2,1)}, bf16[176,2048]{1,0:T(8,128)(2,1)}, u32[]{:S(2)}, u32[]{:S(2)}) collective-permute-start(bf16[176,2048]{1,0:T(8,128)(2,1)} %get-tuple-element.184), channel_id=1, source_target_pairs={{0,6},{2,0},{4,2},{6,4},{1,7},{3,1},{5,3},{7,5},{8,14},{10,8},{12,... | collective-permute-start | bytes 2162696 | tf_op jit(solution)/shard_map/ppermute | solution.py:65
  47.0 4.8 collective-permute-start.10
  91.6 55.6 %all-to-all-start = ((bf16[16,40,1024]{2,1,0:T(8,128)(2,1)}), bf16[16,40,1024]{2,1,0:T(8,128)(2,1)}, u32[]{:S(2)}, u32[]{:S(2)}) async-start(bf16[16,40,1024]{2,1,0:T(8,128)(2,1)} %bitcast.280), calls=%async_computation | async-start | bytes 2621440 | tf_op jit(solution)/shard_map/all_to_all | solution.py:69
  96.7 120.9 %all-gather.8.cloned.1.call-start = ((), (), s32[]{:S(2)}) async-start(), calls=%async_computation.11 | async-start | bytes 5013504 | tf_op jit(solution)/shard_map/all_gather | solution.py:675
  96.7 18.4 %collective-permute-start.11 = (bf16[176,2048]{1,0:T(8,128)(2,1)}, bf16[176,2048]{1,0:T(8,128)(2,1)}, u32[]{:S(2)}, u32[]{:S(2)}) collective-permute-start(bf16[176,2048]{1,0:T(8,128)(2,1)} %get-tuple-element.206), channel_id=1, source_target_pairs={{0,2},{2,4},{4,6},{6,0},{1,3},{3,5},{5,7},{7,1},{8,10},{10,12},{12... | collective-permute-start | bytes 2162696 | tf_op jit(solution)/shard_map/ppermute | solution.py:65
  98.9 33.3 %collective-permute-start.12 = (bf16[176,2048]{1,0:T(8,128)(2,1)}, bf16[176,2048]{1,0:T(8,128)(2,1)}, u32[]{:S(2)}, u32[]{:S(2)}) collective-permute-start(bf16[176,2048]{1,0:T(8,128)(2,1)} %get-tuple-element.207), channel_id=1, source_target_pairs={{0,4},{2,6},{4,0},{6,2},{1,5},{3,7},{5,1},{7,3},{8,12},{10,14},{12... | collective-permute-start | bytes 2162696 | tf_op jit(solution)/shard_map/ppermute | solution.py:65
  100.9 31.2 %collective-permute-start.13 = (bf16[176,2048]{1,0:T(8,128)(2,1)}, bf16[176,2048]{1,0:T(8,128)(2,1)}, u32[]{:S(2)}, u32[]{:S(2)}) collective-permute-start(bf16[176,2048]{1,0:T(8,128)(2,1)} %get-tuple-element.208), channel_id=1, source_target_pairs={{0,6},{2,0},{4,2},{6,4},{1,7},{3,1},{5,3},{7,5},{8,14},{10,8},{12,... | collective-permute-start | bytes 2162696 | tf_op jit(solution)/shard_map/ppermute | solution.py:65
  101.8 44.3 %collective-permute-start.14 = (bf16[176,2048]{1,0:T(8,128)(2,1)}, bf16[176,2048]{1,0:T(8,128)(2,1)}, u32[]{:S(2)}, u32[]{:S(2)}) collective-permute-start(bf16[176,2048]{1,0:T(8,128)(2,1)} %get-tuple-element.210), channel_id=1, source_target_pairs={{0,2},{2,4},{4,6},{6,0},{1,3},{3,5},{5,7},{7,1},{8,10},{10,12},{12... | collective-permute-start | bytes 2162696 | tf_op jit(solution)/shard_map/ppermute | solution.py:65
  102.6 44.6 %collective-permute-start.15 = (bf16[176,2048]{1,0:T(8,128)(2,1)}, bf16[176,2048]{1,0:T(8,128)(2,1)}, u32[]{:S(2)}, u32[]{:S(2)}) collective-permute-start(bf16[176,2048]{1,0:T(8,128)(2,1)} %get-tuple-element.211), channel_id=1, source_target_pairs={{0,6},{2,0},{4,2},{6,4},{1,7},{3,1},{5,3},{7,5},{8,14},{10,8},{12,... | collective-permute-start | bytes 2162696 | tf_op jit(solution)/shard_map/ppermute | solution.py:65
  179.8 6.0 %collective-permute-start.17 = (bf16[32,2048]{1,0:T(8,128)(2,1)S(1)}, bf16[32,2048]{1,0:T(8,128)(2,1)S(1)}, u32[]{:S(2)}, u32[]{:S(2)}) collective-permute-start(bf16[32,2048]{1,0:T(8,128)(2,1)S(1)} %get-tuple-element.528), channel_id=1, source_target_pairs={{0,2},{2,4},{4,6},{6,0},{1,3},{3,5},{5,7},{7,1},{8,10},{10,12},{12... | collective-permute-start | bytes 393224 | tf_op jit(solution)/shard_map/ppermute | solution.py:65
  181.0 8.5 %collective-permute-start.18 = (bf16[32,2048]{1,0:T(8,128)(2,1)S(1)}, bf16[32,2048]{1,0:T(8,128)(2,1)S(1)}, u32[]{:S(2)}, u32[]{:S(2)}) collective-permute-start(bf16[32,2048]{1,0:T(8,128)(2,1)S(1)} %get-tuple-element.530), channel_id=1, source_target_pairs={{0,4},{2,6},{4,0},{6,2},{1,5},{3,7},{5,1},{7,3},{8,12},{10,14},{12... | collective-permute-start | bytes 393224 | tf_op jit(solution)/shard_map/ppermute | solution.py:65
  183.5 6.0 %collective-permute-start.19 = (bf16[32,2048]{1,0:T(8,128)(2,1)S(1)}, bf16[32,2048]{1,0:T(8,128)(2,1)S(1)}, u32[]{:S(2)}, u32[]{:S(2)}) collective-permute-start(bf16[32,2048]{1,0:T(8,128)(2,1)S(1)} %get-tuple-element.529), channel_id=1, source_target_pairs={{0,6},{2,0},{4,2},{6,4},{1,7},{3,1},{5,3},{7,5},{8,14},{10,8},{12,... | collective-permute-start | bytes 393224 | tf_op jit(solution)/shard_map/ppermute | solution.py:65
  190.3 5.5 collective-permute-start.20
  191.5 7.1 %collective-permute-start.21 = (bf16[32,2048]{1,0:T(8,128)(2,1)S(1)}, bf16[32,2048]{1,0:T(8,128)(2,1)S(1)}, u32[]{:S(2)}, u32[]{:S(2)}) collective-permute-start(bf16[32,2048]{1,0:T(8,128)(2,1)S(1)} %get-tuple-element.473), channel_id=1, source_target_pairs={{0,4},{2,6},{4,0},{6,2},{1,5},{3,7},{5,1},{7,3},{8,12},{10,14},{12... | collective-permute-start | bytes 393224 | tf_op jit(solution)/shard_map/ppermute | solution.py:65
  193.7 5.2 collective-permute-start.22
  198.9 3.9 collective-permute-start.23
  208.0 19.8 %collective-permute-start.24 = (bf16[640,1024]{1,0:T(8,128)(2,1)}, bf16[640,1024]{1,0:T(8,128)(2,1)}, u32[]{:S(2)}, u32[]{:S(2)}) collective-permute-start(bf16[640,1024]{1,0:T(8,128)(2,1)} %bitcast.42.g_ref), channel_id=1, source_target_pairs={{0,1},{1,0},{2,3},{3,2},{4,5},{5,4},{6,7},{7,6},{8,9},{9,8},{10,11... | collective-permute-start | bytes 3932168 | tf_op jit(solution)/shard_map/ppermute | solution.py:61
  208.4 19.4 %collective-permute-start.25 = (bf16[176,2048]{1,0:T(8,128)(2,1)}, bf16[176,2048]{1,0:T(8,128)(2,1)}, u32[]{:S(2)}, u32[]{:S(2)}) collective-permute-start(bf16[176,2048]{1,0:T(8,128)(2,1)} %get-tuple-element.227), channel_id=1, source_target_pairs={{0,4},{2,6},{4,0},{6,2},{1,5},{3,7},{5,1},{7,3},{8,12},{10,14},{12... | collective-permute-start | bytes 2162696 | tf_op jit(solution)/shard_map/ppermute | solution.py:65
  210.5 27.8 %all-to-all-start.1 = ((bf16[16,40,1152]{2,1,0:T(8,128)(2,1)}), bf16[16,40,1152]{2,1,0:T(8,128)(2,1)}, u32[]{:S(2)}, u32[]{:S(2)}) async-start(bf16[16,40,1152]{2,1,0:T(8,128)(2,1)} %pad_maximum_fusion), calls=%async_computation.1 | async-start | bytes 2949120 | tf_op jit(solution)/shard_map/all_to_all | solution.py:69
  238.4 5.1 collective-permute-start.26
  273.4 6.8 %collective-permute-start.27 = (bf16[640,1152]{1,0:T(8,128)(2,1)}, bf16[640,1152]{1,0:T(8,128)(2,1)S(1)}, u32[]{:S(2)}, u32[]{:S(2)}) collective-permute-start(bf16[640,1152]{1,0:T(8,128)(2,1)} %get-tuple-element.247), channel_id=1, source_target_pairs={{0,1},{1,0},{2,3},{3,2},{4,5},{5,4},{6,7},{7,6},{8,9},{9,8},{10,11... | collective-permute-start | bytes 4423688 | tf_op jit(solution)/shard_map/ppermute | solution.py:61
  282.3 17.6 %collective-permute-start.28 = (bf16[640,1024]{1,0:T(8,128)(2,1)}, bf16[640,1024]{1,0:T(8,128)(2,1)}, u32[]{:S(2)}, u32[]{:S(2)}) collective-permute-start(bf16[640,1024]{1,0:T(8,128)(2,1)} %get-tuple-element.256), channel_id=1, source_target_pairs={{0,1},{1,0},{2,3},{3,2},{4,5},{5,4},{6,7},{7,6},{8,9},{9,8},{10,11... | collective-permute-start | bytes 3932168 | tf_op jit(solution)/shard_map/ppermute | solution.py:61
  282.5 31.9 %all-to-all-start.2 = ((bf16[16,40,1152]{2,1,0:T(8,128)(2,1)}), bf16[16,40,1152]{2,1,0:T(8,128)(2,1)}, u32[]{:S(2)}, u32[]{:S(2)}) async-start(bf16[16,40,1152]{2,1,0:T(8,128)(2,1)} %bitcast.279), calls=%async_computation.2 | async-start | bytes 2949120 | tf_op jit(solution)/shard_map/all_to_all | solution.py:69
  293.6 17.5 %collective-permute-start.29 = (bf16[176,2048]{1,0:T(8,128)(2,1)S(1)}, bf16[176,2048]{1,0:T(8,128)(2,1)S(1)}, u32[]{:S(2)}, u32[]{:S(2)}) collective-permute-start(bf16[176,2048]{1,0:T(8,128)(2,1)S(1)} %copy-done.65), channel_id=1, source_target_pairs={{0,6},{2,0},{4,2},{6,4},{1,7},{3,1},{5,3},{7,5},{8,14},{10,8},{12,... | collective-permute-start | bytes 2162696 | tf_op jit(solution)/shard_map/ppermute | solution.py:65
  295.2 18.3 %collective-permute-start.30 = (bf16[176,2048]{1,0:T(8,128)(2,1)S(1)}, bf16[176,2048]{1,0:T(8,128)(2,1)S(1)}, u32[]{:S(2)}, u32[]{:S(2)}) collective-permute-start(bf16[176,2048]{1,0:T(8,128)(2,1)S(1)} %copy-done.64), channel_id=1, source_target_pairs={{0,2},{2,4},{4,6},{6,0},{1,3},{3,5},{5,7},{7,1},{8,10},{10,12},{12... | collective-permute-start | bytes 2162696 | tf_op jit(solution)/shard_map/ppermute | solution.py:65
  318.6 3.2 collective-permute-start.31
  322.0 6.8 %collective-permute-start.32 = (bf16[32,2176]{1,0:T(8,128)(2,1)S(1)}, bf16[32,2176]{1,0:T(8,128)(2,1)S(1)}, u32[]{:S(2)}, u32[]{:S(2)}) collective-permute-start(bf16[32,2176]{1,0:T(8,128)(2,1)S(1)} %get-tuple-element.525), channel_id=1, source_target_pairs={{0,2},{2,4},{4,6},{6,0},{1,3},{3,5},{5,7},{7,1},{8,10},{10,12},{12... | collective-permute-start | bytes 417800 | tf_op jit(solution)/shard_map/ppermute | solution.py:65
  322.1 8.5 %collective-permute-start.33 = (bf16[32,2176]{1,0:T(8,128)(2,1)S(1)}, bf16[32,2176]{1,0:T(8,128)(2,1)S(1)}, u32[]{:S(2)}, u32[]{:S(2)}) collective-permute-start(bf16[32,2176]{1,0:T(8,128)(2,1)S(1)} %get-tuple-element.527), channel_id=1, source_target_pairs={{0,4},{2,6},{4,0},{6,2},{1,5},{3,7},{5,1},{7,3},{8,12},{10,14},{12... | collective-permute-start | bytes 417800 | tf_op jit(solution)/shard_map/ppermute | solution.py:65
  324.1 7.4 %collective-permute-start.34 = (bf16[32,2176]{1,0:T(8,128)(2,1)S(1)}, bf16[32,2176]{1,0:T(8,128)(2,1)S(1)}, u32[]{:S(2)}, u32[]{:S(2)}) collective-permute-start(bf16[32,2176]{1,0:T(8,128)(2,1)S(1)} %get-tuple-element.526), channel_id=1, source_target_pairs={{0,6},{2,0},{4,2},{6,4},{1,7},{3,1},{5,3},{7,5},{8,14},{10,8},{12,... | collective-permute-start | bytes 417800 | tf_op jit(solution)/shard_map/ppermute | solution.py:65
  332.6 5.2 collective-permute-start.35
  333.3 8.8 %collective-permute-start.36 = (bf16[32,2048]{1,0:T(8,128)(2,1)S(1)}, bf16[32,2048]{1,0:T(8,128)(2,1)S(1)}, u32[]{:S(2)}, u32[]{:S(2)}) collective-permute-start(bf16[32,2048]{1,0:T(8,128)(2,1)S(1)} %get-tuple-element.469), channel_id=1, source_target_pairs={{0,4},{2,6},{4,0},{6,2},{1,5},{3,7},{5,1},{7,3},{8,12},{10,14},{12... | collective-permute-start | bytes 393224 | tf_op jit(solution)/shard_map/ppermute | solution.py:65
  336.6 5.6 collective-permute-start.37
  342.2 3.3 collective-permute-start.38
  345.9 17.4 %collective-permute-start.39 = (bf16[176,2048]{1,0:T(8,128)(2,1)S(1)}, bf16[176,2048]{1,0:T(8,128)(2,1)S(1)}, u32[]{:S(2)}, u32[]{:S(2)}) collective-permute-start(bf16[176,2048]{1,0:T(8,128)(2,1)S(1)} %copy-done.63), channel_id=1, source_target_pairs={{0,6},{2,0},{4,2},{6,4},{1,7},{3,1},{5,3},{7,5},{8,14},{10,8},{12,... | collective-permute-start | bytes 2162696 | tf_op jit(solution)/shard_map/ppermute | solution.py:65
  347.8 18.4 %collective-permute-start.40 = (bf16[176,2048]{1,0:T(8,128)(2,1)S(1)}, bf16[176,2048]{1,0:T(8,128)(2,1)S(1)}, u32[]{:S(2)}, u32[]{:S(2)}) collective-permute-start(bf16[176,2048]{1,0:T(8,128)(2,1)S(1)} %copy-done.62), channel_id=1, source_target_pairs={{0,2},{2,4},{4,6},{6,0},{1,3},{3,5},{5,7},{7,1},{8,10},{10,12},{12... | collective-permute-start | bytes 2162696 | tf_op jit(solution)/shard_map/ppermute | solution.py:65
  366.2 6.1 %collective-permute-start.41 = (bf16[4,16,32,640]{3,2,1,0:T(8,128)(2,1)S(1)}, bf16[4,16,32,640]{3,2,1,0:T(8,128)(2,1)S(1)}, u32[]{:S(2)}, u32[]{:S(2)}) collective-permute-start(bf16[4,16,32,640]{3,2,1,0:T(8,128)(2,1)S(1)} %get-tuple-element.279), channel_id=1, source_target_pairs={{0,1},{1,0},{2,3},{3,2},{4,5},{5,4},{6,7},{7,6},{8,9},{9,8},{10,11... | collective-permute-start | bytes 7864328 | tf_op jit(solution)/shard_map/ppermute | solution.py:61
  374.5 44.2 %all-to-all-start.3 = ((bf16[16,40,1024]{2,1,0:T(8,128)(2,1)}), bf16[16,40,1024]{2,1,0:T(8,128)(2,1)}, u32[]{:S(2)}, u32[]{:S(2)}) async-start(bf16[16,40,1024]{2,1,0:T(8,128)(2,1)} %bitcast.283), calls=%async_computation.3 | async-start | bytes 2621440 | tf_op jit(solution)/shard_map/all_to_all | solution.py:69
  381.3 170.8 %reduce-scatter.2.cloned.1.call-start = ((), (), s32[]{:S(2)}) async-start(), calls=%async_computation.12 | async-start | bytes 8355840 | tf_op jit(solution)/shard_map/reduce_scatter | solution.py:804
  384.3 31.2 %collective-permute-start.42 = (bf16[16,32,640]{2,1,0:T(8,128)(2,1)}, bf16[16,32,640]{2,1,0:T(8,128)(2,1)}, u32[]{:S(2)}, u32[]{:S(2)}) collective-permute-start(bf16[16,32,640]{2,1,0:T(8,128)(2,1)} %get-tuple-element.502), channel_id=1, source_target_pairs={{0,2},{2,4},{4,6},{6,0},{1,3},{3,5},{5,7},{7,1},{8,10},{10,12},{12... | collective-permute-start | bytes 1966088 | tf_op jit(solution)/shard_map/ppermute | solution.py:65
  384.3 31.2 %collective-permute-start.43 = (bf16[16,32,640]{2,1,0:T(8,128)(2,1)}, bf16[16,32,640]{2,1,0:T(8,128)(2,1)}, u32[]{:S(2)}, u32[]{:S(2)}) collective-permute-start(bf16[16,32,640]{2,1,0:T(8,128)(2,1)} %get-tuple-element.504), channel_id=1, source_target_pairs={{0,4},{2,6},{4,0},{6,2},{1,5},{3,7},{5,1},{7,3},{8,12},{10,14},{12... | collective-permute-start | bytes 1966088 | tf_op jit(solution)/shard_map/ppermute | solution.py:65
  385.4 30.5 %collective-permute-start.44 = (bf16[16,32,640]{2,1,0:T(8,128)(2,1)}, bf16[16,32,640]{2,1,0:T(8,128)(2,1)}, u32[]{:S(2)}, u32[]{:S(2)}) collective-permute-start(bf16[16,32,640]{2,1,0:T(8,128)(2,1)} %get-tuple-element.503), channel_id=1, source_target_pairs={{0,6},{2,0},{4,2},{6,4},{1,7},{3,1},{5,3},{7,5},{8,14},{10,8},{12,... | collective-permute-start | bytes 1966088 | tf_op jit(solution)/shard_map/ppermute | solution.py:65
  424.6 4.2 collective-permute-start.47
  430.9 13.8 %collective-permute-start.48 = (bf16[32,4096]{1,0:T(8,128)(2,1)}, bf16[32,4096]{1,0:T(8,128)(2,1)}, u32[]{:S(2)}, u32[]{:S(2)}) collective-permute-start(bf16[32,4096]{1,0:T(8,128)(2,1)} %get-tuple-element.507), channel_id=1, source_target_pairs={{0,2},{2,4},{4,6},{6,0},{1,3},{3,5},{5,7},{7,1},{8,10},{10,12},{12... | collective-permute-start | bytes 786440 | tf_op jit(solution)/shard_map/ppermute | solution.py:65
  430.9 15.3 %collective-permute-start.49 = (bf16[32,4096]{1,0:T(8,128)(2,1)}, bf16[32,4096]{1,0:T(8,128)(2,1)}, u32[]{:S(2)}, u32[]{:S(2)}) collective-permute-start(bf16[32,4096]{1,0:T(8,128)(2,1)} %get-tuple-element.509), channel_id=1, source_target_pairs={{0,4},{2,6},{4,0},{6,2},{1,5},{3,7},{5,1},{7,3},{8,12},{10,14},{12... | collective-permute-start | bytes 786440 | tf_op jit(solution)/shard_map/ppermute | solution.py:65
  434.1 12.0 %collective-permute-start.50 = (bf16[32,4096]{1,0:T(8,128)(2,1)}, bf16[32,4096]{1,0:T(8,128)(2,1)}, u32[]{:S(2)}, u32[]{:S(2)}) collective-permute-start(bf16[32,4096]{1,0:T(8,128)(2,1)} %get-tuple-element.508), channel_id=1, source_target_pairs={{0,6},{2,0},{4,2},{6,4},{1,7},{3,1},{5,3},{7,5},{8,14},{10,8},{12,... | collective-permute-start | bytes 786440 | tf_op jit(solution)/shard_map/ppermute | solution.py:65
  436.5 24.8 %collective-permute-start.45 = (bf16[176,2048]{1,0:T(8,128)(2,1)}, bf16[176,2048]{1,0:T(8,128)(2,1)S(1)}, u32[]{:S(2)}, u32[]{:S(2)}) collective-permute-start(bf16[176,2048]{1,0:T(8,128)(2,1)} %get-tuple-element.298), channel_id=1, source_target_pairs={{0,6},{2,0},{4,2},{6,4},{1,7},{3,1},{5,3},{7,5},{8,14},{10,8},{12,... | collective-permute-start | bytes 2162696 | tf_op jit(solution)/shard_map/ppermute | solution.py:65
  436.8 24.5 %collective-permute-start.46 = (bf16[176,2048]{1,0:T(8,128)(2,1)}, bf16[176,2048]{1,0:T(8,128)(2,1)S(1)}, u32[]{:S(2)}, u32[]{:S(2)}) collective-permute-start(bf16[176,2048]{1,0:T(8,128)(2,1)} %get-tuple-element.300), channel_id=1, source_target_pairs={{0,2},{2,4},{4,6},{6,0},{1,3},{3,5},{5,7},{7,1},{8,10},{10,12},{12... | collective-permute-start | bytes 2162696 | tf_op jit(solution)/shard_map/ppermute | solution.py:65
  438.0 22.2 %all-to-all-start.4 = ((bf16[16,32,640]{2,1,0:T(8,128)(2,1)}), bf16[16,32,640]{2,1,0:T(8,128)(2,1)}, u32[]{:S(2)}, u32[]{:S(2)}) async-start(bf16[16,32,640]{2,1,0:T(8,128)(2,1)} %fusion.17), calls=%async_computation.4 | async-start | bytes 1310720 | tf_op jit(solution)/shard_map/all_to_all | solution.py:69
  468.3 14.2 %all-to-all-start.5 = ((bf16[8,32,768]{2,1,0:T(8,128)(2,1)}), bf16[8,32,768]{2,1,0:T(8,128)(2,1)}, u32[]{:S(2)}, u32[]{:S(2)}) async-start(bf16[8,32,768]{2,1,0:T(8,128)(2,1)} %broadcast_in_dim.173), calls=%async_computation.5 | async-start | bytes 786432 | tf_op jit(solution)/shard_map/all_to_all | solution.py:69
  484.9 23.8 %collective-permute-start.51 = (bf16[176,2048]{1,0:T(8,128)(2,1)}, bf16[176,2048]{1,0:T(8,128)(2,1)S(1)}, u32[]{:S(2)}, u32[]{:S(2)}) collective-permute-start(bf16[176,2048]{1,0:T(8,128)(2,1)} %get-tuple-element.316), channel_id=1, source_target_pairs={{0,4},{2,6},{4,0},{6,2},{1,5},{3,7},{5,1},{7,3},{8,12},{10,14},{12... | collective-permute-start | bytes 2162696 | tf_op jit(solution)/shard_map/ppermute | solution.py:65
  487.8 21.0 %all-to-all-start.6 = ((bf16[16,128,128]{1,2,0:T(8,128)(2,1)}), bf16[16,128,128]{1,2,0:T(8,128)(2,1)S(1)}, u32[]{:S(2)}, u32[]{:S(2)}) async-start(bf16[16,128,128]{1,2,0:T(8,128)(2,1)} %pad_maximum_fusion.4), calls=%async_computation.6 | async-start | bytes 1048576 | tf_op jit(solution)/shard_map/all_to_all | solution.py:69
  493.8 27.4 %collective-permute-start.52 = (bf16[176,2048]{1,0:T(8,128)(2,1)}, bf16[176,2048]{1,0:T(8,128)(2,1)}, u32[]{:S(2)}, u32[]{:S(2)}) collective-permute-start(bf16[176,2048]{1,0:T(8,128)(2,1)} %get-tuple-element.321), channel_id=1, source_target_pairs={{0,4},{2,6},{4,0},{6,2},{1,5},{3,7},{5,1},{7,3},{8,12},{10,14},{12... | collective-permute-start | bytes 2162696 | tf_op jit(solution)/shard_map/ppermute | solution.py:65
  495.6 39.2 %collective-permute-start.53 = (bf16[176,2048]{1,0:T(8,128)(2,1)}, bf16[176,2048]{1,0:T(8,128)(2,1)}, u32[]{:S(2)}, u32[]{:S(2)}) collective-permute-start(bf16[176,2048]{1,0:T(8,128)(2,1)} %get-tuple-element.325), channel_id=1, source_target_pairs={{0,4},{2,6},{4,0},{6,2},{1,5},{3,7},{5,1},{7,3},{8,12},{10,14},{12... | collective-permute-start | bytes 2162696 | tf_op jit(solution)/shard_map/ppermute | solution.py:65
  509.7 28.5 %all-to-all-start.7 = ((bf16[8,128,128]{1,2,0:T(8,128)(2,1)}), bf16[8,128,128]{1,2,0:T(8,128)(2,1)S(1)}, u32[]{:S(2)}, u32[]{:S(2)}) async-start(bf16[8,128,128]{1,2,0:T(8,128)(2,1)} %broadcast_in_dim.174), calls=%async_computation.7 | async-start | bytes 524288 | tf_op jit(solution)/shard_map/all_to_all | solution.py:69
  (96 other events, 1190.0 us)
Sparse Core Ops, SparseCore 0:
  15.6 64.6 all-gather.3
  91.7 64.1 all-gather.5
  158.6 58.9 all-gather.7
  418.9 95.2 reduce-scatter.1

commit v3 on v2

--- a/solution.py
+++ b/solution.py
@@ -81,23 +81,29 @@
     return jnp.stack([first, second], axis=1).reshape(ROWS, n)
 
 
-def core_sum(value, ci):
+def pair_pieces(keep, send, yi):
+    other = swap_core(send)
+    pieces = []
+    for by in range(4):
+        at = (yi + by) % 4
+        mine = lax.dynamic_index_in_dim(keep, at, 0, keepdims=False).astype(WIDE)
+        theirs = lax.dynamic_index_in_dim(other, at, 0, keepdims=False).astype(WIDE)
+        pieces.append((mine + theirs).astype(HALF))
+    return pieces
+
+
+def add_pieces(pieces):
+    total = pieces[0].astype(WIDE)
+    for by in (1, 2, 3):
+        total = total + shift_y(pieces[by], by).astype(WIDE)
+    return total
+
+
+def sum_rows(value, yi, ci):
     parts = value.reshape(4, 2, OWN, value.shape[1])
     mine = lax.dynamic_index_in_dim(parts, ci, 1, keepdims=False)
     theirs = lax.dynamic_index_in_dim(parts, 1 - ci, 1, keepdims=False)
-    return (mine.astype(WIDE) + swap_core(theirs).astype(WIDE)).astype(HALF)
-
-
-def row_sum(pair, yi):
-    total = lax.dynamic_index_in_dim(pair, yi, 0, keepdims=False).astype(WIDE)
-    for by in (1, 2, 3):
-        piece = lax.dynamic_index_in_dim(pair, (yi + by) % 4, 0, keepdims=False)
-        total = total + shift_y(piece, by).astype(WIDE)
-    return total
-
-
-def sum_rows(value, yi, ci):
-    return row_sum(core_sum(value, ci), yi)
+    return add_pieces(pair_pieces(mine, theirs, yi))
 
 
 def sum_experts(value):
@@ -426,14 +432,17 @@
             out_ref[0] = refs[k][...].astype(WIDE)
 
 
-def place_pieces(yi, pieces):
+def place_pieces(yi, pieces, part):
     return pl.pallas_call(
         place_kernel,
         out_shape=jax.ShapeDtypeStruct((4, FFS, D), WIDE),
         grid_spec=pltpu.PrefetchScalarGridSpec(
             num_scalar_prefetch=1,
             grid=(4,),
-            in_specs=[pl.BlockSpec((FFS, D), lambda k, at: (0, 0))] * 4,
+            in_specs=[
+                pl.BlockSpec((FFS, D), lambda k, at, i=i: (part if i == 2 else 0, 0))
+                for i in range(4)
+            ],
             out_specs=pl.BlockSpec((1, FFS, D), lambda k, at: ((at[0] + k) % 4, 0, 0)),
         ),
         compiler_params=pltpu.CompilerParams(vmem_limit_bytes=24 * 1024 * 1024),
@@ -441,8 +450,52 @@
     )(yi.reshape(1), *pieces)
 
 
-def late_kernel(dq_ref, wq_ref, so_ref, gated_ref, out_ref, core_ref, late_ref):
-    late_ref[:, :D] = dot_nt(dq_ref[...], wq_ref[...]).astype(HALF)
+def expert_grad_kernel(x_ref, dso_ref, hid_ref, dpre_ref, gate_ref, *rest):
+    outs, far_ref = rest[:6], rest[6]
+    targets, sems = rest[7:9], rest[9]
+    copies = []
+
+    def copy(source, target):
+        moved = pltpu.make_async_copy(source, target, sems.at[len(copies)])
+        moved.start()
+        copies.append(moved)
+
+    copy(gate_ref.at[pl.ds(2 * FFS, FFS), :], far_ref.at[pl.ds(0, FFS), :])
+    for part, right in enumerate((x_ref, dso_ref)):
+        target = targets[part]
+        for c in range(FFP // 256):
+            if part == 0:
+                left = dpre_ref[:, FFP + 256 * c : FFP + 256 * c + 256]
+            else:
+                left = hid_ref[:, 256 * c : 256 * c + 256]
+            target[256 * c : 256 * c + 256, :] = dot_tn(left, right[...]).astype(HALF)
+        for i, k in enumerate((0, 1, 3)):
+            copy(target.at[pl.ds(FFS * k, FFS), :], outs[3 * part + i])
+        copy(target.at[pl.ds(2 * FFS, FFS), :], far_ref.at[pl.ds(FFS * (part + 1), FFS), :])
+    for moved in copies:
+        moved.wait()
+
+
+def expert_grads(x_slots, d_slot_out, hidden, d_pre, grad_gate):
+    vmem = pl.BlockSpec(memory_space=pltpu.VMEM)
+    hbm = pl.BlockSpec(memory_space=pl.ANY)
+    outs = pl.pallas_call(
+        expert_grad_kernel,
+        out_shape=(jax.ShapeDtypeStruct((FFS, D), HALF),) * 6
+        + (jax.ShapeDtypeStruct((3 * FFS, D), HALF),),
+        in_specs=[vmem] * 4 + [hbm],
+        out_specs=(hbm,) * 7,
+        scratch_shapes=[pltpu.VMEM((FFP, D), HALF)] * 2 + [pltpu.SemaphoreType.DMA((9,))],
+        compiler_params=pltpu.CompilerParams(vmem_limit_bytes=40 * 1024 * 1024),
+        cost_estimate=pl.CostEstimate(flops=1, bytes_accessed=1, transcendentals=0),
+    )(x_slots, d_slot_out, hidden, d_pre, grad_gate)
+    up_parts = [outs[0], outs[1], None, outs[2]]
+    down_parts = [outs[3], outs[4], None, outs[5]]
+    return up_parts, down_parts, outs[6]
+
+
+def late_kernel(one_ref, so_ref, gated_ref, out_ref, core_ref, late_ref):
+    late_ref[:, :D] = one_ref[...]
     routed = dot_tn(gated_ref[...], out_ref[...])
     half = D // 2
     first = (core_ref[0] == 0).astype(WIDE)
@@ -450,25 +503,28 @@
     late_ref[:, D + half :] = (so_ref[:, half:] + routed * (1.0 - first)).astype(HALF)
 
 
-def late_products(ci, d_queries, wq, shared_out, gated, out_back):
+def late_products(ci, d_one, shared_out, gated, out_back):
     vmem = pl.BlockSpec(memory_space=pltpu.VMEM)
     return pl.pallas_call(
         late_kernel,
         out_shape=jax.ShapeDtypeStruct((ROWS, 2 * D), HALF),
-        in_specs=[vmem] * 5 + [pl.BlockSpec(memory_space=pltpu.SMEM)],
+        in_specs=[vmem] * 4 + [pl.BlockSpec(memory_space=pltpu.SMEM)],
         out_specs=vmem,
         compiler_params=pltpu.CompilerParams(vmem_limit_bytes=32 * 1024 * 1024),
         cost_estimate=pl.CostEstimate(flops=1, bytes_accessed=1, transcendentals=0),
-    )(d_queries, wq, shared_out, gated, out_back, ci.reshape(1))
+    )(d_one, shared_out, gated, out_back, ci.reshape(1))
 
 
 def rest_kernel(
     h_two_ref, dsp_ref, g_ref, sh_ref, h_one_ref, dq_ref, dmid_ref, heads_ref, c_ref, dkv_ref,
-    out_ref, kv_ref,
+    wq_ref, norm_ref, out_ref, one_ref, gain_ref, kv_ref,
 ):
+    d_one = dot_nt(dq_ref[...], wq_ref[...])
+    one_ref[...] = d_one.astype(HALF)
+    gain_ref[...] = jnp.sum(d_one * norm_ref[...], axis=0, keepdims=True)
+
     def step(i, carry):
-        at = pl.multiple_of(i * 256, 256)
-        rows = pl.ds(at, 256)
+        rows = pl.ds(pl.multiple_of(i * 256, 256), 256)
         out_ref[rows, 0:768] = dot_tn(h_two_ref[:, rows], dsp_ref[...]).astype(HALF)
         out_ref[rows, 768:1152] = dot_tn(g_ref[:, rows], sh_ref[...]).astype(HALF)
         out_ref[rows, 1152:1536] = dot_tn(h_one_ref[:, rows], dq_ref[...]).astype(HALF)
@@ -496,9 +552,13 @@
     vmem = pl.BlockSpec(memory_space=pltpu.VMEM)
     return pl.pallas_call(
         rest_kernel,
-        out_shape=jax.ShapeDtypeStruct((D, 1920), HALF),
-        in_specs=[vmem] * 10,
-        out_specs=vmem,
+        out_shape=(
+            jax.ShapeDtypeStruct((D, 1920), HALF),
+            jax.ShapeDtypeStruct((ROWS, D), HALF),
+            jax.ShapeDtypeStruct((1, D), WIDE),
+        ),
+        in_specs=[vmem] * 12,
+        out_specs=(vmem,) * 3,
         scratch_shapes=[pltpu.VMEM((KVL, 512), WIDE)],
         compiler_params=pltpu.CompilerParams(vmem_limit_bytes=48 * 1024 * 1024),
         cost_estimate=pl.CostEstimate(flops=1, bytes_accessed=1, transcendentals=0),
@@ -566,6 +626,14 @@
     def swap_halves(v):
         return jnp.concatenate([v[:, 64:], v[:, :64]], axis=1)
 
+    def ordered_cores(mine, other, axis):
+        return jnp.concatenate(
+            [jnp.where(ci == 0, mine, other), jnp.where(ci == 0, other, mine)], axis=axis
+        )
+
+    def both_cores(value, axis):
+        return ordered_cores(value, swap_core(value), axis)
+
     def own_rows(value):
         return lax.dynamic_slice_in_dim(value, ti * OWN, OWN, 0)
 
@@ -577,9 +645,6 @@
 
     def moved_pieces(sent):
         return [sent[0]] + [shift_y(sent[by], by) for by in (1, 2, 3)]
-
-    def own_pieces(grad):
-        return [grad[FFS * by : FFS * (by + 1)] for by in range(4)]
 
     gain_cols = jnp.stack([gain_attn, gain_ffn, jnp.pad(gain_latent, (0, 96))], axis=1)
     w_router_perm = w_router.reshape(128, 16, 4).transpose(0, 2, 1).reshape(128, EXPERTS)
@@ -732,19 +797,25 @@
         return (keep.astype(WIDE) + swap_core(send).astype(WIDE)).astype(HALF)
 
     in_sent = pair(keep_in, send_in)
-    gate_parts = own_pieces(dot_tn(d_expert_pre[:, :FFP], x_slots).astype(HALF))
-    in_sent, gate_parts, keep_out, send_out, d_slot_out, expert_hidden, d_expert_pre = (
+    grad_gate = dot_tn(d_expert_pre[:, :FFP], x_slots).astype(HALF)
+    in_sent, grad_gate, keep_out, send_out, d_slot_out, expert_hidden, d_expert_pre = (
         lax.optimization_barrier(
-            (in_sent, gate_parts, keep_out, send_out, d_slot_out, expert_hidden, d_expert_pre)
+            (in_sent, grad_gate, keep_out, send_out, d_slot_out, expert_hidden, d_expert_pre)
         )
     )
     in_recv = spread(in_sent.reshape(16, SLOTS, D // 2 + 128), EX)
-    gate_back = [gate_parts[0], shift_y(gate_parts[1], -1), None, shift_y(gate_parts[3], -3)]
+    gate_back = [
+        grad_gate[:FFS],
+        shift_y(grad_gate[FFS : 2 * FFS], -1),
+        None,
+        shift_y(grad_gate[3 * FFS : FFH], -3),
+    ]
     out_sent = pair(keep_out, send_out)
-    up_parts = own_pieces(dot_tn(d_expert_pre[:, FFP:], x_slots).astype(HALF))
-    down_parts = own_pieces(dot_tn(expert_hidden, d_slot_out).astype(HALF))
-    in_recv, out_sent, gate_parts, gate_back, up_parts, down_parts = lax.optimization_barrier(
-        (in_recv, out_sent, gate_parts, gate_back, up_parts, down_parts)
+    up_parts, down_parts, far_parts = expert_grads(
+        x_slots, d_slot_out, expert_hidden, d_expert_pre, grad_gate
+    )
+    in_recv, gate_back, up_parts, down_parts, far_parts = lax.optimization_barrier(
+        (in_recv, gate_back, up_parts, down_parts, far_parts)
     )
 
     in_back = in_recv[:, :, : D // 2].reshape(16 * SLOTS, D // 2)
@@ -779,38 +850,28 @@
     lat_keep, lat_send, d_kv, d_q, up_parts, up_back = lax.optimization_barrier(
         (lat_keep, lat_send, d_kv, d_q, up_parts, up_back)
     )
-    lat_pair = pair(lat_keep, lat_send)
-    lat_pair, d_kv, d_q, d_attn_b, d_shared_pre, shared_hidden, out_sent = lax.optimization_barrier(
-        (lat_pair, d_kv, d_q, d_attn_b, d_shared_pre, shared_hidden, out_sent)
+    lat_pieces = pair_pieces(lat_keep, lat_send, yi)
+    lat_pieces, d_kv, d_q, d_attn_b, out_sent = lax.optimization_barrier(
+        (lat_pieces, d_kv, d_q, d_attn_b, out_sent)
     )
     out_back = spread(out_sent.reshape(16, SLOTS, D // 2), EX).reshape(16 * SLOTS, D // 2)
-    lat_total = lax.dynamic_index_in_dim(lat_pair, yi, 0, keepdims=False).astype(WIDE)
-    lat_pieces = [
-        shift_y(lax.dynamic_index_in_dim(lat_pair, (yi + by) % 4, 0, keepdims=False), by)
-        for by in (1, 2, 3)
-    ]
+    lat_total = add_pieces(lat_pieces)
 
     d_q_rot = d_q[:, 256:]
     d_q_rot = d_q_rot * cos4 - swap_halves(d_q_rot) * sin4
     d_queries = jnp.concatenate([d_q[:, :256], d_q_rot], axis=1).astype(HALF)
-    rest_grads = rest_products(
-        h_two, d_shared_pre, g_rows, shared_hidden, h_one, d_queries, d_attn_b, attn_heads, c_all, d_kv
-    )
-    for piece in lat_pieces:
-        lat_total = lat_total + piece.astype(WIDE)
-    lat_total, d_queries, out_back, down_parts, up_parts, rest_grads = lax.optimization_barrier(
-        (lat_total.astype(HALF), d_queries, out_back, down_parts, up_parts, rest_grads)
+    rest_grads, d_one, gain_one_late = rest_products(
+        h_two, d_shared_pre, g_rows, shared_hidden, h_one, d_queries, d_attn_b, attn_heads,
+        c_all, d_kv, wq_b, normed_in,
+    )
+    lat_total, out_back, down_parts, far_parts, rest_grads = lax.optimization_barrier(
+        (lat_total.astype(HALF), out_back, down_parts, far_parts, rest_grads)
     )
     rest_sum = lax.psum_scatter(rest_grads, EX, scatter_dimension=0, tiled=True)
     lat_parts = spread(lat_total, EX)
+    far_back = shift_y(far_parts, -2)
     down_back = [down_parts[0], shift_y(down_parts[1], -1), None, shift_y(down_parts[3], -3)]
-    late_parts = late_products(ci, d_queries, wq_b, shared_out, gated, out_back)
-    late_own = sum_rows(late_parts, yi, ci)
-    lat_parts, down_parts, down_back, late_own = lax.optimization_barrier(
-        (lat_parts, down_parts, down_back, late_own)
-    )
-    d_one_own = late_own[:, :D]
-    layer_out = (mid_own + late_own[:, D:]).astype(HALF)
+    lat_parts, d_one, out_back = lax.optimization_barrier((lat_parts, d_one, out_back))
     d_lat_own = jnp.sum(lat_parts.astype(WIDE), axis=0)
 
     cos_own, sin_own = own_rows(cos4), own_rows(sin4)
@@ -822,48 +883,57 @@
     d_lat, grad_gain_lat = norm_back(
         d_lat_own[:, :512], own_rows(normed_lat), own_rows(scale_lat), gain_lat
     )
-    d_latent_pad = jnp.pad(jnp.concatenate([d_lat, d_rope], axis=1).astype(HALF), ((0, 0), (0, 64)))
-    d_both = jnp.concatenate([d_latent_pad, d_logits_pad], axis=1)
-    d_both = spread(jnp.broadcast_to(d_both[None], (8, OWN, 768)), ("y", "c")).reshape(ROWS, 768)
-    d_both, up_parts, down_parts, down_back, gate_parts = lax.optimization_barrier(
-        (d_both, up_parts, down_parts, down_back, gate_parts)
-    )
-    d_latent = d_both[:, :576]
-    d_logits_all = d_both[:, 704:768]
-    down_back[2] = shift_y(down_parts[2], -2)
-    gate_back[2] = shift_y(gate_parts[2], -2)
-    up_back[2] = shift_y(up_parts[2], -2)
-    d_h_one = d_one_own + dot_nt(d_latent_pad, blk_b)
+    d_latent = jnp.concatenate([d_lat, d_rope], axis=1).astype(HALF)
+    d_latent_pad = jnp.pad(d_latent, ((0, 0), (0, 64)))
+    d_chip = both_cores(jnp.concatenate([d_latent, d_logits], axis=1), 0)
+    d_chip, d_one, out_back = lax.optimization_barrier((d_chip, d_one, out_back))
+    late_parts = late_products(ci, d_one, shared_out, gated, out_back).reshape(4, 2, OWN, 2 * D)
+    late_pieces = pair_pieces(
+        lax.dynamic_index_in_dim(late_parts, ci, 1, keepdims=False),
+        lax.dynamic_index_in_dim(late_parts, 1 - ci, 1, keepdims=False),
+        yi,
+    )
+    d_lat_one = dot_nt(d_latent_pad, blk_b)
     scale_one = inv_rms(in_own)
     normed_one = in_own * scale_one
-    d_in_norm, gain_one_part = norm_back(d_h_one, normed_one, scale_one, gain_one)
-    grad_inputs = (d_mid_own + d_in_norm).astype(HALF)
-
-    grad_router = dot_tn(h_two, lax.dynamic_slice_in_dim(d_logits_all, ti * 8, 8, 1))
-    grad_dkv = dot_tn(h_one, lax.dynamic_slice_in_dim(d_latent, ti * 72, 72, 1))
+    gain_one_part = gain_one_late[0] + jnp.sum(d_lat_one * normed_one, axis=0)
+
+    def chip_rows(value):
+        return lax.dynamic_slice_in_dim(value, yi * 2 * OWN, 2 * OWN, 0)
+
+    def own_half(value):
+        half = value.shape[1] // 2
+        return jnp.where(ci == 0, value[:, :half], value[:, half:])
+
+    grad_dkv = dot_tn(chip_rows(h_one), own_half(d_chip[:, :576]))
+    grad_router = dot_tn(chip_rows(h_two), own_half(d_chip[:, 576:]))
     gain_lat_wide = jnp.pad(grad_gain_lat.reshape(16, 32), ((0, 0), (0, 96))).reshape(D)
     gain_rows = jnp.stack([gain_one_part, gain_two_part, gain_lat_wide], axis=0).astype(HALF)
     gain_at = (
-        lax.broadcasted_iota(jnp.int32, (3, 48), 0) == lax.broadcasted_iota(jnp.int32, (3, 48), 1)
+        lax.broadcasted_iota(jnp.int32, (3, 64), 0) == lax.broadcasted_iota(jnp.int32, (3, 64), 1)
     ).astype(HALF)
     last_part = jnp.concatenate([grad_dkv, grad_router, dot_tn(gain_rows, gain_at)], axis=1)
-    last_parts = spread(last_part.astype(HALF).reshape(16, 128, 128), EX)
-    last_parts, down_back = lax.optimization_barrier((last_parts, down_back))
-    grad_ed = place_pieces(yi, down_back)
-    last_sum = jnp.sum(last_parts.astype(WIDE), axis=0)
-    last_all = spread(
-        jnp.broadcast_to(last_sum.astype(HALF)[None], (8, 128, 128)), ("y", "c")
-    )
-    last_all, gate_back, up_back = lax.optimization_barrier((last_all, gate_back, up_back))
-    grad_eg = place_pieces(yi, gate_back)
-    grad_eu = place_pieces(yi, up_back)
+    last_parts = spread(last_part.astype(HALF).reshape(16, 128, 384), EX)
+    last_parts, far_back, down_back, late_pieces = lax.optimization_barrier(
+        (last_parts, far_back, down_back, late_pieces)
+    )
+    last_sum = jnp.sum(last_parts.astype(WIDE), axis=0).astype(HALF)
+    last_sum = add_pieces([last_sum] * 4).astype(HALF)
+    last_other = swap_core(last_sum)
+    sum_dkv = ordered_cores(last_sum[:, :288], last_other[:, :288], 1).astype(WIDE)
+    sum_router = ordered_cores(last_sum[:, 288:320], last_other[:, 288:320], 1)
+    sum_router = sum_router.reshape(128, 4, 16).transpose(0, 2, 1).reshape(128, EXPERTS).astype(WIDE)
+    gain_sums = last_sum[:, 320:323].astype(WIDE) + last_other[:, 320:323].astype(WIDE)
+    late_own = add_pieces(late_pieces)
+    up_back[2] = gate_back[2] = down_back[2] = far_back
+    grad_eg = place_pieces(yi, gate_back, 0)
+    grad_eu = place_pieces(yi, up_back, 1)
+    grad_ed = place_pieces(yi, down_back, 2)
+    layer_out = (mid_own + late_own[:, D:]).astype(HALF)
+    d_in_norm, _ = norm_back(late_own[:, :D] + d_lat_one, normed_one, scale_one, gain_one)
+    grad_inputs = (d_mid_own + d_in_norm).astype(HALF)
     rest_sum = rest_sum.astype(WIDE)
     sum_kv = rest_sum[:, 1792:].reshape(4, 32, 128).transpose(1, 0, 2).reshape(32, 512)
-    sum_dkv = last_all[:, :, :72].transpose(1, 0, 2).reshape(128, 576).astype(WIDE)
-    sum_router = last_all[:, :, 72:80].transpose(1, 0, 2).reshape(128, 4, 16)
-    sum_router = sum_router.transpose(0, 2, 1).reshape(128, EXPERTS).astype(WIDE)
-    gain_sums = jnp.sum(last_all[:, :, 80:83].astype(WIDE), axis=0)
-
     return (
         layer_out,
         grad_inputs,

time: 576 us -> 556 us (0.965)
  waiting for transfers between devices: 193 us -> 166 us
  Pallas kernels: 76.2 us -> 85.1 us
    all_to_all x8 -> x6, waiting for transfers between devices: 38.8 us -> 23.8 us  [spread(): return lax.all_to_all(value, axes, split_axis=0, concat_axis=0, tiled=True)]
    all_to_all x8 -> x6, starting transfers between devices: 45.6 us -> 31.5 us  [spread(): return lax.all_to_all(value, axes, split_axis=0, concat_axis=0, tiled=True)]
    pallas_call x1 -> x2, Pallas kernels: 14.7 us -> 26 us  [the longest x1 16.6 us: rest_products(): pl.pallas_call(rest_kernel, out_shape=(jax.ShapeDtypeStruct((D, 1920), HA...]
    ppermute x42 -> x43, waiting for transfers between devices: 122 us -> 111 us  [shift_y(): return lax.ppermute(value, 'y', [(i, (i + by) % 4) for i in range(4)])]
    ppermute x12 -> x14, starting transfers between devices: 16 us -> 22 us  [swap_core(): return lax.ppermute(value, 'c', [(0, 1), (1, 0)])]
    unnamed x193 -> x257, local copies, waits for them, and re-layouts: 22.9 us -> 28.6 us
    dot_general x8 -> x6, matrix products: 14.9 us -> 9.36 us  [dot_tn(): lax.dot_general(left, right, (((0,), (0,)), ((), ())), preferred_element_...]
    ppermute x42 -> x43, starting transfers between devices: 54.7 us -> 58.1 us  [shift_y(): return lax.ppermute(value, 'y', [(i, (i + by) % 4) for i in range(4)])]
  transfers between devices with their start and end apart: 66 -> 67, of which waited for: 43 -> 41; matrix products, arithmetic and copies ran while one was open for 19% -> 19% of each run, Pallas kernels for 9% -> 11%
where the time goes in v3:
time: 556 us; the launch traced here: 545 us
  waiting for transfers between devices  166 us (30%)
  starting transfers between devices  112 us (20%)
  Pallas kernels  85.1 us (15%)
  local copies, waits for them, and re-layouts  73.1 us (13%)
  other arithmetic  51.8 us (9%)
  matrix products  40.6 us (7%)
  between operations  16.4 us (3%)
    ppermute x43, waiting for transfers between devices, shift_y(): return lax.ppermute(value, 'y', [(i, (i + by) % 4) for i in range(4)])  111 us
    ppermute x43, starting transfers between devices, shift_y(): return lax.ppermute(value, 'y', [(i, (i + by) % 4) for i in range(4)])  58.1 us
    all_to_all x6, starting transfers between devices, spread(): return lax.all_to_all(value, axes, split_axis=0, concat_axis=0, tiled=True)  31.5 us
    unnamed x257, local copies, waits for them, and re-layouts  28.6 us
    pallas_call x1, Pallas kernels, run_expert(): pl.pallas_call(expert_kernel, out_shape=(jax.ShapeDtypeStruct((rows, D //...  26.5 us
    all_to_all x6, waiting for transfers between devices, spread(): return lax.all_to_all(value, axes, split_axis=0, concat_axis=0, tiled=True)  23.8 us
    ppermute x14, starting transfers between devices, swap_core(): return lax.ppermute(value, 'c', [(0, 1), (1, 0)])  22 us
    ppermute x14, waiting for transfers between devices, swap_core(): return lax.ppermute(value, 'c', [(0, 1), (1, 0)])  17.9 us
  transfers between devices with their start and end apart: 67, of which 41 were waited for; matrix products, arithmetic and copies ran while one was open for 19% of the time, Pallas kernels for 11%

profile of v3, /device:TPU:1, one launch (start us, length us, event | category | flops | bytes accessed | tf_op | source)
XLA Modules:
  0.0 545.2 jit_solution(2159054836594949406)
XLA Ops:
  15.7 7.2 %fusion.21 = (bf16[176,2048]{1,0:T(8,128)(2,1)}, bf16[176,2048]{1,0:T(8,128)(2,1)}, bf16[176,2048]{1,0:T(8,128)(2,1)}, bf16[176,2048]{1,0:T(8,128)(2,1)}, bf16[1...) fusion(f32[4,176,2048]{2,1,0:T(8,128)} %param.33, ...), kind=kLoop, calls=%fused_computation.69 | loop fusion | bytes 11534352 | tf_op jit(solution)/shard_map/convert_element_type | solution.py:642
  22.9 2.1 collective-permute-start.7
  25.0 2.6 collective-permute-start.8
  32.1 4.4 fusion.29
  43.4 2.1 collective-permute-start.6
  45.6 3.3 collective-permute-start.10
  58.8 13.8 %collective-permute-done.5.rest_2_ = bf16[176,2048]{1,0:T(8,128)(2,1)} collective-permute-done((bf16[176,2048]{1,0:T(8,128)(2,1)}, bf16[176,2048]{1,0:T(8,128)(2,1)}, u32[]{:S(2)}, u32[]{:S(2)}) %collective-permute-start.5) | collective-permute-done | bytes 720928 | tf_op jit(solution)/shard_map/ppermute | solution.py:65
  72.6 3.1 collective-permute-done.6.rest_3_
  75.7 4.6 all-gather.4.cloned.1.call-done
  83.4 3.1 fusion.7
  87.4 2.8 slice.293.wq_ref
  95.2 5.0 all-to-all-start
  101.6 2.4 collective-permute-start.12
  105.7 2.4 collective-permute-start.15
  108.1 2.1 fusion.165
  112.4 2.2 reshape.411.wkv_ref
  118.6 16.5 %collective-permute-done.12.rest_6_ = bf16[176,2048]{1,0:T(8,128)(2,1)} collective-permute-done((bf16[176,2048]{1,0:T(8,128)(2,1)}, bf16[176,2048]{1,0:T(8,128)(2,1)}, u32[]{:S(2)}, u32[]{:S(2)}) %collective-permute-start.12) | collective-permute-done | bytes 720928 | tf_op jit(solution)/shard_map/ppermute | solution.py:65
  135.1 14.4 %collective-permute-done.14.rest_9_ = bf16[176,2048]{1,0:T(8,128)(2,1)} collective-permute-done((bf16[176,2048]{1,0:T(8,128)(2,1)}, bf16[176,2048]{1,0:T(8,128)(2,1)}, u32[]{:S(2)}, u32[]{:S(2)}) %collective-permute-start.14) | collective-permute-done | bytes 720928 | tf_op jit(solution)/shard_map/ppermute | solution.py:65
  150.4 9.1 %all-gather.6.cloned.1.call-done.c_ref = bf16[4096,640]{1,0:T(8,128)(2,1)} async-done(((bf16[256,640]{1,0:T(8,128)(2,1)}), bf16[4096,640]{1,0:T(8,128)(2,1)}) %all-gather.6.cloned.1.call-update) | async-done | bytes 5242896 | tf_op jit(solution)/shard_map/all_gather | solution.py:726
  161.0 4.9 convolution_convert_fusion.kv_ref
  165.9 10.0 %shard_map.323 = (bf16[2,4096,256]{2,1,0:T(8,128)(2,1)S(1)}, f32[256,256]{1,0:T(8,128)S(1)}) custom-call(bf16[256,384]{1,0:T(8,128)(2,1)S(1)} %pad_maximum_fusion.7.q_ref, bf16[4096,512]{1,0:T(8,128)(2,1)S(1)} %convolution_convert_fusion.kv_ref, bf16[4096,128]{1,0:T(8,128)(2,1)S(1)} %slice.301.rot_ref, s32[1,256]{1,0:T(1,128)S(1)} %bitcast.297, ...), custom_call_target="tpu_custom_call" | custom-call | flops 1610612736 | bytes 12582912 | tf_op jit(solution)/shard_map/pallas_call | solution.py:185
  185.3 2.4 collective-permute-start.18
  190.0 3.9 collective-permute-done.18
  197.0 2.1 collective-permute-start.21
  201.4 2.7 collective-permute-done.21
  204.3 2.3 collective-permute-start.23
  214.0 2.1 collective-permute-start.25
  216.1 5.4 all-to-all-start.1
  221.6 3.1 fusion.3
  228.5 2.4 fusion.1
  230.9 2.5 collective-permute-done.25.rest_10_
  233.4 10.5 %all-to-all-done.1 = bf16[16,40,1152]{2,1,0:T(8,128)(2,1)} async-done(((bf16[16,40,1152]{2,1,0:T(8,128)(2,1)}), bf16[16,40,1152]{2,1,0:T(8,128)(2,1)}, u32[]{:S(2)}, u32[]{:S(2)}) %all-to-all-start.1) | async-done | bytes 1474592 | tf_op jit(solution)/shard_map/all_to_all | solution.py:69
  245.9 3.1 collective-permute-done.26.xo_ref
  252.4 26.5 %shard_map.324 = (bf16[640,1152]{1,0:T(8,128)(2,1)}, bf16[640,1152]{1,0:T(8,128)(2,1)}, bf16[640,1024]{1,0:T(8,128)(2,1)}, bf16[640,1024]{1,0:T(8,128)(2,1)}, bf...) custom-call(s32[1]{0:T(128)} %bitcast.56.at_ref.core_ref, ...), custom_call_target="tpu_custom_call" | custom-call | flops 12079595520 | bytes 29360128 | tf_op jit(solution)/shard_map/pallas_call | solution.py:400
  279.3 6.5 %convolution_convert_fusion.1.gate_ref = bf16[768,2048]{1,0:T(8,128)(2,1)} fusion(bf16[640,2048]{1,0:T(8,128)(2,1)} %get-tuple-element.238.x_ref, bf16[640,1536]{1,0:T(8,128)(2,1)} %get-tuple-element.247.dpre_ref), kind=kOutput, calls=%fused_computation.2 | convolution fusion | flops 2014838784 | bytes 6750208 | tf_op jit(solution)/shard_map/dot_general | solution.py:43
  287.3 4.4 all-to-all-start.2
  291.7 2.8 fusion.151
  298.5 9.4 %shard_map.325 = (bf16[176,2048]{1,0:T(8,128)(2,1)S(1)}, bf16[176,2048]{1,0:T(8,128)(2,1)S(1)}, bf16[176,2048]{1,0:T(8,128)(2,1)S(1)}, bf16[176,2048]{1,0:T(8,12...) custom-call(bf16[640,2048]{1,0:T(8,128)(2,1)S(1)} %copy-done.9, ...), custom_call_target="tpu_custom_call" | custom-call | flops 1 | bytes 1 | tf_op jit(solution)/shard_map/pallas_call | solution.py:482
  330.0 3.2 collective-permute-done.32
  333.7 2.1 multiply_reduce_fusion.2
  337.7 3.0 collective-permute-start.35
  342.3 4.3 collective-permute-done.35
  352.8 11.7 %shard_map.326 = (bf16[4,16,32,640]{3,2,1,0:T(8,128)(2,1)S(1)}, bf16[4,16,32,640]{3,2,1,0:T(8,128)(2,1)S(1)}, bf16[4096,512]{1,0:T(8,128)(2,1)S(1)}, f32[256,384]{1,0:T(8,128)S(1)}) custom-call(s32[1]{0:T(128)} %bitcast.56.at_ref.core_ref, bf16[256,384]{1,0:T(8,128)(2,1)S(1)} %copy-done.40, bf16[4096,512]{1,0:T(8,128)(2,1)S(1)} %copy-done.51, ...), custom_call_target="tpu_custom_call" | custom-call | flops 5368709120 | bytes 25165824 | tf_op jit(solution)/shard_map/pallas_call | solution.py:276
  364.6 3.5 collective-permute-done.38.refs_1_
  368.0 2.9 collective-permute-done.39.refs_3_
  372.5 6.5 %collective-permute-done.41 = bf16[640,1024]{1,0:T(8,128)(2,1)S(1)} collective-permute-done((bf16[640,1024]{1,0:T(8,128)(2,1)}, bf16[640,1024]{1,0:T(8,128)(2,1)S(1)}, u32[]{:S(2)}, u32[]{:S(2)}) %collective-permute-start.41) | collective-permute-done | bytes 1310752 | tf_op jit(solution)/shard_map/ppermute | solution.py:61
  382.6 5.9 %all-to-all-start.3 = ((bf16[16,40,1024]{2,1,0:T(8,128)(2,1)}), bf16[16,40,1024]{2,1,0:T(8,128)(2,1)}, u32[]{:S(2)}, u32[]{:S(2)}) async-start(bf16[16,40,1024]{2,1,0:T(8,128)(2,1)} %bitcast.305), calls=%async_computation.3 | async-start | bytes 2621440 | tf_op jit(solution)/shard_map/all_to_all | solution.py:69
  395.6 16.6 %shard_map.327 = (bf16[2048,1920]{1,0:T(8,128)(2,1)}, bf16[256,2048]{1,0:T(8,128)(2,1)S(1)}, f32[1,2048]{1,0:T(1,128)S(1)}) custom-call(bf16[256,2048]{1,0:T(8,128)(2,1)S(1)} %bitcast.288, bf16[256,768]{1,0:T(8,128)(2,1)S(1)} %copy-done.11, bf16[256,2048]{1,0:T(8,128)(2,1)S(1)} %bitcast.294, bf16[256,384]{1,0:T(8,128)(2,1)S(1)} %get-tuple-element.283.sh_ref, ...), custom_call_target="tpu_custom_call" | custom-call | flops 1 | bytes 1 | tf_op jit(solution)/shard_map/pallas_call | solution.py:553
  413.2 6.8 %collective-permute-done.42 = bf16[16,32,640]{2,1,0:T(8,128)(2,1)S(1)} collective-permute-done((bf16[16,32,640]{2,1,0:T(8,128)(2,1)}, bf16[16,32,640]{2,1,0:T(8,128)(2,1)S(1)}, u32[]{:S(2)}, u32[]{:S(2)}) %collective-permute-start.42) | collective-permute-done | bytes 655392 | tf_op jit(solution)/shard_map/ppermute | solution.py:65
  421.6 6.3 %all-to-all-start.4 = ((bf16[16,32,640]{2,1,0:T(8,128)(2,1)}), bf16[16,32,640]{2,1,0:T(8,128)(2,1)}, u32[]{:S(2)}, u32[]{:S(2)}) async-start(bf16[16,32,640]{2,1,0:T(8,128)(2,1)} %add_convert_fusion.2), calls=%async_computation.4 | async-start | bytes 1310720 | tf_op jit(solution)/shard_map/all_to_all | solution.py:69
  431.0 8.1 %all-to-all-done.4 = bf16[16,32,640]{2,1,0:T(8,128)(2,1)} async-done(((bf16[16,32,640]{2,1,0:T(8,128)(2,1)}), bf16[16,32,640]{2,1,0:T(8,128)(2,1)}, u32[]{:S(2)}, u32[]{:S(2)}) %all-to-all-start.4) | async-done | bytes 655392 | tf_op jit(solution)/shard_map/all_to_all | solution.py:69
  445.7 6.9 %collective-permute-start.45 = (bf16[32,640]{1,0:T(8,128)(2,1)}, bf16[32,640]{1,0:T(8,128)(2,1)}, u32[]{:S(2)}, u32[]{:S(2)}) collective-permute-start(bf16[32,640]{1,0:T(8,128)(2,1)} %fusion.103), channel_id=1, source_target_pairs={{0,1},{1,0},{2,3},{3,2},{4,5},{5,4},{6,7},{7,6},{8,9},{9,8},{10,11... | collective-permute-start | bytes 122888 | tf_op jit(solution)/shard_map/ppermute | solution.py:61
  454.0 3.5 fusion.67
  465.6 4.4 all-to-all-start.5
  470.0 2.6 collective-permute-start.47
  472.9 2.6 fusion.43
  475.5 20.4 %collective-permute-done.47.refs_1_ = bf16[176,2048]{1,0:T(8,128)(2,1)S(1)} collective-permute-done((bf16[176,2048]{1,0:T(8,128)(2,1)}, bf16[176,2048]{1,0:T(8,128)(2,1)S(1)}, u32[]{:S(2)}, u32[]{:S(2)}) %collective-permute-start.47) | collective-permute-done | bytes 720928 | tf_op jit(solution)/shard_map/ppermute | solution.py:65
  497.6 4.2 all-to-all-done.5
  503.5 4.1 collective-permute-start.54
  508.4 2.6 collective-permute-done.54
  514.1 2.6 collective-permute-start.51
  519.6 2.9 shard_map.331
  522.6 2.9 shard_map.330
  525.5 2.9 shard_map.329
  (538 shorter events, 174.9 us)
Async XLA Ops:
  7.2 73.0 %all-gather.4.cloned.1.call-start = ((), (), s32[]{:S(2)}) async-start(), calls=%async_computation.7 | async-start | bytes 6684672 | tf_op jit(solution)/shard_map/all_gather | solution.py:662
  15.5 144.1 %all-gather.6.cloned.1.call-start = ((), (), s32[]{:S(2)}) async-start(), calls=%async_computation.8 | async-start | bytes 5570560 | tf_op jit(solution)/shard_map/all_gather | solution.py:726
  22.9 15.8 %collective-permute-start.7 = (bf16[32,2048]{1,0:T(8,128)(2,1)S(1)}, bf16[32,2048]{1,0:T(8,128)(2,1)S(1)}, u32[]{:S(2)}, u32[]{:S(2)}) collective-permute-start(bf16[32,2048]{1,0:T(8,128)(2,1)S(1)} %copy-done.74), channel_id=1, source_target_pairs={{0,2},{2,4},{4,6},{6,0},{1,3},{3,5},{5,7},{7,1},{8,10},{10,12},{12... | collective-permute-start | bytes 393224 | tf_op jit(solution)/shard_map/ppermute | solution.py:65
  25.0 16.6 %collective-permute-start.8 = (bf16[32,2048]{1,0:T(8,128)(2,1)S(1)}, bf16[32,2048]{1,0:T(8,128)(2,1)S(1)}, u32[]{:S(2)}, u32[]{:S(2)}) collective-permute-start(bf16[32,2048]{1,0:T(8,128)(2,1)S(1)} %copy-done.74), channel_id=1, source_target_pairs={{0,4},{2,6},{4,0},{6,2},{1,5},{3,7},{5,1},{7,3},{8,12},{10,14},{12... | collective-permute-start | bytes 393224 | tf_op jit(solution)/shard_map/ppermute | solution.py:65
  27.6 15.8 %collective-permute-start.9 = (bf16[32,2048]{1,0:T(8,128)(2,1)S(1)}, bf16[32,2048]{1,0:T(8,128)(2,1)S(1)}, u32[]{:S(2)}, u32[]{:S(2)}) collective-permute-start(bf16[32,2048]{1,0:T(8,128)(2,1)S(1)} %copy-done.74), channel_id=1, source_target_pairs={{0,6},{2,0},{4,2},{6,4},{1,7},{3,1},{5,3},{7,5},{8,14},{10,8},{12,... | collective-permute-start | bytes 393224 | tf_op jit(solution)/shard_map/ppermute | solution.py:65
  28.7 11.7 %collective-permute-start = (bf16[32,2048]{1,0:T(8,128)(2,1)S(1)}, bf16[32,2048]{1,0:T(8,128)(2,1)S(1)}, u32[]{:S(2)}, u32[]{:S(2)}) collective-permute-start(bf16[32,2048]{1,0:T(8,128)(2,1)S(1)} %copy-done.69), channel_id=1, source_target_pairs={{0,2},{2,4},{4,6},{6,0},{1,3},{3,5},{5,7},{7,1},{8,10},{10,12},{12... | collective-permute-start | bytes 393224 | tf_op jit(solution)/shard_map/ppermute | solution.py:65
  29.1 16.5 %collective-permute-start.1 = (bf16[32,2048]{1,0:T(8,128)(2,1)S(1)}, bf16[32,2048]{1,0:T(8,128)(2,1)S(1)}, u32[]{:S(2)}, u32[]{:S(2)}) collective-permute-start(bf16[32,2048]{1,0:T(8,128)(2,1)S(1)} %copy-done.69), channel_id=1, source_target_pairs={{0,4},{2,6},{4,0},{6,2},{1,5},{3,7},{5,1},{7,3},{8,12},{10,14},{12... | collective-permute-start | bytes 393224 | tf_op jit(solution)/shard_map/ppermute | solution.py:65
  38.7 10.9 %collective-permute-start.2 = (bf16[32,2048]{1,0:T(8,128)(2,1)S(1)}, bf16[32,2048]{1,0:T(8,128)(2,1)S(1)}, u32[]{:S(2)}, u32[]{:S(2)}) collective-permute-start(bf16[32,2048]{1,0:T(8,128)(2,1)S(1)} %copy-done.69), channel_id=1, source_target_pairs={{0,6},{2,0},{4,2},{6,4},{1,7},{3,1},{5,3},{7,5},{8,14},{10,8},{12,... | collective-permute-start | bytes 393224 | tf_op jit(solution)/shard_map/ppermute | solution.py:65
  40.3 17.5 %collective-permute-start.4 = (bf16[176,2048]{1,0:T(8,128)(2,1)}, bf16[176,2048]{1,0:T(8,128)(2,1)S(1)}, u32[]{:S(2)}, u32[]{:S(2)}) collective-permute-start(bf16[176,2048]{1,0:T(8,128)(2,1)} %get-tuple-element.171), channel_id=1, source_target_pairs={{0,2},{2,4},{4,6},{6,0},{1,3},{3,5},{5,7},{7,1},{8,10},{10,12},{12... | collective-permute-start | bytes 2162696 | tf_op jit(solution)/shard_map/ppermute | solution.py:65
  41.6 31.0 %collective-permute-start.5 = (bf16[176,2048]{1,0:T(8,128)(2,1)}, bf16[176,2048]{1,0:T(8,128)(2,1)}, u32[]{:S(2)}, u32[]{:S(2)}) collective-permute-start(bf16[176,2048]{1,0:T(8,128)(2,1)} %get-tuple-element.172), channel_id=1, source_target_pairs={{0,4},{2,6},{4,0},{6,2},{1,5},{3,7},{5,1},{7,3},{8,12},{10,14},{12... | collective-permute-start | bytes 2162696 | tf_op jit(solution)/shard_map/ppermute | solution.py:65
  43.4 32.2 %collective-permute-start.6 = (bf16[176,2048]{1,0:T(8,128)(2,1)}, bf16[176,2048]{1,0:T(8,128)(2,1)}, u32[]{:S(2)}, u32[]{:S(2)}) collective-permute-start(bf16[176,2048]{1,0:T(8,128)(2,1)} %get-tuple-element.173), channel_id=1, source_target_pairs={{0,6},{2,0},{4,2},{6,4},{1,7},{3,1},{5,3},{7,5},{8,14},{10,8},{12,... | collective-permute-start | bytes 2162696 | tf_op jit(solution)/shard_map/ppermute | solution.py:65
  45.6 4.9 collective-permute-start.10
  95.2 55.2 %all-to-all-start = ((bf16[16,40,1024]{2,1,0:T(8,128)(2,1)}), bf16[16,40,1024]{2,1,0:T(8,128)(2,1)}, u32[]{:S(2)}, u32[]{:S(2)}) async-start(bf16[16,40,1024]{2,1,0:T(8,128)(2,1)} %bitcast.302), calls=%async_computation | async-start | bytes 2621440 | tf_op jit(solution)/shard_map/all_to_all | solution.py:69
  100.3 121.3 %all-gather.8.cloned.1.call-start = ((), (), s32[]{:S(2)}) async-start(), calls=%async_computation.9 | async-start | bytes 5013504 | tf_op jit(solution)/shard_map/all_gather | solution.py:740
  100.3 18.3 %collective-permute-start.11 = (bf16[176,2048]{1,0:T(8,128)(2,1)}, bf16[176,2048]{1,0:T(8,128)(2,1)}, u32[]{:S(2)}, u32[]{:S(2)}) collective-permute-start(bf16[176,2048]{1,0:T(8,128)(2,1)} %get-tuple-element.195), channel_id=1, source_target_pairs={{0,2},{2,4},{4,6},{6,0},{1,3},{3,5},{5,7},{7,1},{8,10},{10,12},{12... | collective-permute-start | bytes 2162696 | tf_op jit(solution)/shard_map/ppermute | solution.py:65
  101.6 33.5 %collective-permute-start.12 = (bf16[176,2048]{1,0:T(8,128)(2,1)}, bf16[176,2048]{1,0:T(8,128)(2,1)}, u32[]{:S(2)}, u32[]{:S(2)}) collective-permute-start(bf16[176,2048]{1,0:T(8,128)(2,1)} %get-tuple-element.196), channel_id=1, source_target_pairs={{0,4},{2,6},{4,0},{6,2},{1,5},{3,7},{5,1},{7,3},{8,12},{10,14},{12... | collective-permute-start | bytes 2162696 | tf_op jit(solution)/shard_map/ppermute | solution.py:65
  104.0 31.0 %collective-permute-start.13 = (bf16[176,2048]{1,0:T(8,128)(2,1)}, bf16[176,2048]{1,0:T(8,128)(2,1)}, u32[]{:S(2)}, u32[]{:S(2)}) collective-permute-start(bf16[176,2048]{1,0:T(8,128)(2,1)} %get-tuple-element.197), channel_id=1, source_target_pairs={{0,6},{2,0},{4,2},{6,4},{1,7},{3,1},{5,3},{7,5},{8,14},{10,8},{12,... | collective-permute-start | bytes 2162696 | tf_op jit(solution)/shard_map/ppermute | solution.py:65
  105.4 44.1 %collective-permute-start.14 = (bf16[176,2048]{1,0:T(8,128)(2,1)}, bf16[176,2048]{1,0:T(8,128)(2,1)}, u32[]{:S(2)}, u32[]{:S(2)}) collective-permute-start(bf16[176,2048]{1,0:T(8,128)(2,1)} %get-tuple-element.199), channel_id=1, source_target_pairs={{0,2},{2,4},{4,6},{6,0},{1,3},{3,5},{5,7},{7,1},{8,10},{10,12},{12... | collective-permute-start | bytes 2162696 | tf_op jit(solution)/shard_map/ppermute | solution.py:65
  105.7 44.7 %collective-permute-start.15 = (bf16[176,2048]{1,0:T(8,128)(2,1)}, bf16[176,2048]{1,0:T(8,128)(2,1)}, u32[]{:S(2)}, u32[]{:S(2)}) collective-permute-start(bf16[176,2048]{1,0:T(8,128)(2,1)} %get-tuple-element.200), channel_id=1, source_target_pairs={{0,6},{2,0},{4,2},{6,4},{1,7},{3,1},{5,3},{7,5},{8,14},{10,8},{12,... | collective-permute-start | bytes 2162696 | tf_op jit(solution)/shard_map/ppermute | solution.py:65
  184.0 6.0 %collective-permute-start.17 = (bf16[32,2048]{1,0:T(8,128)(2,1)S(1)}, bf16[32,2048]{1,0:T(8,128)(2,1)S(1)}, u32[]{:S(2)}, u32[]{:S(2)}) collective-permute-start(bf16[32,2048]{1,0:T(8,128)(2,1)S(1)} %get-tuple-element.463), channel_id=1, source_target_pairs={{0,2},{2,4},{4,6},{6,0},{1,3},{3,5},{5,7},{7,1},{8,10},{10,12},{12... | collective-permute-start | bytes 393224 | tf_op jit(solution)/shard_map/ppermute | solution.py:65
  185.3 8.6 %collective-permute-start.18 = (bf16[32,2048]{1,0:T(8,128)(2,1)S(1)}, bf16[32,2048]{1,0:T(8,128)(2,1)}, u32[]{:S(2)}, u32[]{:S(2)}) collective-permute-start(bf16[32,2048]{1,0:T(8,128)(2,1)S(1)} %get-tuple-element.465), channel_id=1, source_target_pairs={{0,4},{2,6},{4,0},{6,2},{1,5},{3,7},{5,1},{7,3},{8,12},{10,14},{12... | collective-permute-start | bytes 393224 | tf_op jit(solution)/shard_map/ppermute | solution.py:65
  187.7 6.2 %collective-permute-start.19 = (bf16[32,2048]{1,0:T(8,128)(2,1)S(1)}, bf16[32,2048]{1,0:T(8,128)(2,1)}, u32[]{:S(2)}, u32[]{:S(2)}) collective-permute-start(bf16[32,2048]{1,0:T(8,128)(2,1)S(1)} %get-tuple-element.464), channel_id=1, source_target_pairs={{0,6},{2,0},{4,2},{6,4},{1,7},{3,1},{5,3},{7,5},{8,14},{10,8},{12,... | collective-permute-start | bytes 393224 | tf_op jit(solution)/shard_map/ppermute | solution.py:65
  195.9 5.5 %collective-permute-start.20 = (bf16[32,2048]{1,0:T(8,128)(2,1)S(1)}, bf16[32,2048]{1,0:T(8,128)(2,1)S(1)}, u32[]{:S(2)}, u32[]{:S(2)}) collective-permute-start(bf16[32,2048]{1,0:T(8,128)(2,1)S(1)} %get-tuple-element.432), channel_id=1, source_target_pairs={{0,2},{2,4},{4,6},{6,0},{1,3},{3,5},{5,7},{7,1},{8,10},{10,12},{12... | collective-permute-start | bytes 393224 | tf_op jit(solution)/shard_map/ppermute | solution.py:65
  197.0 7.0 %collective-permute-start.21 = (bf16[32,2048]{1,0:T(8,128)(2,1)S(1)}, bf16[32,2048]{1,0:T(8,128)(2,1)S(1)}, u32[]{:S(2)}, u32[]{:S(2)}) collective-permute-start(bf16[32,2048]{1,0:T(8,128)(2,1)S(1)} %get-tuple-element.432), channel_id=1, source_target_pairs={{0,4},{2,6},{4,0},{6,2},{1,5},{3,7},{5,1},{7,3},{8,12},{10,14},{12... | collective-permute-start | bytes 393224 | tf_op jit(solution)/shard_map/ppermute | solution.py:65
  199.2 5.1 collective-permute-start.22
  204.3 4.0 collective-permute-start.23
  213.6 19.8 %collective-permute-start.24 = (bf16[640,1024]{1,0:T(8,128)(2,1)}, bf16[640,1024]{1,0:T(8,128)(2,1)}, u32[]{:S(2)}, u32[]{:S(2)}) collective-permute-start(bf16[640,1024]{1,0:T(8,128)(2,1)} %bitcast.43.g_ref), channel_id=1, source_target_pairs={{0,1},{1,0},{2,3},{3,2},{4,5},{5,4},{6,7},{7,6},{8,9},{9,8},{10,11... | collective-permute-start | bytes 3932168 | tf_op jit(solution)/shard_map/ppermute | solution.py:61
  214.0 19.4 %collective-permute-start.25 = (bf16[176,2048]{1,0:T(8,128)(2,1)}, bf16[176,2048]{1,0:T(8,128)(2,1)}, u32[]{:S(2)}, u32[]{:S(2)}) collective-permute-start(bf16[176,2048]{1,0:T(8,128)(2,1)} %get-tuple-element.216), channel_id=1, source_target_pairs={{0,4},{2,6},{4,0},{6,2},{1,5},{3,7},{5,1},{7,3},{8,12},{10,14},{12... | collective-permute-start | bytes 2162696 | tf_op jit(solution)/shard_map/ppermute | solution.py:65
  216.1 27.8 %all-to-all-start.1 = ((bf16[16,40,1152]{2,1,0:T(8,128)(2,1)}), bf16[16,40,1152]{2,1,0:T(8,128)(2,1)}, u32[]{:S(2)}, u32[]{:S(2)}) async-start(bf16[16,40,1152]{2,1,0:T(8,128)(2,1)} %pad_maximum_fusion.1), calls=%async_computation.1 | async-start | bytes 2949120 | tf_op jit(solution)/shard_map/all_to_all | solution.py:69
  243.9 5.1 collective-permute-start.26
  278.9 6.9 %collective-permute-start.27 = (bf16[640,1152]{1,0:T(8,128)(2,1)}, bf16[640,1152]{1,0:T(8,128)(2,1)S(1)}, u32[]{:S(2)}, u32[]{:S(2)}) collective-permute-start(bf16[640,1152]{1,0:T(8,128)(2,1)} %get-tuple-element.236), channel_id=1, source_target_pairs={{0,1},{1,0},{2,3},{3,2},{4,5},{5,4},{6,7},{7,6},{8,9},{9,8},{10,11... | collective-permute-start | bytes 4423688 | tf_op jit(solution)/shard_map/ppermute | solution.py:61
  287.3 29.4 %all-to-all-start.2 = ((bf16[16,40,1152]{2,1,0:T(8,128)(2,1)}), bf16[16,40,1152]{2,1,0:T(8,128)(2,1)}, u32[]{:S(2)}, u32[]{:S(2)}) async-start(bf16[16,40,1152]{2,1,0:T(8,128)(2,1)} %bitcast.301), calls=%async_computation.2 | async-start | bytes 2949120 | tf_op jit(solution)/shard_map/all_to_all | solution.py:69
  294.6 17.7 %collective-permute-start.28 = (bf16[176,2048]{1,0:T(8,128)(2,1)S(1)}, bf16[176,2048]{1,0:T(8,128)(2,1)S(1)}, u32[]{:S(2)}, u32[]{:S(2)}) collective-permute-start(bf16[176,2048]{1,0:T(8,128)(2,1)S(1)} %get-tuple-element.458), channel_id=1, source_target_pairs={{0,6},{2,0},{4,2},{6,4},{1,7},{3,1},{5,3},{7,5},{8,14},{10,8},{12,... | collective-permute-start | bytes 2162696 | tf_op jit(solution)/shard_map/ppermute | solution.py:65
  296.2 18.6 %collective-permute-start.29 = (bf16[176,2048]{1,0:T(8,128)(2,1)S(1)}, bf16[176,2048]{1,0:T(8,128)(2,1)S(1)}, u32[]{:S(2)}, u32[]{:S(2)}) collective-permute-start(bf16[176,2048]{1,0:T(8,128)(2,1)S(1)} %get-tuple-element.457), channel_id=1, source_target_pairs={{0,2},{2,4},{4,6},{6,0},{1,3},{3,5},{5,7},{7,1},{8,10},{10,12},{12... | collective-permute-start | bytes 2162696 | tf_op jit(solution)/shard_map/ppermute | solution.py:65
  323.8 6.2 %collective-permute-start.31 = (bf16[32,2176]{1,0:T(8,128)(2,1)S(1)}, bf16[32,2176]{1,0:T(8,128)(2,1)S(1)}, u32[]{:S(2)}, u32[]{:S(2)}) collective-permute-start(bf16[32,2176]{1,0:T(8,128)(2,1)S(1)} %get-tuple-element.460), channel_id=1, source_target_pairs={{0,2},{2,4},{4,6},{6,0},{1,3},{3,5},{5,7},{7,1},{8,10},{10,12},{12... | collective-permute-start | bytes 417800 | tf_op jit(solution)/shard_map/ppermute | solution.py:65
  324.6 8.5 %collective-permute-start.32 = (bf16[32,2176]{1,0:T(8,128)(2,1)S(1)}, bf16[32,2176]{1,0:T(8,128)(2,1)S(1)}, u32[]{:S(2)}, u32[]{:S(2)}) collective-permute-start(bf16[32,2176]{1,0:T(8,128)(2,1)S(1)} %get-tuple-element.462), channel_id=1, source_target_pairs={{0,4},{2,6},{4,0},{6,2},{1,5},{3,7},{5,1},{7,3},{8,12},{10,14},{12... | collective-permute-start | bytes 417800 | tf_op jit(solution)/shard_map/ppermute | solution.py:65
  326.7 6.5 %collective-permute-start.33 = (bf16[32,2176]{1,0:T(8,128)(2,1)S(1)}, bf16[32,2176]{1,0:T(8,128)(2,1)S(1)}, u32[]{:S(2)}, u32[]{:S(2)}) collective-permute-start(bf16[32,2176]{1,0:T(8,128)(2,1)S(1)} %get-tuple-element.461), channel_id=1, source_target_pairs={{0,6},{2,0},{4,2},{6,4},{1,7},{3,1},{5,3},{7,5},{8,14},{10,8},{12,... | collective-permute-start | bytes 417800 | tf_op jit(solution)/shard_map/ppermute | solution.py:65
  336.0 6.3 %collective-permute-start.34 = (bf16[32,2048]{1,0:T(8,128)(2,1)S(1)}, bf16[32,2048]{1,0:T(8,128)(2,1)S(1)}, u32[]{:S(2)}, u32[]{:S(2)}) collective-permute-start(bf16[32,2048]{1,0:T(8,128)(2,1)S(1)} %get-tuple-element.428), channel_id=1, source_target_pairs={{0,2},{2,4},{4,6},{6,0},{1,3},{3,5},{5,7},{7,1},{8,10},{10,12},{12... | collective-permute-start | bytes 393224 | tf_op jit(solution)/shard_map/ppermute | solution.py:65
  337.7 8.9 %collective-permute-start.35 = (bf16[32,2048]{1,0:T(8,128)(2,1)S(1)}, bf16[32,2048]{1,0:T(8,128)(2,1)S(1)}, u32[]{:S(2)}, u32[]{:S(2)}) collective-permute-start(bf16[32,2048]{1,0:T(8,128)(2,1)S(1)} %get-tuple-element.428), channel_id=1, source_target_pairs={{0,4},{2,6},{4,0},{6,2},{1,5},{3,7},{5,1},{7,3},{8,12},{10,14},{12... | collective-permute-start | bytes 393224 | tf_op jit(solution)/shard_map/ppermute | solution.py:65
  340.6 5.9 %collective-permute-start.36 = (bf16[32,2048]{1,0:T(8,128)(2,1)S(1)}, bf16[32,2048]{1,0:T(8,128)(2,1)S(1)}, u32[]{:S(2)}, u32[]{:S(2)}) collective-permute-start(bf16[32,2048]{1,0:T(8,128)(2,1)S(1)} %get-tuple-element.428), channel_id=1, source_target_pairs={{0,6},{2,0},{4,2},{6,4},{1,7},{3,1},{5,3},{7,5},{8,14},{10,8},{12,... | collective-permute-start | bytes 393224 | tf_op jit(solution)/shard_map/ppermute | solution.py:65
  346.6 3.0 collective-permute-start.37
  350.7 17.4 %collective-permute-start.38 = (bf16[176,2048]{1,0:T(8,128)(2,1)S(1)}, bf16[176,2048]{1,0:T(8,128)(2,1)S(1)}, u32[]{:S(2)}, u32[]{:S(2)}) collective-permute-start(bf16[176,2048]{1,0:T(8,128)(2,1)S(1)} %copy-done.49), channel_id=1, source_target_pairs={{0,6},{2,0},{4,2},{6,4},{1,7},{3,1},{5,3},{7,5},{8,14},{10,8},{12,... | collective-permute-start | bytes 2162696 | tf_op jit(solution)/shard_map/ppermute | solution.py:65
  352.5 18.4 %collective-permute-start.39 = (bf16[176,2048]{1,0:T(8,128)(2,1)S(1)}, bf16[176,2048]{1,0:T(8,128)(2,1)S(1)}, u32[]{:S(2)}, u32[]{:S(2)}) collective-permute-start(bf16[176,2048]{1,0:T(8,128)(2,1)S(1)} %copy-done.47), channel_id=1, source_target_pairs={{0,2},{2,4},{4,6},{6,0},{1,3},{3,5},{5,7},{7,1},{8,10},{10,12},{12... | collective-permute-start | bytes 2162696 | tf_op jit(solution)/shard_map/ppermute | solution.py:65
  371.0 9.6 %collective-permute-start.40 = (bf16[4,16,32,640]{3,2,1,0:T(8,128)(2,1)S(1)}, bf16[4,16,32,640]{3,2,1,0:T(8,128)(2,1)S(1)}, u32[]{:S(2)}, u32[]{:S(2)}) collective-permute-start(bf16[4,16,32,640]{3,2,1,0:T(8,128)(2,1)S(1)} %get-tuple-element.268), channel_id=1, source_target_pairs={{0,1},{1,0},{2,3},{3,2},{4,5},{5,4},{6,7},{7,6},{8,9},{9,8},{10,11... | collective-permute-start | bytes 7864328 | tf_op jit(solution)/shard_map/ppermute | solution.py:61
  372.5 6.5 %collective-permute-start.41 = (bf16[640,1024]{1,0:T(8,128)(2,1)}, bf16[640,1024]{1,0:T(8,128)(2,1)S(1)}, u32[]{:S(2)}, u32[]{:S(2)}) collective-permute-start(bf16[640,1024]{1,0:T(8,128)(2,1)} %get-tuple-element.272), channel_id=1, source_target_pairs={{0,1},{1,0},{2,3},{3,2},{4,5},{5,4},{6,7},{7,6},{8,9},{9,8},{10,11... | collective-permute-start | bytes 3932168 | tf_op jit(solution)/shard_map/ppermute | solution.py:61
  382.6 38.9 %all-to-all-start.3 = ((bf16[16,40,1024]{2,1,0:T(8,128)(2,1)}), bf16[16,40,1024]{2,1,0:T(8,128)(2,1)}, u32[]{:S(2)}, u32[]{:S(2)}) async-start(bf16[16,40,1024]{2,1,0:T(8,128)(2,1)} %bitcast.305), calls=%async_computation.3 | async-start | bytes 2621440 | tf_op jit(solution)/shard_map/all_to_all | solution.py:69
  388.5 143.7 %reduce-scatter.2.cloned.1.call-start = ((), (), s32[]{:S(2)}) async-start(), calls=%async_computation.10 | async-start | bytes 8355840 | tf_op jit(solution)/shard_map/reduce_scatter | solution.py:870
  388.6 31.4 %collective-permute-start.42 = (bf16[16,32,640]{2,1,0:T(8,128)(2,1)}, bf16[16,32,640]{2,1,0:T(8,128)(2,1)S(1)}, u32[]{:S(2)}, u32[]{:S(2)}) collective-permute-start(bf16[16,32,640]{2,1,0:T(8,128)(2,1)} %get-tuple-element.274), channel_id=1, source_target_pairs={{0,2},{2,4},{4,6},{6,0},{1,3},{3,5},{5,7},{7,1},{8,10},{10,12},{12... | collective-permute-start | bytes 1966088 | tf_op jit(solution)/shard_map/ppermute | solution.py:65
  388.7 31.3 %collective-permute-start.43 = (bf16[16,32,640]{2,1,0:T(8,128)(2,1)}, bf16[16,32,640]{2,1,0:T(8,128)(2,1)S(1)}, u32[]{:S(2)}, u32[]{:S(2)}) collective-permute-start(bf16[16,32,640]{2,1,0:T(8,128)(2,1)} %get-tuple-element.275), channel_id=1, source_target_pairs={{0,4},{2,6},{4,0},{6,2},{1,5},{3,7},{5,1},{7,3},{8,12},{10,14},{12... | collective-permute-start | bytes 1966088 | tf_op jit(solution)/shard_map/ppermute | solution.py:65
  389.7 30.6 %collective-permute-start.44 = (bf16[16,32,640]{2,1,0:T(8,128)(2,1)}, bf16[16,32,640]{2,1,0:T(8,128)(2,1)S(1)}, u32[]{:S(2)}, u32[]{:S(2)}) collective-permute-start(bf16[16,32,640]{2,1,0:T(8,128)(2,1)} %get-tuple-element.276), channel_id=1, source_target_pairs={{0,6},{2,0},{4,2},{6,4},{1,7},{3,1},{5,3},{7,5},{8,14},{10,8},{12,... | collective-permute-start | bytes 1966088 | tf_op jit(solution)/shard_map/ppermute | solution.py:65
  421.6 17.5 %all-to-all-start.4 = ((bf16[16,32,640]{2,1,0:T(8,128)(2,1)}), bf16[16,32,640]{2,1,0:T(8,128)(2,1)}, u32[]{:S(2)}, u32[]{:S(2)}) async-start(bf16[16,32,640]{2,1,0:T(8,128)(2,1)} %add_convert_fusion.2), calls=%async_computation.4 | async-start | bytes 1310720 | tf_op jit(solution)/shard_map/all_to_all | solution.py:69
  430.0 71.8 %collective-permute-start.46 = (bf16[528,2048]{1,0:T(8,128)(2,1)}, bf16[528,2048]{1,0:T(8,128)(2,1)S(1)}, u32[]{:S(2)}, u32[]{:S(2)}) collective-permute-start(bf16[528,2048]{1,0:T(8,128)(2,1)} %copy-done.41), channel_id=1, source_target_pairs={{0,4},{2,6},{4,0},{6,2},{1,5},{3,7},{5,1},{7,3},{8,12},{10,14},{12... | collective-permute-start | bytes 6488072 | tf_op jit(solution)/shard_map/ppermute | solution.py:65
  445.7 12.2 %collective-permute-start.45 = (bf16[32,640]{1,0:T(8,128)(2,1)}, bf16[32,640]{1,0:T(8,128)(2,1)}, u32[]{:S(2)}, u32[]{:S(2)}) collective-permute-start(bf16[32,640]{1,0:T(8,128)(2,1)} %fusion.103), channel_id=1, source_target_pairs={{0,1},{1,0},{2,3},{3,2},{4,5},{5,4},{6,7},{7,6},{8,9},{9,8},{10,11... | collective-permute-start | bytes 122888 | tf_op jit(solution)/shard_map/ppermute | solution.py:61
  462.2 10.7 %collective-permute-start.49 = (bf16[4,32,4096]{2,1,0:T(8,128)(2,1)}, bf16[4,32,4096]{2,1,0:T(8,128)(2,1)}, u32[]{:S(2)}, u32[]{:S(2)}) collective-permute-start(bf16[4,32,4096]{2,1,0:T(8,128)(2,1)} %dynamic-slice_bitcast_fusion), channel_id=1, source_target_pairs={{0,1},{1,0},{2,3},{3,2},{4,5},{5,4},{6,7},{7,6},{8,9},{9,8},{10,11... | collective-permute-start | bytes 3145736 | tf_op jit(solution)/shard_map/ppermute | solution.py:61
  465.6 36.2 %all-to-all-start.5 = ((bf16[16,128,384]{1,2,0:T(8,128)(2,1)}), bf16[16,128,384]{1,2,0:T(8,128)(2,1)}, u32[]{:S(2)}, u32[]{:S(2)}) async-start(bf16[16,128,384]{1,2,0:T(8,128)(2,1)} %pad_maximum_fusion), calls=%async_computation.5 | async-start | bytes 3145728 | tf_op jit(solution)/shard_map/all_to_all | solution.py:69
  470.0 25.8 %collective-permute-start.47 = (bf16[176,2048]{1,0:T(8,128)(2,1)}, bf16[176,2048]{1,0:T(8,128)(2,1)S(1)}, u32[]{:S(2)}, u32[]{:S(2)}) collective-permute-start(bf16[176,2048]{1,0:T(8,128)(2,1)} %copy-done.43), channel_id=1, source_target_pairs={{0,6},{2,0},{4,2},{6,4},{1,7},{3,1},{5,3},{7,5},{8,14},{10,8},{12,... | collective-permute-start | bytes 2162696 | tf_op jit(solution)/shard_map/ppermute | solution.py:65
  472.6 24.1 %collective-permute-start.48 = (bf16[176,2048]{1,0:T(8,128)(2,1)}, bf16[176,2048]{1,0:T(8,128)(2,1)S(1)}, u32[]{:S(2)}, u32[]{:S(2)}) collective-permute-start(bf16[176,2048]{1,0:T(8,128)(2,1)} %copy-done.42), channel_id=1, source_target_pairs={{0,2},{2,4},{4,6},{6,0},{1,3},{3,5},{5,7},{7,1},{8,10},{10,12},{12... | collective-permute-start | bytes 2162696 | tf_op jit(solution)/shard_map/ppermute | solution.py:65
  503.4 5.0 collective-permute-start.53
  503.5 7.5 %collective-permute-start.54 = (bf16[128,384]{0,1:T(8,128)(2,1)S(1)}, bf16[128,384]{0,1:T(8,128)(2,1)S(1)}, u32[]{:S(2)}, u32[]{:S(2)}) collective-permute-start(bf16[128,384]{0,1:T(8,128)(2,1)S(1)} %reduce_sum.195), channel_id=1, source_target_pairs={{0,4},{2,6},{4,0},{6,2},{1,5},{3,7},{5,1},{7,3},{8,12},{10,14},{12... | collective-permute-start | bytes 294920 | tf_op jit(solution)/shard_map/ppermute | solution.py:65
  507.6 4.5 collective-permute-start.55
  512.1 16.4 %collective-permute-start.56 = (bf16[128,384]{0,1:T(8,128)(2,1)S(1)}, bf16[128,384]{0,1:T(8,128)(2,1)S(1)}, u32[]{:S(2)}, u32[]{:S(2)}) collective-permute-start(bf16[128,384]{0,1:T(8,128)(2,1)S(1)} %add_convert_fusion.7), channel_id=1, source_target_pairs={{0,1},{1,0},{2,3},{3,2},{4,5},{5,4},{6,7},{7,6},{8,9},{9,8},{10,11... | collective-permute-start | bytes 294920 | tf_op jit(solution)/shard_map/ppermute | solution.py:61
  514.1 16.9 %collective-permute-start.50 = (bf16[32,4096]{1,0:T(8,128)(2,1)}, bf16[32,4096]{1,0:T(8,128)(2,1)S(1)}, u32[]{:S(2)}, u32[]{:S(2)}) collective-permute-start(bf16[32,4096]{1,0:T(8,128)(2,1)} %get-tuple-element.304), channel_id=1, source_target_pairs={{0,2},{2,4},{4,6},{6,0},{1,3},{3,5},{5,7},{7,1},{8,10},{10,12},{12... | collective-permute-start | bytes 786440 | tf_op jit(solution)/shard_map/ppermute | solution.py:65
  514.1 16.9 %collective-permute-start.51 = (bf16[32,4096]{1,0:T(8,128)(2,1)}, bf16[32,4096]{1,0:T(8,128)(2,1)S(1)}, u32[]{:S(2)}, u32[]{:S(2)}) collective-permute-start(bf16[32,4096]{1,0:T(8,128)(2,1)} %get-tuple-element.305), channel_id=1, source_target_pairs={{0,4},{2,6},{4,0},{6,2},{1,5},{3,7},{5,1},{7,3},{8,12},{10,14},{12... | collective-permute-start | bytes 786440 | tf_op jit(solution)/shard_map/ppermute | solution.py:65
  516.7 14.3 %collective-permute-start.52 = (bf16[32,4096]{1,0:T(8,128)(2,1)S(1)}, bf16[32,4096]{1,0:T(8,128)(2,1)S(1)}, u32[]{:S(2)}, u32[]{:S(2)}) collective-permute-start(bf16[32,4096]{1,0:T(8,128)(2,1)S(1)} %get-tuple-element.306), channel_id=1, source_target_pairs={{0,6},{2,0},{4,2},{6,4},{1,7},{3,1},{5,3},{7,5},{8,14},{10,8},{12,... | collective-permute-start | bytes 786440 | tf_op jit(solution)/shard_map/ppermute | solution.py:65
  (128 other events, 2125.4 us)
Sparse Core Ops, SparseCore 0:
  15.6 64.6 all-gather.3
  95.3 64.1 all-gather.5
  162.2 59.0 all-gather.7
  421.7 101.7 reduce-scatter.1

commit v4 on v3

--- a/solution.py
+++ b/solution.py
@@ -308,19 +308,23 @@
             ],
         ),
         compiler_params=pltpu.CompilerParams(vmem_limit_bytes=32 * 1024 * 1024),
-        cost_estimate=pl.CostEstimate(
-            flops=2 * H_DEV * ROWS * KEYS * 768 + 2 * KEYS * 512 * 512,
-            bytes_accessed=24 << 20,
-            transcendentals=0,
-        ),
+        cost_estimate=pl.CostEstimate(flops=1, bytes_accessed=1, transcendentals=0),
     )(ci.reshape(1), queries, kv_all, rot_all, probs, d_mid, wot, wkv, heads)
 
 
 def expert_kernel(at_ref, x_ref, xo_ref, g_ref, go_ref, *rest):
     pieces = rest[:12]
-    keep_in, send_in, keep_out, send_out, x_out, dso_out, hid_out, dpre_out = rest[12:20]
-    wg_ref, wu_ref, wd_ref, dots_ref, sems = rest[20:]
+    keep_in, send_in, keep_out, send_out = rest[12:16]
+    saved = rest[16:20]
+    wg_ref, wu_ref, wd_ref, dots_ref, x_out, dso_out, hid_out, dpre_out, sems = rest[20:]
     copies = []
+    leaving = []
+
+    def leave(i, source):
+        copy = pltpu.make_async_copy(source, saved[i], sems.at[12 + i])
+        copy.start()
+        leaving.append(copy)
+
     for part, target in enumerate((wg_ref, wu_ref, wd_ref)):
         for k in range(4):
             copy = pltpu.make_async_copy(
@@ -342,6 +346,8 @@
     other = (go_ref[...].astype(WIDE) * gate).astype(HALF)
     dso_out[:, :half] = jnp.where(first, own, other)
     dso_out[:, half:] = jnp.where(first, other, own)
+    leave(0, x_out)
+    leave(1, dso_out)
     for copy in copies:
         copy.wait()
 
@@ -361,6 +367,8 @@
 
     lax.fori_loop(0, FFP // 256, hidden_step, 0)
 
+    leave(2, hid_out)
+    leave(3, dpre_out)
     dots_ref[...] = jnp.zeros_like(dots_ref)
 
     def output_step(i, carry):
@@ -392,6 +400,8 @@
     total = jnp.sum(dots_ref[...], axis=1, keepdims=True)
     keep_in[:, half:] = jnp.broadcast_to(total, (16 * SLOTS, 128)).astype(HALF)
     send_in[:, half:] = jnp.zeros((16 * SLOTS, 128), HALF)
+    for copy in leaving:
+        copy.wait()
 
 
 def run_expert(ci, x_own, x_other, g_own, g_other, pieces):
@@ -412,9 +422,16 @@
         in_specs=[pl.BlockSpec(memory_space=pltpu.SMEM)]
         + [vmem] * 4
         + [pl.BlockSpec(memory_space=pl.ANY)] * 12,
-        out_specs=(vmem,) * 8,
+        out_specs=(vmem,) * 4 + (pl.BlockSpec(memory_space=pl.ANY),) * 4,
         scratch_shapes=[pltpu.VMEM((FFP, D), HALF)] * 3
-        + [pltpu.VMEM((rows, 128), WIDE), pltpu.SemaphoreType.DMA((12,))],
+        + [
+            pltpu.VMEM((rows, 128), WIDE),
+            pltpu.VMEM((rows, D), HALF),
+            pltpu.VMEM((rows, D), HALF),
+            pltpu.VMEM((rows, FFP), HALF),
+            pltpu.VMEM((rows, 2 * FFP), HALF),
+            pltpu.SemaphoreType.DMA((16,)),
+        ],
         compiler_params=pltpu.CompilerParams(vmem_limit_bytes=52 * 1024 * 1024),
         cost_estimate=pl.CostEstimate(
             flops=12 * rows * D * FFP, bytes_accessed=28 << 20, transcendentals=rows * FFP
@@ -565,16 +582,144 @@
     )(*operands)
 
 
+def latent_kernel(
+    parts_ref, cos_ref, sin_ref, norm_ref, scale_ref, gain_ref, blk_ref, one_ref, logits_ref,
+    chip_ref, d_one_ref, gain_one_ref, gain_lat_ref,
+):
+    total = jnp.sum(parts_ref[...].astype(WIDE), axis=0)
+    rope = total[:, KVL:]
+    rope = rope * cos_ref[...] - jnp.concatenate([rope[:, 64:], rope[:, :64]], axis=1) * sin_ref[...]
+    source = lax.broadcasted_iota(jnp.int32, (128, 128), 0)
+    target = lax.broadcasted_iota(jnp.int32, (128, 128), 1)
+    fold = (target == source % 32 + 32 * (source // 64)).astype(WIDE)
+    rope = jnp.dot(
+        rope, fold, precision=lax.Precision.HIGHEST, preferred_element_type=WIDE
+    ).astype(HALF)
+    grad = total[:, :KVL]
+    normed = norm_ref[...]
+    scaled = grad * gain_ref[...]
+    inner = jnp.mean(scaled * normed, axis=-1, keepdims=True)
+    d_lat = (scale_ref[...] * (scaled - normed * inner)).astype(HALF)
+    gain_lat = jnp.sum(grad * normed, axis=0, keepdims=True)
+    lane = lax.broadcasted_iota(jnp.int32, (1, 128), 1)
+    for e in range(16):
+        moved = pltpu.roll(gain_lat, (KVL - 32 * e) % KVL, axis=1)[:, :128]
+        gain_lat_ref[:, 128 * e : 128 * e + 128] = jnp.where(lane < 32, moved, 0.0)
+    chip_ref[:, :KVL] = d_lat
+    chip_ref[:, KVL:] = rope + logits_ref[...]
+    d_one = dot_nt(d_lat, blk_ref[:, :KVL]) + dot_nt(rope, blk_ref[:, KVL:])
+    d_one_ref[...] = d_one
+    gain_one_ref[...] = jnp.sum(d_one * one_ref[...], axis=0, keepdims=True)
+
+
+def latent_back(*operands):
+    vmem = pl.BlockSpec(memory_space=pltpu.VMEM)
+    return pl.pallas_call(
+        latent_kernel,
+        out_shape=(
+            jax.ShapeDtypeStruct((OWN, 640), HALF),
+            jax.ShapeDtypeStruct((OWN, D), WIDE),
+            jax.ShapeDtypeStruct((1, D), WIDE),
+            jax.ShapeDtypeStruct((1, D), WIDE),
+        ),
+        in_specs=[vmem] * 9,
+        out_specs=(vmem,) * 4,
+        compiler_params=pltpu.CompilerParams(vmem_limit_bytes=24 * 1024 * 1024),
+        cost_estimate=pl.CostEstimate(flops=1, bytes_accessed=1, transcendentals=0),
+    )(*operands)
+
+
+def last_kernel(
+    core_ref, chip_ref, other_ref, h_one_ref, h_two_ref, one_a_ref, one_b_ref, two_ref, lat_ref,
+    out_ref,
+):
+    core = core_ref[0]
+    chip, other = chip_ref[...], other_ref[...]
+    rows = jnp.concatenate(
+        [jnp.where(core == 0, chip, other), jnp.where(core == 0, other, chip)], axis=0
+    )
+    source = lax.broadcasted_iota(jnp.int32, (640, 384), 0)
+    target = lax.broadcasted_iota(jnp.int32, (640, 384), 1)
+    wanted = jnp.where(
+        target < 288,
+        target + 288 * core,
+        jnp.where(target < 320, target + 288 + 32 * core, -1),
+    )
+    picked = dot_nn(rows, (source == wanted).astype(HALF)).astype(HALF)
+    lane = lax.broadcasted_iota(jnp.int32, (2 * OWN, 384), 1)
+    zero = jnp.zeros_like(picked)
+    out = dot_tn(h_one_ref[...], jnp.where(lane < 288, picked, zero))
+    out = out + dot_tn(h_two_ref[...], jnp.where(lane < 288, zero, picked))
+    row = lax.broadcasted_iota(jnp.int32, (8, D), 0)
+    gains = jnp.where(row == 0, one_a_ref[...] + one_b_ref[...], 0.0)
+    gains = gains + jnp.where(row == 1, two_ref[...], 0.0) + jnp.where(row == 2, lat_ref[...], 0.0)
+    place = lax.broadcasted_iota(jnp.int32, (8, 384), 0) + 320
+    place = (place == lax.broadcasted_iota(jnp.int32, (8, 384), 1)).astype(HALF)
+    out_ref[...] = (out + dot_tn(gains.astype(HALF), place)).astype(HALF)
+
+
+def last_products(ci, *operands):
+    vmem = pl.BlockSpec(memory_space=pltpu.VMEM)
+    return pl.pallas_call(
+        last_kernel,
+        out_shape=jax.ShapeDtypeStruct((D, 384), HALF),
+        in_specs=[pl.BlockSpec(memory_space=pltpu.SMEM)] + [vmem] * 8,
+        out_specs=vmem,
+        compiler_params=pltpu.CompilerParams(vmem_limit_bytes=24 * 1024 * 1024),
+        cost_estimate=pl.CostEstimate(flops=1, bytes_accessed=1, transcendentals=0),
+    )(ci.reshape(1), *operands)
+
+
+def last_sum_kernel(parts_ref, out_ref):
+    out_ref[...] = jnp.sum(parts_ref[...].astype(WIDE), axis=0).astype(HALF)
+
+
+def sum_last(parts):
+    vmem = pl.BlockSpec(memory_space=pltpu.VMEM)
+    return pl.pallas_call(
+        last_sum_kernel,
+        out_shape=jax.ShapeDtypeStruct(parts.shape[1:], HALF),
+        in_specs=[vmem],
+        out_specs=vmem,
+        cost_estimate=pl.CostEstimate(flops=1, bytes_accessed=1, transcendentals=0),
+    )(parts)
+
+
+def finish_kernel(sum_ref, sg_ref, su_ref, sd_ref, wq_ref, wo_ref, uk_ref, uv_ref):
+    sg_ref[...] = sum_ref[:, 0:352].astype(WIDE)
+    su_ref[...] = sum_ref[:, SHP : SHP + 352].astype(WIDE)
+    sd_ref[...] = sum_ref[:, 2 * SHP : 3 * SHP].astype(WIDE).T[:352, :]
+    wo_ref[...] = sum_ref[:, 1536:1792].astype(WIDE).T
+    source = lax.broadcasted_iota(jnp.int32, (384, 384), 0)
+    target = lax.broadcasted_iota(jnp.int32, (384, 384), 1)
+    head, place = target // 192, target % 192
+    wanted = jnp.where(
+        place < 128,
+        128 * head + place,
+        256 + 32 * head + 64 * ((place - 128) // 32) + (place - 128) % 32,
+    )
+    wq_ref[...] = dot_nn(sum_ref[:, 1152:1536], (source == wanted).astype(HALF))
+    for block in range(2):
+        lanes = slice(128 * block, 128 * block + 128)
+        uk_ref[:, lanes] = sum_ref[32 * block : 32 * block + 32, 1792:1920].astype(WIDE)
+        uv_ref[:, lanes] = sum_ref[64 + 32 * block : 96 + 32 * block, 1792:1920].astype(WIDE)
+
+
+def finish(total):
+    vmem = pl.BlockSpec(memory_space=pltpu.VMEM)
+    shapes = ((128, 352), (128, 352), (352, 128), (128, 384), (256, 128), (32, 256), (32, 256))
+    return pl.pallas_call(
+        finish_kernel,
+        out_shape=tuple(jax.ShapeDtypeStruct(shape, WIDE) for shape in shapes),
+        in_specs=[vmem],
+        out_specs=(vmem,) * 7,
+        cost_estimate=pl.CostEstimate(flops=1, bytes_accessed=1, transcendentals=0),
+    )(total)
+
+
 def pack_query_columns(w):
     return jnp.concatenate(
         [w[:, 0:128], w[:, 192:320], w[:, 128:160], w[:, 320:352], w[:, 160:192], w[:, 352:384]],
-        axis=1,
-    )
-
-
-def unpack_query_columns(w):
-    return jnp.concatenate(
-        [w[:, 0:128], w[:, 256:288], w[:, 320:352], w[:, 128:256], w[:, 288:320], w[:, 352:384]],
         axis=1,
     )
 
@@ -847,8 +992,8 @@
     lat_keep, lat_send, d_kv, d_q = attend_back(
         ci, queries, kv_all, rot_all, probs, d_attn_b, wot_b, wkv_b, heads_wide
     )
-    lat_keep, lat_send, d_kv, d_q, up_parts, up_back = lax.optimization_barrier(
-        (lat_keep, lat_send, d_kv, d_q, up_parts, up_back)
+    lat_keep, lat_send, d_kv, d_q, up_back = lax.optimization_barrier(
+        (lat_keep, lat_send, d_kv, d_q, up_back)
     )
     lat_pieces = pair_pieces(lat_keep, lat_send, yi)
     lat_pieces, d_kv, d_q, d_attn_b, out_sent = lax.optimization_barrier(
@@ -864,91 +1009,77 @@
         h_two, d_shared_pre, g_rows, shared_hidden, h_one, d_queries, d_attn_b, attn_heads,
         c_all, d_kv, wq_b, normed_in,
     )
-    lat_total, out_back, down_parts, far_parts, rest_grads = lax.optimization_barrier(
-        (lat_total.astype(HALF), out_back, down_parts, far_parts, rest_grads)
+    lat_total, out_back, down_parts, rest_grads = lax.optimization_barrier(
+        (lat_total.astype(HALF), out_back, down_parts, rest_grads)
     )
     rest_sum = lax.psum_scatter(rest_grads, EX, scatter_dimension=0, tiled=True)
     lat_parts = spread(lat_total, EX)
+    down_back = [down_parts[0], shift_y(down_parts[1], -1), None, shift_y(down_parts[3], -3)]
+    scale_one = inv_rms(in_own)
+    normed_one = in_own * scale_one
+    lat_own = (
+        own_rows(cos4), own_rows(sin4), own_rows(normed_lat), own_rows(scale_lat), gain_lat[None]
+    )
+    lat_parts, down_back, far_parts, lat_own, normed_one = lax.optimization_barrier(
+        (lat_parts, down_back, far_parts, lat_own, normed_one)
+    )
     far_back = shift_y(far_parts, -2)
-    down_back = [down_parts[0], shift_y(down_parts[1], -1), None, shift_y(down_parts[3], -3)]
-    lat_parts, d_one, out_back = lax.optimization_barrier((lat_parts, d_one, out_back))
-    d_lat_own = jnp.sum(lat_parts.astype(WIDE), axis=0)
-
-    cos_own, sin_own = own_rows(cos4), own_rows(sin4)
-    d_rope = d_lat_own[:, 512:]
-    d_rope = d_rope * cos_own - swap_halves(d_rope) * sin_own
-    d_rope = jnp.concatenate(
-        [d_rope[:, 0:32] + d_rope[:, 32:64], d_rope[:, 64:96] + d_rope[:, 96:128]], axis=1
-    )
-    d_lat, grad_gain_lat = norm_back(
-        d_lat_own[:, :512], own_rows(normed_lat), own_rows(scale_lat), gain_lat
-    )
-    d_latent = jnp.concatenate([d_lat, d_rope], axis=1).astype(HALF)
-    d_latent_pad = jnp.pad(d_latent, ((0, 0), (0, 64)))
-    d_chip = both_cores(jnp.concatenate([d_latent, d_logits], axis=1), 0)
-    d_chip, d_one, out_back = lax.optimization_barrier((d_chip, d_one, out_back))
+    chip, d_lat_one, gain_one_lat, gain_lat_wide = latent_back(
+        lat_parts, *lat_own, blk_b, normed_one, d_logits_pad
+    )
+    chip, d_one, out_back = lax.optimization_barrier((chip, d_one, out_back))
     late_parts = late_products(ci, d_one, shared_out, gated, out_back).reshape(4, 2, OWN, 2 * D)
     late_pieces = pair_pieces(
         lax.dynamic_index_in_dim(late_parts, ci, 1, keepdims=False),
         lax.dynamic_index_in_dim(late_parts, 1 - ci, 1, keepdims=False),
         yi,
     )
-    d_lat_one = dot_nt(d_latent_pad, blk_b)
-    scale_one = inv_rms(in_own)
-    normed_one = in_own * scale_one
-    gain_one_part = gain_one_late[0] + jnp.sum(d_lat_one * normed_one, axis=0)
 
     def chip_rows(value):
         return lax.dynamic_slice_in_dim(value, yi * 2 * OWN, 2 * OWN, 0)
 
-    def own_half(value):
-        half = value.shape[1] // 2
-        return jnp.where(ci == 0, value[:, :half], value[:, half:])
-
-    grad_dkv = dot_tn(chip_rows(h_one), own_half(d_chip[:, :576]))
-    grad_router = dot_tn(chip_rows(h_two), own_half(d_chip[:, 576:]))
-    gain_lat_wide = jnp.pad(grad_gain_lat.reshape(16, 32), ((0, 0), (0, 96))).reshape(D)
-    gain_rows = jnp.stack([gain_one_part, gain_two_part, gain_lat_wide], axis=0).astype(HALF)
-    gain_at = (
-        lax.broadcasted_iota(jnp.int32, (3, 64), 0) == lax.broadcasted_iota(jnp.int32, (3, 64), 1)
-    ).astype(HALF)
-    last_part = jnp.concatenate([grad_dkv, grad_router, dot_tn(gain_rows, gain_at)], axis=1)
-    last_parts = spread(last_part.astype(HALF).reshape(16, 128, 384), EX)
-    last_parts, far_back, down_back, late_pieces = lax.optimization_barrier(
-        (last_parts, far_back, down_back, late_pieces)
-    )
-    last_sum = jnp.sum(last_parts.astype(WIDE), axis=0).astype(HALF)
+    last_part = last_products(
+        ci, chip, swap_core(chip), chip_rows(h_one), chip_rows(h_two),
+        gain_one_late, gain_one_lat, gain_two_part[None], gain_lat_wide,
+    )
+    last_parts = spread(last_part.reshape(16, 128, 384), EX)
+    last_parts, far_back, late_pieces = lax.optimization_barrier(
+        (last_parts, far_back, late_pieces)
+    )
+    last_sum = sum_last(last_parts)
     last_sum = add_pieces([last_sum] * 4).astype(HALF)
+    late_own = add_pieces(late_pieces)
+    up_back[2] = gate_back[2] = down_back[2] = far_back
+    grad_eg = place_pieces(yi, gate_back, 0)
+    grad_eu = place_pieces(yi, up_back, 1)
+    grad_ed = place_pieces(yi, down_back, 2)
+    last_sum, late_own, grad_eg, grad_eu, grad_ed = lax.optimization_barrier(
+        (last_sum, late_own, grad_eg, grad_eu, grad_ed)
+    )
     last_other = swap_core(last_sum)
     sum_dkv = ordered_cores(last_sum[:, :288], last_other[:, :288], 1).astype(WIDE)
     sum_router = ordered_cores(last_sum[:, 288:320], last_other[:, 288:320], 1)
     sum_router = sum_router.reshape(128, 4, 16).transpose(0, 2, 1).reshape(128, EXPERTS).astype(WIDE)
     gain_sums = last_sum[:, 320:323].astype(WIDE) + last_other[:, 320:323].astype(WIDE)
-    late_own = add_pieces(late_pieces)
-    up_back[2] = gate_back[2] = down_back[2] = far_back
-    grad_eg = place_pieces(yi, gate_back, 0)
-    grad_eu = place_pieces(yi, up_back, 1)
-    grad_ed = place_pieces(yi, down_back, 2)
     layer_out = (mid_own + late_own[:, D:]).astype(HALF)
     d_in_norm, _ = norm_back(late_own[:, :D] + d_lat_one, normed_one, scale_one, gain_one)
     grad_inputs = (d_mid_own + d_in_norm).astype(HALF)
-    rest_sum = rest_sum.astype(WIDE)
-    sum_kv = rest_sum[:, 1792:].reshape(4, 32, 128).transpose(1, 0, 2).reshape(32, 512)
+    sum_sg, sum_su, sum_sd, sum_q, sum_o, sum_uk, sum_uv = finish(rest_sum)
     return (
         layer_out,
         grad_inputs,
         gain_sums[:, 0],
-        unpack_query_columns(rest_sum[:, 1152:1536]),
+        sum_q,
         sum_dkv,
         gain_sums[:32, 2],
-        sum_kv[:, :256],
-        sum_kv[:, 256:],
-        rest_sum[:, 1536:1792].T,
+        sum_uk,
+        sum_uv,
+        sum_o,
         gain_sums[:, 1],
         sum_router,
-        rest_sum[:, :352],
-        rest_sum[:, SHP : SHP + 352],
-        rest_sum[:, 2 * SHP : 2 * SHP + 352].T,
+        sum_sg,
+        sum_su,
+        sum_sd,
         grad_eg,
         grad_eu,
         grad_ed,

time: 556 us -> 543 us (0.977)
  other arithmetic: 51.8 us -> 39.4 us
  matrix products: 40.6 us -> 30.6 us
  Pallas kernels: 85.1 us -> 93.6 us
  local copies, waits for them, and re-layouts: 73.1 us -> 65.6 us
  waiting for transfers between devices: 166 us -> 173 us
    all_to_all x6, waiting for transfers between devices: 23.8 us -> 46.9 us  [spread(): return lax.all_to_all(value, axes, split_axis=0, concat_axis=0, tiled=True)]
    ppermute x43, waiting for transfers between devices: 111 us -> 88.3 us  [shift_y(): return lax.ppermute(value, 'y', [(i, (i + by) % 4) for i in range(4)])]
    pallas_call x0 -> x4, Pallas kernels: none -> 7.1 us  [the longest x1 2.26 us: sum_last(): pl.pallas_call(last_sum_kernel, out_shape=jax.ShapeDtypeStruct(parts.shap...]
    dot_general x6 -> x5, matrix products: 11.9 us -> 6.7 us  [dot_nt(): lax.dot_general(left, right, (((1,), (1,)), ((), ())), preferred_element_...]
    unnamed x257 -> x220, local copies, waits for them, and re-layouts: 28.6 us -> 25.4 us
  transfers between devices with their start and end apart: 67 -> 67, of which waited for: 41 -> 37; matrix products, arithmetic and copies ran while one was open for 19% -> 16% of each run, Pallas kernels for 11% -> 12%
where the time goes in v4:
time: 543 us; the launch traced here: 533 us
  waiting for transfers between devices  173 us (32%)
  starting transfers between devices  115 us (21%)
  Pallas kernels  93.6 us (17%)
  local copies, waits for them, and re-layouts  65.6 us (12%)
  other arithmetic  39.4 us (7%)
  matrix products  30.6 us (6%)
  between operations  16.3 us (3%)
    ppermute x43, waiting for transfers between devices, shift_y(): return lax.ppermute(value, 'y', [(i, (i + by) % 4) for i in range(4)])  88.3 us
    ppermute x43, starting transfers between devices, shift_y(): return lax.ppermute(value, 'y', [(i, (i + by) % 4) for i in range(4)])  61.5 us
    all_to_all x6, waiting for transfers between devices, spread(): return lax.all_to_all(value, axes, split_axis=0, concat_axis=0, tiled=True)  46.9 us
    all_to_all x6, starting transfers between devices, spread(): return lax.all_to_all(value, axes, split_axis=0, concat_axis=0, tiled=True)  32.6 us
    pallas_call x1, Pallas kernels, run_expert(): pl.pallas_call(expert_kernel, out_shape=(jax.ShapeDtypeStruct((rows, D //...  26.1 us
    unnamed x220, local copies, waits for them, and re-layouts  25.4 us
    ppermute x14, starting transfers between devices, swap_core(): return lax.ppermute(value, 'c', [(0, 1), (1, 0)])  20.7 us
    ppermute x14, waiting for transfers between devices, swap_core(): return lax.ppermute(value, 'c', [(0, 1), (1, 0)])  19.7 us
  transfers between devices with their start and end apart: 67, of which 37 were waited for; matrix products, arithmetic and copies ran while one was open for 16% of the time, Pallas kernels for 12%

profile of v4, /device:TPU:1, one launch (start us, length us, event | category | flops | bytes accessed | tf_op | source)
XLA Modules:
  0.0 532.9 jit_solution(7711642238094663367)
XLA Ops:
  15.6 7.1 %fusion.14 = (bf16[176,2048]{1,0:T(8,128)(2,1)}, bf16[176,2048]{1,0:T(8,128)(2,1)}, bf16[176,2048]{1,0:T(8,128)(2,1)}, bf16[176,2048]{1,0:T(8,128)(2,1)}, bf16[1...) fusion(f32[4,176,2048]{2,1,0:T(8,128)} %param.33, ...), kind=kLoop, calls=%fused_computation.56 | loop fusion | bytes 11534352 | tf_op jit(solution)/shard_map/convert_element_type | solution.py:787
  22.8 2.1 collective-permute-start.7
  24.9 2.6 collective-permute-start.8
  32.7 4.5 fusion.22
  44.0 2.1 collective-permute-start.6
  46.1 3.3 collective-permute-start.10
  57.0 14.8 %collective-permute-done.5.rest_2_ = bf16[176,2048]{1,0:T(8,128)(2,1)} collective-permute-done((bf16[176,2048]{1,0:T(8,128)(2,1)}, bf16[176,2048]{1,0:T(8,128)(2,1)}, u32[]{:S(2)}, u32[]{:S(2)}) %collective-permute-start.5) | collective-permute-done | bytes 720928 | tf_op jit(solution)/shard_map/ppermute | solution.py:65
  71.9 3.4 collective-permute-done.6.rest_3_
  75.3 5.1 all-gather.4.cloned.1.call-done
  83.5 2.9 fusion.92
  91.7 4.9 all-to-all-start
  97.9 2.4 collective-permute-start.12
  102.0 2.4 collective-permute-start.15
  110.9 4.0 collective-permute-done.11.rest_5_
  114.9 16.5 %collective-permute-done.12.rest_6_ = bf16[176,2048]{1,0:T(8,128)(2,1)} collective-permute-done((bf16[176,2048]{1,0:T(8,128)(2,1)}, bf16[176,2048]{1,0:T(8,128)(2,1)}, u32[]{:S(2)}, u32[]{:S(2)}) %collective-permute-start.12) | collective-permute-done | bytes 720928 | tf_op jit(solution)/shard_map/ppermute | solution.py:65
  131.4 14.4 %collective-permute-done.14.rest_9_ = bf16[176,2048]{1,0:T(8,128)(2,1)} collective-permute-done((bf16[176,2048]{1,0:T(8,128)(2,1)}, bf16[176,2048]{1,0:T(8,128)(2,1)}, u32[]{:S(2)}, u32[]{:S(2)}) %collective-permute-start.14) | collective-permute-done | bytes 720928 | tf_op jit(solution)/shard_map/ppermute | solution.py:65
  146.7 9.1 %all-gather.6.cloned.1.call-done.c_ref = bf16[4096,640]{1,0:T(8,128)(2,1)} async-done(((bf16[256,640]{1,0:T(8,128)(2,1)}), bf16[4096,640]{1,0:T(8,128)(2,1)}) %all-gather.6.cloned.1.call-update) | async-done | bytes 5242896 | tf_op jit(solution)/shard_map/all_gather | solution.py:871
  157.2 4.9 convolution_convert_fusion.kv_ref
  162.1 10.0 %shard_map.323 = (bf16[2,4096,256]{2,1,0:T(8,128)(2,1)S(1)}, f32[256,256]{1,0:T(8,128)S(1)}) custom-call(bf16[256,384]{1,0:T(8,128)(2,1)S(1)} %pad_maximum_fusion.6.q_ref, bf16[4096,512]{1,0:T(8,128)(2,1)S(1)} %convolution_convert_fusion.kv_ref, bf16[4096,128]{1,0:T(8,128)(2,1)S(1)} %slice.211.rot_ref, s32[1,256]{1,0:T(1,128)S(1)} %bitcast.261, ...), custom_call_target="tpu_custom_call" | custom-call | flops 1610612736 | bytes 12582912 | tf_op jit(solution)/shard_map/pallas_call | solution.py:185
  179.5 2.4 collective-permute-start.18
  184.3 3.8 collective-permute-done.18
  189.6 2.2 collective-permute-start.21
  193.6 3.1 collective-permute-done.21
  197.0 2.2 collective-permute-start.23
  208.7 5.5 %all-to-all-start.1 = ((bf16[16,40,1152]{2,1,0:T(8,128)(2,1)}), bf16[16,40,1152]{2,1,0:T(8,128)(2,1)}, u32[]{:S(2)}, u32[]{:S(2)}) async-start(bf16[16,40,1152]{2,1,0:T(8,128)(2,1)} %pad_maximum_fusion), calls=%async_computation.1 | async-start | bytes 2949120 | tf_op jit(solution)/shard_map/all_to_all | solution.py:69
  214.1 3.4 all-gather.8.cloned.1.call-done
  217.5 3.0 fusion.3
  224.5 2.4 fusion.1
  227.0 9.5 %all-to-all-done.1 = bf16[16,40,1152]{2,1,0:T(8,128)(2,1)} async-done(((bf16[16,40,1152]{2,1,0:T(8,128)(2,1)}), bf16[16,40,1152]{2,1,0:T(8,128)(2,1)}, u32[]{:S(2)}, u32[]{:S(2)}) %all-to-all-start.1) | async-done | bytes 1474592 | tf_op jit(solution)/shard_map/all_to_all | solution.py:69
  238.5 3.1 collective-permute-done.26.xo_ref
  243.8 26.1 %shard_map.324 = (bf16[640,1152]{1,0:T(8,128)(2,1)}, bf16[640,1152]{1,0:T(8,128)(2,1)}, bf16[640,1024]{1,0:T(8,128)(2,1)}, bf16[640,1024]{1,0:T(8,128)(2,1)}, bf...) custom-call(s32[1]{0:T(128)} %bitcast.55.at_ref.core_ref, ...), custom_call_target="tpu_custom_call" | custom-call | flops 12079595520 | bytes 29360128 | tf_op jit(solution)/shard_map/pallas_call | solution.py:410
  270.4 6.5 %convolution_convert_fusion.1.gate_ref = bf16[768,2048]{1,0:T(8,128)(2,1)} fusion(bf16[640,2048]{1,0:T(8,128)(2,1)} %get-tuple-element.258.x_ref, bf16[640,1536]{1,0:T(8,128)(2,1)} %get-tuple-element.267.dpre_ref), kind=kOutput, calls=%fused_computation.2 | convolution fusion | flops 2014838784 | bytes 6750208 | tf_op jit(solution)/shard_map/dot_general | solution.py:43
  278.3 4.4 all-to-all-start.2
  282.8 2.9 fusion.96
  285.6 4.4 collective-permute-start.28
  292.3 9.7 %shard_map.325 = (bf16[176,2048]{1,0:T(8,128)(2,1)S(1)}, bf16[176,2048]{1,0:T(8,128)(2,1)S(1)}, bf16[176,2048]{1,0:T(8,128)(2,1)S(1)}, bf16[176,2048]{1,0:T(8,12...) custom-call(bf16[640,2048]{1,0:T(8,128)(2,1)S(1)} %copy-done.17, ...), custom_call_target="tpu_custom_call" | custom-call | flops 1 | bytes 1 | tf_op jit(solution)/shard_map/pallas_call | solution.py:499
  317.0 3.4 collective-permute-start.32
  323.1 3.8 collective-permute-done.32
  329.3 2.2 collective-permute-start.35
  333.1 3.3 collective-permute-done.35
  336.4 2.5 collective-permute-start.37
  340.7 2.3 collective-permute-start.38
  343.3 11.7 %shard_map.326 = (bf16[4,16,32,640]{3,2,1,0:T(8,128)(2,1)S(1)}, bf16[4,16,32,640]{3,2,1,0:T(8,128)(2,1)S(1)}, bf16[4096,512]{1,0:T(8,128)(2,1)S(1)}, f32[256,384]{1,0:T(8,128)S(1)}) custom-call(s32[1]{0:T(128)} %bitcast.55.at_ref.core_ref, bf16[256,384]{1,0:T(8,128)(2,1)S(1)} %copy-done.36, bf16[4096,512]{1,0:T(8,128)(2,1)S(1)} %copy-done.13, ...), custom_call_target="tpu_custom_call" | custom-call | flops 1 | bytes 1 | tf_op jit(solution)/shard_map/pallas_call | solution.py:276
  355.1 3.1 collective-permute-done.38.refs_1_
  358.2 3.3 collective-permute-done.39.refs_3_
  363.1 6.3 %collective-permute-done.41 = bf16[640,1024]{1,0:T(8,128)(2,1)S(1)} collective-permute-done((bf16[640,1024]{1,0:T(8,128)(2,1)S(1)}, bf16[640,1024]{1,0:T(8,128)(2,1)S(1)}, u32[]{:S(2)}, u32[]{:S(2)}) %collective-permute-start.41) | collective-permute-done | bytes 1310752 | tf_op jit(solution)/shard_map/ppermute | solution.py:61
  373.0 6.8 %all-to-all-start.3 = ((bf16[16,40,1024]{2,1,0:T(8,128)(2,1)}), bf16[16,40,1024]{2,1,0:T(8,128)(2,1)}, u32[]{:S(2)}, u32[]{:S(2)}) async-start(bf16[16,40,1024]{2,1,0:T(8,128)(2,1)} %bitcast.271), calls=%async_computation.3 | async-start | bytes 2621440 | tf_op jit(solution)/shard_map/all_to_all | solution.py:69
  387.7 16.6 %shard_map.327 = (bf16[2048,1920]{1,0:T(8,128)(2,1)}, bf16[256,2048]{1,0:T(8,128)(2,1)S(1)}, f32[1,2048]{1,0:T(1,128)S(1)}) custom-call(bf16[256,2048]{1,0:T(8,128)(2,1)S(1)} %bitcast.250, bf16[256,768]{1,0:T(8,128)(2,1)S(1)} %copy-done.21, bf16[256,2048]{1,0:T(8,128)(2,1)S(1)} %bitcast.258, bf16[256,384]{1,0:T(8,128)(2,1)S(1)} %copy-done.34, ...), custom_call_target="tpu_custom_call" | custom-call | flops 1 | bytes 1 | tf_op jit(solution)/shard_map/pallas_call | solution.py:570
  405.3 5.8 %collective-permute-done.42 = bf16[16,32,640]{2,1,0:T(8,128)(2,1)S(1)} collective-permute-done((bf16[16,32,640]{2,1,0:T(8,128)(2,1)}, bf16[16,32,640]{2,1,0:T(8,128)(2,1)S(1)}, u32[]{:S(2)}, u32[]{:S(2)}) %collective-permute-start.42) | collective-permute-done | bytes 655392 | tf_op jit(solution)/shard_map/ppermute | solution.py:65
  412.6 3.1 collective-permute-start.45
  415.7 6.6 %all-to-all-start.4 = ((bf16[16,32,640]{2,1,0:T(8,128)(2,1)}), bf16[16,32,640]{2,1,0:T(8,128)(2,1)S(1)}, u32[]{:S(2)}, u32[]{:S(2)}) async-start(bf16[16,32,640]{2,1,0:T(8,128)(2,1)} %add_convert_fusion.2), calls=%async_computation.4 | async-start | bytes 1310720 | tf_op jit(solution)/shard_map/all_to_all | solution.py:69
  423.9 3.5 slice.194.blk_ref
  430.0 8.3 %all-to-all-done.4.parts_ref = bf16[16,32,640]{2,1,0:T(8,128)(2,1)S(1)} async-done(((bf16[16,32,640]{2,1,0:T(8,128)(2,1)}), bf16[16,32,640]{2,1,0:T(8,128)(2,1)S(1)}, u32[]{:S(2)}, u32[]{:S(2)}) %all-to-all-start.4) | async-done | bytes 655392 | tf_op jit(solution)/shard_map/all_to_all | solution.py:69
  443.5 2.2 shard_map.330
  446.8 4.0 collective-permute-start.49
  455.8 4.4 all-to-all-start.5
  460.2 2.7 fusion.36
  462.9 29.0 %all-to-all-done.5.parts_ref = bf16[16,128,384]{2,1,0:T(8,128)(2,1)} async-done(((bf16[16,128,384]{2,1,0:T(8,128)(2,1)}), bf16[16,128,384]{2,1,0:T(8,128)(2,1)}, u32[]{:S(2)}, u32[]{:S(2)}) %all-to-all-start.5) | async-done | bytes 1572896 | tf_op jit(solution)/shard_map/all_to_all | solution.py:69
  491.9 2.3 shard_map.331
  494.9 2.3 collective-permute-start.51
  501.3 4.4 shard_map.334
  505.7 2.9 shard_map.333
  508.7 2.9 shard_map.332
  520.3 2.1 shard_map.335
  (489 shorter events, 153.6 us)
Async XLA Ops:
  7.2 73.2 %all-gather.4.cloned.1.call-start = ((), (), s32[]{:S(2)}) async-start(), calls=%async_computation.7 | async-start | bytes 6684672 | tf_op jit(solution)/shard_map/all_gather | solution.py:807
  15.4 140.4 %all-gather.6.cloned.1.call-start = ((), (), s32[]{:S(2)}) async-start(), calls=%async_computation.8 | async-start | bytes 5570560 | tf_op jit(solution)/shard_map/all_gather | solution.py:871
  22.8 15.2 %collective-permute-start.7 = (bf16[32,2048]{1,0:T(8,128)(2,1)S(1)}, bf16[32,2048]{1,0:T(8,128)(2,1)S(1)}, u32[]{:S(2)}, u32[]{:S(2)}) collective-permute-start(bf16[32,2048]{1,0:T(8,128)(2,1)S(1)} %copy-done.79), channel_id=1, source_target_pairs={{0,2},{2,4},{4,6},{6,0},{1,3},{3,5},{5,7},{7,1},{8,10},{10,12},{12... | collective-permute-start | bytes 393224 | tf_op jit(solution)/shard_map/ppermute | solution.py:65
  24.9 16.2 %collective-permute-start.8 = (bf16[32,2048]{1,0:T(8,128)(2,1)S(1)}, bf16[32,2048]{1,0:T(8,128)(2,1)}, u32[]{:S(2)}, u32[]{:S(2)}) collective-permute-start(bf16[32,2048]{1,0:T(8,128)(2,1)S(1)} %copy-done.79), channel_id=1, source_target_pairs={{0,4},{2,6},{4,0},{6,2},{1,5},{3,7},{5,1},{7,3},{8,12},{10,14},{12... | collective-permute-start | bytes 393224 | tf_op jit(solution)/shard_map/ppermute | solution.py:65
  27.5 16.4 %collective-permute-start.9 = (bf16[32,2048]{1,0:T(8,128)(2,1)S(1)}, bf16[32,2048]{1,0:T(8,128)(2,1)S(1)}, u32[]{:S(2)}, u32[]{:S(2)}) collective-permute-start(bf16[32,2048]{1,0:T(8,128)(2,1)S(1)} %copy-done.79), channel_id=1, source_target_pairs={{0,6},{2,0},{4,2},{6,4},{1,7},{3,1},{5,3},{7,5},{8,14},{10,8},{12,... | collective-permute-start | bytes 393224 | tf_op jit(solution)/shard_map/ppermute | solution.py:65
  28.6 11.0 %collective-permute-start = (bf16[32,2048]{1,0:T(8,128)(2,1)S(1)}, bf16[32,2048]{1,0:T(8,128)(2,1)}, u32[]{:S(2)}, u32[]{:S(2)}) collective-permute-start(bf16[32,2048]{1,0:T(8,128)(2,1)S(1)} %copy-done.76), channel_id=1, source_target_pairs={{0,2},{2,4},{4,6},{6,0},{1,3},{3,5},{5,7},{7,1},{8,10},{10,12},{12... | collective-permute-start | bytes 393224 | tf_op jit(solution)/shard_map/ppermute | solution.py:65
  29.0 17.1 %collective-permute-start.1 = (bf16[32,2048]{1,0:T(8,128)(2,1)S(1)}, bf16[32,2048]{1,0:T(8,128)(2,1)S(1)}, u32[]{:S(2)}, u32[]{:S(2)}) collective-permute-start(bf16[32,2048]{1,0:T(8,128)(2,1)S(1)} %copy-done.76), channel_id=1, source_target_pairs={{0,4},{2,6},{4,0},{6,2},{1,5},{3,7},{5,1},{7,3},{8,12},{10,14},{12... | collective-permute-start | bytes 393224 | tf_op jit(solution)/shard_map/ppermute | solution.py:65
  37.9 11.4 %collective-permute-start.2 = (bf16[32,2048]{1,0:T(8,128)(2,1)S(1)}, bf16[32,2048]{1,0:T(8,128)(2,1)S(1)}, u32[]{:S(2)}, u32[]{:S(2)}) collective-permute-start(bf16[32,2048]{1,0:T(8,128)(2,1)S(1)} %copy-done.76), channel_id=1, source_target_pairs={{0,6},{2,0},{4,2},{6,4},{1,7},{3,1},{5,3},{7,5},{8,14},{10,8},{12,... | collective-permute-start | bytes 393224 | tf_op jit(solution)/shard_map/ppermute | solution.py:65
  39.6 17.4 %collective-permute-start.4 = (bf16[176,2048]{1,0:T(8,128)(2,1)}, bf16[176,2048]{1,0:T(8,128)(2,1)S(1)}, u32[]{:S(2)}, u32[]{:S(2)}) collective-permute-start(bf16[176,2048]{1,0:T(8,128)(2,1)} %get-tuple-element.191), channel_id=1, source_target_pairs={{0,2},{2,4},{4,6},{6,0},{1,3},{3,5},{5,7},{7,1},{8,10},{10,12},{12... | collective-permute-start | bytes 2162696 | tf_op jit(solution)/shard_map/ppermute | solution.py:65
  41.2 30.7 %collective-permute-start.5 = (bf16[176,2048]{1,0:T(8,128)(2,1)}, bf16[176,2048]{1,0:T(8,128)(2,1)}, u32[]{:S(2)}, u32[]{:S(2)}) collective-permute-start(bf16[176,2048]{1,0:T(8,128)(2,1)} %get-tuple-element.192), channel_id=1, source_target_pairs={{0,4},{2,6},{4,0},{6,2},{1,5},{3,7},{5,1},{7,3},{8,12},{10,14},{12... | collective-permute-start | bytes 2162696 | tf_op jit(solution)/shard_map/ppermute | solution.py:65
  44.0 31.3 %collective-permute-start.6 = (bf16[176,2048]{1,0:T(8,128)(2,1)}, bf16[176,2048]{1,0:T(8,128)(2,1)}, u32[]{:S(2)}, u32[]{:S(2)}) collective-permute-start(bf16[176,2048]{1,0:T(8,128)(2,1)} %get-tuple-element.193), channel_id=1, source_target_pairs={{0,6},{2,0},{4,2},{6,4},{1,7},{3,1},{5,3},{7,5},{8,14},{10,8},{12,... | collective-permute-start | bytes 2162696 | tf_op jit(solution)/shard_map/ppermute | solution.py:65
  46.1 4.8 collective-permute-start.10
  91.7 55.1 %all-to-all-start = ((bf16[16,40,1024]{2,1,0:T(8,128)(2,1)}), bf16[16,40,1024]{2,1,0:T(8,128)(2,1)}, u32[]{:S(2)}, u32[]{:S(2)}) async-start(bf16[16,40,1024]{2,1,0:T(8,128)(2,1)} %bitcast.268), calls=%async_computation | async-start | bytes 2621440 | tf_op jit(solution)/shard_map/all_to_all | solution.py:69
  96.6 121.0 %all-gather.8.cloned.1.call-start = ((), (), s32[]{:S(2)}) async-start(), calls=%async_computation.9 | async-start | bytes 5013504 | tf_op jit(solution)/shard_map/all_gather | solution.py:885
  96.6 18.3 %collective-permute-start.11 = (bf16[176,2048]{1,0:T(8,128)(2,1)}, bf16[176,2048]{1,0:T(8,128)(2,1)}, u32[]{:S(2)}, u32[]{:S(2)}) collective-permute-start(bf16[176,2048]{1,0:T(8,128)(2,1)} %get-tuple-element.215), channel_id=1, source_target_pairs={{0,2},{2,4},{4,6},{6,0},{1,3},{3,5},{5,7},{7,1},{8,10},{10,12},{12... | collective-permute-start | bytes 2162696 | tf_op jit(solution)/shard_map/ppermute | solution.py:65
  97.9 33.5 %collective-permute-start.12 = (bf16[176,2048]{1,0:T(8,128)(2,1)}, bf16[176,2048]{1,0:T(8,128)(2,1)}, u32[]{:S(2)}, u32[]{:S(2)}) collective-permute-start(bf16[176,2048]{1,0:T(8,128)(2,1)} %get-tuple-element.216), channel_id=1, source_target_pairs={{0,4},{2,6},{4,0},{6,2},{1,5},{3,7},{5,1},{7,3},{8,12},{10,14},{12... | collective-permute-start | bytes 2162696 | tf_op jit(solution)/shard_map/ppermute | solution.py:65
  100.3 31.0 %collective-permute-start.13 = (bf16[176,2048]{1,0:T(8,128)(2,1)}, bf16[176,2048]{1,0:T(8,128)(2,1)}, u32[]{:S(2)}, u32[]{:S(2)}) collective-permute-start(bf16[176,2048]{1,0:T(8,128)(2,1)} %get-tuple-element.217), channel_id=1, source_target_pairs={{0,6},{2,0},{4,2},{6,4},{1,7},{3,1},{5,3},{7,5},{8,14},{10,8},{12,... | collective-permute-start | bytes 2162696 | tf_op jit(solution)/shard_map/ppermute | solution.py:65
  101.7 44.1 %collective-permute-start.14 = (bf16[176,2048]{1,0:T(8,128)(2,1)}, bf16[176,2048]{1,0:T(8,128)(2,1)}, u32[]{:S(2)}, u32[]{:S(2)}) collective-permute-start(bf16[176,2048]{1,0:T(8,128)(2,1)} %get-tuple-element.219), channel_id=1, source_target_pairs={{0,2},{2,4},{4,6},{6,0},{1,3},{3,5},{5,7},{7,1},{8,10},{10,12},{12... | collective-permute-start | bytes 2162696 | tf_op jit(solution)/shard_map/ppermute | solution.py:65
  102.0 44.7 %collective-permute-start.15 = (bf16[176,2048]{1,0:T(8,128)(2,1)}, bf16[176,2048]{1,0:T(8,128)(2,1)}, u32[]{:S(2)}, u32[]{:S(2)}) collective-permute-start(bf16[176,2048]{1,0:T(8,128)(2,1)} %get-tuple-element.220), channel_id=1, source_target_pairs={{0,6},{2,0},{4,2},{6,4},{1,7},{3,1},{5,3},{7,5},{8,14},{10,8},{12,... | collective-permute-start | bytes 2162696 | tf_op jit(solution)/shard_map/ppermute | solution.py:65
  178.3 6.0 %collective-permute-start.17 = (bf16[32,2048]{1,0:T(8,128)(2,1)S(1)}, bf16[32,2048]{1,0:T(8,128)(2,1)S(1)}, u32[]{:S(2)}, u32[]{:S(2)}) collective-permute-start(bf16[32,2048]{1,0:T(8,128)(2,1)S(1)} %get-tuple-element.520), channel_id=1, source_target_pairs={{0,2},{2,4},{4,6},{6,0},{1,3},{3,5},{5,7},{7,1},{8,10},{10,12},{12... | collective-permute-start | bytes 393224 | tf_op jit(solution)/shard_map/ppermute | solution.py:65
  179.5 8.5 %collective-permute-start.18 = (bf16[32,2048]{1,0:T(8,128)(2,1)S(1)}, bf16[32,2048]{1,0:T(8,128)(2,1)S(1)}, u32[]{:S(2)}, u32[]{:S(2)}) collective-permute-start(bf16[32,2048]{1,0:T(8,128)(2,1)S(1)} %get-tuple-element.522), channel_id=1, source_target_pairs={{0,4},{2,6},{4,0},{6,2},{1,5},{3,7},{5,1},{7,3},{8,12},{10,14},{12... | collective-permute-start | bytes 393224 | tf_op jit(solution)/shard_map/ppermute | solution.py:65
  182.0 6.1 %collective-permute-start.19 = (bf16[32,2048]{1,0:T(8,128)(2,1)S(1)}, bf16[32,2048]{1,0:T(8,128)(2,1)S(1)}, u32[]{:S(2)}, u32[]{:S(2)}) collective-permute-start(bf16[32,2048]{1,0:T(8,128)(2,1)S(1)} %get-tuple-element.521), channel_id=1, source_target_pairs={{0,6},{2,0},{4,2},{6,4},{1,7},{3,1},{5,3},{7,5},{8,14},{10,8},{12,... | collective-permute-start | bytes 393224 | tf_op jit(solution)/shard_map/ppermute | solution.py:65
  188.5 5.1 collective-permute-start.20
  189.6 7.1 %collective-permute-start.21 = (bf16[32,2048]{1,0:T(8,128)(2,1)S(1)}, bf16[32,2048]{1,0:T(8,128)(2,1)S(1)}, u32[]{:S(2)}, u32[]{:S(2)}) collective-permute-start(bf16[32,2048]{1,0:T(8,128)(2,1)S(1)} %get-tuple-element.489), channel_id=1, source_target_pairs={{0,4},{2,6},{4,0},{6,2},{1,5},{3,7},{5,1},{7,3},{8,12},{10,14},{12... | collective-permute-start | bytes 393224 | tf_op jit(solution)/shard_map/ppermute | solution.py:65
  191.8 5.2 collective-permute-start.22
  197.0 3.9 collective-permute-start.23
  206.2 20.8 %collective-permute-start.24 = (bf16[640,1024]{1,0:T(8,128)(2,1)}, bf16[640,1024]{1,0:T(8,128)(2,1)}, u32[]{:S(2)}, u32[]{:S(2)}) collective-permute-start(bf16[640,1024]{1,0:T(8,128)(2,1)} %bitcast.42.g_ref), channel_id=1, source_target_pairs={{0,1},{1,0},{2,3},{3,2},{4,5},{5,4},{6,7},{7,6},{8,9},{9,8},{10,11... | collective-permute-start | bytes 3932168 | tf_op jit(solution)/shard_map/ppermute | solution.py:61
  206.6 20.4 %collective-permute-start.25 = (bf16[176,2048]{1,0:T(8,128)(2,1)}, bf16[176,2048]{1,0:T(8,128)(2,1)}, u32[]{:S(2)}, u32[]{:S(2)}) collective-permute-start(bf16[176,2048]{1,0:T(8,128)(2,1)} %get-tuple-element.236), channel_id=1, source_target_pairs={{0,4},{2,6},{4,0},{6,2},{1,5},{3,7},{5,1},{7,3},{8,12},{10,14},{12... | collective-permute-start | bytes 2162696 | tf_op jit(solution)/shard_map/ppermute | solution.py:65
  208.7 27.8 %all-to-all-start.1 = ((bf16[16,40,1152]{2,1,0:T(8,128)(2,1)}), bf16[16,40,1152]{2,1,0:T(8,128)(2,1)}, u32[]{:S(2)}, u32[]{:S(2)}) async-start(bf16[16,40,1152]{2,1,0:T(8,128)(2,1)} %pad_maximum_fusion), calls=%async_computation.1 | async-start | bytes 2949120 | tf_op jit(solution)/shard_map/all_to_all | solution.py:69
  236.5 5.1 collective-permute-start.26
  270.0 6.9 %collective-permute-start.27 = (bf16[640,1152]{1,0:T(8,128)(2,1)}, bf16[640,1152]{1,0:T(8,128)(2,1)S(1)}, u32[]{:S(2)}, u32[]{:S(2)}) collective-permute-start(bf16[640,1152]{1,0:T(8,128)(2,1)} %get-tuple-element.256), channel_id=1, source_target_pairs={{0,1},{1,0},{2,3},{3,2},{4,5},{5,4},{6,7},{7,6},{8,9},{9,8},{10,11... | collective-permute-start | bytes 4423688 | tf_op jit(solution)/shard_map/ppermute | solution.py:61
  278.3 31.2 %all-to-all-start.2 = ((bf16[16,40,1152]{2,1,0:T(8,128)(2,1)}), bf16[16,40,1152]{2,1,0:T(8,128)(2,1)}, u32[]{:S(2)}, u32[]{:S(2)}) async-start(bf16[16,40,1152]{2,1,0:T(8,128)(2,1)} %bitcast.267), calls=%async_computation.2 | async-start | bytes 2949120 | tf_op jit(solution)/shard_map/all_to_all | solution.py:69
  285.6 21.1 %collective-permute-start.28 = (bf16[176,2048]{1,0:T(8,128)(2,1)S(1)}, bf16[176,2048]{1,0:T(8,128)(2,1)S(1)}, u32[]{:S(2)}, u32[]{:S(2)}) collective-permute-start(bf16[176,2048]{1,0:T(8,128)(2,1)S(1)} %get-tuple-element.515), channel_id=1, source_target_pairs={{0,6},{2,0},{4,2},{6,4},{1,7},{3,1},{5,3},{7,5},{8,14},{10,8},{12,... | collective-permute-start | bytes 2162696 | tf_op jit(solution)/shard_map/ppermute | solution.py:65
  290.0 18.6 %collective-permute-start.29 = (bf16[176,2048]{1,0:T(8,128)(2,1)S(1)}, bf16[176,2048]{1,0:T(8,128)(2,1)S(1)}, u32[]{:S(2)}, u32[]{:S(2)}) collective-permute-start(bf16[176,2048]{1,0:T(8,128)(2,1)S(1)} %get-tuple-element.514), channel_id=1, source_target_pairs={{0,2},{2,4},{4,6},{6,0},{1,3},{3,5},{5,7},{7,1},{8,10},{10,12},{12... | collective-permute-start | bytes 2162696 | tf_op jit(solution)/shard_map/ppermute | solution.py:65
  313.8 2.9 collective-permute-start.30
  316.9 6.2 %collective-permute-start.31 = (bf16[32,2176]{1,0:T(8,128)(2,1)S(1)}, bf16[32,2176]{1,0:T(8,128)(2,1)S(1)}, u32[]{:S(2)}, u32[]{:S(2)}) collective-permute-start(bf16[32,2176]{1,0:T(8,128)(2,1)S(1)} %get-tuple-element.517), channel_id=1, source_target_pairs={{0,2},{2,4},{4,6},{6,0},{1,3},{3,5},{5,7},{7,1},{8,10},{10,12},{12... | collective-permute-start | bytes 417800 | tf_op jit(solution)/shard_map/ppermute | solution.py:65
  317.0 9.9 %collective-permute-start.32 = (bf16[32,2176]{1,0:T(8,128)(2,1)S(1)}, bf16[32,2176]{1,0:T(8,128)(2,1)S(1)}, u32[]{:S(2)}, u32[]{:S(2)}) collective-permute-start(bf16[32,2176]{1,0:T(8,128)(2,1)S(1)} %get-tuple-element.519), channel_id=1, source_target_pairs={{0,4},{2,6},{4,0},{6,2},{1,5},{3,7},{5,1},{7,3},{8,12},{10,14},{12... | collective-permute-start | bytes 417800 | tf_op jit(solution)/shard_map/ppermute | solution.py:65
  320.4 6.4 %collective-permute-start.33 = (bf16[32,2176]{1,0:T(8,128)(2,1)S(1)}, bf16[32,2176]{1,0:T(8,128)(2,1)S(1)}, u32[]{:S(2)}, u32[]{:S(2)}) collective-permute-start(bf16[32,2176]{1,0:T(8,128)(2,1)S(1)} %get-tuple-element.518), channel_id=1, source_target_pairs={{0,6},{2,0},{4,2},{6,4},{1,7},{3,1},{5,3},{7,5},{8,14},{10,8},{12,... | collective-permute-start | bytes 417800 | tf_op jit(solution)/shard_map/ppermute | solution.py:65
  327.9 5.1 collective-permute-start.34
  329.3 7.1 %collective-permute-start.35 = (bf16[32,2048]{1,0:T(8,128)(2,1)S(1)}, bf16[32,2048]{1,0:T(8,128)(2,1)S(1)}, u32[]{:S(2)}, u32[]{:S(2)}) collective-permute-start(bf16[32,2048]{1,0:T(8,128)(2,1)S(1)} %get-tuple-element.485), channel_id=1, source_target_pairs={{0,4},{2,6},{4,0},{6,2},{1,5},{3,7},{5,1},{7,3},{8,12},{10,14},{12... | collective-permute-start | bytes 393224 | tf_op jit(solution)/shard_map/ppermute | solution.py:65
  331.4 4.9 collective-permute-start.36
  336.4 4.0 collective-permute-start.37
  340.7 17.5 %collective-permute-start.38 = (bf16[176,2048]{1,0:T(8,128)(2,1)S(1)}, bf16[176,2048]{1,0:T(8,128)(2,1)S(1)}, u32[]{:S(2)}, u32[]{:S(2)}) collective-permute-start(bf16[176,2048]{1,0:T(8,128)(2,1)S(1)} %copy-done.57), channel_id=1, source_target_pairs={{0,6},{2,0},{4,2},{6,4},{1,7},{3,1},{5,3},{7,5},{8,14},{10,8},{12,... | collective-permute-start | bytes 2162696 | tf_op jit(solution)/shard_map/ppermute | solution.py:65
  343.0 18.4 %collective-permute-start.39 = (bf16[176,2048]{1,0:T(8,128)(2,1)S(1)}, bf16[176,2048]{1,0:T(8,128)(2,1)S(1)}, u32[]{:S(2)}, u32[]{:S(2)}) collective-permute-start(bf16[176,2048]{1,0:T(8,128)(2,1)S(1)} %copy-done.55), channel_id=1, source_target_pairs={{0,2},{2,4},{4,6},{6,0},{1,3},{3,5},{5,7},{7,1},{8,10},{10,12},{12... | collective-permute-start | bytes 2162696 | tf_op jit(solution)/shard_map/ppermute | solution.py:65
  361.5 9.5 %collective-permute-start.40 = (bf16[4,16,32,640]{3,2,1,0:T(8,128)(2,1)S(1)}, bf16[4,16,32,640]{3,2,1,0:T(8,128)(2,1)S(1)}, u32[]{:S(2)}, u32[]{:S(2)}) collective-permute-start(bf16[4,16,32,640]{3,2,1,0:T(8,128)(2,1)S(1)} %get-tuple-element.288), channel_id=1, source_target_pairs={{0,1},{1,0},{2,3},{3,2},{4,5},{5,4},{6,7},{7,6},{8,9},{9,8},{10,11... | collective-permute-start | bytes 7864328 | tf_op jit(solution)/shard_map/ppermute | solution.py:61
  363.0 6.4 %collective-permute-start.41 = (bf16[640,1024]{1,0:T(8,128)(2,1)S(1)}, bf16[640,1024]{1,0:T(8,128)(2,1)S(1)}, u32[]{:S(2)}, u32[]{:S(2)}) collective-permute-start(bf16[640,1024]{1,0:T(8,128)(2,1)S(1)} %copy-done.104), channel_id=1, source_target_pairs={{0,1},{1,0},{2,3},{3,2},{4,5},{5,4},{6,7},{7,6},{8,9},{9,8},{10,11... | collective-permute-start | bytes 3932168 | tf_op jit(solution)/shard_map/ppermute | solution.py:61
  373.0 39.6 %all-to-all-start.3 = ((bf16[16,40,1024]{2,1,0:T(8,128)(2,1)}), bf16[16,40,1024]{2,1,0:T(8,128)(2,1)}, u32[]{:S(2)}, u32[]{:S(2)}) async-start(bf16[16,40,1024]{2,1,0:T(8,128)(2,1)} %bitcast.271), calls=%async_computation.3 | async-start | bytes 2621440 | tf_op jit(solution)/shard_map/all_to_all | solution.py:69
  379.8 140.5 %reduce-scatter.2.cloned.1.call-start = ((), (), s32[]{:S(2)}) async-start(), calls=%async_computation.10 | async-start | bytes 8355840 | tf_op jit(solution)/shard_map/reduce_scatter | solution.py:1015
  379.9 31.2 %collective-permute-start.42 = (bf16[16,32,640]{2,1,0:T(8,128)(2,1)}, bf16[16,32,640]{2,1,0:T(8,128)(2,1)S(1)}, u32[]{:S(2)}, u32[]{:S(2)}) collective-permute-start(bf16[16,32,640]{2,1,0:T(8,128)(2,1)} %get-tuple-element.294), channel_id=1, source_target_pairs={{0,2},{2,4},{4,6},{6,0},{1,3},{3,5},{5,7},{7,1},{8,10},{10,12},{12... | collective-permute-start | bytes 1966088 | tf_op jit(solution)/shard_map/ppermute | solution.py:65
  380.0 31.1 %collective-permute-start.43 = (bf16[16,32,640]{2,1,0:T(8,128)(2,1)}, bf16[16,32,640]{2,1,0:T(8,128)(2,1)S(1)}, u32[]{:S(2)}, u32[]{:S(2)}) collective-permute-start(bf16[16,32,640]{2,1,0:T(8,128)(2,1)} %get-tuple-element.295), channel_id=1, source_target_pairs={{0,4},{2,6},{4,0},{6,2},{1,5},{3,7},{5,1},{7,3},{8,12},{10,14},{12... | collective-permute-start | bytes 1966088 | tf_op jit(solution)/shard_map/ppermute | solution.py:65
  381.0 30.4 %collective-permute-start.44 = (bf16[16,32,640]{2,1,0:T(8,128)(2,1)}, bf16[16,32,640]{2,1,0:T(8,128)(2,1)S(1)}, u32[]{:S(2)}, u32[]{:S(2)}) collective-permute-start(bf16[16,32,640]{2,1,0:T(8,128)(2,1)} %get-tuple-element.296), channel_id=1, source_target_pairs={{0,6},{2,0},{4,2},{6,4},{1,7},{3,1},{5,3},{7,5},{8,14},{10,8},{12,... | collective-permute-start | bytes 1966088 | tf_op jit(solution)/shard_map/ppermute | solution.py:65
  412.6 25.7 %collective-permute-start.45 = (bf16[176,2048]{1,0:T(8,128)(2,1)}, bf16[176,2048]{1,0:T(8,128)(2,1)}, u32[]{:S(2)}, u32[]{:S(2)}) collective-permute-start(bf16[176,2048]{1,0:T(8,128)(2,1)} %get-tuple-element.309), channel_id=1, source_target_pairs={{0,6},{2,0},{4,2},{6,4},{1,7},{3,1},{5,3},{7,5},{8,14},{10,8},{12,... | collective-permute-start | bytes 2162696 | tf_op jit(solution)/shard_map/ppermute | solution.py:65
  415.7 22.7 %collective-permute-start.46 = (bf16[176,2048]{1,0:T(8,128)(2,1)}, bf16[176,2048]{1,0:T(8,128)(2,1)}, u32[]{:S(2)}, u32[]{:S(2)}) collective-permute-start(bf16[176,2048]{1,0:T(8,128)(2,1)} %get-tuple-element.310), channel_id=1, source_target_pairs={{0,2},{2,4},{4,6},{6,0},{1,3},{3,5},{5,7},{7,1},{8,10},{10,12},{12... | collective-permute-start | bytes 2162696 | tf_op jit(solution)/shard_map/ppermute | solution.py:65
  415.7 22.6 %all-to-all-start.4 = ((bf16[16,32,640]{2,1,0:T(8,128)(2,1)}), bf16[16,32,640]{2,1,0:T(8,128)(2,1)S(1)}, u32[]{:S(2)}, u32[]{:S(2)}) async-start(bf16[16,32,640]{2,1,0:T(8,128)(2,1)} %add_convert_fusion.2), calls=%async_computation.4 | async-start | bytes 1310720 | tf_op jit(solution)/shard_map/all_to_all | solution.py:69
  442.2 49.7 %collective-permute-start.48 = (bf16[528,2048]{1,0:T(8,128)(2,1)}, bf16[528,2048]{1,0:T(8,128)(2,1)S(1)}, u32[]{:S(2)}, u32[]{:S(2)}) collective-permute-start(bf16[528,2048]{1,0:T(8,128)(2,1)} %copy-done.51), channel_id=1, source_target_pairs={{0,4},{2,6},{4,0},{6,2},{1,5},{3,7},{5,1},{7,3},{8,12},{10,14},{12... | collective-permute-start | bytes 6488072 | tf_op jit(solution)/shard_map/ppermute | solution.py:65
  446.8 13.4 %collective-permute-start.49 = (bf16[4,32,4096]{2,1,0:T(8,128)(2,1)}, bf16[4,32,4096]{2,1,0:T(8,128)(2,1)}, u32[]{:S(2)}, u32[]{:S(2)}) collective-permute-start(bf16[4,32,4096]{2,1,0:T(8,128)(2,1)} %dynamic-slice_bitcast_fusion), channel_id=1, source_target_pairs={{0,1},{1,0},{2,3},{3,2},{4,5},{5,4},{6,7},{7,6},{8,9},{9,8},{10,11... | collective-permute-start | bytes 3145736 | tf_op jit(solution)/shard_map/ppermute | solution.py:61
  455.8 36.1 %all-to-all-start.5 = ((bf16[16,128,384]{2,1,0:T(8,128)(2,1)}), bf16[16,128,384]{2,1,0:T(8,128)(2,1)}, u32[]{:S(2)}, u32[]{:S(2)}) async-start(bf16[16,128,384]{2,1,0:T(8,128)(2,1)} %bitcast.259), calls=%async_computation.5 | async-start | bytes 3145728 | tf_op jit(solution)/shard_map/all_to_all | solution.py:69
  494.2 5.3 collective-permute-start.50
  494.9 16.8 %collective-permute-start.51 = (bf16[128,384]{1,0:T(8,128)(2,1)}, bf16[128,384]{1,0:T(8,128)(2,1)S(1)}, u32[]{:S(2)}, u32[]{:S(2)}) collective-permute-start(bf16[128,384]{1,0:T(8,128)(2,1)} %shard_map.331), channel_id=1, source_target_pairs={{0,4},{2,6},{4,0},{6,2},{1,5},{3,7},{5,1},{7,3},{8,12},{10,14},{12... | collective-permute-start | bytes 294920 | tf_op jit(solution)/shard_map/ppermute | solution.py:65
  497.2 14.5 %collective-permute-start.52 = (bf16[128,384]{1,0:T(8,128)(2,1)}, bf16[128,384]{1,0:T(8,128)(2,1)S(1)}, u32[]{:S(2)}, u32[]{:S(2)}) collective-permute-start(bf16[128,384]{1,0:T(8,128)(2,1)} %shard_map.331), channel_id=1, source_target_pairs={{0,6},{2,0},{4,2},{6,4},{1,7},{3,1},{5,3},{7,5},{8,14},{10,8},{12,... | collective-permute-start | bytes 294920 | tf_op jit(solution)/shard_map/ppermute | solution.py:65
  498.3 13.5 %collective-permute-start.53 = (bf16[32,4096]{1,0:T(8,128)(2,1)}, bf16[32,4096]{1,0:T(8,128)(2,1)S(1)}, u32[]{:S(2)}, u32[]{:S(2)}) collective-permute-start(bf16[32,4096]{1,0:T(8,128)(2,1)} %get-tuple-element.332), channel_id=1, source_target_pairs={{0,2},{2,4},{4,6},{6,0},{1,3},{3,5},{5,7},{7,1},{8,10},{10,12},{12... | collective-permute-start | bytes 786440 | tf_op jit(solution)/shard_map/ppermute | solution.py:65
  498.6 13.2 %collective-permute-start.54 = (bf16[32,4096]{1,0:T(8,128)(2,1)}, bf16[32,4096]{1,0:T(8,128)(2,1)S(1)}, u32[]{:S(2)}, u32[]{:S(2)}) collective-permute-start(bf16[32,4096]{1,0:T(8,128)(2,1)} %get-tuple-element.333), channel_id=1, source_target_pairs={{0,4},{2,6},{4,0},{6,2},{1,5},{3,7},{5,1},{7,3},{8,12},{10,14},{12... | collective-permute-start | bytes 786440 | tf_op jit(solution)/shard_map/ppermute | solution.py:65
  499.5 14.4 %collective-permute-start.55 = (bf16[32,4096]{1,0:T(8,128)(2,1)}, bf16[32,4096]{1,0:T(8,128)(2,1)S(1)}, u32[]{:S(2)}, u32[]{:S(2)}) collective-permute-start(bf16[32,4096]{1,0:T(8,128)(2,1)} %get-tuple-element.334), channel_id=1, source_target_pairs={{0,6},{2,0},{4,2},{6,4},{1,7},{3,1},{5,3},{7,5},{8,14},{10,8},{12,... | collective-permute-start | bytes 786440 | tf_op jit(solution)/shard_map/ppermute | solution.py:65
  514.0 2.9 collective-permute-start.56
  (112 other events, 1260.9 us)
Sparse Core Ops, SparseCore 0:
  15.6 64.7 all-gather.3
  91.8 63.9 all-gather.5
  158.5 58.9 all-gather.7
  412.7 104.7 reduce-scatter.1

commit v5 on v4

--- a/solution.py
+++ b/solution.py
@@ -717,11 +717,49 @@
     )(total)
 
 
-def pack_query_columns(w):
-    return jnp.concatenate(
-        [w[:, 0:128], w[:, 192:320], w[:, 128:160], w[:, 320:352], w[:, 160:192], w[:, 352:384]],
-        axis=1,
-    )
+def spots(rows, cols, wanted):
+    source = lax.broadcasted_iota(jnp.int32, (rows, cols), 0)
+    target = lax.broadcasted_iota(jnp.int32, (rows, cols), 1)
+    return (source == wanted(target)).astype(HALF)
+
+
+def pack_kernel(dkv_ref, router_ref, uk_ref, uv_ref, gains_ref, wq_ref, wo_ref, out_ref):
+    out_ref[:, 0:512] = dkv_ref[0:512, :].T.astype(HALF)
+    rope = dot_tn(dkv_ref[512:576, :].astype(HALF), spots(64, 128, lambda j: j))
+    router = dot_tn(
+        router_ref[...].astype(HALF),
+        spots(64, 128, lambda j: jnp.where(j < 64, -1, 4 * (j % 16) + (j - 64) // 16)),
+    )
+    out_ref[:, 512:640] = (rope + router).astype(HALF)
+    for block in range(2):
+        lanes = slice(128 * block, 128 * block + 128)
+        out_ref[32 * block : 32 * block + 32, 640:768] = uk_ref[:, lanes].astype(HALF)
+        out_ref[64 + 32 * block : 96 + 32 * block, 640:768] = uv_ref[:, lanes].astype(HALF)
+    out_ref[:, 768:896] = dot_tn(gains_ref[...].astype(HALF), spots(8, 128, lambda j: j)).astype(HALF)
+
+    def query_column(j):
+        rot = j - 256
+        return jnp.where(
+            j < 256,
+            j + 64 * (j // 128),
+            128 + 192 * ((rot // 32) % 2) + 32 * (rot // 64) + rot % 32,
+        )
+
+    out_ref[:, 896:1280] = dot_nn(
+        wq_ref[...].astype(HALF), spots(384, 384, query_column)
+    ).astype(HALF)
+    out_ref[:, 1280:1536] = wo_ref[...].T.astype(HALF)
+
+
+def pack_first(*operands):
+    vmem = pl.BlockSpec(memory_space=pltpu.VMEM)
+    return pl.pallas_call(
+        pack_kernel,
+        out_shape=jax.ShapeDtypeStruct((128, 1536), HALF),
+        in_specs=[vmem] * 7,
+        out_specs=vmem,
+        cost_estimate=pl.CostEstimate(flops=1, bytes_accessed=1, transcendentals=0),
+    )(*operands)
 
 
 def pad_cols(w, width):
@@ -791,19 +829,10 @@
     def moved_pieces(sent):
         return [sent[0]] + [shift_y(sent[by], by) for by in (1, 2, 3)]
 
-    gain_cols = jnp.stack([gain_attn, gain_ffn, jnp.pad(gain_latent, (0, 96))], axis=1)
-    w_router_perm = w_router.reshape(128, 16, 4).transpose(0, 2, 1).reshape(128, EXPERTS)
-    first_pack = jnp.concatenate(
-        [
-            w_dkv,
-            w_router_perm,
-            jnp.concatenate([w_uk, w_uv], axis=1).reshape(128, 128),
-            pad_cols(gain_cols, 128),
-            pack_query_columns(w_q),
-            w_o.T,
-        ],
-        axis=1,
-    ).astype(HALF)
+    gain_own = jnp.stack([gain_attn, gain_ffn, jnp.pad(gain_latent, (0, 96))], axis=0)
+    first_pack = pack_first(
+        w_dkv.T, w_router.T, w_uk, w_uv, jnp.pad(gain_own, ((0, 5), (0, 0))), w_q, w_o
+    )
     first_all = lax.all_gather(first_pack, EX, axis=0, tiled=True)
     gate_sent, up_sent, down_sent = sent_pieces(w_eg), sent_pieces(w_eu), sent_pieces(w_ed)
     gate_sent, up_sent, inputs_b, out_grad_b = lax.optimization_barrier(
@@ -871,7 +900,7 @@
     c_all = lax.all_gather(c_local, EX, axis=0, tiled=True)
     up_pieces = moved_pieces(up_sent)
     down_first = [down_sent[0], shift_y(down_sent[1], 1), None, shift_y(down_sent[3], 3)]
-    wkv_b = wkv_b.reshape(KVL, 512)
+    wkv_b = wkv_b.reshape(16, 4, 32, 128).transpose(0, 2, 1, 3).reshape(KVL, 512)
     q_raw = dot_nn(h_one, wq_b)
     q_rot = q_raw[:, 256:]
     q_rot = q_rot * cos4 + swap_halves(q_rot) * sin4

time: 543 us -> 539 us (level)
  other arithmetic: 39.4 us -> 33.2 us
    unnamed x220 -> x218, local copies, waits for them, and re-layouts: 25.4 us -> 24.5 us
  transfers between devices with their start and end apart: 67 -> 67, of which waited for: 37 -> 38; matrix products, arithmetic and copies ran while one was open for 16% -> 15% of each run, Pallas kernels for 12% -> 12%
where the time goes in v5:
time: 539 us; the launch traced here: 529 us
  waiting for transfers between devices  176 us (33%)
  starting transfers between devices  115 us (21%)
  Pallas kernels  95.8 us (18%)
  local copies, waits for them, and re-layouts  61.7 us (11%)
  other arithmetic  33.2 us (6%)
  matrix products  30.6 us (6%)
  between operations  16.3 us (3%)
    ppermute x43, waiting for transfers between devices, shift_y(): return lax.ppermute(value, 'y', [(i, (i + by) % 4) for i in range(4)])  92.2 us
    ppermute x43, starting transfers between devices, shift_y(): return lax.ppermute(value, 'y', [(i, (i + by) % 4) for i in range(4)])  61.9 us
    all_to_all x6, waiting for transfers between devices, spread(): return lax.all_to_all(value, axes, split_axis=0, concat_axis=0, tiled=True)  46.6 us
    all_to_all x6, starting transfers between devices, spread(): return lax.all_to_all(value, axes, split_axis=0, concat_axis=0, tiled=True)  32.6 us
    pallas_call x1, Pallas kernels, run_expert(): pl.pallas_call(expert_kernel, out_shape=(jax.ShapeDtypeStruct((rows, D //...  26.1 us
    unnamed x218, local copies, waits for them, and re-layouts  24.5 us
    ppermute x14, starting transfers between devices, swap_core(): return lax.ppermute(value, 'c', [(0, 1), (1, 0)])  20.6 us
    ppermute x14, waiting for transfers between devices, swap_core(): return lax.ppermute(value, 'c', [(0, 1), (1, 0)])  19.7 us
  transfers between devices with their start and end apart: 67, of which 38 were waited for; matrix products, arithmetic and copies ran while one was open for 15% of the time, Pallas kernels for 12%

profile of v5, /device:TPU:1, one launch (start us, length us, event | category | flops | bytes accessed | tf_op | source)
XLA Modules:
  0.0 529.0 jit_solution(11944541422707097980)
XLA Ops:
  9.2 2.2 shard_map.323
  11.6 7.1 %fusion.14 = (bf16[176,2048]{1,0:T(8,128)(2,1)}, bf16[176,2048]{1,0:T(8,128)(2,1)}, bf16[176,2048]{1,0:T(8,128)(2,1)}, bf16[176,2048]{1,0:T(8,128)(2,1)}, bf16[1...) fusion(f32[4,176,2048]{2,1,0:T(8,128)} %param.33, ...), kind=kLoop, calls=%fused_computation.56 | loop fusion | bytes 11534352 | tf_op jit(solution)/shard_map/convert_element_type | solution.py:825
  18.7 2.1 collective-permute-start.7
  20.9 2.6 collective-permute-start.8
  28.6 4.5 fusion.22
  42.1 3.3 collective-permute-start.10
  53.0 14.8 %collective-permute-done.5.rest_2_ = bf16[176,2048]{1,0:T(8,128)(2,1)} collective-permute-done((bf16[176,2048]{1,0:T(8,128)(2,1)}, bf16[176,2048]{1,0:T(8,128)(2,1)}, u32[]{:S(2)}, u32[]{:S(2)}) %collective-permute-start.5) | collective-permute-done | bytes 720928 | tf_op jit(solution)/shard_map/ppermute | solution.py:65
  67.8 3.4 collective-permute-done.6.rest_3_
  71.2 5.1 all-gather.4.cloned.1.call-done
  79.4 2.9 fusion.92
  87.6 4.9 all-to-all-start
  93.9 2.4 collective-permute-start.12
  98.0 2.4 collective-permute-start.15
  103.1 7.8 %collective-permute-done.11.rest_5_ = bf16[176,2048]{1,0:T(8,128)(2,1)} collective-permute-done((bf16[176,2048]{1,0:T(8,128)(2,1)}, bf16[176,2048]{1,0:T(8,128)(2,1)}, u32[]{:S(2)}, u32[]{:S(2)}) %collective-permute-start.11) | collective-permute-done | bytes 720928 | tf_op jit(solution)/shard_map/ppermute | solution.py:65
  110.8 16.5 %collective-permute-done.12.rest_6_ = bf16[176,2048]{1,0:T(8,128)(2,1)} collective-permute-done((bf16[176,2048]{1,0:T(8,128)(2,1)}, bf16[176,2048]{1,0:T(8,128)(2,1)}, u32[]{:S(2)}, u32[]{:S(2)}) %collective-permute-start.12) | collective-permute-done | bytes 720928 | tf_op jit(solution)/shard_map/ppermute | solution.py:65
  127.3 14.4 %collective-permute-done.14.rest_9_ = bf16[176,2048]{1,0:T(8,128)(2,1)} collective-permute-done((bf16[176,2048]{1,0:T(8,128)(2,1)}, bf16[176,2048]{1,0:T(8,128)(2,1)}, u32[]{:S(2)}, u32[]{:S(2)}) %collective-permute-start.14) | collective-permute-done | bytes 720928 | tf_op jit(solution)/shard_map/ppermute | solution.py:65
  142.7 9.1 %all-gather.6.cloned.1.call-done.c_ref = bf16[4096,640]{1,0:T(8,128)(2,1)} async-done(((bf16[256,640]{1,0:T(8,128)(2,1)}), bf16[4096,640]{1,0:T(8,128)(2,1)}) %all-gather.6.cloned.1.call-update) | async-done | bytes 5242896 | tf_op jit(solution)/shard_map/all_gather | solution.py:900
  153.1 4.9 convolution_convert_fusion.kv_ref
  158.1 10.0 %shard_map.324 = (bf16[2,4096,256]{2,1,0:T(8,128)(2,1)S(1)}, f32[256,256]{1,0:T(8,128)S(1)}) custom-call(bf16[256,384]{1,0:T(8,128)(2,1)S(1)} %pad_maximum_fusion.6.q_ref, bf16[4096,512]{1,0:T(8,128)(2,1)S(1)} %convolution_convert_fusion.kv_ref, bf16[4096,128]{1,0:T(8,128)(2,1)S(1)} %slice.181.rot_ref, s32[1,256]{1,0:T(1,128)S(1)} %bitcast.264, ...), custom_call_target="tpu_custom_call" | custom-call | flops 1610612736 | bytes 12582912 | tf_op jit(solution)/shard_map/pallas_call | solution.py:185
  175.5 2.4 collective-permute-start.18
  180.2 3.8 collective-permute-done.18
  185.5 2.2 collective-permute-start.21
  189.5 3.1 collective-permute-done.21
  192.9 2.2 collective-permute-start.23
  204.6 5.4 %all-to-all-start.1 = ((bf16[16,40,1152]{2,1,0:T(8,128)(2,1)}), bf16[16,40,1152]{2,1,0:T(8,128)(2,1)}, u32[]{:S(2)}, u32[]{:S(2)}) async-start(bf16[16,40,1152]{2,1,0:T(8,128)(2,1)} %pad_maximum_fusion), calls=%async_computation.1 | async-start | bytes 2949120 | tf_op jit(solution)/shard_map/all_to_all | solution.py:69
  210.1 3.4 all-gather.8.cloned.1.call-done
  213.5 3.1 fusion.3
  220.5 2.4 fusion.1
  222.9 9.5 %all-to-all-done.1 = bf16[16,40,1152]{2,1,0:T(8,128)(2,1)} async-done(((bf16[16,40,1152]{2,1,0:T(8,128)(2,1)}), bf16[16,40,1152]{2,1,0:T(8,128)(2,1)}, u32[]{:S(2)}, u32[]{:S(2)}) %all-to-all-start.1) | async-done | bytes 1474592 | tf_op jit(solution)/shard_map/all_to_all | solution.py:69
  234.5 3.1 collective-permute-done.26.xo_ref
  239.8 26.1 %shard_map.325 = (bf16[640,1152]{1,0:T(8,128)(2,1)}, bf16[640,1152]{1,0:T(8,128)(2,1)}, bf16[640,1024]{1,0:T(8,128)(2,1)}, bf16[640,1024]{1,0:T(8,128)(2,1)}, bf...) custom-call(s32[1]{0:T(128)} %bitcast.55.at_ref.core_ref, ...), custom_call_target="tpu_custom_call" | custom-call | flops 12079595520 | bytes 29360128 | tf_op jit(solution)/shard_map/pallas_call | solution.py:410
  266.4 6.5 %convolution_convert_fusion.1.gate_ref = bf16[768,2048]{1,0:T(8,128)(2,1)} fusion(bf16[640,2048]{1,0:T(8,128)(2,1)} %get-tuple-element.258.x_ref, bf16[640,1536]{1,0:T(8,128)(2,1)} %get-tuple-element.267.dpre_ref), kind=kOutput, calls=%fused_computation.2 | convolution fusion | flops 2014838784 | bytes 6750208 | tf_op jit(solution)/shard_map/dot_general | solution.py:43
  274.3 4.4 all-to-all-start.2
  278.8 2.8 fusion.96
  281.6 4.4 collective-permute-start.28
  288.2 9.7 %shard_map.326 = (bf16[176,2048]{1,0:T(8,128)(2,1)S(1)}, bf16[176,2048]{1,0:T(8,128)(2,1)S(1)}, bf16[176,2048]{1,0:T(8,128)(2,1)S(1)}, bf16[176,2048]{1,0:T(8,12...) custom-call(bf16[640,2048]{1,0:T(8,128)(2,1)S(1)} %copy-done.17, ...), custom_call_target="tpu_custom_call" | custom-call | flops 1 | bytes 1 | tf_op jit(solution)/shard_map/pallas_call | solution.py:499
  312.9 3.5 collective-permute-start.32
  319.0 3.9 collective-permute-done.32
  325.2 2.2 collective-permute-start.35
  329.1 3.2 collective-permute-done.35
  332.3 2.5 collective-permute-start.37
  336.6 2.3 collective-permute-start.38
  339.3 11.7 %shard_map.327 = (bf16[4,16,32,640]{3,2,1,0:T(8,128)(2,1)S(1)}, bf16[4,16,32,640]{3,2,1,0:T(8,128)(2,1)S(1)}, bf16[4096,512]{1,0:T(8,128)(2,1)S(1)}, f32[256,384]{1,0:T(8,128)S(1)}) custom-call(s32[1]{0:T(128)} %bitcast.55.at_ref.core_ref, bf16[256,384]{1,0:T(8,128)(2,1)S(1)} %copy-done.36, bf16[4096,512]{1,0:T(8,128)(2,1)S(1)} %copy-done.13, ...), custom_call_target="tpu_custom_call" | custom-call | flops 1 | bytes 1 | tf_op jit(solution)/shard_map/pallas_call | solution.py:276
  351.0 3.1 collective-permute-done.38.refs_1_
  354.1 3.3 collective-permute-done.39.refs_3_
  359.0 6.3 %collective-permute-done.41 = bf16[640,1024]{1,0:T(8,128)(2,1)S(1)} collective-permute-done((bf16[640,1024]{1,0:T(8,128)(2,1)S(1)}, bf16[640,1024]{1,0:T(8,128)(2,1)S(1)}, u32[]{:S(2)}, u32[]{:S(2)}) %collective-permute-start.41) | collective-permute-done | bytes 1310752 | tf_op jit(solution)/shard_map/ppermute | solution.py:61
  369.0 6.8 %all-to-all-start.3 = ((bf16[16,40,1024]{2,1,0:T(8,128)(2,1)}), bf16[16,40,1024]{2,1,0:T(8,128)(2,1)}, u32[]{:S(2)}, u32[]{:S(2)}) async-start(bf16[16,40,1024]{2,1,0:T(8,128)(2,1)} %bitcast.275), calls=%async_computation.3 | async-start | bytes 2621440 | tf_op jit(solution)/shard_map/all_to_all | solution.py:69
  383.7 16.6 %shard_map.328 = (bf16[2048,1920]{1,0:T(8,128)(2,1)}, bf16[256,2048]{1,0:T(8,128)(2,1)S(1)}, f32[1,2048]{1,0:T(1,128)S(1)}) custom-call(bf16[256,2048]{1,0:T(8,128)(2,1)S(1)} %bitcast.251, bf16[256,768]{1,0:T(8,128)(2,1)S(1)} %copy-done.21, bf16[256,2048]{1,0:T(8,128)(2,1)S(1)} %bitcast.259, bf16[256,384]{1,0:T(8,128)(2,1)S(1)} %copy-done.34, ...), custom_call_target="tpu_custom_call" | custom-call | flops 1 | bytes 1 | tf_op jit(solution)/shard_map/pallas_call | solution.py:570
  401.2 5.8 %collective-permute-done.42 = bf16[16,32,640]{2,1,0:T(8,128)(2,1)S(1)} collective-permute-done((bf16[16,32,640]{2,1,0:T(8,128)(2,1)}, bf16[16,32,640]{2,1,0:T(8,128)(2,1)S(1)}, u32[]{:S(2)}, u32[]{:S(2)}) %collective-permute-start.42) | collective-permute-done | bytes 655392 | tf_op jit(solution)/shard_map/ppermute | solution.py:65
  408.5 3.1 collective-permute-start.45
  411.6 6.6 %all-to-all-start.4 = ((bf16[16,32,640]{2,1,0:T(8,128)(2,1)}), bf16[16,32,640]{2,1,0:T(8,128)(2,1)S(1)}, u32[]{:S(2)}, u32[]{:S(2)}) async-start(bf16[16,32,640]{2,1,0:T(8,128)(2,1)} %add_convert_fusion.2), calls=%async_computation.4 | async-start | bytes 1310720 | tf_op jit(solution)/shard_map/all_to_all | solution.py:69
  419.8 3.5 slice.164.blk_ref
  426.0 8.3 %all-to-all-done.4.parts_ref = bf16[16,32,640]{2,1,0:T(8,128)(2,1)S(1)} async-done(((bf16[16,32,640]{2,1,0:T(8,128)(2,1)}), bf16[16,32,640]{2,1,0:T(8,128)(2,1)S(1)}, u32[]{:S(2)}, u32[]{:S(2)}) %all-to-all-start.4) | async-done | bytes 655392 | tf_op jit(solution)/shard_map/all_to_all | solution.py:69
  439.4 2.2 shard_map.331
  442.7 4.0 collective-permute-start.49
  451.7 4.4 all-to-all-start.5
  456.1 2.7 fusion.36
  458.8 28.8 %all-to-all-done.5.parts_ref = bf16[16,128,384]{2,1,0:T(8,128)(2,1)} async-done(((bf16[16,128,384]{2,1,0:T(8,128)(2,1)}), bf16[16,128,384]{2,1,0:T(8,128)(2,1)}, u32[]{:S(2)}, u32[]{:S(2)}) %all-to-all-start.5) | async-done | bytes 1572896 | tf_op jit(solution)/shard_map/all_to_all | solution.py:69
  487.6 2.3 shard_map.332
  490.7 2.8 collective-permute-start.51
  497.4 4.4 shard_map.335
  501.8 2.9 shard_map.334
  504.8 2.9 shard_map.333
  516.5 2.1 shard_map.336
  (471 shorter events, 145.6 us)
Async XLA Ops:
  7.2 69.1 %all-gather.4.cloned.1.call-start = ((), (), s32[]{:S(2)}) async-start(), calls=%async_computation.7 | async-start | bytes 6684672 | tf_op jit(solution)/shard_map/all_gather | solution.py:836
  11.4 140.4 %all-gather.6.cloned.1.call-start = ((), (), s32[]{:S(2)}) async-start(), calls=%async_computation.8 | async-start | bytes 5570560 | tf_op jit(solution)/shard_map/all_gather | solution.py:900
  18.7 15.2 %collective-permute-start.7 = (bf16[32,2048]{1,0:T(8,128)(2,1)S(1)}, bf16[32,2048]{1,0:T(8,128)(2,1)S(1)}, u32[]{:S(2)}, u32[]{:S(2)}) collective-permute-start(bf16[32,2048]{1,0:T(8,128)(2,1)S(1)} %copy-done.78), channel_id=1, source_target_pairs={{0,2},{2,4},{4,6},{6,0},{1,3},{3,5},{5,7},{7,1},{8,10},{10,12},{12... | collective-permute-start | bytes 393224 | tf_op jit(solution)/shard_map/ppermute | solution.py:65
  20.9 16.2 %collective-permute-start.8 = (bf16[32,2048]{1,0:T(8,128)(2,1)S(1)}, bf16[32,2048]{1,0:T(8,128)(2,1)}, u32[]{:S(2)}, u32[]{:S(2)}) collective-permute-start(bf16[32,2048]{1,0:T(8,128)(2,1)S(1)} %copy-done.78), channel_id=1, source_target_pairs={{0,4},{2,6},{4,0},{6,2},{1,5},{3,7},{5,1},{7,3},{8,12},{10,14},{12... | collective-permute-start | bytes 393224 | tf_op jit(solution)/shard_map/ppermute | solution.py:65
  23.5 16.4 %collective-permute-start.9 = (bf16[32,2048]{1,0:T(8,128)(2,1)S(1)}, bf16[32,2048]{1,0:T(8,128)(2,1)S(1)}, u32[]{:S(2)}, u32[]{:S(2)}) collective-permute-start(bf16[32,2048]{1,0:T(8,128)(2,1)S(1)} %copy-done.78), channel_id=1, source_target_pairs={{0,6},{2,0},{4,2},{6,4},{1,7},{3,1},{5,3},{7,5},{8,14},{10,8},{12,... | collective-permute-start | bytes 393224 | tf_op jit(solution)/shard_map/ppermute | solution.py:65
  24.6 11.0 %collective-permute-start = (bf16[32,2048]{1,0:T(8,128)(2,1)S(1)}, bf16[32,2048]{1,0:T(8,128)(2,1)}, u32[]{:S(2)}, u32[]{:S(2)}) collective-permute-start(bf16[32,2048]{1,0:T(8,128)(2,1)S(1)} %copy-done.75), channel_id=1, source_target_pairs={{0,2},{2,4},{4,6},{6,0},{1,3},{3,5},{5,7},{7,1},{8,10},{10,12},{12... | collective-permute-start | bytes 393224 | tf_op jit(solution)/shard_map/ppermute | solution.py:65
  25.0 17.1 %collective-permute-start.1 = (bf16[32,2048]{1,0:T(8,128)(2,1)S(1)}, bf16[32,2048]{1,0:T(8,128)(2,1)S(1)}, u32[]{:S(2)}, u32[]{:S(2)}) collective-permute-start(bf16[32,2048]{1,0:T(8,128)(2,1)S(1)} %copy-done.75), channel_id=1, source_target_pairs={{0,4},{2,6},{4,0},{6,2},{1,5},{3,7},{5,1},{7,3},{8,12},{10,14},{12... | collective-permute-start | bytes 393224 | tf_op jit(solution)/shard_map/ppermute | solution.py:65
  33.9 11.4 %collective-permute-start.2 = (bf16[32,2048]{1,0:T(8,128)(2,1)S(1)}, bf16[32,2048]{1,0:T(8,128)(2,1)S(1)}, u32[]{:S(2)}, u32[]{:S(2)}) collective-permute-start(bf16[32,2048]{1,0:T(8,128)(2,1)S(1)} %copy-done.75), channel_id=1, source_target_pairs={{0,6},{2,0},{4,2},{6,4},{1,7},{3,1},{5,3},{7,5},{8,14},{10,8},{12,... | collective-permute-start | bytes 393224 | tf_op jit(solution)/shard_map/ppermute | solution.py:65
  35.5 17.4 %collective-permute-start.4 = (bf16[176,2048]{1,0:T(8,128)(2,1)}, bf16[176,2048]{1,0:T(8,128)(2,1)S(1)}, u32[]{:S(2)}, u32[]{:S(2)}) collective-permute-start(bf16[176,2048]{1,0:T(8,128)(2,1)} %get-tuple-element.191), channel_id=1, source_target_pairs={{0,2},{2,4},{4,6},{6,0},{1,3},{3,5},{5,7},{7,1},{8,10},{10,12},{12... | collective-permute-start | bytes 2162696 | tf_op jit(solution)/shard_map/ppermute | solution.py:65
  37.1 30.7 %collective-permute-start.5 = (bf16[176,2048]{1,0:T(8,128)(2,1)}, bf16[176,2048]{1,0:T(8,128)(2,1)}, u32[]{:S(2)}, u32[]{:S(2)}) collective-permute-start(bf16[176,2048]{1,0:T(8,128)(2,1)} %get-tuple-element.192), channel_id=1, source_target_pairs={{0,4},{2,6},{4,0},{6,2},{1,5},{3,7},{5,1},{7,3},{8,12},{10,14},{12... | collective-permute-start | bytes 2162696 | tf_op jit(solution)/shard_map/ppermute | solution.py:65
  39.9 31.3 %collective-permute-start.6 = (bf16[176,2048]{1,0:T(8,128)(2,1)}, bf16[176,2048]{1,0:T(8,128)(2,1)}, u32[]{:S(2)}, u32[]{:S(2)}) collective-permute-start(bf16[176,2048]{1,0:T(8,128)(2,1)} %get-tuple-element.193), channel_id=1, source_target_pairs={{0,6},{2,0},{4,2},{6,4},{1,7},{3,1},{5,3},{7,5},{8,14},{10,8},{12,... | collective-permute-start | bytes 2162696 | tf_op jit(solution)/shard_map/ppermute | solution.py:65
  42.1 4.8 collective-permute-start.10
  87.6 55.1 %all-to-all-start = ((bf16[16,40,1024]{2,1,0:T(8,128)(2,1)}), bf16[16,40,1024]{2,1,0:T(8,128)(2,1)}, u32[]{:S(2)}, u32[]{:S(2)}) async-start(bf16[16,40,1024]{2,1,0:T(8,128)(2,1)} %bitcast.272), calls=%async_computation | async-start | bytes 2621440 | tf_op jit(solution)/shard_map/all_to_all | solution.py:69
  92.5 121.0 %all-gather.8.cloned.1.call-start = ((), (), s32[]{:S(2)}) async-start(), calls=%async_computation.9 | async-start | bytes 5013504 | tf_op jit(solution)/shard_map/all_gather | solution.py:914
  92.6 18.3 %collective-permute-start.11 = (bf16[176,2048]{1,0:T(8,128)(2,1)}, bf16[176,2048]{1,0:T(8,128)(2,1)}, u32[]{:S(2)}, u32[]{:S(2)}) collective-permute-start(bf16[176,2048]{1,0:T(8,128)(2,1)} %get-tuple-element.215), channel_id=1, source_target_pairs={{0,2},{2,4},{4,6},{6,0},{1,3},{3,5},{5,7},{7,1},{8,10},{10,12},{12... | collective-permute-start | bytes 2162696 | tf_op jit(solution)/shard_map/ppermute | solution.py:65
  93.9 33.5 %collective-permute-start.12 = (bf16[176,2048]{1,0:T(8,128)(2,1)}, bf16[176,2048]{1,0:T(8,128)(2,1)}, u32[]{:S(2)}, u32[]{:S(2)}) collective-permute-start(bf16[176,2048]{1,0:T(8,128)(2,1)} %get-tuple-element.216), channel_id=1, source_target_pairs={{0,4},{2,6},{4,0},{6,2},{1,5},{3,7},{5,1},{7,3},{8,12},{10,14},{12... | collective-permute-start | bytes 2162696 | tf_op jit(solution)/shard_map/ppermute | solution.py:65
  96.3 31.0 %collective-permute-start.13 = (bf16[176,2048]{1,0:T(8,128)(2,1)}, bf16[176,2048]{1,0:T(8,128)(2,1)}, u32[]{:S(2)}, u32[]{:S(2)}) collective-permute-start(bf16[176,2048]{1,0:T(8,128)(2,1)} %get-tuple-element.217), channel_id=1, source_target_pairs={{0,6},{2,0},{4,2},{6,4},{1,7},{3,1},{5,3},{7,5},{8,14},{10,8},{12,... | collective-permute-start | bytes 2162696 | tf_op jit(solution)/shard_map/ppermute | solution.py:65
  97.5 44.3 %collective-permute-start.14 = (bf16[176,2048]{1,0:T(8,128)(2,1)}, bf16[176,2048]{1,0:T(8,128)(2,1)}, u32[]{:S(2)}, u32[]{:S(2)}) collective-permute-start(bf16[176,2048]{1,0:T(8,128)(2,1)} %get-tuple-element.219), channel_id=1, source_target_pairs={{0,2},{2,4},{4,6},{6,0},{1,3},{3,5},{5,7},{7,1},{8,10},{10,12},{12... | collective-permute-start | bytes 2162696 | tf_op jit(solution)/shard_map/ppermute | solution.py:65
  98.0 44.7 %collective-permute-start.15 = (bf16[176,2048]{1,0:T(8,128)(2,1)}, bf16[176,2048]{1,0:T(8,128)(2,1)}, u32[]{:S(2)}, u32[]{:S(2)}) collective-permute-start(bf16[176,2048]{1,0:T(8,128)(2,1)} %get-tuple-element.220), channel_id=1, source_target_pairs={{0,6},{2,0},{4,2},{6,4},{1,7},{3,1},{5,3},{7,5},{8,14},{10,8},{12,... | collective-permute-start | bytes 2162696 | tf_op jit(solution)/shard_map/ppermute | solution.py:65
  174.2 6.0 %collective-permute-start.17 = (bf16[32,2048]{1,0:T(8,128)(2,1)S(1)}, bf16[32,2048]{1,0:T(8,128)(2,1)S(1)}, u32[]{:S(2)}, u32[]{:S(2)}) collective-permute-start(bf16[32,2048]{1,0:T(8,128)(2,1)S(1)} %get-tuple-element.520), channel_id=1, source_target_pairs={{0,2},{2,4},{4,6},{6,0},{1,3},{3,5},{5,7},{7,1},{8,10},{10,12},{12... | collective-permute-start | bytes 393224 | tf_op jit(solution)/shard_map/ppermute | solution.py:65
  175.5 8.5 %collective-permute-start.18 = (bf16[32,2048]{1,0:T(8,128)(2,1)S(1)}, bf16[32,2048]{1,0:T(8,128)(2,1)S(1)}, u32[]{:S(2)}, u32[]{:S(2)}) collective-permute-start(bf16[32,2048]{1,0:T(8,128)(2,1)S(1)} %get-tuple-element.522), channel_id=1, source_target_pairs={{0,4},{2,6},{4,0},{6,2},{1,5},{3,7},{5,1},{7,3},{8,12},{10,14},{12... | collective-permute-start | bytes 393224 | tf_op jit(solution)/shard_map/ppermute | solution.py:65
  177.9 6.1 %collective-permute-start.19 = (bf16[32,2048]{1,0:T(8,128)(2,1)S(1)}, bf16[32,2048]{1,0:T(8,128)(2,1)S(1)}, u32[]{:S(2)}, u32[]{:S(2)}) collective-permute-start(bf16[32,2048]{1,0:T(8,128)(2,1)S(1)} %get-tuple-element.521), channel_id=1, source_target_pairs={{0,6},{2,0},{4,2},{6,4},{1,7},{3,1},{5,3},{7,5},{8,14},{10,8},{12,... | collective-permute-start | bytes 393224 | tf_op jit(solution)/shard_map/ppermute | solution.py:65
  184.4 5.1 collective-permute-start.20
  185.5 7.1 %collective-permute-start.21 = (bf16[32,2048]{1,0:T(8,128)(2,1)S(1)}, bf16[32,2048]{1,0:T(8,128)(2,1)S(1)}, u32[]{:S(2)}, u32[]{:S(2)}) collective-permute-start(bf16[32,2048]{1,0:T(8,128)(2,1)S(1)} %get-tuple-element.489), channel_id=1, source_target_pairs={{0,4},{2,6},{4,0},{6,2},{1,5},{3,7},{5,1},{7,3},{8,12},{10,14},{12... | collective-permute-start | bytes 393224 | tf_op jit(solution)/shard_map/ppermute | solution.py:65
  187.7 5.2 collective-permute-start.22
  192.9 3.9 collective-permute-start.23
  202.2 20.8 %collective-permute-start.24 = (bf16[640,1024]{1,0:T(8,128)(2,1)}, bf16[640,1024]{1,0:T(8,128)(2,1)}, u32[]{:S(2)}, u32[]{:S(2)}) collective-permute-start(bf16[640,1024]{1,0:T(8,128)(2,1)} %bitcast.42.g_ref), channel_id=1, source_target_pairs={{0,1},{1,0},{2,3},{3,2},{4,5},{5,4},{6,7},{7,6},{8,9},{9,8},{10,11... | collective-permute-start | bytes 3932168 | tf_op jit(solution)/shard_map/ppermute | solution.py:61
  202.5 20.4 %collective-permute-start.25 = (bf16[176,2048]{1,0:T(8,128)(2,1)}, bf16[176,2048]{1,0:T(8,128)(2,1)}, u32[]{:S(2)}, u32[]{:S(2)}) collective-permute-start(bf16[176,2048]{1,0:T(8,128)(2,1)} %get-tuple-element.236), channel_id=1, source_target_pairs={{0,4},{2,6},{4,0},{6,2},{1,5},{3,7},{5,1},{7,3},{8,12},{10,14},{12... | collective-permute-start | bytes 2162696 | tf_op jit(solution)/shard_map/ppermute | solution.py:65
  204.6 27.8 %all-to-all-start.1 = ((bf16[16,40,1152]{2,1,0:T(8,128)(2,1)}), bf16[16,40,1152]{2,1,0:T(8,128)(2,1)}, u32[]{:S(2)}, u32[]{:S(2)}) async-start(bf16[16,40,1152]{2,1,0:T(8,128)(2,1)} %pad_maximum_fusion), calls=%async_computation.1 | async-start | bytes 2949120 | tf_op jit(solution)/shard_map/all_to_all | solution.py:69
  232.4 5.1 collective-permute-start.26
  265.9 6.9 %collective-permute-start.27 = (bf16[640,1152]{1,0:T(8,128)(2,1)}, bf16[640,1152]{1,0:T(8,128)(2,1)S(1)}, u32[]{:S(2)}, u32[]{:S(2)}) collective-permute-start(bf16[640,1152]{1,0:T(8,128)(2,1)} %get-tuple-element.256), channel_id=1, source_target_pairs={{0,1},{1,0},{2,3},{3,2},{4,5},{5,4},{6,7},{7,6},{8,9},{9,8},{10,11... | collective-permute-start | bytes 4423688 | tf_op jit(solution)/shard_map/ppermute | solution.py:61
  274.3 31.2 %all-to-all-start.2 = ((bf16[16,40,1152]{2,1,0:T(8,128)(2,1)}), bf16[16,40,1152]{2,1,0:T(8,128)(2,1)}, u32[]{:S(2)}, u32[]{:S(2)}) async-start(bf16[16,40,1152]{2,1,0:T(8,128)(2,1)} %bitcast.271), calls=%async_computation.2 | async-start | bytes 2949120 | tf_op jit(solution)/shard_map/all_to_all | solution.py:69
  281.6 21.2 %collective-permute-start.28 = (bf16[176,2048]{1,0:T(8,128)(2,1)S(1)}, bf16[176,2048]{1,0:T(8,128)(2,1)S(1)}, u32[]{:S(2)}, u32[]{:S(2)}) collective-permute-start(bf16[176,2048]{1,0:T(8,128)(2,1)S(1)} %get-tuple-element.515), channel_id=1, source_target_pairs={{0,6},{2,0},{4,2},{6,4},{1,7},{3,1},{5,3},{7,5},{8,14},{10,8},{12,... | collective-permute-start | bytes 2162696 | tf_op jit(solution)/shard_map/ppermute | solution.py:65
  286.0 18.6 %collective-permute-start.29 = (bf16[176,2048]{1,0:T(8,128)(2,1)S(1)}, bf16[176,2048]{1,0:T(8,128)(2,1)S(1)}, u32[]{:S(2)}, u32[]{:S(2)}) collective-permute-start(bf16[176,2048]{1,0:T(8,128)(2,1)S(1)} %get-tuple-element.514), channel_id=1, source_target_pairs={{0,2},{2,4},{4,6},{6,0},{1,3},{3,5},{5,7},{7,1},{8,10},{10,12},{12... | collective-permute-start | bytes 2162696 | tf_op jit(solution)/shard_map/ppermute | solution.py:65
  309.8 2.9 collective-permute-start.30
  312.8 6.2 %collective-permute-start.31 = (bf16[32,2176]{1,0:T(8,128)(2,1)S(1)}, bf16[32,2176]{1,0:T(8,128)(2,1)S(1)}, u32[]{:S(2)}, u32[]{:S(2)}) collective-permute-start(bf16[32,2176]{1,0:T(8,128)(2,1)S(1)} %get-tuple-element.517), channel_id=1, source_target_pairs={{0,2},{2,4},{4,6},{6,0},{1,3},{3,5},{5,7},{7,1},{8,10},{10,12},{12... | collective-permute-start | bytes 417800 | tf_op jit(solution)/shard_map/ppermute | solution.py:65
  312.9 9.9 %collective-permute-start.32 = (bf16[32,2176]{1,0:T(8,128)(2,1)S(1)}, bf16[32,2176]{1,0:T(8,128)(2,1)S(1)}, u32[]{:S(2)}, u32[]{:S(2)}) collective-permute-start(bf16[32,2176]{1,0:T(8,128)(2,1)S(1)} %get-tuple-element.519), channel_id=1, source_target_pairs={{0,4},{2,6},{4,0},{6,2},{1,5},{3,7},{5,1},{7,3},{8,12},{10,14},{12... | collective-permute-start | bytes 417800 | tf_op jit(solution)/shard_map/ppermute | solution.py:65
  316.4 6.4 %collective-permute-start.33 = (bf16[32,2176]{1,0:T(8,128)(2,1)S(1)}, bf16[32,2176]{1,0:T(8,128)(2,1)S(1)}, u32[]{:S(2)}, u32[]{:S(2)}) collective-permute-start(bf16[32,2176]{1,0:T(8,128)(2,1)S(1)} %get-tuple-element.518), channel_id=1, source_target_pairs={{0,6},{2,0},{4,2},{6,4},{1,7},{3,1},{5,3},{7,5},{8,14},{10,8},{12,... | collective-permute-start | bytes 417800 | tf_op jit(solution)/shard_map/ppermute | solution.py:65
  324.0 5.1 collective-permute-start.34
  325.2 7.1 %collective-permute-start.35 = (bf16[32,2048]{1,0:T(8,128)(2,1)S(1)}, bf16[32,2048]{1,0:T(8,128)(2,1)S(1)}, u32[]{:S(2)}, u32[]{:S(2)}) collective-permute-start(bf16[32,2048]{1,0:T(8,128)(2,1)S(1)} %get-tuple-element.485), channel_id=1, source_target_pairs={{0,4},{2,6},{4,0},{6,2},{1,5},{3,7},{5,1},{7,3},{8,12},{10,14},{12... | collective-permute-start | bytes 393224 | tf_op jit(solution)/shard_map/ppermute | solution.py:65
  327.4 4.9 collective-permute-start.36
  332.3 4.0 collective-permute-start.37
  336.6 17.5 %collective-permute-start.38 = (bf16[176,2048]{1,0:T(8,128)(2,1)S(1)}, bf16[176,2048]{1,0:T(8,128)(2,1)S(1)}, u32[]{:S(2)}, u32[]{:S(2)}) collective-permute-start(bf16[176,2048]{1,0:T(8,128)(2,1)S(1)} %copy-done.57), channel_id=1, source_target_pairs={{0,6},{2,0},{4,2},{6,4},{1,7},{3,1},{5,3},{7,5},{8,14},{10,8},{12,... | collective-permute-start | bytes 2162696 | tf_op jit(solution)/shard_map/ppermute | solution.py:65
  339.0 18.4 %collective-permute-start.39 = (bf16[176,2048]{1,0:T(8,128)(2,1)S(1)}, bf16[176,2048]{1,0:T(8,128)(2,1)S(1)}, u32[]{:S(2)}, u32[]{:S(2)}) collective-permute-start(bf16[176,2048]{1,0:T(8,128)(2,1)S(1)} %copy-done.55), channel_id=1, source_target_pairs={{0,2},{2,4},{4,6},{6,0},{1,3},{3,5},{5,7},{7,1},{8,10},{10,12},{12... | collective-permute-start | bytes 2162696 | tf_op jit(solution)/shard_map/ppermute | solution.py:65
  357.4 9.5 %collective-permute-start.40 = (bf16[4,16,32,640]{3,2,1,0:T(8,128)(2,1)S(1)}, bf16[4,16,32,640]{3,2,1,0:T(8,128)(2,1)S(1)}, u32[]{:S(2)}, u32[]{:S(2)}) collective-permute-start(bf16[4,16,32,640]{3,2,1,0:T(8,128)(2,1)S(1)} %get-tuple-element.288), channel_id=1, source_target_pairs={{0,1},{1,0},{2,3},{3,2},{4,5},{5,4},{6,7},{7,6},{8,9},{9,8},{10,11... | collective-permute-start | bytes 7864328 | tf_op jit(solution)/shard_map/ppermute | solution.py:61
  358.9 6.4 %collective-permute-start.41 = (bf16[640,1024]{1,0:T(8,128)(2,1)S(1)}, bf16[640,1024]{1,0:T(8,128)(2,1)S(1)}, u32[]{:S(2)}, u32[]{:S(2)}) collective-permute-start(bf16[640,1024]{1,0:T(8,128)(2,1)S(1)} %copy-done.103), channel_id=1, source_target_pairs={{0,1},{1,0},{2,3},{3,2},{4,5},{5,4},{6,7},{7,6},{8,9},{9,8},{10,11... | collective-permute-start | bytes 3932168 | tf_op jit(solution)/shard_map/ppermute | solution.py:61
  369.0 39.6 %all-to-all-start.3 = ((bf16[16,40,1024]{2,1,0:T(8,128)(2,1)}), bf16[16,40,1024]{2,1,0:T(8,128)(2,1)}, u32[]{:S(2)}, u32[]{:S(2)}) async-start(bf16[16,40,1024]{2,1,0:T(8,128)(2,1)} %bitcast.275), calls=%async_computation.3 | async-start | bytes 2621440 | tf_op jit(solution)/shard_map/all_to_all | solution.py:69
  375.8 140.7 %reduce-scatter.2.cloned.1.call-start = ((), (), s32[]{:S(2)}) async-start(), calls=%async_computation.10 | async-start | bytes 8355840 | tf_op jit(solution)/shard_map/reduce_scatter | solution.py:1044
  375.8 31.2 %collective-permute-start.42 = (bf16[16,32,640]{2,1,0:T(8,128)(2,1)}, bf16[16,32,640]{2,1,0:T(8,128)(2,1)S(1)}, u32[]{:S(2)}, u32[]{:S(2)}) collective-permute-start(bf16[16,32,640]{2,1,0:T(8,128)(2,1)} %get-tuple-element.294), channel_id=1, source_target_pairs={{0,2},{2,4},{4,6},{6,0},{1,3},{3,5},{5,7},{7,1},{8,10},{10,12},{12... | collective-permute-start | bytes 1966088 | tf_op jit(solution)/shard_map/ppermute | solution.py:65
  375.9 31.1 %collective-permute-start.43 = (bf16[16,32,640]{2,1,0:T(8,128)(2,1)}, bf16[16,32,640]{2,1,0:T(8,128)(2,1)S(1)}, u32[]{:S(2)}, u32[]{:S(2)}) collective-permute-start(bf16[16,32,640]{2,1,0:T(8,128)(2,1)} %get-tuple-element.295), channel_id=1, source_target_pairs={{0,4},{2,6},{4,0},{6,2},{1,5},{3,7},{5,1},{7,3},{8,12},{10,14},{12... | collective-permute-start | bytes 1966088 | tf_op jit(solution)/shard_map/ppermute | solution.py:65
  377.0 30.4 %collective-permute-start.44 = (bf16[16,32,640]{2,1,0:T(8,128)(2,1)}, bf16[16,32,640]{2,1,0:T(8,128)(2,1)S(1)}, u32[]{:S(2)}, u32[]{:S(2)}) collective-permute-start(bf16[16,32,640]{2,1,0:T(8,128)(2,1)} %get-tuple-element.296), channel_id=1, source_target_pairs={{0,6},{2,0},{4,2},{6,4},{1,7},{3,1},{5,3},{7,5},{8,14},{10,8},{12,... | collective-permute-start | bytes 1966088 | tf_op jit(solution)/shard_map/ppermute | solution.py:65
  408.5 25.7 %collective-permute-start.45 = (bf16[176,2048]{1,0:T(8,128)(2,1)}, bf16[176,2048]{1,0:T(8,128)(2,1)}, u32[]{:S(2)}, u32[]{:S(2)}) collective-permute-start(bf16[176,2048]{1,0:T(8,128)(2,1)} %get-tuple-element.309), channel_id=1, source_target_pairs={{0,6},{2,0},{4,2},{6,4},{1,7},{3,1},{5,3},{7,5},{8,14},{10,8},{12,... | collective-permute-start | bytes 2162696 | tf_op jit(solution)/shard_map/ppermute | solution.py:65
  411.6 22.7 %collective-permute-start.46 = (bf16[176,2048]{1,0:T(8,128)(2,1)}, bf16[176,2048]{1,0:T(8,128)(2,1)}, u32[]{:S(2)}, u32[]{:S(2)}) collective-permute-start(bf16[176,2048]{1,0:T(8,128)(2,1)} %get-tuple-element.310), channel_id=1, source_target_pairs={{0,2},{2,4},{4,6},{6,0},{1,3},{3,5},{5,7},{7,1},{8,10},{10,12},{12... | collective-permute-start | bytes 2162696 | tf_op jit(solution)/shard_map/ppermute | solution.py:65
  411.6 22.6 %all-to-all-start.4 = ((bf16[16,32,640]{2,1,0:T(8,128)(2,1)}), bf16[16,32,640]{2,1,0:T(8,128)(2,1)S(1)}, u32[]{:S(2)}, u32[]{:S(2)}) async-start(bf16[16,32,640]{2,1,0:T(8,128)(2,1)} %add_convert_fusion.2), calls=%async_computation.4 | async-start | bytes 1310720 | tf_op jit(solution)/shard_map/all_to_all | solution.py:69
  438.1 49.5 %collective-permute-start.48 = (bf16[528,2048]{1,0:T(8,128)(2,1)}, bf16[528,2048]{1,0:T(8,128)(2,1)S(1)}, u32[]{:S(2)}, u32[]{:S(2)}) collective-permute-start(bf16[528,2048]{1,0:T(8,128)(2,1)} %copy-done.51), channel_id=1, source_target_pairs={{0,4},{2,6},{4,0},{6,2},{1,5},{3,7},{5,1},{7,3},{8,12},{10,14},{12... | collective-permute-start | bytes 6488072 | tf_op jit(solution)/shard_map/ppermute | solution.py:65
  442.7 13.4 %collective-permute-start.49 = (bf16[4,32,4096]{2,1,0:T(8,128)(2,1)}, bf16[4,32,4096]{2,1,0:T(8,128)(2,1)}, u32[]{:S(2)}, u32[]{:S(2)}) collective-permute-start(bf16[4,32,4096]{2,1,0:T(8,128)(2,1)} %dynamic-slice_bitcast_fusion), channel_id=1, source_target_pairs={{0,1},{1,0},{2,3},{3,2},{4,5},{5,4},{6,7},{7,6},{8,9},{9,8},{10,11... | collective-permute-start | bytes 3145736 | tf_op jit(solution)/shard_map/ppermute | solution.py:61
  451.7 35.9 %all-to-all-start.5 = ((bf16[16,128,384]{2,1,0:T(8,128)(2,1)}), bf16[16,128,384]{2,1,0:T(8,128)(2,1)}, u32[]{:S(2)}, u32[]{:S(2)}) async-start(bf16[16,128,384]{2,1,0:T(8,128)(2,1)} %bitcast.260), calls=%async_computation.5 | async-start | bytes 3145728 | tf_op jit(solution)/shard_map/all_to_all | solution.py:69
  489.8 5.8 %collective-permute-start.50 = (bf16[128,384]{1,0:T(8,128)(2,1)}, bf16[128,384]{1,0:T(8,128)(2,1)S(1)}, u32[]{:S(2)}, u32[]{:S(2)}) collective-permute-start(bf16[128,384]{1,0:T(8,128)(2,1)} %shard_map.332), channel_id=1, source_target_pairs={{0,2},{2,4},{4,6},{6,0},{1,3},{3,5},{5,7},{7,1},{8,10},{10,12},{12... | collective-permute-start | bytes 294920 | tf_op jit(solution)/shard_map/ppermute | solution.py:65
  490.7 17.1 %collective-permute-start.51 = (bf16[128,384]{1,0:T(8,128)(2,1)}, bf16[128,384]{1,0:T(8,128)(2,1)S(1)}, u32[]{:S(2)}, u32[]{:S(2)}) collective-permute-start(bf16[128,384]{1,0:T(8,128)(2,1)} %shard_map.332), channel_id=1, source_target_pairs={{0,4},{2,6},{4,0},{6,2},{1,5},{3,7},{5,1},{7,3},{8,12},{10,14},{12... | collective-permute-start | bytes 294920 | tf_op jit(solution)/shard_map/ppermute | solution.py:65
  493.5 14.3 %collective-permute-start.52 = (bf16[128,384]{1,0:T(8,128)(2,1)}, bf16[128,384]{1,0:T(8,128)(2,1)S(1)}, u32[]{:S(2)}, u32[]{:S(2)}) collective-permute-start(bf16[128,384]{1,0:T(8,128)(2,1)} %shard_map.332), channel_id=1, source_target_pairs={{0,6},{2,0},{4,2},{6,4},{1,7},{3,1},{5,3},{7,5},{8,14},{10,8},{12,... | collective-permute-start | bytes 294920 | tf_op jit(solution)/shard_map/ppermute | solution.py:65
  494.4 13.4 %collective-permute-start.53 = (bf16[32,4096]{1,0:T(8,128)(2,1)}, bf16[32,4096]{1,0:T(8,128)(2,1)S(1)}, u32[]{:S(2)}, u32[]{:S(2)}) collective-permute-start(bf16[32,4096]{1,0:T(8,128)(2,1)} %get-tuple-element.332), channel_id=1, source_target_pairs={{0,2},{2,4},{4,6},{6,0},{1,3},{3,5},{5,7},{7,1},{8,10},{10,12},{12... | collective-permute-start | bytes 786440 | tf_op jit(solution)/shard_map/ppermute | solution.py:65
  495.0 13.1 %collective-permute-start.54 = (bf16[32,4096]{1,0:T(8,128)(2,1)}, bf16[32,4096]{1,0:T(8,128)(2,1)S(1)}, u32[]{:S(2)}, u32[]{:S(2)}) collective-permute-start(bf16[32,4096]{1,0:T(8,128)(2,1)} %get-tuple-element.333), channel_id=1, source_target_pairs={{0,4},{2,6},{4,0},{6,2},{1,5},{3,7},{5,1},{7,3},{8,12},{10,14},{12... | collective-permute-start | bytes 786440 | tf_op jit(solution)/shard_map/ppermute | solution.py:65
  495.6 14.5 %collective-permute-start.55 = (bf16[32,4096]{1,0:T(8,128)(2,1)}, bf16[32,4096]{1,0:T(8,128)(2,1)S(1)}, u32[]{:S(2)}, u32[]{:S(2)}) collective-permute-start(bf16[32,4096]{1,0:T(8,128)(2,1)} %get-tuple-element.334), channel_id=1, source_target_pairs={{0,6},{2,0},{4,2},{6,4},{1,7},{3,1},{5,3},{7,5},{8,14},{10,8},{12,... | collective-permute-start | bytes 786440 | tf_op jit(solution)/shard_map/ppermute | solution.py:65
  510.3 2.8 collective-permute-start.56
  (111 other events, 1259.4 us)
Sparse Core Ops, SparseCore 0:
  11.5 64.7 all-gather.3
  87.7 64.0 all-gather.5
  154.5 58.9 all-gather.7
  408.7 104.7 reduce-scatter.1
